TPU v7x, 32 devices: a whole 2x2x4 slice. The times are simulated.
32 devices in a mesh: dp: 16 (over z, y, x), space: 2 (over core).
Axes of the slice: x: 2, y: 2, z: 4, core: 2. Of those that a mesh axis runs over, the one named last changes fastest.
Arguments:
- features: bfloat16 [16, 16, 96, 512], P('dp', 'space'), may hold values from -6 to 6
- top_down: bfloat16 [16, 8, 48, 256], P('dp', 'space'), may hold values from -6 to 6
- lateral_weight: bfloat16 [512, 256], replicated, may hold values from -0.25 to 0.25
- out_kernel: bfloat16 [3, 3, 256, 256], replicated, may hold values from -0.125 to 0.125
- cotangent: bfloat16 [16, 16, 96, 256], P('dp', 'space'), may hold values from -1.5 to 1.5
Outputs:
- p3_out: bfloat16 [16, 16, 96, 256], P('dp', 'space')
- grad_top: bfloat16 [16, 8, 48, 256], P('dp', 'space')
- grad_kernel: bfloat16 [3, 3, 256, 256], replicated
- grad_lateral: bfloat16 [512, 256], replicated
All inputs are finite; a program needn't handle non-finite values.
Results may differ from a plain program's by a relative error of at most 0.0053.
Values may be sent and summed in bfloat16 or wider, within the bound.
No kernel may reach another device: no remote copies, remote signals or barrier semaphores. Data moves between devices by JAX's collectives and lax.ppermute only.
A program may use at most 64 MiB of HBM per device.

v0:
```python
import jax
import jax.numpy as jnp
from jax import lax
from jax.sharding import PartitionSpec as P


def with_halo(array, sides, width):
    for axis, dim in sides:
        peers, length = (lax.axis_size(axis), array.shape[dim])
        up = [(i, (i + 1) % peers) for i in range(peers - 1)]
        down = [(j, i) for i, j in up]
        last = lax.slice_in_dim(array, length - width, length, axis=dim)
        initial = lax.slice_in_dim(array, 0, width, axis=dim)
        before = lax.ppermute(last, axis, up)
        after = lax.ppermute(initial, axis, down)
        array = jnp.concatenate([before, array, after], axis=dim)
    return array


def row_band(source, tap_row, row_count, col_count):
    pieces = [
        source[:, tap_row : tap_row + row_count, tap_col : tap_col + col_count, :]
        for tap_col in range(3)
    ]
    joined = jnp.concatenate(pieces, axis=-1)
    return joined.reshape(-1, joined.shape[-1])


def local(features, top_down, lateral_weight, out_kernel, cotangent):
    image_count, row_count, col_count, in_channels = features.shape
    channels = lateral_weight.shape[1]
    cell_count = image_count * row_count * col_count
    flat_feat = features.reshape(cell_count, in_channels)
    lateral = jnp.dot(flat_feat, lateral_weight, preferred_element_type=jnp.float32).reshape(
        image_count, row_count, col_count, channels
    )
    upsampled = jnp.repeat(jnp.repeat(top_down, 2, axis=1), 2, axis=2).astype(jnp.float32)
    merged = (lateral + upsampled).astype(jnp.bfloat16)
    merged_rows = with_halo(merged, (("space", 1),), 1)
    padded = jnp.pad(merged_rows, ((0, 0), (0, 0), (1, 1), (0, 0)))
    forward_stack = out_kernel.reshape(3, 3 * channels, channels)
    flat_cot = cotangent.reshape(cell_count, channels)
    output = jnp.zeros((cell_count, channels), jnp.float32)
    kernel_terms = []
    for tap_row in range(3):
        strip = row_band(padded, tap_row, row_count, col_count)
        output = output + jnp.dot(strip, forward_stack[tap_row], preferred_element_type=jnp.float32)
        kernel_terms.append(
            lax.dot_general(
                strip, flat_cot, (((0,), (0,)), ((), ())), preferred_element_type=jnp.float32
            ).reshape(3, channels, channels)
        )
    p3_out = output.astype(jnp.bfloat16).reshape(image_count, row_count, col_count, channels)
    kernel_part = jnp.stack(kernel_terms)
    cot_rows = with_halo(cotangent, (("space", 1),), 1)
    cot_padded = jnp.pad(cot_rows, ((0, 0), (0, 0), (1, 1), (0, 0)))
    backward_stack = jnp.transpose(out_kernel[:, ::-1], (0, 1, 3, 2)).reshape(
        3, 3 * channels, channels
    )
    grad_acc = jnp.zeros((cell_count, channels), jnp.float32)
    for tap_row in range(3):
        strip = row_band(cot_padded, 2 - tap_row, row_count, col_count)
        grad_acc = grad_acc + jnp.dot(
            strip, backward_stack[tap_row], preferred_element_type=jnp.float32
        )
    grad_merged = grad_acc.astype(jnp.bfloat16)
    grad_top = (
        grad_merged.astype(jnp.float32)
        .reshape(image_count, row_count // 2, 2, col_count // 2, 2, channels)
        .sum(axis=(2, 4))
        .astype(jnp.bfloat16)
    )
    lateral_part = lax.dot_general(
        flat_feat, grad_merged, (((0,), (0,)), ((), ())), preferred_element_type=jnp.float32
    )
    total_images = image_count * lax.axis_size("dp")
    kernel_total, lateral_total = lax.psum((kernel_part, lateral_part), ("dp", "space"))
    grad_kernel = (kernel_total / total_images).astype(jnp.bfloat16)
    grad_lateral = (lateral_total / total_images).astype(jnp.bfloat16)
    return (p3_out, grad_top, grad_kernel, grad_lateral)


def solution(mesh):
    return jax.shard_map(
        local,
        mesh=mesh,
        in_specs=(
            P("dp", "space", None, None),
            P("dp", "space", None, None),
            P(),
            P(),
            P("dp", "space", None, None),
        ),
        out_specs=(P("dp", "space", None, None), P("dp", "space", None, None), P(), P()),
        check_vma=False,
    )
```

profile of v0, /device:TPU:0, one launch (start us, length us, event | category | flops | bytes accessed | tf_op | source)
XLA Modules:
  0.0 198.7 jit_solution(5310826414376496113)
XLA Ops:
  7.2 1.5 fusion.21
  8.8 3.0 %collective-permute-start.2 = (bf16[1,1,96,256]{3,2,1,0:T(8,128)(2,1)}, bf16[1,1,96,256]{3,2,1,0:T(8,128)(2,1)}, u32[]{:S(2)}, u32[]{:S(2)}) collective-permute-start(bf16[1,1,96,256]{3,2,1,0:T(8,128)(2,1)} %get-tuple-element.35), channel_id=1, source_target_pairs={{0,1},{2,3},{4,5},{6,7},{8,9},{10,11},{12,13},{14,15},{16,17},{18,... | collective-permute-start | bytes 147464 | tf_op jit(solution)/shard_map/ppermute | solution.py:14
  11.7 1.3 collective-permute-start.3
  13.0 0.9 bitcast_convert_fusion
  15.3 0.7 fusion.22
  16.0 1.3 collective-permute-start.1
  17.3 4.8 %collective-permute-start = (bf16[1,1,96,256]{3,2,1,0:T(8,128)(2,1)}, bf16[1,1,96,256]{3,2,1,0:T(8,128)(2,1)}, u32[]{:S(2)}, u32[]{:S(2)}) collective-permute-start(bf16[1,1,96,256]{3,2,1,0:T(8,128)(2,1)} %get-tuple-element.40), channel_id=1, source_target_pairs={{0,1},{2,3},{4,5},{6,7},{8,9},{10,11},{12,13},{14,15},{16,17},{18,... | collective-permute-start | bytes 147464 | tf_op jit(solution)/shard_map/ppermute | solution.py:14
  22.1 0.7 copy.13
  22.9 1.0 fusion.17
  24.1 1.0 select_maximum_fusion
  25.1 1.5 fusion.19
  26.6 1.0 select_maximum_fusion.2
  27.6 1.4 fusion.20
  29.0 0.7 copy-done.8
  29.8 1.4 copy.15
  31.3 1.8 fusion.8
  33.0 1.5 copy.14
  34.5 2.7 %convolution_bitcast_fusion.1 = f32[1,3,256,256]{3,2,1,0:T(8,128)} fusion(bf16[3,256,768]{2,1,0:T(8,128)(2,1)} %bitcast.83, bf16[768,256,1]{1,0,2:T(8,128)(2,1)S(1)} %bitcast.70), kind=kOutput, calls=%fused_computation.5 | convolution fusion | flops 301989888 | bytes 2359296 | tf_op jit(solution)/shard_map/dot_general | solution.py:49
  37.2 1.4 convolution_bitcast_fusion.2
  38.6 1.4 copy.16
  40.1 1.9 convolution_bitcast_fusion
  42.1 1.2 fusion.4
  45.8 1.2 convolution_bitcast_fusion.3
  47.3 1.6 pad_maximum_fusion
  48.9 2.3 %fusion.18 = (bf16[1,3,256,256]{3,2,1,0:T(8,128)(2,1)}, bf16[1,3,256,256]{3,2,1,0:T(8,128)(2,1)}, bf16[1,3,256,256]{3,2,1,0:T(8,128)(2,1)}) fusion(bf16[3,3,256,256]{3,2,1,0:T(8,128)(2,1)} %param.8), kind=kLoop, calls=%fused_computation.44 | loop fusion | bytes 2359296 | tf_op jit(solution)/shard_map/slice | solution.py:47
  51.2 0.9 reshape.110
  52.1 2.3 %reduce.1 = bf16[4,48,256]{2,1,0:T(8,128)(2,1)} reduce(bf16[4,2,48,2,256]{4,3,2,1,0:T(2,128)(2,1)} %reshape.110, bf16[]{:T(256)} %constant.3.clone.1), dimensions={1,3}, to_apply=%region_0.1.clone | reduce | flops 147456 | bytes 491522 | tf_op jit(solution)/shard_map/reduce_sum | solution.py:70
  54.4 1.6 fusion.23
  57.1 1.2 fusion.1
  58.3 129.6 %all-reduce.5.cloned.1.call-done = (f32[3,3,256,256]{3,2,1,0:T(8,128)}, f32[512,256]{0,1:T(8,128)}) async-done(((f32[3,3,256,256]{3,2,1,0:T(8,128)}, f32[512,256]{0,1:T(8,128)}), (f32[3,3,256,256]{3,2,1,0:T(8,128)}, f32[512,256]{0,1:T(8,128)})) %all-reduce.5.cloned.1.call-update) | async-done | bytes 2883600 | tf_op jit(solution)/shard_map/psum | solution.py:77
  188.0 3.0 %multiply_convert_fusion = bf16[3,3,256,256]{3,2,1,0:T(8,128)(2,1)} fusion(f32[3,3,256,256]{3,2,1,0:T(8,128)} %get-tuple-element.12), kind=kLoop, calls=%fused_computation.1 | loop fusion | flops 1179648 | bytes 3538944 | tf_op jit(solution)/shard_map/convert_element_type | solution.py:78
  191.0 0.8 copy.17
  (66 shorter events, 5.7 us)
Async XLA Ops:
  7.2 7.6 %copy-start = (bf16[1,8,96,512]{3,2,1,0:T(8,128)(2,1)S(1)}, bf16[1,8,96,512]{3,2,1,0:T(8,128)(2,1)}, u32[]{:S(2)}) copy-start(bf16[1,8,96,512]{3,2,1,0:T(8,128)(2,1)} %param.5) | copy-start | bytes 2359300
  7.2 180.8 %all-reduce.5.cloned.1.call-start = ((), (), s32[]{:S(2)}) async-start(), calls=%async_computation | async-start | bytes 5767168 | tf_op jit(solution)/shard_map/psum | solution.py:77
  8.8 15.2 %collective-permute-start.2 = (bf16[1,1,96,256]{3,2,1,0:T(8,128)(2,1)}, bf16[1,1,96,256]{3,2,1,0:T(8,128)(2,1)}, u32[]{:S(2)}, u32[]{:S(2)}) collective-permute-start(bf16[1,1,96,256]{3,2,1,0:T(8,128)(2,1)} %get-tuple-element.35), channel_id=1, source_target_pairs={{0,1},{2,3},{4,5},{6,7},{8,9},{10,11},{12,13},{14,15},{16,17},{18,... | collective-permute-start | bytes 147464 | tf_op jit(solution)/shard_map/ppermute | solution.py:14
  11.7 12.3 %collective-permute-start.3 = (bf16[1,1,96,256]{3,2,1,0:T(8,128)(2,1)}, bf16[1,1,96,256]{3,2,1,0:T(8,128)(2,1)}, u32[]{:S(2)}, u32[]{:S(2)}) collective-permute-start(bf16[1,1,96,256]{3,2,1,0:T(8,128)(2,1)} %get-tuple-element.36), channel_id=1, source_target_pairs={{1,0},{3,2},{5,4},{7,6},{9,8},{11,10},{13,12},{15,14},{17,16},{19,... | collective-permute-start | bytes 147464 | tf_op jit(solution)/shard_map/ppermute | solution.py:15
  14.0 1.0 copy-start.24
  14.9 7.2 %copy-start.4 = (bf16[3,3,256,256]{3,2,1,0:T(8,128)(2,1)S(1)}, bf16[3,3,256,256]{3,2,1,0:T(8,128)(2,1)}, u32[]{:S(2)}) copy-start(bf16[3,3,256,256]{3,2,1,0:T(8,128)(2,1)} %param.8) | copy-start | bytes 3538948
  15.3 13.6 %copy-start.2 = (bf16[8,96,256]{2,1,0:T(8,128)(2,1)}, bf16[8,96,256]{2,1,0:T(8,128)(2,1)S(1)}, u32[]{:S(2)}) copy-start(bf16[8,96,256]{2,1,0:T(8,128)(2,1)S(1)} %fusion) | copy-start | bytes 1179652
  16.0 10.6 %collective-permute-start.1 = (bf16[1,1,96,256]{3,2,1,0:T(8,128)(2,1)}, bf16[1,1,96,256]{3,2,1,0:T(8,128)(2,1)}, u32[]{:S(2)}, u32[]{:S(2)}) collective-permute-start(bf16[1,1,96,256]{3,2,1,0:T(8,128)(2,1)} %get-tuple-element.39), channel_id=1, source_target_pairs={{1,0},{3,2},{5,4},{7,6},{9,8},{11,10},{13,12},{15,14},{17,16},{19,... | collective-permute-start | bytes 147464 | tf_op jit(solution)/shard_map/ppermute | solution.py:15
  17.3 9.3 %collective-permute-start = (bf16[1,1,96,256]{3,2,1,0:T(8,128)(2,1)}, bf16[1,1,96,256]{3,2,1,0:T(8,128)(2,1)}, u32[]{:S(2)}, u32[]{:S(2)}) collective-permute-start(bf16[1,1,96,256]{3,2,1,0:T(8,128)(2,1)} %get-tuple-element.40), channel_id=1, source_target_pairs={{0,1},{2,3},{4,5},{6,7},{8,9},{10,11},{12,13},{14,15},{16,17},{18,... | collective-permute-start | bytes 147464 | tf_op jit(solution)/shard_map/ppermute | solution.py:14
  22.9 1.2 copy-start.1
  28.9 0.8 copy-start.8
  28.9 0.9 copy-start.10
  34.5 2.7 %copy-start.5 = (bf16[768,768]{1,0:T(8,128)(2,1)S(1)}, bf16[768,768]{1,0:T(8,128)(2,1)}, u32[]{:S(2)}) copy-start(bf16[768,768]{1,0:T(8,128)(2,1)} %copy.14) | copy-start | bytes 3538948
  40.0 1.9 copy-start.14
  40.0 1.9 copy-start.15
  40.1 2.0 copy-start.16
  40.1 2.0 copy-start.17
  40.1 2.0 copy-start.18
  40.1 2.0 copy-start.19
  42.0 1.3 copy-start.13
  43.3 1.0 copy-start.12
  44.3 1.0 copy-start.20
  45.8 1.2 copy-start.6
  45.8 1.5 copy-start.7
  54.4 1.6 copy-start.3
  54.4 1.6 copy-start.9
  54.4 1.6 copy-start.11
  54.4 1.6 copy-start.23
  56.0 1.1 copy-start.21
  188.0 3.0 %copy-start.22 = (f32[512,256]{0,1:T(8,128)S(1)}, f32[512,256]{0,1:T(8,128)}, u32[]{:S(2)}) copy-start(f32[512,256]{0,1:T(8,128)} %get-tuple-element.13) | copy-start | bytes 1572868
Sparse Core Ops, SparseCore 0:
  49.0 138.8 all-reduce.4
where the time goes:
time: 199 us
  waiting for transfers between devices  130 us (65%)
  local copies, waits for them, and re-layouts  19.2 us (10%)
  between operations  14.4 us (7%)
  other arithmetic  12.8 us (6%)
  matrix products  12.2 us (6%)
  starting transfers between devices  10.4 us (5%)
    psum x1, waiting for transfers between devices, local(): lax.psum((kernel_part, lateral_part), ('dp', 'space'))  130 us
    ppermute x2, starting transfers between devices, with_halo(): before = lax.ppermute(last, axis, up)  7.81 us
    dot_general x3, matrix products, local(): lax.dot_general(strip, flat_cot, (((0,), (0,)), ((), ())), preferred_elem...  5.98 us
    unnamed x52, local copies, waits for them, and re-layouts  4.58 us
    dot_general x3, local copies, waits for them, and re-layouts, local(): lax.dot_general(strip, flat_cot, (((0,), (0,)), ((), ())), preferred_elem...  4.36 us
  transfers between devices with their start and end apart: 5, of which 1 were waited for; matrix products, arithmetic and copies ran while one was open for 8% of the time, Pallas kernels for 0%

commit v1 on v0

v1 whole, which is shorter than its diff:
```python
import functools

import jax
import jax.numpy as jnp
from jax import lax
from jax.experimental import pallas as pl
from jax.experimental.pallas import tpu as pltpu
from jax.sharding import PartitionSpec as P

F32 = jnp.float32
BF16 = jnp.bfloat16


def neighbour_rows(array):
    peers = lax.axis_size("space")
    rows = array.shape[0]
    if peers == 1:
        return array[0], array[0]
    if peers == 2:
        here = lax.axis_index("space")
        edge = lax.dynamic_index_in_dim(array, (1 - here) * (rows - 1), 0, keepdims=False)
        got = lax.ppermute(edge, "space", [(0, 1), (1, 0)])
        return got, got
    up = [(i, i + 1) for i in range(peers - 1)]
    down = [(j, i) for i, j in up]
    return lax.ppermute(array[-1], "space", up), lax.ppermute(array[0], "space", down)


def put_shifted(stack, slot, row, sign):
    cols, channels = row.shape
    wide = row.astype(F32)
    place = lax.broadcasted_iota(jnp.int32, (cols, channels), 0)
    later = jnp.where(place == cols - 1, 0.0, pltpu.roll(wide, cols - 1, 0)).astype(BF16)
    earlier = jnp.where(place == 0, 0.0, pltpu.roll(wide, 1, 0)).astype(BF16)
    first, last = (earlier, later) if sign < 0 else (later, earlier)
    stack[slot, :, 0:channels] = first
    stack[slot, :, channels : 2 * channels] = row
    stack[slot, :, 2 * channels :] = last


def put_halo(stack, before, after, rows, peers, sign):
    here = lax.axis_index("space")
    zero = jnp.zeros(before.shape, BF16)
    put_shifted(stack, 0, jnp.where(here > 0, before[...], zero), sign)
    put_shifted(stack, rows + 1, jnp.where(here < peers - 1, after[...], zero), sign)


def grads_kernel(peers, feat, top, lat_w, out_w, cot, before, after, merged, grad_top, *rest):
    outs, stack = rest[:-1], rest[-1]
    rows, cols, channels = cot.shape
    cells = rows * cols
    half = cols // 2
    in_channels = lat_w.shape[0]
    upper = lax.broadcasted_iota(jnp.int32, (cols, half), 0)
    spread = jnp.where(upper // 2 == lax.broadcasted_iota(jnp.int32, (cols, half), 1), 1.0, 0.0).astype(BF16)
    lateral = jnp.dot(feat[...], lat_w[...], preferred_element_type=F32)
    for q in range(rows // 2):
        lifted = jnp.dot(spread, top[q], preferred_element_type=F32)
        for r in (2 * q, 2 * q + 1):
            merged[r * cols : (r + 1) * cols, :] = (lateral[r * cols : (r + 1) * cols] + lifted).astype(BF16)
    for r in range(rows):
        put_shifted(stack, r + 1, cot[r], 1)
    put_halo(stack, before, after, rows, peers, 1)

    def put(start, block):
        if len(outs) == 1:
            outs[0][start : start + block.shape[0], :] = block
            return
        here = lax.axis_index("space")
        left, right = block[:, : channels // 2], block[:, channels // 2 :]
        mine, theirs = outs
        mine[start : start + block.shape[0], :] = jnp.where(here == 0, left, right)
        theirs[start : start + block.shape[0], :] = jnp.where(here == 0, right, left).astype(BF16)

    merged_t = jnp.transpose(merged[...])
    for i in range(3):
        strip = stack[2 - i : 2 - i + rows].reshape(cells, 3 * channels)
        part = jnp.dot(merged_t, strip, preferred_element_type=F32)
        for j in range(3):
            put((3 * i + j) * channels, part[:, j * channels : (j + 1) * channels])
    total = jnp.zeros((cells, channels), F32)
    for i in range(3):
        strip = stack[2 - i : 2 - i + rows].reshape(cells, 3 * channels)
        taps = jnp.concatenate([out_w[3 * i + j] for j in range(3)], axis=1)
        total = total + lax.dot_general(strip, taps, (((1,), (1,)), ((), ())), preferred_element_type=F32)
    grad = total.astype(BF16)
    lower = lax.broadcasted_iota(jnp.int32, (half, 2 * cols), 1)
    lower = jnp.where(lower >= cols, lower - cols, lower)
    pool = jnp.where(lower // 2 == lax.broadcasted_iota(jnp.int32, (half, 2 * cols), 0), 1.0, 0.0).astype(BF16)
    for q in range(rows // 2):
        pair = grad[2 * q * cols : (2 * q + 2) * cols]
        grad_top[q] = jnp.dot(pool, pair, preferred_element_type=F32).astype(BF16)
    feat_t = jnp.transpose(feat[...])
    put(9 * channels, jnp.dot(feat_t, grad, preferred_element_type=F32))


def forward_kernel(peers, merged, out_w, before, after, out, stack):
    rows, cols, channels = merged.shape
    for r in range(rows):
        put_shifted(stack, r + 1, merged[r], -1)
    put_halo(stack, before, after, rows, peers, -1)
    total = jnp.zeros((rows * cols, channels), F32)
    for i in range(3):
        strip = stack[i : i + rows].reshape(rows * cols, 3 * channels)
        taps = out_w[3 * i : 3 * i + 3].reshape(3 * channels, channels)
        total = total + jnp.dot(strip, taps, preferred_element_type=F32)
    out[...] = total.astype(BF16).reshape(out.shape)


def sum_everywhere(mine, theirs, scale):
    length, width = mine.shape
    parts = lax.axis_size("dp")
    swap = [(0, 1), (1, 0)]
    got = lax.ppermute(theirs, "space", swap)
    pair = (mine + got.astype(F32)).astype(BF16)
    share = -(-length // (16 * parts)) * 16
    pair = jnp.pad(pair, ((0, share * parts - length), (0, 0))).reshape(parts, share, width)
    terms = lax.all_to_all(pair, "dp", 0, 0, tiled=True)
    total = (jnp.sum(terms.astype(F32), axis=0) * scale).astype(BF16)
    copies = jnp.broadcast_to(total[None], terms.shape)
    whole = lax.all_to_all(copies, "dp", 0, 0, tiled=True).reshape(parts * share, width)[:length]
    other = lax.ppermute(whole, "space", swap)
    first = lax.axis_index("space") == 0
    return jnp.concatenate([jnp.where(first, whole, other), jnp.where(first, other, whole)], axis=1)


def local(features, top_down, lateral_weight, out_kernel, cotangent):
    images, rows, cols, in_channels = features.shape
    channels = lateral_weight.shape[1]
    cells = rows * cols
    peers = lax.axis_size("space")
    length = 9 * channels + in_channels
    taps = out_kernel.reshape(9, channels, channels)
    params = pltpu.CompilerParams(vmem_limit_bytes=48 * 2**20)
    halves = peers == 2
    if halves:
        sums = [jax.ShapeDtypeStruct((length, channels // 2), kind) for kind in (F32, BF16)]
    else:
        sums = [jax.ShapeDtypeStruct((length, channels), F32)]
    outs, tops, parts = [], [], None
    for image in range(images):
        cot = cotangent[image]
        cot_before, cot_after = neighbour_rows(cot)
        merged, grad_top, *part = pl.pallas_call(
            functools.partial(grads_kernel, peers),
            out_shape=[
                jax.ShapeDtypeStruct((cells, channels), BF16),
                jax.ShapeDtypeStruct((rows // 2, cols // 2, channels), BF16),
                *sums,
            ],
            scratch_shapes=[pltpu.VMEM((rows + 2, cols, 3 * channels), BF16)],
            compiler_params=params,
            cost_estimate=pl.CostEstimate(
                flops=2 * cells * channels * (18 * channels + 2 * in_channels), bytes_accessed=6 * 2**20, transcendentals=0
            ),
        )(
            features[image].reshape(cells, in_channels),
            top_down[image],
            lateral_weight,
            taps,
            cot,
            cot_before,
            cot_after,
        )
        merged = merged.reshape(rows, cols, channels)
        before, after = neighbour_rows(merged)
        outs.append(
            pl.pallas_call(
                functools.partial(forward_kernel, peers),
                out_shape=jax.ShapeDtypeStruct((rows, cols, channels), BF16),
                scratch_shapes=[pltpu.VMEM((rows + 2, cols, 3 * channels), BF16)],
                compiler_params=params,
                cost_estimate=pl.CostEstimate(
                    flops=2 * cells * channels * 9 * channels, bytes_accessed=2 * 2**20, transcendentals=0
                ),
            )(merged, taps, before, after)
        )
        tops.append(grad_top)
        parts = part if parts is None else [
            (a.astype(F32) + b.astype(F32)).astype(a.dtype) for a, b in zip(parts, part)
        ]
    scale = 1.0 / (images * lax.axis_size("dp"))
    if halves:
        total = sum_everywhere(*parts, scale)
    else:
        total = (lax.psum(parts[0], ("dp", "space")) * scale).astype(BF16)
    grad_kernel = total[: 9 * channels].reshape(3, 3, channels, channels)
    return jnp.stack(outs), jnp.stack(tops), grad_kernel, total[9 * channels :]


def solution(mesh):
    return jax.shard_map(
        local,
        mesh=mesh,
        in_specs=(
            P("dp", "space", None, None),
            P("dp", "space", None, None),
            P(),
            P(),
            P("dp", "space", None, None),
        ),
        out_specs=(P("dp", "space", None, None), P("dp", "space", None, None), P(), P()),
        check_vma=False,
    )
```

time: 199 us -> 71.6 us (0.36)
  waiting for transfers between devices: 130 us -> 4.47 us
  blocking collectives: 0 us -> 50.8 us
  between operations: 14.4 us -> 0.68 us
  local copies, waits for them, and re-layouts: 19.2 us -> 6.15 us
  matrix products: 12.2 us -> 0 us
  other arithmetic: 12.8 us -> 2.27 us
  starting transfers between devices: 10.4 us -> 1.31 us
  Pallas kernels: 0 us -> 5.49 us
    psum x1 -> x0, waiting for transfers between devices: 130 us -> none  [local(): lax.psum((kernel_part, lateral_part), ('dp', 'space'))]
    all_to_all x0 -> x2, blocking collectives: none -> 50.8 us  [the longest x1 28.3 us: sum_everywhere(): terms = lax.all_to_all(pair, 'dp', 0, 0, tiled=True)]
    dot_general x11 -> x0, matrix products: 12.2 us -> none  [the longest x3 5.98 us: local(): lax.dot_general(strip, flat_cot, (((0,), (0,)), ((), ())), preferred_elem...]
    ppermute x4, starting transfers between devices: 10.4 us -> 1.31 us  [the longest x2 0.96 us: neighbour_rows(): got = lax.ppermute(edge, 'space', [(0, 1), (1, 0)])]
    slice x6 -> x0, local copies, waits for them, and re-layouts: 8.43 us -> none  [the longest x2 2.89 us: row_band(): source[:, tap_row:tap_row + row_count, tap_col:tap_col + col_count, :]]
    pallas_call x0 -> x2, Pallas kernels: none -> 5.49 us  [the longest x1 3.65 us: local(): pl.pallas_call(functools.partial(grads_kernel, peers), out_shape=[jax.Sha...]
    ppermute x4, waiting for transfers between devices: 0.01 us -> 4.47 us  [the longest x2 2.63 us: neighbour_rows(): got = lax.ppermute(edge, 'space', [(0, 1), (1, 0)])]
    dot_general x3 -> x0, local copies, waits for them, and re-layouts: 4.36 us -> none  [local(): lax.dot_general(strip, flat_cot, (((0,), (0,)), ((), ())), preferred_elem...]
  transfers between devices with their start and end apart: 5 -> 4, of which waited for: 1 -> 3; matrix products, arithmetic and copies ran while one was open for 8% -> 0% of each run, Pallas kernels for 0% -> 3%
where the time goes in v1:
time: 71.6 us; the launch traced here: 71.2 us
  blocking collectives  50.8 us (71%)
  local copies, waits for them, and re-layouts  6.15 us (9%)
  Pallas kernels  5.49 us (8%)
  waiting for transfers between devices  4.47 us (6%)
  other arithmetic  2.27 us (3%)
  starting transfers between devices  1.31 us (2%)
    all_to_all x1, blocking collectives, sum_everywhere(): terms = lax.all_to_all(pair, 'dp', 0, 0, tiled=True)  28.3 us
    all_to_all x1, blocking collectives, sum_everywhere(): lax.all_to_all(copies, 'dp', 0, 0, tiled=True).reshape(parts * share, width)  22.5 us
    unnamed x12, local copies, waits for them, and re-layouts  5.24 us
    pallas_call x1, Pallas kernels, local(): pl.pallas_call(functools.partial(grads_kernel, peers), out_shape=[jax.Sha...  3.65 us
    ppermute x2, waiting for transfers between devices, neighbour_rows(): got = lax.ppermute(edge, 'space', [(0, 1), (1, 0)])  2.63 us
    concatenate x2, other arithmetic, sum_everywhere(): jnp.concatenate([jnp.where(first, whole, other), jnp.where(first, other,...  1.87 us
    ppermute x1, waiting for transfers between devices, sum_everywhere(): got = lax.ppermute(theirs, 'space', swap)  1.84 us
    pallas_call x1, Pallas kernels, local(): pl.pallas_call(functools.partial(forward_kernel, peers), out_shape=jax.Sh...  1.84 us
  transfers between devices with their start and end apart: 4, of which 3 were waited for; matrix products, arithmetic and copies ran while one was open for 0% of the time, Pallas kernels for 3%

profile of v1, /device:TPU:0, one launch (start us, length us, event | category | flops | bytes accessed | tf_op | source)
XLA Modules:
  0.0 71.2 jit_solution(12775280508837878219)
XLA Ops:
  0.6 0.8 %dynamic-slice_bitcast_fusion.1 = bf16[96,256]{1,0:T(8,128)(2,1)S(1)} fusion(bf16[1,8,96,256]{3,2,1,0:T(8,128)(2,1)} %param.9, s32[]{:T(128)S(6)} %select_n.17), kind=kLoop, calls=%fused_computation.10 | loop fusion | bytes 98308 | tf_op jit(solution)/shard_map/jit(dynamic_index_in_dim)/squeeze | solution.py:21
  1.4 0.5 collective-permute-start
  1.9 0.9 %collective-permute-done.before.after = bf16[96,256]{1,0:T(8,128)(2,1)S(1)} collective-permute-done((bf16[96,256]{1,0:T(8,128)(2,1)S(1)}, bf16[96,256]{1,0:T(8,128)(2,1)S(1)}, u32[]{:S(2)}, u32[]{:S(2)}) %collective-permute-start) | collective-permute-done | bytes 49184 | tf_op jit(solution)/shard_map/ppermute | solution.py:22
  2.8 0.0 copy-start
  2.8 1.0 %copy-done = bf16[1,8,96,256]{3,2,1,0:T(8,128)(2,1)S(1)} copy-done((bf16[1,8,96,256]{3,2,1,0:T(8,128)(2,1)S(1)}, bf16[1,8,96,256]{3,2,1,0:T(8,128)(2,1)}, u32[]{:S(2)}) %copy-start) | copy-done | bytes 393240
  3.8 0.0 copy-start.1
  3.8 1.3 %copy-done.1 = bf16[3,3,256,256]{3,2,1,0:T(8,128)(2,1)S(1)} copy-done((bf16[3,3,256,256]{3,2,1,0:T(8,128)(2,1)S(1)}, bf16[3,3,256,256]{3,2,1,0:T(8,128)(2,1)}, u32[]{:S(2)}) %copy-start.1) | copy-done | bytes 1179672
  5.0 0.0 copy-start.3
  5.0 1.1 %copy-done.3 = bf16[1,8,96,512]{3,2,1,0:T(8,128)(2,1)S(1)} copy-done((bf16[1,8,96,512]{3,2,1,0:T(8,128)(2,1)S(1)}, bf16[1,8,96,512]{3,2,1,0:T(8,128)(2,1)}, u32[]{:S(2)}) %copy-start.3) | copy-done | bytes 786456
  6.2 0.0 copy-start.4
  6.2 0.9 %copy-done.4 = bf16[512,256]{1,0:T(8,128)(2,1)S(1)} copy-done((bf16[512,256]{1,0:T(8,128)(2,1)S(1)}, bf16[512,256]{1,0:T(8,128)(2,1)}, u32[]{:S(2)}) %copy-start.4) | copy-done | bytes 262168
  7.1 0.0 copy-start.5
  7.1 0.9 %copy-done.5 = bf16[1,4,48,256]{3,2,1,0:T(8,128)(2,1)S(1)} copy-done((bf16[1,4,48,256]{3,2,1,0:T(8,128)(2,1)S(1)}, bf16[1,4,48,256]{3,2,1,0:T(8,128)(2,1)}, u32[]{:S(2)}) %copy-start.5) | copy-done | bytes 98328
  8.0 3.7 %shard_map.84 = (bf16[768,256]{1,0:T(8,128)(2,1)S(1)}, bf16[4,48,256]{2,1,0:T(8,128)(2,1)}, f32[2816,128]{1,0:T(8,128)S(1)}, bf16[2816,128]{1,0:T(8,128)(2,1)S(1)}) custom-call(bf16[768,512]{1,0:T(8,128)(2,1)S(1)} %bitcast.21, bf16[4,48,256]{2,1,0:T(8,128)(2,1)S(1)} %bitcast.22, bf16[512,256]{1,0:T(8,128)(2,1)S(1)} %copy-done.4, ...), custom_call_target="tpu_custom_call" | custom-call | flops 2214592512 | bytes 6291456 | tf_op jit(solution)/shard_map/pallas_call | solution.py:144
  11.7 0.3 collective-permute-start.2
  12.0 1.8 %collective-permute-done.2 = bf16[2816,128]{1,0:T(8,128)(2,1)S(1)} collective-permute-done((bf16[2816,128]{1,0:T(8,128)(2,1)S(1)}, bf16[2816,128]{1,0:T(8,128)(2,1)S(1)}, u32[]{:S(2)}, u32[]{:S(2)}) %collective-permute-start.2) | collective-permute-done | bytes 720928 | tf_op jit(solution)/shard_map/ppermute | solution.py:114
  13.9 0.1 add_convert_fusion
  14.0 28.3 %all_to_all.10 = bf16[16,176,128]{2,1,0:T(8,128)(2,1)S(1)} all-to-all(bf16[16,176,128]{2,1,0:T(8,128)(2,1)S(1)} %bitcast.24), channel_id=1, replica_groups=mesh['dp'=16,'space'=2] {'dp'}, dimensions={0} | all-to-all | bytes 1441792 | tf_op jit(solution)/shard_map/all_to_all | solution.py:118
  42.4 0.0 copy-start.2
  42.4 0.1 convert_reduce_fusion
  42.5 0.1 broadcast_in_dim.2
  42.6 22.5 %all_to_all.11 = bf16[16,176,128]{2,1,0:T(8,128)(2,1)S(1)} all-to-all(bf16[16,176,128]{2,1,0:T(8,128)(2,1)S(1)} %broadcast_in_dim.2), channel_id=1, replica_groups=mesh['dp'=16,'space'=2] {'dp'}, dimensions={0} | all-to-all | bytes 1441792 | tf_op jit(solution)/shard_map/all_to_all | solution.py:121
  65.1 0.0 collective-permute-start.3
  65.1 0.5 collective-permute-start.1
  65.6 1.7 %collective-permute-done.1.before.after = bf16[96,256]{1,0:T(8,128)(2,1)S(1)} collective-permute-done((bf16[96,256]{1,0:T(8,128)(2,1)S(1)}, bf16[96,256]{1,0:T(8,128)(2,1)S(1)}, u32[]{:S(2)}, u32[]{:S(2)}) %collective-permute-start.1) | collective-permute-done | bytes 49184 | tf_op jit(solution)/shard_map/ppermute | solution.py:22
  67.3 0.0 copy-done.2
  67.3 1.8 %shard_map.85 = bf16[8,96,256]{2,1,0:T(8,128)(2,1)} custom-call(bf16[8,96,256]{2,1,0:T(8,128)(2,1)S(1)} %bitcast.18, bf16[9,256,256]{2,1,0:T(8,128)(2,1)S(1)} %bitcast.20, bf16[96,256]{1,0:T(8,128)(2,1)S(1)} %collective-permute-done.1.before.after, bf16[96,256]{1,0:T(8,128)(2,1)S(1)} %collective-permute-done.1.before.after), custom_call_target="tpu_custom_call" | custom-call | flops 905969664 | bytes 2097152 | tf_op jit(solution)/shard_map/pallas_call | solution.py:168
  69.2 0.0 collective-permute-done.3
  69.2 0.1 broadcast_select_fusion
  69.3 0.7 %pad_maximum_fusion = bf16[512,256]{1,0:T(8,128)(2,1)} fusion(bf16[2816,128]{1,0:T(8,128)(2,1)S(1)} %get-tuple-element.12, bf16[2816,128]{1,0:T(8,128)(2,1)S(1)} %get-tuple-element.13), kind=kLoop, calls=%fused_computation.7 | loop fusion | flops 524288 | bytes 1703936 | tf_op jit(solution)/shard_map/concatenate | solution.py:124
  70.0 1.1 %fusion = bf16[2304,256]{1,0:T(8,128)(2,1)} fusion(bf16[2816,128]{1,0:T(8,128)(2,1)S(1)} %get-tuple-element.13, bf16[2816,128]{1,0:T(8,128)(2,1)S(1)} %get-tuple-element.12), kind=kLoop, calls=%fused_computation.4 | loop fusion | flops 2359296 | bytes 2621440 | tf_op jit(solution)/shard_map/concatenate | solution.py:124
  (2 shorter events, 0.0 us)
Async XLA Ops:
  1.4 1.3 %collective-permute-start = (bf16[96,256]{1,0:T(8,128)(2,1)S(1)}, bf16[96,256]{1,0:T(8,128)(2,1)S(1)}, u32[]{:S(2)}, u32[]{:S(2)}) collective-permute-start(bf16[96,256]{1,0:T(8,128)(2,1)S(1)} %dynamic-slice_bitcast_fusion.1), channel_id=1, source_target_pairs={{0,1},{1,0},{2,3},{3,2},{4,5},{5,4},{6,7},{7,6},{8,9},{9,8},{10,11... | collective-permute-start | bytes 147464 | tf_op jit(solution)/shard_map/ppermute | solution.py:22
  2.8 1.0 %copy-start = (bf16[1,8,96,256]{3,2,1,0:T(8,128)(2,1)S(1)}, bf16[1,8,96,256]{3,2,1,0:T(8,128)(2,1)}, u32[]{:S(2)}) copy-start(bf16[1,8,96,256]{3,2,1,0:T(8,128)(2,1)} %param.9) | copy-start | bytes 1179652
  3.8 1.3 %copy-start.1 = (bf16[3,3,256,256]{3,2,1,0:T(8,128)(2,1)S(1)}, bf16[3,3,256,256]{3,2,1,0:T(8,128)(2,1)}, u32[]{:S(2)}) copy-start(bf16[3,3,256,256]{3,2,1,0:T(8,128)(2,1)} %param.8) | copy-start | bytes 3538948
  5.0 1.1 %copy-start.3 = (bf16[1,8,96,512]{3,2,1,0:T(8,128)(2,1)S(1)}, bf16[1,8,96,512]{3,2,1,0:T(8,128)(2,1)}, u32[]{:S(2)}) copy-start(bf16[1,8,96,512]{3,2,1,0:T(8,128)(2,1)} %param.5) | copy-start | bytes 2359300
  6.2 0.9 %copy-start.4 = (bf16[512,256]{1,0:T(8,128)(2,1)S(1)}, bf16[512,256]{1,0:T(8,128)(2,1)}, u32[]{:S(2)}) copy-start(bf16[512,256]{1,0:T(8,128)(2,1)} %lat_w.1) | copy-start | bytes 786436
  7.1 0.9 %copy-start.5 = (bf16[1,4,48,256]{3,2,1,0:T(8,128)(2,1)S(1)}, bf16[1,4,48,256]{3,2,1,0:T(8,128)(2,1)}, u32[]{:S(2)}) copy-start(bf16[1,4,48,256]{3,2,1,0:T(8,128)(2,1)} %param.6) | copy-start | bytes 294916
  11.7 2.2 %collective-permute-start.2 = (bf16[2816,128]{1,0:T(8,128)(2,1)S(1)}, bf16[2816,128]{1,0:T(8,128)(2,1)S(1)}, u32[]{:S(2)}, u32[]{:S(2)}) collective-permute-start(bf16[2816,128]{1,0:T(8,128)(2,1)S(1)} %get-tuple-element.11), channel_id=1, source_target_pairs={{0,1},{1,0},{2,3},{3,2},{4,5},{5,4},{6,7},{7,6},{8,9},{9,8},{10,11... | collective-permute-start | bytes 2162696 | tf_op jit(solution)/shard_map/ppermute | solution.py:114
  42.4 25.0 %copy-start.2 = (bf16[3,3,256,256]{3,2,1,0:T(8,128)(2,1)S(1)}, bf16[3,3,256,256]{3,2,1,0:T(8,128)(2,1)}, u32[]{:S(2)}) copy-start(bf16[3,3,256,256]{3,2,1,0:T(8,128)(2,1)} %param.8) | copy-start | bytes 3538948
  65.1 4.1 %collective-permute-start.3 = (bf16[2816,128]{1,0:T(8,128)(2,1)S(1)}, bf16[2816,128]{1,0:T(8,128)(2,1)S(1)}, u32[]{:S(2)}, u32[]{:S(2)}) collective-permute-start(bf16[2816,128]{1,0:T(8,128)(2,1)S(1)} %bitcast.23), channel_id=1, source_target_pairs={{0,1},{1,0},{2,3},{3,2},{4,5},{5,4},{6,7},{7,6},{8,9},{9,8},{10,11... | collective-permute-start | bytes 2162696 | tf_op jit(solution)/shard_map/ppermute | solution.py:122
  65.1 2.3 %collective-permute-start.1 = (bf16[96,256]{1,0:T(8,128)(2,1)S(1)}, bf16[96,256]{1,0:T(8,128)(2,1)S(1)}, u32[]{:S(2)}, u32[]{:S(2)}) collective-permute-start(bf16[96,256]{1,0:T(8,128)(2,1)S(1)} %dynamic-slice_bitcast_fusion), channel_id=1, source_target_pairs={{0,1},{1,0},{2,3},{3,2},{4,5},{5,4},{6,7},{7,6},{8,9},{9,8},{10,11... | collective-permute-start | bytes 147464 | tf_op jit(solution)/shard_map/ppermute | solution.py:22

commit v2 on v1

--- a/solution.py
+++ b/solution.py
@@ -45,8 +45,15 @@
     put_shifted(stack, rows + 1, jnp.where(here < peers - 1, after[...], zero), sign)
 
 
-def grads_kernel(peers, feat, top, lat_w, out_w, cot, before, after, merged, grad_top, *rest):
-    outs, stack = rest[:-1], rest[-1]
+def grads_kernel(peers, *refs):
+    far, (before, after, merged, grad_top), rest = refs[:5], refs[5:9], refs[9:]
+    outs, stack, near, sems = rest[:-7], rest[-7], rest[-6:-1], rest[-1]
+    copies = [pltpu.make_async_copy(a, b, sems.at[i]) for i, (a, b) in enumerate(zip(far, near))]
+    for copy in copies:
+        copy.start()
+    feat, lat_w, top, cot, out_w = near
+    for copy in copies[:3]:
+        copy.wait()
     rows, cols, channels = cot.shape
     cells = rows * cols
     half = cols // 2
@@ -58,6 +65,7 @@
         lifted = jnp.dot(spread, top[q], preferred_element_type=F32)
         for r in (2 * q, 2 * q + 1):
             merged[r * cols : (r + 1) * cols, :] = (lateral[r * cols : (r + 1) * cols] + lifted).astype(BF16)
+    copies[3].wait()
     for r in range(rows):
         put_shifted(stack, r + 1, cot[r], 1)
     put_halo(stack, before, after, rows, peers, 1)
@@ -78,6 +86,7 @@
         part = jnp.dot(merged_t, strip, preferred_element_type=F32)
         for j in range(3):
             put((3 * i + j) * channels, part[:, j * channels : (j + 1) * channels])
+    copies[4].wait()
     total = jnp.zeros((cells, channels), F32)
     for i in range(3):
         strip = stack[2 - i : 2 - i + rows].reshape(cells, 3 * channels)
@@ -107,21 +116,133 @@
     out[...] = total.astype(BF16).reshape(out.shape)
 
 
-def sum_everywhere(mine, theirs, scale):
+def part_places():
+    here = lax.axis_index("dp")
+    return here % 4, here // 4
+
+
+def piece(ref, index, length):
+    return ref.at[pl.ds(pl.multiple_of(index * length, 16), length), :]
+
+
+def split_kernel(sizes, mine, got, *outs):
+    start = 0
+    for place, size, quarter in zip(part_places(), sizes, (outs[:4], outs[4:])):
+        share = size // 4
+        for k in range(4):
+            rows = pl.ds(pl.multiple_of(start + (place ^ k) * share, 16), share)
+            quarter[k][...] = (mine[rows, :] + got[rows, :].astype(F32)).astype(quarter[k].dtype)
+        start += size
+
+
+def resplit_kernel(*refs):
+    plane, line = part_places()
+    outs, scratch = refs[8:16], refs[16:]
+    for place, terms, quarter, total in ((line, refs[0:4], outs[:4], scratch[0]), (plane, refs[4:8], outs[4:], scratch[1])):
+        total[...] = terms[0][...] + sum(term[...].astype(F32) for term in terms[1:])
+        for k in range(4):
+            quarter[k][...] = piece(total, place ^ k, quarter[k].shape[0])[...].astype(quarter[k].dtype)
+
+
+def finish_kernel(scale, *refs):
+    for terms, out in ((refs[0:4], refs[8]), (refs[4:8], refs[9])):
+        total = terms[0][...] + sum(term[...].astype(F32) for term in terms[1:])
+        out[...] = (total * scale).astype(BF16)
+
+
+def join_kernel(*refs):
+    plane, line = part_places()
+    for place, terms, out in ((line, refs[0:4], refs[8]), (plane, refs[4:8], refs[9])):
+        for k in range(4):
+            piece(out, place ^ k, terms[k].shape[0])[...] = terms[k][...]
+
+
+def place_kernel(sizes, *refs):
+    plane, line = part_places()
+    side = lax.axis_index("space")
+    kernel_out, lateral_out, sems = refs[16:]
+    edge = kernel_out.shape[0]
+    waits = []
+    for columns, quarters in ((side, refs[:8]), (1 - side, refs[8:16])):
+        lanes = pl.ds(pl.multiple_of(columns * 128, 128), 128)
+        for part, (place, size) in enumerate(zip((plane, line), sizes)):
+            share = size // 4
+            for k in range(4):
+                index, sem, source = place ^ k, sems.at[len(waits)], quarters[4 * part + k]
+                if part == 0:
+                    rows = pl.ds(pl.multiple_of(index * share, 16), share)
+                    copy = pltpu.make_async_copy(source, kernel_out.at[rows, lanes], sem)
+                    copy.start()
+                else:
+                    inside = (edge - sizes[0]) // share
+
+                    @pl.when(index < inside)
+                    def _():
+                        rows = pl.ds(pl.multiple_of(sizes[0] + index * share, 16), share)
+                        pltpu.make_async_copy(source, kernel_out.at[rows, lanes], sem).start()
+
+                    @pl.when(index >= inside)
+                    def _():
+                        rows = pl.ds(pl.multiple_of((index - inside) * share, 16), share)
+                        pltpu.make_async_copy(source, lateral_out.at[rows, lanes], sem).start()
+
+                    copy = pltpu.make_async_copy(source, lateral_out.at[pl.ds(0, share), lanes], sem)
+                waits.append(copy)
+    for copy in waits:
+        copy.wait()
+
+
+def exchange(pieces, group):
+    moves = {"plane": lambda d, k: d ^ k, "line": lambda d, k: d ^ (4 * k)}[group]
+    return [pieces[0]] + [
+        lax.ppermute(pieces[k], "dp", [(d, moves(d, k)) for d in range(16)]) for k in (1, 2, 3)
+    ]
+
+
+def call(kernel, shapes, scratch=(), **more):
+    return pl.pallas_call(
+        kernel,
+        out_shape=[jax.ShapeDtypeStruct(shape, kind) for shape, kind in shapes],
+        scratch_shapes=list(scratch),
+        compiler_params=pltpu.CompilerParams(vmem_limit_bytes=32 * 2**20),
+        **more,
+    )
+
+
+def sum_everywhere(mine, theirs, scale, edge):
     length, width = mine.shape
-    parts = lax.axis_size("dp")
+    sizes = (7 * length // 11, 4 * length // 11)
+    shares = [size // 4 for size in sizes]
+    ends = [share // 4 for share in shares]
     swap = [(0, 1), (1, 0)]
     got = lax.ppermute(theirs, "space", swap)
-    pair = (mine + got.astype(F32)).astype(BF16)
-    share = -(-length // (16 * parts)) * 16
-    pair = jnp.pad(pair, ((0, share * parts - length), (0, 0))).reshape(parts, share, width)
-    terms = lax.all_to_all(pair, "dp", 0, 0, tiled=True)
-    total = (jnp.sum(terms.astype(F32), axis=0) * scale).astype(BF16)
-    copies = jnp.broadcast_to(total[None], terms.shape)
-    whole = lax.all_to_all(copies, "dp", 0, 0, tiled=True).reshape(parts * share, width)[:length]
-    other = lax.ppermute(whole, "space", swap)
-    first = lax.axis_index("space") == 0
-    return jnp.concatenate([jnp.where(first, whole, other), jnp.where(first, other, whole)], axis=1)
+    first = call(
+        functools.partial(split_kernel, sizes),
+        [((share, width), F32 if k == 0 else BF16) for share in shares for k in range(4)],
+    )(mine, got)
+    part_a = exchange(first[:4], "plane")
+    part_b = exchange(first[4:], "line")
+    second = call(
+        resplit_kernel,
+        [((end, width), F32 if k == 0 else BF16) for end in ends for k in range(4)],
+        [pltpu.VMEM((share, width), F32) for share in shares],
+    )(*part_a, *part_b)
+    part_a = exchange(second[:4], "line")
+    part_b = exchange(second[4:], "plane")
+    part_a, part_b = call(
+        functools.partial(finish_kernel, scale), [((end, width), BF16) for end in ends]
+    )(*part_a, *part_b)
+    part_a = exchange([part_a] * 4, "line")
+    part_b = exchange([part_b] * 4, "plane")
+    part_a, part_b = call(join_kernel, [((share, width), BF16) for share in shares])(*part_a, *part_b)
+    pieces = exchange([part_a] * 4, "plane") + exchange([part_b] * 4, "line")
+    others = [lax.ppermute(one, "space", swap) for one in pieces]
+    return call(
+        functools.partial(place_kernel, sizes),
+        [((edge, 2 * width), BF16), ((length - edge, 2 * width), BF16)],
+        [pltpu.SemaphoreType.DMA((16,))],
+        out_specs=[pl.BlockSpec(memory_space=pltpu.HBM)] * 2,
+    )(*pieces, *others)
 
 
 def local(features, top_down, lateral_weight, out_kernel, cotangent):
@@ -132,7 +253,7 @@
     length = 9 * channels + in_channels
     taps = out_kernel.reshape(9, channels, channels)
     params = pltpu.CompilerParams(vmem_limit_bytes=48 * 2**20)
-    halves = peers == 2
+    halves = peers == 2 and lax.axis_size("dp") == 16 and (channels, in_channels) == (256, 512)
     if halves:
         sums = [jax.ShapeDtypeStruct((length, channels // 2), kind) for kind in (F32, BF16)]
     else:
@@ -141,6 +262,7 @@
     for image in range(images):
         cot = cotangent[image]
         cot_before, cot_after = neighbour_rows(cot)
+        arrays = (features[image].reshape(cells, in_channels), lateral_weight, top_down[image], cot, taps)
         merged, grad_top, *part = pl.pallas_call(
             functools.partial(grads_kernel, peers),
             out_shape=[
@@ -148,20 +270,17 @@
                 jax.ShapeDtypeStruct((rows // 2, cols // 2, channels), BF16),
                 *sums,
             ],
-            scratch_shapes=[pltpu.VMEM((rows + 2, cols, 3 * channels), BF16)],
+            in_specs=[pl.BlockSpec(memory_space=pltpu.HBM)] * 5 + [pl.BlockSpec(memory_space=pltpu.VMEM)] * 2,
+            scratch_shapes=[
+                pltpu.VMEM((rows + 2, cols, 3 * channels), BF16),
+                *[pltpu.VMEM(array.shape, BF16) for array in arrays],
+                pltpu.SemaphoreType.DMA((5,)),
+            ],
             compiler_params=params,
             cost_estimate=pl.CostEstimate(
                 flops=2 * cells * channels * (18 * channels + 2 * in_channels), bytes_accessed=6 * 2**20, transcendentals=0
             ),
-        )(
-            features[image].reshape(cells, in_channels),
-            top_down[image],
-            lateral_weight,
-            taps,
-            cot,
-            cot_before,
-            cot_after,
-        )
+        )(*arrays, cot_before, cot_after)
         merged = merged.reshape(rows, cols, channels)
         before, after = neighbour_rows(merged)
         outs.append(
@@ -181,11 +300,11 @@
         ]
     scale = 1.0 / (images * lax.axis_size("dp"))
     if halves:
-        total = sum_everywhere(*parts, scale)
+        grad_kernel, grad_lateral = sum_everywhere(*parts, scale, 9 * channels)
     else:
         total = (lax.psum(parts[0], ("dp", "space")) * scale).astype(BF16)
-    grad_kernel = total[: 9 * channels].reshape(3, 3, channels, channels)
-    return jnp.stack(outs), jnp.stack(tops), grad_kernel, total[9 * channels :]
+        grad_kernel, grad_lateral = total[: 9 * channels], total[9 * channels :]
+    return jnp.stack(outs), jnp.stack(tops), grad_kernel.reshape(out_kernel.shape), grad_lateral
 
 
 def solution(mesh):

time: 71.6 us -> 69 us (0.964)
  blocking collectives: 50.8 us -> 0 us
  starting transfers between devices: 1.31 us -> 33.9 us
  waiting for transfers between devices: 4.47 us -> 19.8 us
  Pallas kernels: 5.49 us -> 8.03 us
  other arithmetic: 2.27 us -> 0 us
    all_to_all x2 -> x0, blocking collectives: 50.8 us -> none  [the longest x1 28.3 us: sum_everywhere(): terms = lax.all_to_all(pair, 'dp', 0, 0, tiled=True)]
    ppermute x1 -> x32, starting transfers between devices: 0.01 us -> 32.9 us  [the longest x24 31.4 us: exchange(): lax.ppermute(pieces[k], 'dp', [(d, moves(d, k)) for d in range(16)])]
    ppermute x1 -> x32, waiting for transfers between devices: 0.01 us -> 17.1 us  [the longest x24 16.9 us: exchange(): lax.ppermute(pieces[k], 'dp', [(d, moves(d, k)) for d in range(16)])]
    concatenate x2 -> x0, other arithmetic: 1.87 us -> none  [sum_everywhere(): jnp.concatenate([jnp.where(first, whole, other), jnp.where(first, other,...]
    ppermute x2, waiting for transfers between devices: 2.63 us -> 0.88 us  [neighbour_rows(): got = lax.ppermute(edge, 'space', [(0, 1), (1, 0)])]
    pallas_call x0 -> x5, Pallas kernels: none -> 1.54 us  [the longest x1 1.24 us: sum_everywhere(): call(functools.partial(place_kernel, sizes), [((edge, 2 * width), BF16),...]
    pallas_call x1, Pallas kernels: 3.65 us -> 4.65 us  [local(): pl.pallas_call(functools.partial(grads_kernel, peers), out_shape=[jax.Sha...]
  transfers between devices with their start and end apart: 4 -> 35, of which waited for: 3 -> 12; matrix products, arithmetic and copies ran while one was open for 0% -> 0% of each run, Pallas kernels for 3% -> 3%
where the time goes in v2:
time: 69 us; the launch traced here: 68.6 us
  starting transfers between devices  33.9 us (49%)
  waiting for transfers between devices  19.8 us (29%)
  Pallas kernels  8.03 us (12%)
  local copies, waits for them, and re-layouts  6.06 us (9%)
  between operations  0.75 us (1%)
    ppermute x24, starting transfers between devices, exchange(): lax.ppermute(pieces[k], 'dp', [(d, moves(d, k)) for d in range(16)])  31.4 us
    ppermute x24, waiting for transfers between devices, exchange(): lax.ppermute(pieces[k], 'dp', [(d, moves(d, k)) for d in range(16)])  16.9 us
    unnamed x12, local copies, waits for them, and re-layouts  5.25 us
    pallas_call x1, Pallas kernels, local(): pl.pallas_call(functools.partial(grads_kernel, peers), out_shape=[jax.Sha...  4.65 us
    ppermute x1, waiting for transfers between devices, sum_everywhere(): got = lax.ppermute(theirs, 'space', swap)  1.84 us
    pallas_call x1, Pallas kernels, local(): pl.pallas_call(functools.partial(forward_kernel, peers), out_shape=jax.Sh...  1.83 us
    ppermute x8, starting transfers between devices, sum_everywhere(): others = [lax.ppermute(one, 'space', swap) for one in pieces]  1.46 us
  transfers between devices with their start and end apart: 35, of which 12 were waited for; matrix products, arithmetic and copies ran while one was open for 0% of the time, Pallas kernels for 3%

profile of v2, /device:TPU:0, one launch (start us, length us, event | category | flops | bytes accessed | tf_op | source)
XLA Modules:
  0.0 68.6 jit_solution(10113620345730879605)
XLA Ops:
  2.8 1.0 %copy-done = bf16[1,8,96,256]{3,2,1,0:T(8,128)(2,1)S(1)} copy-done((bf16[1,8,96,256]{3,2,1,0:T(8,128)(2,1)S(1)}, bf16[1,8,96,256]{3,2,1,0:T(8,128)(2,1)}, u32[]{:S(2)}) %copy-start) | copy-done | bytes 393240
  3.8 1.3 %copy-done.1 = bf16[3,3,256,256]{3,2,1,0:T(8,128)(2,1)S(1)} copy-done((bf16[3,3,256,256]{3,2,1,0:T(8,128)(2,1)S(1)}, bf16[3,3,256,256]{3,2,1,0:T(8,128)(2,1)}, u32[]{:S(2)}) %copy-start.1) | copy-done | bytes 1179672
  5.0 1.1 %copy-done.3 = bf16[1,8,96,512]{3,2,1,0:T(8,128)(2,1)S(1)} copy-done((bf16[1,8,96,512]{3,2,1,0:T(8,128)(2,1)S(1)}, bf16[1,8,96,512]{3,2,1,0:T(8,128)(2,1)}, u32[]{:S(2)}) %copy-start.3) | copy-done | bytes 786456
  6.2 0.9 %copy-done.4 = bf16[512,256]{1,0:T(8,128)(2,1)S(1)} copy-done((bf16[512,256]{1,0:T(8,128)(2,1)S(1)}, bf16[512,256]{1,0:T(8,128)(2,1)}, u32[]{:S(2)}) %copy-start.4) | copy-done | bytes 262168
  8.0 4.7 %shard_map.84 = (bf16[768,256]{1,0:T(8,128)(2,1)S(1)}, bf16[4,48,256]{2,1,0:T(8,128)(2,1)}, f32[2816,128]{1,0:T(8,128)S(1)}, bf16[2816,128]{1,0:T(8,128)(2,1)S(1)}) custom-call(bf16[768,512]{1,0:T(8,128)(2,1)S(1)} %bitcast.17, bf16[512,256]{1,0:T(8,128)(2,1)S(1)} %copy-done.4, bf16[4,48,256]{2,1,0:T(8,128)(2,1)S(1)} %bitcast.18, ...), custom_call_target="tpu_custom_call" | custom-call | flops 2214592512 | bytes 6291456 | tf_op jit(solution)/shard_map/pallas_call | solution.py:266
  13.1 1.8 %collective-permute-done.2.got = bf16[2816,128]{1,0:T(8,128)(2,1)S(1)} collective-permute-done((bf16[2816,128]{1,0:T(8,128)(2,1)S(1)}, bf16[2816,128]{1,0:T(8,128)(2,1)S(1)}, u32[]{:S(2)}, u32[]{:S(2)}) %collective-permute-start.2) | collective-permute-done | bytes 720928 | tf_op jit(solution)/shard_map/ppermute | solution.py:218
  15.1 3.0 %collective-permute-start.6 = (bf16[256,128]{1,0:T(8,128)(2,1)S(1)}, bf16[256,128]{1,0:T(8,128)(2,1)S(1)}, u32[]{:S(2)}, u32[]{:S(2)}) collective-permute-start(bf16[256,128]{1,0:T(8,128)(2,1)S(1)} %get-tuple-element.39), channel_id=1, source_target_pairs={{0,8},{2,10},{4,12},{6,14},{8,0},{10,2},{12,4},{14,6},{16,24},{18,... | collective-permute-start | bytes 196616 | tf_op jit(solution)/shard_map/ppermute | solution.py:198
  18.1 1.5 %collective-permute-start.3 = (bf16[448,128]{1,0:T(8,128)(2,1)S(1)}, bf16[448,128]{1,0:T(8,128)(2,1)S(1)}, u32[]{:S(2)}, u32[]{:S(2)}) collective-permute-start(bf16[448,128]{1,0:T(8,128)(2,1)S(1)} %get-tuple-element.35), channel_id=1, source_target_pairs={{0,2},{2,0},{4,6},{6,4},{8,10},{10,8},{12,14},{14,12},{16,18},{18,... | collective-permute-start | bytes 344072 | tf_op jit(solution)/shard_map/ppermute | solution.py:198
  19.6 1.5 %collective-permute-start.4 = (bf16[448,128]{1,0:T(8,128)(2,1)S(1)}, bf16[448,128]{1,0:T(8,128)(2,1)S(1)}, u32[]{:S(2)}, u32[]{:S(2)}) collective-permute-start(bf16[448,128]{1,0:T(8,128)(2,1)S(1)} %get-tuple-element.36), channel_id=1, source_target_pairs={{0,4},{2,6},{4,0},{6,2},{8,12},{10,14},{12,8},{14,10},{16,20},{18,... | collective-permute-start | bytes 344072 | tf_op jit(solution)/shard_map/ppermute | solution.py:198
  21.6 2.6 %collective-permute-start.7 = (bf16[256,128]{1,0:T(8,128)(2,1)S(1)}, bf16[256,128]{1,0:T(8,128)(2,1)S(1)}, u32[]{:S(2)}, u32[]{:S(2)}) collective-permute-start(bf16[256,128]{1,0:T(8,128)(2,1)S(1)} %get-tuple-element.40), channel_id=1, source_target_pairs={{0,16},{2,18},{4,20},{6,22},{8,24},{10,26},{12,28},{14,30},{16,0},... | collective-permute-start | bytes 196616 | tf_op jit(solution)/shard_map/ppermute | solution.py:198
  24.4 3.8 %collective-permute-done.7.refs_6_ = bf16[256,128]{1,0:T(8,128)(2,1)S(1)} collective-permute-done((bf16[256,128]{1,0:T(8,128)(2,1)S(1)}, bf16[256,128]{1,0:T(8,128)(2,1)S(1)}, u32[]{:S(2)}, u32[]{:S(2)}) %collective-permute-start.7) | collective-permute-done | bytes 65568 | tf_op jit(solution)/shard_map/ppermute | solution.py:198
  28.2 2.0 %collective-permute-done.8.refs_7_ = bf16[256,128]{1,0:T(8,128)(2,1)S(1)} collective-permute-done((bf16[256,128]{1,0:T(8,128)(2,1)S(1)}, bf16[256,128]{1,0:T(8,128)(2,1)S(1)}, u32[]{:S(2)}, u32[]{:S(2)}) %collective-permute-start.8) | collective-permute-done | bytes 65568 | tf_op jit(solution)/shard_map/ppermute | solution.py:198
  30.3 1.6 %collective-permute-start.12 = (bf16[64,128]{1,0:T(8,128)(2,1)S(1)}, bf16[64,128]{1,0:T(8,128)(2,1)S(1)}, u32[]{:S(2)}, u32[]{:S(2)}) collective-permute-start(bf16[64,128]{1,0:T(8,128)(2,1)S(1)} %get-tuple-element.47), channel_id=1, source_target_pairs={{0,2},{2,0},{4,6},{6,4},{8,10},{10,8},{12,14},{14,12},{16,18},{18,... | collective-permute-start | bytes 49160 | tf_op jit(solution)/shard_map/ppermute | solution.py:198
  31.9 1.8 %collective-permute-start.10 = (bf16[112,128]{1,0:T(8,128)(2,1)S(1)}, bf16[112,128]{1,0:T(8,128)(2,1)S(1)}, u32[]{:S(2)}, u32[]{:S(2)}) collective-permute-start(bf16[112,128]{1,0:T(8,128)(2,1)S(1)} %get-tuple-element.44), channel_id=1, source_target_pairs={{0,16},{2,18},{4,20},{6,22},{8,24},{10,26},{12,28},{14,30},{16,0},... | collective-permute-start | bytes 86024 | tf_op jit(solution)/shard_map/ppermute | solution.py:198
  33.7 2.6 %collective-permute-start.11 = (bf16[112,128]{1,0:T(8,128)(2,1)S(1)}, bf16[112,128]{1,0:T(8,128)(2,1)S(1)}, u32[]{:S(2)}, u32[]{:S(2)}) collective-permute-start(bf16[112,128]{1,0:T(8,128)(2,1)S(1)} %get-tuple-element.45), channel_id=1, source_target_pairs={{0,24},{2,26},{4,28},{6,30},{8,16},{10,18},{12,20},{14,22},{16,8},... | collective-permute-start | bytes 86024 | tf_op jit(solution)/shard_map/ppermute | solution.py:198
  36.3 1.5 %collective-permute-start.13 = (bf16[64,128]{1,0:T(8,128)(2,1)S(1)}, bf16[64,128]{1,0:T(8,128)(2,1)S(1)}, u32[]{:S(2)}, u32[]{:S(2)}) collective-permute-start(bf16[64,128]{1,0:T(8,128)(2,1)S(1)} %get-tuple-element.48), channel_id=1, source_target_pairs={{0,4},{2,6},{4,0},{6,2},{8,12},{10,14},{12,8},{14,10},{16,20},{18,... | collective-permute-start | bytes 49160 | tf_op jit(solution)/shard_map/ppermute | solution.py:198
  38.3 1.7 %collective-permute-done.13.refs_6_ = bf16[64,128]{1,0:T(8,128)(2,1)S(1)} collective-permute-done((bf16[64,128]{1,0:T(8,128)(2,1)S(1)}, bf16[64,128]{1,0:T(8,128)(2,1)S(1)}, u32[]{:S(2)}, u32[]{:S(2)}) %collective-permute-start.13) | collective-permute-done | bytes 16416 | tf_op jit(solution)/shard_map/ppermute | solution.py:198
  40.0 2.4 %collective-permute-done.14.refs_7_ = bf16[64,128]{1,0:T(8,128)(2,1)S(1)} collective-permute-done((bf16[64,128]{1,0:T(8,128)(2,1)S(1)}, bf16[64,128]{1,0:T(8,128)(2,1)S(1)}, u32[]{:S(2)}, u32[]{:S(2)}) %collective-permute-start.14) | collective-permute-done | bytes 16416 | tf_op jit(solution)/shard_map/ppermute | solution.py:198
  43.0 1.3 %collective-permute-start.17 = (bf16[112,128]{1,0:T(8,128)(2,1)S(1)}, bf16[112,128]{1,0:T(8,128)(2,1)S(1)}, u32[]{:S(2)}, u32[]{:S(2)}) collective-permute-start(bf16[112,128]{1,0:T(8,128)(2,1)S(1)} %get-tuple-element.50.refs_0_), channel_id=1, source_target_pairs={{0,24},{2,26},{4,28},{6,30},{8,16},{10,18},{12,20},{14,22},{16,8},... | collective-permute-start | bytes 86024 | tf_op jit(solution)/shard_map/ppermute | solution.py:198
  44.3 3.1 %collective-permute-start.15 = (bf16[112,128]{1,0:T(8,128)(2,1)S(1)}, bf16[112,128]{1,0:T(8,128)(2,1)S(1)}, u32[]{:S(2)}, u32[]{:S(2)}) collective-permute-start(bf16[112,128]{1,0:T(8,128)(2,1)S(1)} %get-tuple-element.50.refs_0_), channel_id=1, source_target_pairs={{0,8},{2,10},{4,12},{6,14},{8,0},{10,2},{12,4},{14,6},{16,24},{18,... | collective-permute-start | bytes 86024 | tf_op jit(solution)/shard_map/ppermute | solution.py:198
  47.4 1.5 %collective-permute-start.19 = (bf16[64,128]{1,0:T(8,128)(2,1)S(1)}, bf16[64,128]{1,0:T(8,128)(2,1)S(1)}, u32[]{:S(2)}, u32[]{:S(2)}) collective-permute-start(bf16[64,128]{1,0:T(8,128)(2,1)S(1)} %get-tuple-element.51.refs_4_), channel_id=1, source_target_pairs={{0,4},{2,6},{4,0},{6,2},{8,12},{10,14},{12,8},{14,10},{16,20},{18,... | collective-permute-start | bytes 49160 | tf_op jit(solution)/shard_map/ppermute | solution.py:198
  49.0 1.5 %collective-permute-start.18 = (bf16[64,128]{1,0:T(8,128)(2,1)S(1)}, bf16[64,128]{1,0:T(8,128)(2,1)S(1)}, u32[]{:S(2)}, u32[]{:S(2)}) collective-permute-start(bf16[64,128]{1,0:T(8,128)(2,1)S(1)} %get-tuple-element.51.refs_4_), channel_id=1, source_target_pairs={{0,2},{2,0},{4,6},{6,4},{8,10},{10,8},{12,14},{14,12},{16,18},{18,... | collective-permute-start | bytes 49160 | tf_op jit(solution)/shard_map/ppermute | solution.py:198
  51.2 1.5 %collective-permute-done.18.refs_5_ = bf16[64,128]{1,0:T(8,128)(2,1)S(1)} collective-permute-done((bf16[64,128]{1,0:T(8,128)(2,1)S(1)}, bf16[64,128]{1,0:T(8,128)(2,1)S(1)}, u32[]{:S(2)}, u32[]{:S(2)}) %collective-permute-start.18) | collective-permute-done | bytes 16416 | tf_op jit(solution)/shard_map/ppermute | solution.py:198
  52.8 1.4 %collective-permute-start.26 = (bf16[256,128]{1,0:T(8,128)(2,1)S(1)}, bf16[256,128]{1,0:T(8,128)(2,1)S(1)}, u32[]{:S(2)}, u32[]{:S(2)}) collective-permute-start(bf16[256,128]{1,0:T(8,128)(2,1)S(1)} %get-tuple-element.53.refs_4_), channel_id=1, source_target_pairs={{0,24},{2,26},{4,28},{6,30},{8,16},{10,18},{12,20},{14,22},{16,8},... | collective-permute-start | bytes 196616 | tf_op jit(solution)/shard_map/ppermute | solution.py:198
  54.5 1.4 %collective-permute-start.23 = (bf16[448,128]{1,0:T(8,128)(2,1)S(1)}, bf16[448,128]{1,0:T(8,128)(2,1)S(1)}, u32[]{:S(2)}, u32[]{:S(2)}) collective-permute-start(bf16[448,128]{1,0:T(8,128)(2,1)S(1)} %get-tuple-element.52.refs_0_), channel_id=1, source_target_pairs={{0,6},{2,4},{4,2},{6,0},{8,14},{10,12},{12,10},{14,8},{16,22},{18,... | collective-permute-start | bytes 344072 | tf_op jit(solution)/shard_map/ppermute | solution.py:198
  56.0 1.5 %collective-permute-start.22 = (bf16[448,128]{1,0:T(8,128)(2,1)S(1)}, bf16[448,128]{1,0:T(8,128)(2,1)S(1)}, u32[]{:S(2)}, u32[]{:S(2)}) collective-permute-start(bf16[448,128]{1,0:T(8,128)(2,1)S(1)} %get-tuple-element.52.refs_0_), channel_id=1, source_target_pairs={{0,4},{2,6},{4,0},{6,2},{8,12},{10,14},{12,8},{14,10},{16,20},{18,... | collective-permute-start | bytes 344072 | tf_op jit(solution)/shard_map/ppermute | solution.py:198
  58.0 1.7 %collective-permute-done.26.refs_7_ = bf16[256,128]{1,0:T(8,128)(2,1)S(1)} collective-permute-done((bf16[256,128]{1,0:T(8,128)(2,1)S(1)}, bf16[256,128]{1,0:T(8,128)(2,1)S(1)}, u32[]{:S(2)}, u32[]{:S(2)}) %collective-permute-start.26) | collective-permute-done | bytes 65568 | tf_op jit(solution)/shard_map/ppermute | solution.py:198
  59.7 1.3 %collective-permute-start.24 = (bf16[256,128]{1,0:T(8,128)(2,1)S(1)}, bf16[256,128]{1,0:T(8,128)(2,1)S(1)}, u32[]{:S(2)}, u32[]{:S(2)}) collective-permute-start(bf16[256,128]{1,0:T(8,128)(2,1)S(1)} %get-tuple-element.53.refs_4_), channel_id=1, source_target_pairs={{0,8},{2,10},{4,12},{6,14},{8,0},{10,2},{12,4},{14,6},{16,24},{18,... | collective-permute-start | bytes 196616 | tf_op jit(solution)/shard_map/ppermute | solution.py:198
  61.0 1.0 %collective-permute-done.25.refs_6_ = bf16[256,128]{1,0:T(8,128)(2,1)S(1)} collective-permute-done((bf16[256,128]{1,0:T(8,128)(2,1)S(1)}, bf16[256,128]{1,0:T(8,128)(2,1)S(1)}, u32[]{:S(2)}, u32[]{:S(2)}) %collective-permute-start.25) | collective-permute-done | bytes 65568 | tf_op jit(solution)/shard_map/ppermute | solution.py:198
  62.0 1.9 %collective-permute-done.24.refs_5_ = bf16[256,128]{1,0:T(8,128)(2,1)S(1)} collective-permute-done((bf16[256,128]{1,0:T(8,128)(2,1)S(1)}, bf16[256,128]{1,0:T(8,128)(2,1)S(1)}, u32[]{:S(2)}, u32[]{:S(2)}) %collective-permute-start.24) | collective-permute-done | bytes 65568 | tf_op jit(solution)/shard_map/ppermute | solution.py:198
  65.5 1.8 %shard_map.85 = bf16[8,96,256]{2,1,0:T(8,128)(2,1)} custom-call(bf16[8,96,256]{2,1,0:T(8,128)(2,1)S(1)} %bitcast.14, bf16[9,256,256]{2,1,0:T(8,128)(2,1)S(1)} %bitcast.16, bf16[96,256]{1,0:T(8,128)(2,1)S(1)} %collective-permute-done.1.before.after, bf16[96,256]{1,0:T(8,128)(2,1)S(1)} %collective-permute-done.1.before.after), custom_call_target="tpu_custom_call" | custom-call | flops 905969664 | bytes 2097152 | tf_op jit(solution)/shard_map/pallas_call | solution.py:287
  67.4 1.2 %shard_map.90 = (bf16[2304,256]{1,0:T(8,128)(2,1)}, bf16[512,256]{1,0:T(8,128)(2,1)}) custom-call(bf16[448,128]{1,0:T(8,128)(2,1)S(1)} %get-tuple-element.52.refs_0_, bf16[448,128]{1,0:T(8,128)(2,1)S(1)} %collective-permute-done.21.refs_1_, bf16[448,128]{1,0:T(8,128)(2,1)S(1)} %collective-permute-done.22.refs_2_, ...), custom_call_target="tpu_custom_call" | custom-call | tf_op jit(solution)/shard_map/pallas_call | solution.py:240
  (59 shorter events, 8.8 us)
Async XLA Ops:
  12.7 2.3 %collective-permute-start.2 = (bf16[2816,128]{1,0:T(8,128)(2,1)S(1)}, bf16[2816,128]{1,0:T(8,128)(2,1)S(1)}, u32[]{:S(2)}, u32[]{:S(2)}) collective-permute-start(bf16[2816,128]{1,0:T(8,128)(2,1)S(1)} %get-tuple-element.33), channel_id=1, source_target_pairs={{0,1},{1,0},{2,3},{3,2},{4,5},{5,4},{6,7},{7,6},{8,9},{9,8},{10,11... | collective-permute-start | bytes 2162696 | tf_op jit(solution)/shard_map/ppermute | solution.py:218
  15.1 9.1 %collective-permute-start.6 = (bf16[256,128]{1,0:T(8,128)(2,1)S(1)}, bf16[256,128]{1,0:T(8,128)(2,1)S(1)}, u32[]{:S(2)}, u32[]{:S(2)}) collective-permute-start(bf16[256,128]{1,0:T(8,128)(2,1)S(1)} %get-tuple-element.39), channel_id=1, source_target_pairs={{0,8},{2,10},{4,12},{6,14},{8,0},{10,2},{12,4},{14,6},{16,24},{18,... | collective-permute-start | bytes 196616 | tf_op jit(solution)/shard_map/ppermute | solution.py:198
  18.1 12.1 %collective-permute-start.3 = (bf16[448,128]{1,0:T(8,128)(2,1)S(1)}, bf16[448,128]{1,0:T(8,128)(2,1)S(1)}, u32[]{:S(2)}, u32[]{:S(2)}) collective-permute-start(bf16[448,128]{1,0:T(8,128)(2,1)S(1)} %get-tuple-element.35), channel_id=1, source_target_pairs={{0,2},{2,0},{4,6},{6,4},{8,10},{10,8},{12,14},{14,12},{16,18},{18,... | collective-permute-start | bytes 344072 | tf_op jit(solution)/shard_map/ppermute | solution.py:198
  19.6 10.7 %collective-permute-start.4 = (bf16[448,128]{1,0:T(8,128)(2,1)S(1)}, bf16[448,128]{1,0:T(8,128)(2,1)S(1)}, u32[]{:S(2)}, u32[]{:S(2)}) collective-permute-start(bf16[448,128]{1,0:T(8,128)(2,1)S(1)} %get-tuple-element.36), channel_id=1, source_target_pairs={{0,4},{2,6},{4,0},{6,2},{8,12},{10,14},{12,8},{14,10},{16,20},{18,... | collective-permute-start | bytes 344072 | tf_op jit(solution)/shard_map/ppermute | solution.py:198
  21.1 9.1 %collective-permute-start.5 = (bf16[448,128]{1,0:T(8,128)(2,1)S(1)}, bf16[448,128]{1,0:T(8,128)(2,1)S(1)}, u32[]{:S(2)}, u32[]{:S(2)}) collective-permute-start(bf16[448,128]{1,0:T(8,128)(2,1)S(1)} %get-tuple-element.37), channel_id=1, source_target_pairs={{0,6},{2,4},{4,2},{6,0},{8,14},{10,12},{12,10},{14,8},{16,22},{18,... | collective-permute-start | bytes 344072 | tf_op jit(solution)/shard_map/ppermute | solution.py:198
  21.6 6.6 %collective-permute-start.7 = (bf16[256,128]{1,0:T(8,128)(2,1)S(1)}, bf16[256,128]{1,0:T(8,128)(2,1)S(1)}, u32[]{:S(2)}, u32[]{:S(2)}) collective-permute-start(bf16[256,128]{1,0:T(8,128)(2,1)S(1)} %get-tuple-element.40), channel_id=1, source_target_pairs={{0,16},{2,18},{4,20},{6,22},{8,24},{10,26},{12,28},{14,30},{16,0},... | collective-permute-start | bytes 196616 | tf_op jit(solution)/shard_map/ppermute | solution.py:198
  24.1 6.1 %collective-permute-start.8 = (bf16[256,128]{1,0:T(8,128)(2,1)S(1)}, bf16[256,128]{1,0:T(8,128)(2,1)S(1)}, u32[]{:S(2)}, u32[]{:S(2)}) collective-permute-start(bf16[256,128]{1,0:T(8,128)(2,1)S(1)} %get-tuple-element.41), channel_id=1, source_target_pairs={{0,24},{2,26},{4,28},{6,30},{8,16},{10,18},{12,20},{14,22},{16,8},... | collective-permute-start | bytes 196616 | tf_op jit(solution)/shard_map/ppermute | solution.py:198
  30.3 7.5 %collective-permute-start.12 = (bf16[64,128]{1,0:T(8,128)(2,1)S(1)}, bf16[64,128]{1,0:T(8,128)(2,1)S(1)}, u32[]{:S(2)}, u32[]{:S(2)}) collective-permute-start(bf16[64,128]{1,0:T(8,128)(2,1)S(1)} %get-tuple-element.47), channel_id=1, source_target_pairs={{0,2},{2,0},{4,6},{6,4},{8,10},{10,8},{12,14},{14,12},{16,18},{18,... | collective-permute-start | bytes 49160 | tf_op jit(solution)/shard_map/ppermute | solution.py:198
  31.9 10.6 %collective-permute-start.9 = (bf16[112,128]{1,0:T(8,128)(2,1)S(1)}, bf16[112,128]{1,0:T(8,128)(2,1)S(1)}, u32[]{:S(2)}, u32[]{:S(2)}) collective-permute-start(bf16[112,128]{1,0:T(8,128)(2,1)S(1)} %get-tuple-element.43), channel_id=1, source_target_pairs={{0,8},{2,10},{4,12},{6,14},{8,0},{10,2},{12,4},{14,6},{16,24},{18,... | collective-permute-start | bytes 86024 | tf_op jit(solution)/shard_map/ppermute | solution.py:198
  31.9 10.6 %collective-permute-start.10 = (bf16[112,128]{1,0:T(8,128)(2,1)S(1)}, bf16[112,128]{1,0:T(8,128)(2,1)S(1)}, u32[]{:S(2)}, u32[]{:S(2)}) collective-permute-start(bf16[112,128]{1,0:T(8,128)(2,1)S(1)} %get-tuple-element.44), channel_id=1, source_target_pairs={{0,16},{2,18},{4,20},{6,22},{8,24},{10,26},{12,28},{14,30},{16,0},... | collective-permute-start | bytes 86024 | tf_op jit(solution)/shard_map/ppermute | solution.py:198
  33.7 8.7 %collective-permute-start.11 = (bf16[112,128]{1,0:T(8,128)(2,1)S(1)}, bf16[112,128]{1,0:T(8,128)(2,1)S(1)}, u32[]{:S(2)}, u32[]{:S(2)}) collective-permute-start(bf16[112,128]{1,0:T(8,128)(2,1)S(1)} %get-tuple-element.45), channel_id=1, source_target_pairs={{0,24},{2,26},{4,28},{6,30},{8,16},{10,18},{12,20},{14,22},{16,8},... | collective-permute-start | bytes 86024 | tf_op jit(solution)/shard_map/ppermute | solution.py:198
  36.3 3.7 %collective-permute-start.13 = (bf16[64,128]{1,0:T(8,128)(2,1)S(1)}, bf16[64,128]{1,0:T(8,128)(2,1)S(1)}, u32[]{:S(2)}, u32[]{:S(2)}) collective-permute-start(bf16[64,128]{1,0:T(8,128)(2,1)S(1)} %get-tuple-element.48), channel_id=1, source_target_pairs={{0,4},{2,6},{4,0},{6,2},{8,12},{10,14},{12,8},{14,10},{16,20},{18,... | collective-permute-start | bytes 49160 | tf_op jit(solution)/shard_map/ppermute | solution.py:198
  37.8 4.6 %collective-permute-start.14 = (bf16[64,128]{1,0:T(8,128)(2,1)S(1)}, bf16[64,128]{1,0:T(8,128)(2,1)S(1)}, u32[]{:S(2)}, u32[]{:S(2)}) collective-permute-start(bf16[64,128]{1,0:T(8,128)(2,1)S(1)} %get-tuple-element.49), channel_id=1, source_target_pairs={{0,6},{2,4},{4,2},{6,0},{8,14},{10,12},{12,10},{14,8},{16,22},{18,... | collective-permute-start | bytes 49160 | tf_op jit(solution)/shard_map/ppermute | solution.py:198
  42.5 6.5 %collective-permute-start.20 = (bf16[64,128]{1,0:T(8,128)(2,1)S(1)}, bf16[64,128]{1,0:T(8,128)(2,1)S(1)}, u32[]{:S(2)}, u32[]{:S(2)}) collective-permute-start(bf16[64,128]{1,0:T(8,128)(2,1)S(1)} %get-tuple-element.51.refs_4_), channel_id=1, source_target_pairs={{0,6},{2,4},{4,2},{6,0},{8,14},{10,12},{12,10},{14,8},{16,22},{18,... | collective-permute-start | bytes 49160 | tf_op jit(solution)/shard_map/ppermute | solution.py:198
  43.0 9.7 %collective-permute-start.17 = (bf16[112,128]{1,0:T(8,128)(2,1)S(1)}, bf16[112,128]{1,0:T(8,128)(2,1)S(1)}, u32[]{:S(2)}, u32[]{:S(2)}) collective-permute-start(bf16[112,128]{1,0:T(8,128)(2,1)S(1)} %get-tuple-element.50.refs_0_), channel_id=1, source_target_pairs={{0,24},{2,26},{4,28},{6,30},{8,16},{10,18},{12,20},{14,22},{16,8},... | collective-permute-start | bytes 86024 | tf_op jit(solution)/shard_map/ppermute | solution.py:198
  44.3 8.4 %collective-permute-start.16 = (bf16[112,128]{1,0:T(8,128)(2,1)S(1)}, bf16[112,128]{1,0:T(8,128)(2,1)S(1)}, u32[]{:S(2)}, u32[]{:S(2)}) collective-permute-start(bf16[112,128]{1,0:T(8,128)(2,1)S(1)} %get-tuple-element.50.refs_0_), channel_id=1, source_target_pairs={{0,16},{2,18},{4,20},{6,22},{8,24},{10,26},{12,28},{14,30},{16,0},... | collective-permute-start | bytes 86024 | tf_op jit(solution)/shard_map/ppermute | solution.py:198
  44.3 8.4 %collective-permute-start.15 = (bf16[112,128]{1,0:T(8,128)(2,1)S(1)}, bf16[112,128]{1,0:T(8,128)(2,1)S(1)}, u32[]{:S(2)}, u32[]{:S(2)}) collective-permute-start(bf16[112,128]{1,0:T(8,128)(2,1)S(1)} %get-tuple-element.50.refs_0_), channel_id=1, source_target_pairs={{0,8},{2,10},{4,12},{6,14},{8,0},{10,2},{12,4},{14,6},{16,24},{18,... | collective-permute-start | bytes 86024 | tf_op jit(solution)/shard_map/ppermute | solution.py:198
  47.4 3.7 %collective-permute-start.19 = (bf16[64,128]{1,0:T(8,128)(2,1)S(1)}, bf16[64,128]{1,0:T(8,128)(2,1)S(1)}, u32[]{:S(2)}, u32[]{:S(2)}) collective-permute-start(bf16[64,128]{1,0:T(8,128)(2,1)S(1)} %get-tuple-element.51.refs_4_), channel_id=1, source_target_pairs={{0,4},{2,6},{4,0},{6,2},{8,12},{10,14},{12,8},{14,10},{16,20},{18,... | collective-permute-start | bytes 49160 | tf_op jit(solution)/shard_map/ppermute | solution.py:198
  49.0 3.7 %collective-permute-start.18 = (bf16[64,128]{1,0:T(8,128)(2,1)S(1)}, bf16[64,128]{1,0:T(8,128)(2,1)S(1)}, u32[]{:S(2)}, u32[]{:S(2)}) collective-permute-start(bf16[64,128]{1,0:T(8,128)(2,1)S(1)} %get-tuple-element.51.refs_4_), channel_id=1, source_target_pairs={{0,2},{2,0},{4,6},{6,4},{8,10},{10,8},{12,14},{14,12},{16,18},{18,... | collective-permute-start | bytes 49160 | tf_op jit(solution)/shard_map/ppermute | solution.py:198
  52.8 4.7 %collective-permute-start.31 = (bf16[256,128]{1,0:T(8,128)(2,1)S(1)}, bf16[256,128]{1,0:T(8,128)(2,1)S(1)}, u32[]{:S(2)}, u32[]{:S(2)}) collective-permute-start(bf16[256,128]{1,0:T(8,128)(2,1)S(1)} %get-tuple-element.53.refs_4_), channel_id=1, source_target_pairs={{0,1},{1,0},{2,3},{3,2},{4,5},{5,4},{6,7},{7,6},{8,9},{9,8},{10,11... | collective-permute-start | bytes 196616 | tf_op jit(solution)/shard_map/ppermute | solution.py:239
  52.8 6.9 %collective-permute-start.26 = (bf16[256,128]{1,0:T(8,128)(2,1)S(1)}, bf16[256,128]{1,0:T(8,128)(2,1)S(1)}, u32[]{:S(2)}, u32[]{:S(2)}) collective-permute-start(bf16[256,128]{1,0:T(8,128)(2,1)S(1)} %get-tuple-element.53.refs_4_), channel_id=1, source_target_pairs={{0,24},{2,26},{4,28},{6,30},{8,16},{10,18},{12,20},{14,22},{16,8},... | collective-permute-start | bytes 196616 | tf_op jit(solution)/shard_map/ppermute | solution.py:198
  54.4 7.7 %collective-permute-start.25 = (bf16[256,128]{1,0:T(8,128)(2,1)S(1)}, bf16[256,128]{1,0:T(8,128)(2,1)S(1)}, u32[]{:S(2)}, u32[]{:S(2)}) collective-permute-start(bf16[256,128]{1,0:T(8,128)(2,1)S(1)} %get-tuple-element.53.refs_4_), channel_id=1, source_target_pairs={{0,16},{2,18},{4,20},{6,22},{8,24},{10,26},{12,28},{14,30},{16,0},... | collective-permute-start | bytes 196616 | tf_op jit(solution)/shard_map/ppermute | solution.py:198
  54.5 9.4 %collective-permute-start.23 = (bf16[448,128]{1,0:T(8,128)(2,1)S(1)}, bf16[448,128]{1,0:T(8,128)(2,1)S(1)}, u32[]{:S(2)}, u32[]{:S(2)}) collective-permute-start(bf16[448,128]{1,0:T(8,128)(2,1)S(1)} %get-tuple-element.52.refs_0_), channel_id=1, source_target_pairs={{0,6},{2,4},{4,2},{6,0},{8,14},{10,12},{12,10},{14,8},{16,22},{18,... | collective-permute-start | bytes 344072 | tf_op jit(solution)/shard_map/ppermute | solution.py:198
  56.0 8.5 %collective-permute-start.22 = (bf16[448,128]{1,0:T(8,128)(2,1)S(1)}, bf16[448,128]{1,0:T(8,128)(2,1)S(1)}, u32[]{:S(2)}, u32[]{:S(2)}) collective-permute-start(bf16[448,128]{1,0:T(8,128)(2,1)S(1)} %get-tuple-element.52.refs_0_), channel_id=1, source_target_pairs={{0,4},{2,6},{4,0},{6,2},{8,12},{10,14},{12,8},{14,10},{16,20},{18,... | collective-permute-start | bytes 344072 | tf_op jit(solution)/shard_map/ppermute | solution.py:198
  57.5 7.1 %collective-permute-start.21 = (bf16[448,128]{1,0:T(8,128)(2,1)S(1)}, bf16[448,128]{1,0:T(8,128)(2,1)S(1)}, u32[]{:S(2)}, u32[]{:S(2)}) collective-permute-start(bf16[448,128]{1,0:T(8,128)(2,1)S(1)} %get-tuple-element.52.refs_0_), channel_id=1, source_target_pairs={{0,2},{2,0},{4,6},{6,4},{8,10},{10,8},{12,14},{14,12},{16,18},{18,... | collective-permute-start | bytes 344072 | tf_op jit(solution)/shard_map/ppermute | solution.py:198
  59.7 4.3 %collective-permute-start.24 = (bf16[256,128]{1,0:T(8,128)(2,1)S(1)}, bf16[256,128]{1,0:T(8,128)(2,1)S(1)}, u32[]{:S(2)}, u32[]{:S(2)}) collective-permute-start(bf16[256,128]{1,0:T(8,128)(2,1)S(1)} %get-tuple-element.53.refs_4_), channel_id=1, source_target_pairs={{0,8},{2,10},{4,12},{6,14},{8,0},{10,2},{12,4},{14,6},{16,24},{18,... | collective-permute-start | bytes 196616 | tf_op jit(solution)/shard_map/ppermute | solution.py:198
  62.0 3.0 %collective-permute-start.27 = (bf16[448,128]{1,0:T(8,128)(2,1)S(1)}, bf16[448,128]{1,0:T(8,128)(2,1)S(1)}, u32[]{:S(2)}, u32[]{:S(2)}) collective-permute-start(bf16[448,128]{1,0:T(8,128)(2,1)S(1)} %get-tuple-element.52.refs_0_), channel_id=1, source_target_pairs={{0,1},{1,0},{2,3},{3,2},{4,5},{5,4},{6,7},{7,6},{8,9},{9,8},{10,11... | collective-permute-start | bytes 344072 | tf_op jit(solution)/shard_map/ppermute | solution.py:239
  64.0 3.4 %collective-permute-start.30 = (bf16[448,128]{1,0:T(8,128)(2,1)S(1)}, bf16[448,128]{1,0:T(8,128)(2,1)S(1)}, u32[]{:S(2)}, u32[]{:S(2)}) collective-permute-start(bf16[448,128]{1,0:T(8,128)(2,1)S(1)} %collective-permute-done.23.refs_3_), channel_id=1, source_target_pairs={{0,1},{1,0},{2,3},{3,2},{4,5},{5,4},{6,7},{7,6},{8,9},{9,8},{10,11... | collective-permute-start | bytes 344072 | tf_op jit(solution)/shard_map/ppermute | solution.py:239
  64.5 2.9 %collective-permute-start.29 = (bf16[448,128]{1,0:T(8,128)(2,1)S(1)}, bf16[448,128]{1,0:T(8,128)(2,1)S(1)}, u32[]{:S(2)}, u32[]{:S(2)}) collective-permute-start(bf16[448,128]{1,0:T(8,128)(2,1)S(1)} %collective-permute-done.22.refs_2_), channel_id=1, source_target_pairs={{0,1},{1,0},{2,3},{3,2},{4,5},{5,4},{6,7},{7,6},{8,9},{9,8},{10,11... | collective-permute-start | bytes 344072 | tf_op jit(solution)/shard_map/ppermute | solution.py:239
  64.5 2.8 %collective-permute-start.28 = (bf16[448,128]{1,0:T(8,128)(2,1)S(1)}, bf16[448,128]{1,0:T(8,128)(2,1)S(1)}, u32[]{:S(2)}, u32[]{:S(2)}) collective-permute-start(bf16[448,128]{1,0:T(8,128)(2,1)S(1)} %collective-permute-done.21.refs_1_), channel_id=1, source_target_pairs={{0,1},{1,0},{2,3},{3,2},{4,5},{5,4},{6,7},{7,6},{8,9},{9,8},{10,11... | collective-permute-start | bytes 344072 | tf_op jit(solution)/shard_map/ppermute | solution.py:239
  65.0 2.4 %collective-permute-start.33 = (bf16[256,128]{1,0:T(8,128)(2,1)S(1)}, bf16[256,128]{1,0:T(8,128)(2,1)S(1)}, u32[]{:S(2)}, u32[]{:S(2)}) collective-permute-start(bf16[256,128]{1,0:T(8,128)(2,1)S(1)} %collective-permute-done.25.refs_6_), channel_id=1, source_target_pairs={{0,1},{1,0},{2,3},{3,2},{4,5},{5,4},{6,7},{7,6},{8,9},{9,8},{10,11... | collective-permute-start | bytes 196616 | tf_op jit(solution)/shard_map/ppermute | solution.py:239
  65.2 2.1 %collective-permute-start.32 = (bf16[256,128]{1,0:T(8,128)(2,1)S(1)}, bf16[256,128]{1,0:T(8,128)(2,1)S(1)}, u32[]{:S(2)}, u32[]{:S(2)}) collective-permute-start(bf16[256,128]{1,0:T(8,128)(2,1)S(1)} %collective-permute-done.24.refs_5_), channel_id=1, source_target_pairs={{0,1},{1,0},{2,3},{3,2},{4,5},{5,4},{6,7},{7,6},{8,9},{9,8},{10,11... | collective-permute-start | bytes 196616 | tf_op jit(solution)/shard_map/ppermute | solution.py:239
  (9 other events, 60.1 us)

commit v3 on v1

--- a/solution.py
+++ b/solution.py
@@ -41,12 +41,19 @@
 def put_halo(stack, before, after, rows, peers, sign):
     here = lax.axis_index("space")
     zero = jnp.zeros(before.shape, BF16)
-    put_shifted(stack, 0, jnp.where(here > 0, before[...], zero), sign)
-    put_shifted(stack, rows + 1, jnp.where(here < peers - 1, after[...], zero), sign)
-
-
-def grads_kernel(peers, feat, top, lat_w, out_w, cot, before, after, merged, grad_top, *rest):
-    outs, stack = rest[:-1], rest[-1]
+    put_shifted(stack, 0, jnp.where(here > 0, before, zero), sign)
+    put_shifted(stack, rows + 1, jnp.where(here < peers - 1, after, zero), sign)
+
+
+def grads_kernel(peers, *refs):
+    far, (before, after, merged, grad_top), rest = refs[:5], refs[5:9], refs[9:]
+    outs, stack, near, sems = rest[:-7], rest[-7], rest[-6:-1], rest[-1]
+    copies = [pltpu.make_async_copy(a, b, sems.at[i]) for i, (a, b) in enumerate(zip(far, near))]
+    for copy in copies:
+        copy.start()
+    feat, lat_w, top, cot, out_w = near
+    for copy in copies[:3]:
+        copy.wait()
     rows, cols, channels = cot.shape
     cells = rows * cols
     half = cols // 2
@@ -58,9 +65,10 @@
         lifted = jnp.dot(spread, top[q], preferred_element_type=F32)
         for r in (2 * q, 2 * q + 1):
             merged[r * cols : (r + 1) * cols, :] = (lateral[r * cols : (r + 1) * cols] + lifted).astype(BF16)
+    copies[3].wait()
     for r in range(rows):
         put_shifted(stack, r + 1, cot[r], 1)
-    put_halo(stack, before, after, rows, peers, 1)
+    put_halo(stack, before[...], after[...], rows, peers, 1)
 
     def put(start, block):
         if len(outs) == 1:
@@ -72,12 +80,19 @@
         mine[start : start + block.shape[0], :] = jnp.where(here == 0, left, right)
         theirs[start : start + block.shape[0], :] = jnp.where(here == 0, right, left).astype(BF16)
 
+    if len(outs) == 2:
+        here = lax.axis_index("space")
+        edge = jnp.where(here == 0, merged[cells - cols :, :], merged[:cols, :])
+        start = 9 * channels + in_channels
+        outs[1][start : start + cols, :] = edge[:, : channels // 2]
+        outs[1][start + cols :, :] = edge[:, channels // 2 :]
     merged_t = jnp.transpose(merged[...])
     for i in range(3):
         strip = stack[2 - i : 2 - i + rows].reshape(cells, 3 * channels)
         part = jnp.dot(merged_t, strip, preferred_element_type=F32)
         for j in range(3):
             put((3 * i + j) * channels, part[:, j * channels : (j + 1) * channels])
+    copies[4].wait()
     total = jnp.zeros((cells, channels), F32)
     for i in range(3):
         strip = stack[2 - i : 2 - i + rows].reshape(cells, 3 * channels)
@@ -94,11 +109,17 @@
     put(9 * channels, jnp.dot(feat_t, grad, preferred_element_type=F32))
 
 
-def forward_kernel(peers, merged, out_w, before, after, out, stack):
+def forward_kernel(peers, merged, out_w, *refs):
+    edges, (out, stack) = refs[:-2], refs[-2:]
     rows, cols, channels = merged.shape
     for r in range(rows):
         put_shifted(stack, r + 1, merged[r], -1)
-    put_halo(stack, before, after, rows, peers, -1)
+    if len(edges) == 1:
+        start = edges[0].shape[0] - 2 * cols
+        edge = jnp.concatenate([edges[0][start : start + cols, :], edges[0][start + cols :, :]], axis=1)
+        put_halo(stack, edge, edge, rows, peers, -1)
+    else:
+        put_halo(stack, edges[0][...], edges[1][...], rows, peers, -1)
     total = jnp.zeros((rows * cols, channels), F32)
     for i in range(3):
         strip = stack[i : i + rows].reshape(rows * cols, 3 * channels)
@@ -107,21 +128,48 @@
     out[...] = total.astype(BF16).reshape(out.shape)
 
 
-def sum_everywhere(mine, theirs, scale):
+def place_kernel(mine, other, kernel_out, lateral_out, sems):
+    side = lax.axis_index("space")
+    edge, rest = kernel_out.shape[0], lateral_out.shape[0]
+    copies = []
+    for columns, half in ((side, mine), (1 - side, other)):
+        lanes = pl.ds(pl.multiple_of(columns * 128, 128), 128)
+        copies.append((half.at[pl.ds(0, edge), :], kernel_out.at[:, lanes]))
+        copies.append((half.at[pl.ds(edge, rest), :], lateral_out.at[:, lanes]))
+    copies = [pltpu.make_async_copy(source, to, sems.at[i]) for i, (source, to) in enumerate(copies)]
+    for copy in copies:
+        copy.start()
+    for copy in copies:
+        copy.wait()
+
+
+def peer_groups():
+    plane = [[4 * z + q for q in range(4)] for z in range(4)]
+    line = [[4 * z + q for z in range(4)] for q in range(4)]
+    pick = lambda chips, core: [[2 * chip + core for chip in group] for group in chips]
+    return pick(plane, 0) + pick(line, 1), pick(line, 0) + pick(plane, 1)
+
+
+def swap_pieces(pieces, groups):
+    return lax.all_to_all(pieces, ("dp", "space"), 0, 0, axis_index_groups=groups, tiled=True)
+
+
+def sum_everywhere(mine, got, scale, edge):
     length, width = mine.shape
-    parts = lax.axis_size("dp")
     swap = [(0, 1), (1, 0)]
-    got = lax.ppermute(theirs, "space", swap)
-    pair = (mine + got.astype(F32)).astype(BF16)
-    share = -(-length // (16 * parts)) * 16
-    pair = jnp.pad(pair, ((0, share * parts - length), (0, 0))).reshape(parts, share, width)
-    terms = lax.all_to_all(pair, "dp", 0, 0, tiled=True)
-    total = (jnp.sum(terms.astype(F32), axis=0) * scale).astype(BF16)
-    copies = jnp.broadcast_to(total[None], terms.shape)
-    whole = lax.all_to_all(copies, "dp", 0, 0, tiled=True).reshape(parts * share, width)[:length]
-    other = lax.ppermute(whole, "space", swap)
-    first = lax.axis_index("space") == 0
-    return jnp.concatenate([jnp.where(first, whole, other), jnp.where(first, other, whole)], axis=1)
+    first, second = peer_groups()
+    pair = (mine + got[:length].astype(F32)).astype(BF16).reshape(4, length // 4, width)
+    total = jnp.sum(swap_pieces(pair, first).astype(F32), axis=0).astype(BF16).reshape(4, length // 16, width)
+    total = (jnp.sum(swap_pieces(total, second).astype(F32), axis=0) * scale).astype(BF16)
+    total = swap_pieces(jnp.broadcast_to(total[None], (4, *total.shape)), second).reshape(length // 4, width)
+    total = swap_pieces(jnp.broadcast_to(total[None], (4, *total.shape)), first).reshape(length, width)
+    other = lax.ppermute(total, "space", swap)
+    return pl.pallas_call(
+        place_kernel,
+        out_shape=[jax.ShapeDtypeStruct((rows, 2 * width), BF16) for rows in (edge, length - edge)],
+        out_specs=[pl.BlockSpec(memory_space=pltpu.HBM)] * 2,
+        scratch_shapes=[pltpu.SemaphoreType.DMA((4,))],
+    )(total, other)
 
 
 def local(features, top_down, lateral_weight, out_kernel, cotangent):
@@ -132,15 +180,20 @@
     length = 9 * channels + in_channels
     taps = out_kernel.reshape(9, channels, channels)
     params = pltpu.CompilerParams(vmem_limit_bytes=48 * 2**20)
-    halves = peers == 2
+    halves = peers == 2 and lax.axis_size("dp") == 16 and images == 1 and (channels, in_channels) == (256, 512)
     if halves:
-        sums = [jax.ShapeDtypeStruct((length, channels // 2), kind) for kind in (F32, BF16)]
+        sums = [
+            jax.ShapeDtypeStruct((length, channels // 2), F32),
+            jax.ShapeDtypeStruct((length + 2 * cols, channels // 2), BF16),
+        ]
     else:
         sums = [jax.ShapeDtypeStruct((length, channels), F32)]
     outs, tops, parts = [], [], None
     for image in range(images):
         cot = cotangent[image]
         cot_before, cot_after = neighbour_rows(cot)
+        arrays = (features[image].reshape(cells, in_channels), lateral_weight, top_down[image], cot, taps)
+        arrays = [pltpu.with_memory_space_constraint(array, pltpu.HBM) for array in arrays]
         merged, grad_top, *part = pl.pallas_call(
             functools.partial(grads_kernel, peers),
             out_shape=[
@@ -148,22 +201,21 @@
                 jax.ShapeDtypeStruct((rows // 2, cols // 2, channels), BF16),
                 *sums,
             ],
-            scratch_shapes=[pltpu.VMEM((rows + 2, cols, 3 * channels), BF16)],
+            in_specs=[pl.BlockSpec(memory_space=pltpu.HBM)] * 5 + [pl.BlockSpec(memory_space=pltpu.VMEM)] * 2,
+            scratch_shapes=[
+                pltpu.VMEM((rows + 2, cols, 3 * channels), BF16),
+                *[pltpu.VMEM(array.shape, BF16) for array in arrays],
+                pltpu.SemaphoreType.DMA((5,)),
+            ],
             compiler_params=params,
             cost_estimate=pl.CostEstimate(
                 flops=2 * cells * channels * (18 * channels + 2 * in_channels), bytes_accessed=6 * 2**20, transcendentals=0
             ),
-        )(
-            features[image].reshape(cells, in_channels),
-            top_down[image],
-            lateral_weight,
-            taps,
-            cot,
-            cot_before,
-            cot_after,
-        )
+        )(*arrays, cot_before, cot_after)
         merged = merged.reshape(rows, cols, channels)
-        before, after = neighbour_rows(merged)
+        if halves:
+            part[1] = lax.ppermute(part[1], "space", [(0, 1), (1, 0)])
+        edges = (part[1],) if halves else neighbour_rows(merged)
         outs.append(
             pl.pallas_call(
                 functools.partial(forward_kernel, peers),
@@ -173,19 +225,17 @@
                 cost_estimate=pl.CostEstimate(
                     flops=2 * cells * channels * 9 * channels, bytes_accessed=2 * 2**20, transcendentals=0
                 ),
-            )(merged, taps, before, after)
+            )(merged, taps, *edges)
         )
         tops.append(grad_top)
-        parts = part if parts is None else [
-            (a.astype(F32) + b.astype(F32)).astype(a.dtype) for a, b in zip(parts, part)
-        ]
+        parts = part if parts is None else [a + b for a, b in zip(parts, part)]
     scale = 1.0 / (images * lax.axis_size("dp"))
     if halves:
-        total = sum_everywhere(*parts, scale)
+        grad_kernel, grad_lateral = sum_everywhere(*parts, scale, 9 * channels)
     else:
         total = (lax.psum(parts[0], ("dp", "space")) * scale).astype(BF16)
-    grad_kernel = total[: 9 * channels].reshape(3, 3, channels, channels)
-    return jnp.stack(outs), jnp.stack(tops), grad_kernel, total[9 * channels :]
+        grad_kernel, grad_lateral = total[: 9 * channels], total[9 * channels :]
+    return jnp.stack(outs), jnp.stack(tops), grad_kernel.reshape(out_kernel.shape), grad_lateral
 
 
 def solution(mesh):

time: 71.6 us -> 61.8 us (0.86)
  blocking collectives: 50.8 us -> 44.6 us
  local copies, waits for them, and re-layouts: 6.15 us -> 1.82 us
  Pallas kernels: 5.49 us -> 9.53 us
  other arithmetic: 2.27 us -> 0.32 us
  waiting for transfers between devices: 4.47 us -> 2.8 us
    all_to_all x2 -> x4, blocking collectives: 50.8 us -> 44.6 us  [swap_pieces(): lax.all_to_all(pieces, ('dp', 'space'), 0, 0, axis_index_groups=groups, t...]
    unnamed x12 -> x6, local copies, waits for them, and re-layouts: 5.24 us -> 0.89 us
    pallas_call x0 -> x1, Pallas kernels: none -> 2.45 us  [sum_everywhere(): pl.pallas_call(place_kernel, out_shape=[jax.ShapeDtypeStruct((rows, 2 * w...]
    concatenate x2 -> x0, other arithmetic: 1.87 us -> none  [sum_everywhere(): jnp.concatenate([jnp.where(first, whole, other), jnp.where(first, other,...]
    ppermute x2 -> x1, waiting for transfers between devices: 2.63 us -> 0.88 us  [neighbour_rows(): got = lax.ppermute(edge, 'space', [(0, 1), (1, 0)])]
    pallas_call x1, Pallas kernels: 3.65 us -> 5.25 us  [local(): pl.pallas_call(functools.partial(grads_kernel, peers), out_shape=[jax.Sha...]
    ppermute x2, starting transfers between devices: 0.35 us -> 1.14 us  [the longest x1 0.73 us: sum_everywhere(): other = lax.ppermute(total, 'space', swap)]
  transfers between devices with their start and end apart: 4 -> 3, of which waited for: 3 -> 2; matrix products, arithmetic and copies ran while one was open for 0% -> 0% of each run, Pallas kernels for 3% -> 3%
where the time goes in v3:
time: 61.8 us; the launch traced here: 61.4 us
  blocking collectives  44.6 us (72%)
  Pallas kernels  9.53 us (15%)
  waiting for transfers between devices  2.8 us (5%)
  local copies, waits for them, and re-layouts  1.82 us (3%)
  starting transfers between devices  1.6 us (3%)
  between operations  0.69 us (1%)
    all_to_all x4, blocking collectives, swap_pieces(): lax.all_to_all(pieces, ('dp', 'space'), 0, 0, axis_index_groups=groups, t...  44.6 us
    pallas_call x1, Pallas kernels, local(): pl.pallas_call(functools.partial(grads_kernel, peers), out_shape=[jax.Sha...  5.25 us
    pallas_call x1, Pallas kernels, sum_everywhere(): pl.pallas_call(place_kernel, out_shape=[jax.ShapeDtypeStruct((rows, 2 * w...  2.45 us
    ppermute x1, waiting for transfers between devices, local(): part[1] = lax.ppermute(part[1], 'space', [(0, 1), (1, 0)])  1.91 us
    pallas_call x1, Pallas kernels, local(): pl.pallas_call(functools.partial(forward_kernel, peers), out_shape=jax.Sh...  1.83 us
  transfers between devices with their start and end apart: 3, of which 2 were waited for; matrix products, arithmetic and copies ran while one was open for 0% of the time, Pallas kernels for 3%

profile of v3, /device:TPU:0, one launch (start us, length us, event | category | flops | bytes accessed | tf_op | source)
XLA Modules:
  0.0 61.4 jit_solution(4594674187904698039)
XLA Ops:
  0.6 0.8 %dynamic-slice_bitcast_fusion = bf16[96,256]{1,0:T(8,128)(2,1)S(1)} fusion(bf16[1,8,96,256]{3,2,1,0:T(8,128)(2,1)} %param.9, s32[]{:T(128)S(6)} %select_n.4), kind=kLoop, calls=%fused_computation.3 | loop fusion | bytes 98308 | tf_op jit(solution)/shard_map/jit(dynamic_index_in_dim)/squeeze | solution.py:21
  1.4 0.5 collective-permute-start
  1.9 0.9 %collective-permute-done.refs_5_.refs_6_ = bf16[96,256]{1,0:T(8,128)(2,1)S(1)} collective-permute-done((bf16[96,256]{1,0:T(8,128)(2,1)S(1)}, bf16[96,256]{1,0:T(8,128)(2,1)S(1)}, u32[]{:S(2)}, u32[]{:S(2)}) %collective-permute-start) | collective-permute-done | bytes 49184 | tf_op jit(solution)/shard_map/ppermute | solution.py:22
  2.8 5.2 %shard_map.84 = (bf16[768,256]{1,0:T(8,128)(2,1)S(1)}, bf16[4,48,256]{2,1,0:T(8,128)(2,1)}, f32[2816,128]{1,0:T(8,128)S(1)}, bf16[3008,128]{1,0:T(8,128)(2,1)S(1)}) custom-call(bf16[768,512]{1,0:T(8,128)(2,1)} %bitcast.24, bf16[512,256]{1,0:T(8,128)(2,1)} %refs_1_.1, bf16[4,48,256]{2,1,0:T(8,128)(2,1)} %bitcast.25, bf16[8,96,256]{2,1,0:T(8,128)(2,1)} %bitcast.22, ...), custom_call_target="tpu_custom_call" | custom-call | flops 2214592512 | bytes 6291456 | tf_op jit(solution)/shard_map/pallas_call | solution.py:197
  8.0 0.4 collective-permute-start.1
  8.4 1.9 %collective-permute-done.1.refs_0_ = bf16[3008,128]{1,0:T(8,128)(2,1)S(1)} collective-permute-done((bf16[3008,128]{1,0:T(8,128)(2,1)S(1)}, bf16[3008,128]{1,0:T(8,128)(2,1)S(1)}, u32[]{:S(2)}, u32[]{:S(2)}) %collective-permute-start.1) | collective-permute-done | bytes 770080 | tf_op jit(solution)/shard_map/ppermute | solution.py:217
  10.4 0.1 add_convert_fusion
  10.5 13.2 %all_to_all.20 = bf16[4,704,128]{2,1,0:T(8,128)(2,1)S(1)} all-to-all(bf16[4,704,128]{2,1,0:T(8,128)(2,1)S(1)} %bitcast.19), channel_id=1, replica_groups={{0,2,4,6},{8,10,12,14},{16,18,20,22},{24,26,28,30},{1,9,17,25},{3,11,19..., dimensions={0} | all-to-all | bytes 1441792 | tf_op jit(solution)/shard_map/all_to_all | solution.py:154
  23.7 0.1 reduce_sum.21
  23.9 11.4 %all_to_all.21 = bf16[4,176,128]{2,1,0:T(8,128)(2,1)S(1)} all-to-all(bf16[4,176,128]{2,1,0:T(8,128)(2,1)S(1)} %bitcast.21), channel_id=1, replica_groups={{0,8,16,24},{2,10,18,26},{4,12,20,28},{6,14,22,30},{1,3,5,7},{9,11,13,1..., dimensions={0} | all-to-all | bytes 360448 | tf_op jit(solution)/shard_map/all_to_all | solution.py:154
  35.3 0.0 copy-start
  35.4 9.2 %all_to_all.22 = bf16[4,176,128]{2,1,0:T(8,128)(2,1)S(1)} all-to-all(bf16[4,176,128]{2,1,0:T(8,128)(2,1)S(1)} %broadcast_in_dim.6), channel_id=1, replica_groups={{0,8,16,24},{2,10,18,26},{4,12,20,28},{6,14,22,30},{1,3,5,7},{9,11,13,1..., dimensions={0} | all-to-all | bytes 360448 | tf_op jit(solution)/shard_map/all_to_all | solution.py:154
  44.6 0.1 broadcast_in_dim.15
  44.7 10.7 %all_to_all.23 = bf16[4,704,128]{2,1,0:T(8,128)(2,1)S(1)} all-to-all(bf16[4,704,128]{2,1,0:T(8,128)(2,1)S(1)} %broadcast_in_dim.15), channel_id=1, replica_groups={{0,2,4,6},{8,10,12,14},{16,18,20,22},{24,26,28,30},{1,9,17,25},{3,11,19..., dimensions={0} | all-to-all | bytes 1441792 | tf_op jit(solution)/shard_map/all_to_all | solution.py:154
  55.5 0.0 copy-start.1
  55.5 0.7 %collective-permute-start.2 = (bf16[2816,128]{1,0:T(8,128)(2,1)S(1)}, bf16[2816,128]{1,0:T(8,128)(2,1)S(1)}, u32[]{:S(2)}, u32[]{:S(2)}) collective-permute-start(bf16[2816,128]{1,0:T(8,128)(2,1)S(1)} %bitcast.17), channel_id=1, source_target_pairs={{0,1},{1,0},{2,3},{3,2},{4,5},{5,4},{6,7},{7,6},{8,9},{9,8},{10,11... | collective-permute-start | bytes 2162696 | tf_op jit(solution)/shard_map/ppermute | solution.py:166
  56.2 0.0 copy-done
  56.2 1.8 %shard_map.85 = bf16[8,96,256]{2,1,0:T(8,128)(2,1)} custom-call(bf16[8,96,256]{2,1,0:T(8,128)(2,1)S(1)} %bitcast.16, bf16[9,256,256]{2,1,0:T(8,128)(2,1)S(1)} %bitcast.15, bf16[3008,128]{1,0:T(8,128)(2,1)S(1)} %collective-permute-done.1.refs_0_), custom_call_target="tpu_custom_call" | custom-call | flops 905969664 | bytes 2097152 | tf_op jit(solution)/shard_map/pallas_call | solution.py:220
  58.0 0.0 copy-done.1
  58.0 0.0 collective-permute-done.2.other
  58.0 0.0 copy-start.2
  58.1 0.9 %copy-done.2 = bf16[2816,128]{1,0:T(8,128)(2,1)} copy-done((bf16[2816,128]{1,0:T(8,128)(2,1)}, bf16[2816,128]{1,0:T(8,128)(2,1)S(1)}, u32[]{:S(2)}) %copy-start.2) | copy-done | bytes 720920
  58.9 2.4 %shard_map.86 = (bf16[2304,256]{1,0:T(8,128)(2,1)}, bf16[512,256]{1,0:T(8,128)(2,1)}) custom-call(bf16[2816,128]{1,0:T(8,128)(2,1)} %bitcast.18, bf16[2816,128]{1,0:T(8,128)(2,1)} %copy-done.2), custom_call_target="tpu_custom_call" | custom-call | tf_op jit(solution)/shard_map/pallas_call | solution.py:167
  (3 shorter events, 0.1 us)
Async XLA Ops:
  1.4 1.3 %collective-permute-start = (bf16[96,256]{1,0:T(8,128)(2,1)S(1)}, bf16[96,256]{1,0:T(8,128)(2,1)S(1)}, u32[]{:S(2)}, u32[]{:S(2)}) collective-permute-start(bf16[96,256]{1,0:T(8,128)(2,1)S(1)} %dynamic-slice_bitcast_fusion), channel_id=1, source_target_pairs={{0,1},{1,0},{2,3},{3,2},{4,5},{5,4},{6,7},{7,6},{8,9},{9,8},{10,11... | collective-permute-start | bytes 147464 | tf_op jit(solution)/shard_map/ppermute | solution.py:22
  8.0 2.3 %collective-permute-start.1 = (bf16[3008,128]{1,0:T(8,128)(2,1)S(1)}, bf16[3008,128]{1,0:T(8,128)(2,1)S(1)}, u32[]{:S(2)}, u32[]{:S(2)}) collective-permute-start(bf16[3008,128]{1,0:T(8,128)(2,1)S(1)} %get-tuple-element.11), channel_id=1, source_target_pairs={{0,1},{1,0},{2,3},{3,2},{4,5},{5,4},{6,7},{7,6},{8,9},{9,8},{10,11... | collective-permute-start | bytes 2310152 | tf_op jit(solution)/shard_map/ppermute | solution.py:217
  35.3 20.9 %copy-start = (bf16[3,3,256,256]{3,2,1,0:T(8,128)(2,1)S(1)}, bf16[3,3,256,256]{3,2,1,0:T(8,128)(2,1)}, u32[]{:S(2)}) copy-start(bf16[3,3,256,256]{3,2,1,0:T(8,128)(2,1)} %param.8) | copy-start | bytes 3538948
  55.5 2.6 %copy-start.1 = (bf16[4,704,128]{2,1,0:T(8,128)(2,1)}, bf16[4,704,128]{2,1,0:T(8,128)(2,1)S(1)}, u32[]{:S(2)}) copy-start(bf16[4,704,128]{2,1,0:T(8,128)(2,1)S(1)} %all_to_all.23) | copy-start | bytes 2162692
  55.5 2.6 %collective-permute-start.2 = (bf16[2816,128]{1,0:T(8,128)(2,1)S(1)}, bf16[2816,128]{1,0:T(8,128)(2,1)S(1)}, u32[]{:S(2)}, u32[]{:S(2)}) collective-permute-start(bf16[2816,128]{1,0:T(8,128)(2,1)S(1)} %bitcast.17), channel_id=1, source_target_pairs={{0,1},{1,0},{2,3},{3,2},{4,5},{5,4},{6,7},{7,6},{8,9},{9,8},{10,11... | collective-permute-start | bytes 2162696 | tf_op jit(solution)/shard_map/ppermute | solution.py:166
  58.0 0.9 %copy-start.2 = (bf16[2816,128]{1,0:T(8,128)(2,1)}, bf16[2816,128]{1,0:T(8,128)(2,1)S(1)}, u32[]{:S(2)}) copy-start(bf16[2816,128]{1,0:T(8,128)(2,1)S(1)} %collective-permute-done.2.other) | copy-start | bytes 2162692

commit v4 on v3

--- a/solution.py
+++ b/solution.py
@@ -110,7 +110,7 @@
 
 
 def forward_kernel(peers, merged, out_w, *refs):
-    edges, (out, stack) = refs[:-2], refs[-2:]
+    edges, (out, stack, near, sem) = refs[:-4], refs[-4:]
     rows, cols, channels = merged.shape
     for r in range(rows):
         put_shifted(stack, r + 1, merged[r], -1)
@@ -125,51 +125,141 @@
         strip = stack[i : i + rows].reshape(rows * cols, 3 * channels)
         taps = out_w[3 * i : 3 * i + 3].reshape(3 * channels, channels)
         total = total + jnp.dot(strip, taps, preferred_element_type=F32)
-    out[...] = total.astype(BF16).reshape(out.shape)
-
-
-def place_kernel(mine, other, kernel_out, lateral_out, sems):
+    near[...] = total.astype(BF16).reshape(out.shape)
+    copy = pltpu.make_async_copy(near, out, sem)
+    copy.start()
+    copy.wait()
+
+
+def places():
+    chip, core = lax.axis_index("dp"), lax.axis_index("space")
+    x, y = chip % 2, (chip // 2) % 2
+    return jnp.where(core == 0, x, y), jnp.where(core == 0, y, x), chip // 4
+
+
+def block(index, length):
+    return pl.ds(pl.multiple_of(index * length, 16), length)
+
+
+def wide(ref):
+    return ref[...].astype(F32)
+
+
+def start_kernel(mine, got, for_both, for_first, for_second, own):
+    first, second, _ = places()
+    share = own.shape[0]
+    for out, a, b in (
+        (for_both, 1 - first, 1 - second),
+        (for_first, 1 - first, second),
+        (for_second, first, 1 - second),
+        (own, first, second),
+    ):
+        rows = block(2 * a + b, share)
+        out[...] = (mine[rows, :] + got[rows, :].astype(F32)).astype(out.dtype)
+
+
+def add_kernel(mine, got, out):
+    out[...] = (mine[...] + wide(got)).astype(out.dtype)
+
+
+def line_kernel(mine, got_first, got_second, own, *sends):
+    *_, z = places()
+    share = own.shape[0]
+    for k, out in enumerate((own, *sends)):
+        rows = block(z ^ k, share)
+        total = mine[rows, :] + got_first[rows, :].astype(F32) + got_second[rows, :].astype(F32)
+        out[...] = total.astype(out.dtype)
+
+
+def finish_kernel(scale, mine, *refs):
+    total = mine[...]
+    for got in refs[:-1]:
+        total = total + wide(got)
+    refs[-1][...] = (total * scale).astype(BF16)
+
+
+def join_kernel(*refs):
+    *_, z = places()
+    for k, part in enumerate(refs[:-1]):
+        refs[-1][block(z ^ k, part.shape[0]), :] = part[...]
+
+
+def place_kernel(*refs):
+    first, second, _ = places()
     side = lax.axis_index("space")
-    edge, rest = kernel_out.shape[0], lateral_out.shape[0]
-    copies = []
-    for columns, half in ((side, mine), (1 - side, other)):
+    kernel_out, lateral_out, sems = refs[8:]
+    edge, share = kernel_out.shape[0], refs[0].shape[0]
+    inside = edge - 3 * share
+    waits = []
+    for columns, quarters, a, b in ((side, refs[:4], first, second), (1 - side, refs[4:8], second, first)):
         lanes = pl.ds(pl.multiple_of(columns * 128, 128), 128)
-        copies.append((half.at[pl.ds(0, edge), :], kernel_out.at[:, lanes]))
-        copies.append((half.at[pl.ds(edge, rest), :], lateral_out.at[:, lanes]))
-    copies = [pltpu.make_async_copy(source, to, sems.at[i]) for i, (source, to) in enumerate(copies)]
-    for copy in copies:
-        copy.start()
-    for copy in copies:
+        for quarter, (i, j) in zip(quarters, ((0, 0), (0, 1), (1, 0), (1, 1))):
+            index = 2 * (a if i == 0 else 1 - a) + (b if j == 0 else 1 - b)
+            base = pl.multiple_of(index * share, 16)
+            head, tail = quarter.at[pl.ds(0, inside), :], quarter.at[pl.ds(inside, share - inside), :]
+            sem = sems.at[len(waits)]
+            copy = pltpu.make_async_copy(head, kernel_out.at[pl.ds(base, inside), lanes], sem)
+            copy.start()
+            waits.append(copy)
+            sem = sems.at[len(waits)]
+
+            @pl.when(index < 3)
+            def _():
+                rows = pl.ds(base + inside, share - inside)
+                pltpu.make_async_copy(tail, kernel_out.at[rows, lanes], sem).start()
+
+            @pl.when(index == 3)
+            def _():
+                pltpu.make_async_copy(tail, lateral_out.at[:, lanes], sem).start()
+
+            waits.append(pltpu.make_async_copy(tail, lateral_out.at[:, lanes], sem))
+    for copy in waits:
         copy.wait()
 
 
-def peer_groups():
-    plane = [[4 * z + q for q in range(4)] for z in range(4)]
-    line = [[4 * z + q for z in range(4)] for q in range(4)]
-    pick = lambda chips, core: [[2 * chip + core for chip in group] for group in chips]
-    return pick(plane, 0) + pick(line, 1), pick(line, 0) + pick(plane, 1)
-
-
-def swap_pieces(pieces, groups):
-    return lax.all_to_all(pieces, ("dp", "space"), 0, 0, axis_index_groups=groups, tiled=True)
+def exchange(array, step):
+    pairs = []
+    for chip in range(16):
+        for core in range(2):
+            flip = {"first": 1 + core, "second": 2 - core}.get(step) or 4 * step
+            pairs.append((2 * chip + core, 2 * (chip ^ flip) + core))
+    return lax.ppermute(array, ("dp", "space"), pairs)
+
+
+def swap(array):
+    return lax.ppermute(array, "space", [(0, 1), (1, 0)])
+
+
+def call(kernel, *shapes, **more):
+    return pl.pallas_call(
+        kernel, out_shape=[jax.ShapeDtypeStruct(shape, kind) for shape, kind in shapes], **more
+    )
 
 
 def sum_everywhere(mine, got, scale, edge):
     length, width = mine.shape
-    swap = [(0, 1), (1, 0)]
-    first, second = peer_groups()
-    pair = (mine + got[:length].astype(F32)).astype(BF16).reshape(4, length // 4, width)
-    total = jnp.sum(swap_pieces(pair, first).astype(F32), axis=0).astype(BF16).reshape(4, length // 16, width)
-    total = (jnp.sum(swap_pieces(total, second).astype(F32), axis=0) * scale).astype(BF16)
-    total = swap_pieces(jnp.broadcast_to(total[None], (4, *total.shape)), second).reshape(length // 4, width)
-    total = swap_pieces(jnp.broadcast_to(total[None], (4, *total.shape)), first).reshape(length, width)
-    other = lax.ppermute(total, "space", swap)
-    return pl.pallas_call(
+    quarter, part = (length // 4, width), (length // 16, width)
+    for_both, for_first, for_second, own = call(start_kernel, (quarter, BF16), (quarter, BF16), (quarter, F32), (quarter, F32))(mine, got)
+    got_both = exchange(for_both, "first")
+    got_first = exchange(for_first, "first")
+    [for_second] = call(add_kernel, (quarter, BF16))(for_second, got_both)
+    got_second = exchange(for_second, "second")
+    own, *sends = call(line_kernel, (part, F32), *[(part, BF16)] * 3)(own, got_first, got_second)
+    parts = [exchange(sends[k - 1], k) for k in (3, 2, 1)]
+    [total] = call(functools.partial(finish_kernel, scale), (part, BF16))(own, *parts)
+    parts = [exchange(total, k) for k in (3, 2, 1)]
+    [here] = call(join_kernel, (quarter, BF16))(total, *parts[::-1])
+    from_second = exchange(here, "second")
+    from_first = exchange(here, "first")
+    from_both = exchange(from_second, "first")
+    quarters = [here, from_second, from_first, from_both]
+    return call(
         place_kernel,
-        out_shape=[jax.ShapeDtypeStruct((rows, 2 * width), BF16) for rows in (edge, length - edge)],
+        ((edge, 2 * width), BF16),
+        ((length - edge, 2 * width), BF16),
         out_specs=[pl.BlockSpec(memory_space=pltpu.HBM)] * 2,
-        scratch_shapes=[pltpu.SemaphoreType.DMA((4,))],
-    )(total, other)
+        scratch_shapes=[pltpu.SemaphoreType.DMA((16,))],
+    )(*quarters, *[swap(one) for one in quarters])
 
 
 def local(features, top_down, lateral_weight, out_kernel, cotangent):
@@ -214,13 +304,18 @@
         )(*arrays, cot_before, cot_after)
         merged = merged.reshape(rows, cols, channels)
         if halves:
-            part[1] = lax.ppermute(part[1], "space", [(0, 1), (1, 0)])
+            part[1] = swap(part[1])
         edges = (part[1],) if halves else neighbour_rows(merged)
         outs.append(
             pl.pallas_call(
                 functools.partial(forward_kernel, peers),
                 out_shape=jax.ShapeDtypeStruct((rows, cols, channels), BF16),
-                scratch_shapes=[pltpu.VMEM((rows + 2, cols, 3 * channels), BF16)],
+                out_specs=pl.BlockSpec(memory_space=pltpu.HBM),
+                scratch_shapes=[
+                    pltpu.VMEM((rows + 2, cols, 3 * channels), BF16),
+                    pltpu.VMEM((rows, cols, channels), BF16),
+                    pltpu.SemaphoreType.DMA,
+                ],
                 compiler_params=params,
                 cost_estimate=pl.CostEstimate(
                     flops=2 * cells * channels * 9 * channels, bytes_accessed=2 * 2**20, transcendentals=0

time: 61.8 us -> 71.9 us (1.16)
  blocking collectives: 44.6 us -> 0 us
  waiting for transfers between devices: 2.8 us -> 25.4 us
  starting transfers between devices: 1.6 us -> 19.9 us
  Pallas kernels: 9.53 us -> 19.1 us
  local copies, waits for them, and re-layouts: 1.82 us -> 6.36 us
    all_to_all x4 -> x0, blocking collectives: 44.6 us -> none  [swap_pieces(): lax.all_to_all(pieces, ('dp', 'space'), 0, 0, axis_index_groups=groups, t...]
    ppermute x2 -> x17, waiting for transfers between devices: 1.91 us -> 24.5 us  [the longest x12 22.6 us: exchange(): return lax.ppermute(array, ('dp', 'space'), pairs)]
    ppermute x2 -> x17, starting transfers between devices: 1.14 us -> 19.4 us  [the longest x12 18.5 us: exchange(): return lax.ppermute(array, ('dp', 'space'), pairs)]
    pallas_call x1 -> x6, Pallas kernels: 2.45 us -> 12 us  [the longest x1 2.66 us: sum_everywhere(): call(start_kernel, (quarter, BF16), (quarter, BF16), (quarter, F32), (qua...]
    unnamed x6 -> x38, local copies, waits for them, and re-layouts: 0.89 us -> 5.55 us
  transfers between devices with their start and end apart: 3 -> 18, of which waited for: 2 -> 11; matrix products, arithmetic and copies ran while one was open for 0% -> 0% of each run, Pallas kernels for 3% -> 5%
where the time goes in v4:
time: 71.9 us; the launch traced here: 71.5 us
  waiting for transfers between devices  25.4 us (35%)
  starting transfers between devices  19.9 us (28%)
  Pallas kernels  19.1 us (27%)
  local copies, waits for them, and re-layouts  6.36 us (9%)
  between operations  0.79 us (1%)
    ppermute x12, waiting for transfers between devices, exchange(): return lax.ppermute(array, ('dp', 'space'), pairs)  22.6 us
    ppermute x12, starting transfers between devices, exchange(): return lax.ppermute(array, ('dp', 'space'), pairs)  18.5 us
    unnamed x38, local copies, waits for them, and re-layouts  5.55 us
    pallas_call x1, Pallas kernels, local(): pl.pallas_call(functools.partial(grads_kernel, peers), out_shape=[jax.Sha...  5.25 us
    pallas_call x1, Pallas kernels, sum_everywhere(): call(start_kernel, (quarter, BF16), (quarter, BF16), (quarter, F32), (qua...  2.66 us
    pallas_call x1, Pallas kernels, sum_everywhere(): call(place_kernel, ((edge, 2 * width), BF16), ((length - edge, 2 * width)...  2.63 us
    ppermute x5, waiting for transfers between devices, swap(): return lax.ppermute(array, 'space', [(0, 1), (1, 0)])  1.92 us
    pallas_call x1, Pallas kernels, sum_everywhere(): call(line_kernel, (part, F32), *[(part, BF16)] * 3)  1.85 us
  transfers between devices with their start and end apart: 18, of which 11 were waited for; matrix products, arithmetic and copies ran while one was open for 0% of the time, Pallas kernels for 5%

profile of v4, /device:TPU:0, one launch (start us, length us, event | category | flops | bytes accessed | tf_op | source)
XLA Modules:
  0.0 71.5 jit_solution(8929635979332392928)
XLA Ops:
  0.6 0.8 %dynamic-slice_bitcast_fusion = bf16[96,256]{1,0:T(8,128)(2,1)S(1)} fusion(bf16[1,8,96,256]{3,2,1,0:T(8,128)(2,1)} %param.9, s32[]{:T(128)S(6)} %select_n.4), kind=kLoop, calls=%fused_computation | loop fusion | bytes 98308 | tf_op jit(solution)/shard_map/jit(dynamic_index_in_dim)/squeeze | solution.py:21
  1.9 0.9 %collective-permute-done.refs_5_.refs_6_ = bf16[96,256]{1,0:T(8,128)(2,1)S(1)} collective-permute-done((bf16[96,256]{1,0:T(8,128)(2,1)S(1)}, bf16[96,256]{1,0:T(8,128)(2,1)S(1)}, u32[]{:S(2)}, u32[]{:S(2)}) %collective-permute-start) | collective-permute-done | bytes 49184 | tf_op jit(solution)/shard_map/ppermute | solution.py:22
  2.8 5.2 %shard_map.84 = (bf16[768,256]{1,0:T(8,128)(2,1)S(1)}, bf16[4,48,256]{2,1,0:T(8,128)(2,1)}, f32[2816,128]{1,0:T(8,128)S(1)}, bf16[3008,128]{1,0:T(8,128)(2,1)S(1)}) custom-call(bf16[768,512]{1,0:T(8,128)(2,1)} %bitcast.15, bf16[512,256]{1,0:T(8,128)(2,1)} %refs_1_.1, bf16[4,48,256]{2,1,0:T(8,128)(2,1)} %bitcast.16, bf16[8,96,256]{2,1,0:T(8,128)(2,1)} %bitcast.13, ...), custom_call_target="tpu_custom_call" | custom-call | flops 2214592512 | bytes 6291456 | tf_op jit(solution)/shard_map/pallas_call | solution.py:287
  8.0 1.1 %copy-done = f32[2816,128]{1,0:T(8,128)} copy-done((f32[2816,128]{1,0:T(8,128)}, f32[2816,128]{1,0:T(8,128)S(1)}, u32[]{:S(2)}) %copy-start) | copy-done | bytes 1441816
  9.5 1.9 %collective-permute-done.1.refs_0_.got = bf16[3008,128]{1,0:T(8,128)(2,1)S(1)} collective-permute-done((bf16[3008,128]{1,0:T(8,128)(2,1)S(1)}, bf16[3008,128]{1,0:T(8,128)(2,1)S(1)}, u32[]{:S(2)}, u32[]{:S(2)}) %collective-permute-start.1) | collective-permute-done | bytes 770080 | tf_op jit(solution)/shard_map/ppermute | solution.py:230
  11.4 0.9 %copy-done.1 = bf16[3008,128]{1,0:T(8,128)(2,1)} copy-done((bf16[3008,128]{1,0:T(8,128)(2,1)}, bf16[3008,128]{1,0:T(8,128)(2,1)S(1)}, u32[]{:S(2)}) %copy-start.1) | copy-done | bytes 770072
  12.3 2.7 %shard_map.86 = (bf16[704,128]{1,0:T(8,128)(2,1)}, bf16[704,128]{1,0:T(8,128)(2,1)}, f32[704,128]{1,0:T(8,128)}, f32[704,128]{1,0:T(8,128)}) custom-call(f32[2816,128]{1,0:T(8,128)} %copy-done, bf16[3008,128]{1,0:T(8,128)(2,1)} %copy-done.1), custom_call_target="tpu_custom_call" | custom-call | tf_op jit(solution)/shard_map/pallas_call | solution.py:242
  15.0 2.8 %collective-permute-start.3 = (bf16[704,128]{1,0:T(8,128)(2,1)}, bf16[704,128]{1,0:T(8,128)(2,1)S(1)}, u32[]{:S(2)}, u32[]{:S(2)}) collective-permute-start(bf16[704,128]{1,0:T(8,128)(2,1)} %get-tuple-element.25), channel_id=1, source_target_pairs={{0,2},{1,5},{2,0},{3,7},{4,6},{5,1},{6,4},{7,3},{8,10},{9,13},{10,... | collective-permute-start | bytes 540680 | tf_op jit(solution)/shard_map/ppermute | solution.py:226
  17.9 3.6 %collective-permute-done.3.got = bf16[704,128]{1,0:T(8,128)(2,1)S(1)} collective-permute-done((bf16[704,128]{1,0:T(8,128)(2,1)}, bf16[704,128]{1,0:T(8,128)(2,1)S(1)}, u32[]{:S(2)}, u32[]{:S(2)}) %collective-permute-start.3) | collective-permute-done | bytes 180256 | tf_op jit(solution)/shard_map/ppermute | solution.py:226
  21.5 0.7 copy-done.12
  22.2 1.7 %shard_map.87 = bf16[704,128]{1,0:T(8,128)(2,1)} custom-call(f32[704,128]{1,0:T(8,128)} %get-tuple-element.24.mine, bf16[704,128]{1,0:T(8,128)(2,1)} %copy-done.12), custom_call_target="tpu_custom_call" | custom-call | tf_op jit(solution)/shard_map/pallas_call | solution.py:245
  23.9 2.0 %collective-permute-start.4 = (bf16[704,128]{1,0:T(8,128)(2,1)}, bf16[704,128]{1,0:T(8,128)(2,1)S(1)}, u32[]{:S(2)}, u32[]{:S(2)}) collective-permute-start(bf16[704,128]{1,0:T(8,128)(2,1)} %shard_map.87), channel_id=1, source_target_pairs={{0,4},{1,3},{2,6},{3,1},{4,0},{5,7},{6,2},{7,5},{8,12},{9,11},{10,... | collective-permute-start | bytes 540680 | tf_op jit(solution)/shard_map/ppermute | solution.py:226
  26.0 3.7 %collective-permute-done.4.got_second = bf16[704,128]{1,0:T(8,128)(2,1)S(1)} collective-permute-done((bf16[704,128]{1,0:T(8,128)(2,1)}, bf16[704,128]{1,0:T(8,128)(2,1)S(1)}, u32[]{:S(2)}, u32[]{:S(2)}) %collective-permute-start.4) | collective-permute-done | bytes 180256 | tf_op jit(solution)/shard_map/ppermute | solution.py:226
  29.6 0.7 copy-done.11
  30.3 1.8 %shard_map.88 = (f32[176,128]{1,0:T(8,128)}, bf16[176,128]{1,0:T(8,128)(2,1)}, bf16[176,128]{1,0:T(8,128)(2,1)}, bf16[176,128]{1,0:T(8,128)(2,1)}) custom-call(f32[704,128]{1,0:T(8,128)} %get-tuple-element.22.mine, bf16[704,128]{1,0:T(8,128)(2,1)} %copy-done.10, bf16[704,128]{1,0:T(8,128)(2,1)} %copy-done.11), custom_call_target="tpu_custom_call" | custom-call | tf_op jit(solution)/shard_map/pallas_call | solution.py:247
  32.1 4.1 %collective-permute-start.5 = (bf16[176,128]{1,0:T(8,128)(2,1)}, bf16[176,128]{1,0:T(8,128)(2,1)S(1)}, u32[]{:S(2)}, u32[]{:S(2)}) collective-permute-start(bf16[176,128]{1,0:T(8,128)(2,1)} %get-tuple-element.27), channel_id=1, source_target_pairs={{0,24},{1,25},{2,26},{3,27},{4,28},{5,29},{6,30},{7,31},{8,16},{9,... | collective-permute-start | bytes 135176 | tf_op jit(solution)/shard_map/ppermute | solution.py:226
  36.8 1.7 %collective-permute-done.5.refs_0_ = bf16[176,128]{1,0:T(8,128)(2,1)S(1)} collective-permute-done((bf16[176,128]{1,0:T(8,128)(2,1)}, bf16[176,128]{1,0:T(8,128)(2,1)S(1)}, u32[]{:S(2)}, u32[]{:S(2)}) %collective-permute-start.5) | collective-permute-done | bytes 45088 | tf_op jit(solution)/shard_map/ppermute | solution.py:226
  38.5 2.9 %collective-permute-done.6.refs_1_ = bf16[176,128]{1,0:T(8,128)(2,1)S(1)} collective-permute-done((bf16[176,128]{1,0:T(8,128)(2,1)}, bf16[176,128]{1,0:T(8,128)(2,1)S(1)}, u32[]{:S(2)}, u32[]{:S(2)}) %collective-permute-start.6) | collective-permute-done | bytes 45088 | tf_op jit(solution)/shard_map/ppermute | solution.py:226
  42.0 1.6 %shard_map.89.refs_0_ = bf16[176,128]{1,0:T(8,128)(2,1)} custom-call(f32[176,128]{1,0:T(8,128)} %get-tuple-element.26.mine, bf16[176,128]{1,0:T(8,128)(2,1)} %copy-done.13, bf16[176,128]{1,0:T(8,128)(2,1)} %copy-done.14, bf16[176,128]{1,0:T(8,128)(2,1)} %copy-done.16), custom_call_target="tpu_custom_call" | custom-call | tf_op jit(solution)/shard_map/pallas_call | solution.py:249
  43.6 1.4 %collective-permute-start.10 = (bf16[176,128]{1,0:T(8,128)(2,1)}, bf16[176,128]{1,0:T(8,128)(2,1)S(1)}, u32[]{:S(2)}, u32[]{:S(2)}) collective-permute-start(bf16[176,128]{1,0:T(8,128)(2,1)} %shard_map.89.refs_0_), channel_id=1, source_target_pairs={{0,24},{1,25},{2,26},{3,27},{4,28},{5,29},{6,30},{7,31},{8,16},{9,... | collective-permute-start | bytes 135176 | tf_op jit(solution)/shard_map/ppermute | solution.py:226
  45.6 2.4 %collective-permute-start.8 = (bf16[176,128]{1,0:T(8,128)(2,1)}, bf16[176,128]{1,0:T(8,128)(2,1)S(1)}, u32[]{:S(2)}, u32[]{:S(2)}) collective-permute-start(bf16[176,128]{1,0:T(8,128)(2,1)} %shard_map.89.refs_0_), channel_id=1, source_target_pairs={{0,8},{1,9},{2,10},{3,11},{4,12},{5,13},{6,14},{7,15},{8,0},{9,1},... | collective-permute-start | bytes 135176 | tf_op jit(solution)/shard_map/ppermute | solution.py:226
  48.0 1.7 %collective-permute-done.10.refs_3_ = bf16[176,128]{1,0:T(8,128)(2,1)S(1)} collective-permute-done((bf16[176,128]{1,0:T(8,128)(2,1)}, bf16[176,128]{1,0:T(8,128)(2,1)S(1)}, u32[]{:S(2)}, u32[]{:S(2)}) %collective-permute-start.10) | collective-permute-done | bytes 45088 | tf_op jit(solution)/shard_map/ppermute | solution.py:226
  50.9 0.6 copy-done.18
  51.5 1.5 %shard_map.90.refs_0_ = bf16[704,128]{1,0:T(8,128)(2,1)} custom-call(bf16[176,128]{1,0:T(8,128)(2,1)} %shard_map.89.refs_0_, bf16[176,128]{1,0:T(8,128)(2,1)} %copy-done.18, bf16[176,128]{1,0:T(8,128)(2,1)} %copy-done.17, bf16[176,128]{1,0:T(8,128)(2,1)} %copy-done.15), custom_call_target="tpu_custom_call" | custom-call | tf_op jit(solution)/shard_map/pallas_call | solution.py:251
  53.0 1.5 %collective-permute-start.11 = (bf16[704,128]{1,0:T(8,128)(2,1)}, bf16[704,128]{1,0:T(8,128)(2,1)S(1)}, u32[]{:S(2)}, u32[]{:S(2)}) collective-permute-start(bf16[704,128]{1,0:T(8,128)(2,1)} %shard_map.90.refs_0_), channel_id=1, source_target_pairs={{0,4},{1,3},{2,6},{3,1},{4,0},{5,7},{6,2},{7,5},{8,12},{9,11},{10,... | collective-permute-start | bytes 540680 | tf_op jit(solution)/shard_map/ppermute | solution.py:226
  54.6 1.5 %collective-permute-start.12 = (bf16[704,128]{1,0:T(8,128)(2,1)}, bf16[704,128]{1,0:T(8,128)(2,1)S(1)}, u32[]{:S(2)}, u32[]{:S(2)}) collective-permute-start(bf16[704,128]{1,0:T(8,128)(2,1)} %shard_map.90.refs_0_), channel_id=1, source_target_pairs={{0,2},{1,5},{2,0},{3,7},{4,6},{5,1},{6,4},{7,3},{8,10},{9,13},{10,... | collective-permute-start | bytes 540680 | tf_op jit(solution)/shard_map/ppermute | solution.py:226
  56.0 4.6 %collective-permute-done.11.refs_1_ = bf16[704,128]{1,0:T(8,128)(2,1)S(1)} collective-permute-done((bf16[704,128]{1,0:T(8,128)(2,1)}, bf16[704,128]{1,0:T(8,128)(2,1)S(1)}, u32[]{:S(2)}, u32[]{:S(2)}) %collective-permute-start.11) | collective-permute-done | bytes 180256 | tf_op jit(solution)/shard_map/ppermute | solution.py:226
  60.6 1.5 %collective-permute-start.13 = (bf16[704,128]{1,0:T(8,128)(2,1)S(1)}, bf16[704,128]{1,0:T(8,128)(2,1)S(1)}, u32[]{:S(2)}, u32[]{:S(2)}) collective-permute-start(bf16[704,128]{1,0:T(8,128)(2,1)S(1)} %collective-permute-done.11.refs_1_), channel_id=1, source_target_pairs={{0,2},{1,5},{2,0},{3,7},{4,6},{5,1},{6,4},{7,3},{8,10},{9,13},{10,... | collective-permute-start | bytes 540680 | tf_op jit(solution)/shard_map/ppermute | solution.py:226
  62.7 3.4 %collective-permute-done.13.refs_3_ = bf16[704,128]{1,0:T(8,128)(2,1)S(1)} collective-permute-done((bf16[704,128]{1,0:T(8,128)(2,1)S(1)}, bf16[704,128]{1,0:T(8,128)(2,1)S(1)}, u32[]{:S(2)}, u32[]{:S(2)}) %collective-permute-start.13) | collective-permute-done | bytes 180256 | tf_op jit(solution)/shard_map/ppermute | solution.py:226
  66.1 1.8 %shard_map.85 = bf16[8,96,256]{2,1,0:T(8,128)(2,1)} custom-call(bf16[8,96,256]{2,1,0:T(8,128)(2,1)S(1)} %bitcast.12, bf16[9,256,256]{2,1,0:T(8,128)(2,1)S(1)} %bitcast.11, bf16[3008,128]{1,0:T(8,128)(2,1)S(1)} %copy-done.2), custom_call_target="tpu_custom_call" | custom-call | flops 905969664 | bytes 2097152 | tf_op jit(solution)/shard_map/pallas_call | solution.py:310
  68.1 0.6 copy-done.7
  68.8 2.6 %shard_map.91 = (bf16[2304,256]{1,0:T(8,128)(2,1)}, bf16[512,256]{1,0:T(8,128)(2,1)}) custom-call(bf16[704,128]{1,0:T(8,128)(2,1)} %shard_map.90.refs_0_, bf16[704,128]{1,0:T(8,128)(2,1)} %copy-done.4, bf16[704,128]{1,0:T(8,128)(2,1)} %copy-done.5, bf16[704,128]{1,0:T(8,128)(2,1)} %copy-done.6, bf16[704,128]{1,0:T(8,128)(2,1)} %copy-done.7, ...), custom_call_target="tpu_custom_call" | custom-call | tf_op jit(solution)/shard_map/pallas_call | solution.py:256
  (51 shorter events, 4.6 us)
Async XLA Ops:
  1.4 1.3 %collective-permute-start = (bf16[96,256]{1,0:T(8,128)(2,1)S(1)}, bf16[96,256]{1,0:T(8,128)(2,1)S(1)}, u32[]{:S(2)}, u32[]{:S(2)}) collective-permute-start(bf16[96,256]{1,0:T(8,128)(2,1)S(1)} %dynamic-slice_bitcast_fusion), channel_id=1, source_target_pairs={{0,1},{1,0},{2,3},{3,2},{4,5},{5,4},{6,7},{7,6},{8,9},{9,8},{10,11... | collective-permute-start | bytes 147464 | tf_op jit(solution)/shard_map/ppermute | solution.py:22
  8.0 1.2 %copy-start = (f32[2816,128]{1,0:T(8,128)}, f32[2816,128]{1,0:T(8,128)S(1)}, u32[]{:S(2)}) copy-start(f32[2816,128]{1,0:T(8,128)S(1)} %get-tuple-element.21.mine) | copy-start | bytes 4325380
  9.2 2.3 %collective-permute-start.1 = (bf16[3008,128]{1,0:T(8,128)(2,1)S(1)}, bf16[3008,128]{1,0:T(8,128)(2,1)S(1)}, u32[]{:S(2)}, u32[]{:S(2)}) collective-permute-start(bf16[3008,128]{1,0:T(8,128)(2,1)S(1)} %get-tuple-element.19), channel_id=1, source_target_pairs={{0,1},{1,0},{2,3},{3,2},{4,5},{5,4},{6,7},{7,6},{8,9},{9,8},{10,11... | collective-permute-start | bytes 2310152 | tf_op jit(solution)/shard_map/ppermute | solution.py:230
  11.4 0.9 %copy-start.1 = (bf16[3008,128]{1,0:T(8,128)(2,1)}, bf16[3008,128]{1,0:T(8,128)(2,1)S(1)}, u32[]{:S(2)}) copy-start(bf16[3008,128]{1,0:T(8,128)(2,1)S(1)} %collective-permute-done.1.refs_0_.got) | copy-start | bytes 2310148
  15.0 51.1 %copy-start.2 = (bf16[3008,128]{1,0:T(8,128)(2,1)S(1)}, bf16[3008,128]{1,0:T(8,128)(2,1)}, u32[]{:S(2)}) copy-start(bf16[3008,128]{1,0:T(8,128)(2,1)} %copy-done.1) | copy-start | bytes 2310148
  15.0 51.2 %copy-start.3 = (bf16[3,3,256,256]{3,2,1,0:T(8,128)(2,1)S(1)}, bf16[3,3,256,256]{3,2,1,0:T(8,128)(2,1)}, u32[]{:S(2)}) copy-start(bf16[3,3,256,256]{3,2,1,0:T(8,128)(2,1)} %param.8) | copy-start | bytes 3538948
  15.0 6.5 %collective-permute-start.3 = (bf16[704,128]{1,0:T(8,128)(2,1)}, bf16[704,128]{1,0:T(8,128)(2,1)S(1)}, u32[]{:S(2)}, u32[]{:S(2)}) collective-permute-start(bf16[704,128]{1,0:T(8,128)(2,1)} %get-tuple-element.25), channel_id=1, source_target_pairs={{0,2},{1,5},{2,0},{3,7},{4,6},{5,1},{6,4},{7,3},{8,10},{9,13},{10,... | collective-permute-start | bytes 540680 | tf_op jit(solution)/shard_map/ppermute | solution.py:226
  17.8 8.1 %collective-permute-start.2 = (bf16[704,128]{1,0:T(8,128)(2,1)}, bf16[704,128]{1,0:T(8,128)(2,1)S(1)}, u32[]{:S(2)}, u32[]{:S(2)}) collective-permute-start(bf16[704,128]{1,0:T(8,128)(2,1)} %get-tuple-element.23), channel_id=1, source_target_pairs={{0,2},{1,5},{2,0},{3,7},{4,6},{5,1},{6,4},{7,3},{8,10},{9,13},{10,... | collective-permute-start | bytes 540680 | tf_op jit(solution)/shard_map/ppermute | solution.py:226
  21.5 0.7 copy-start.12
  23.9 5.7 %collective-permute-start.4 = (bf16[704,128]{1,0:T(8,128)(2,1)}, bf16[704,128]{1,0:T(8,128)(2,1)S(1)}, u32[]{:S(2)}, u32[]{:S(2)}) collective-permute-start(bf16[704,128]{1,0:T(8,128)(2,1)} %shard_map.87), channel_id=1, source_target_pairs={{0,4},{1,3},{2,6},{3,1},{4,0},{5,7},{6,2},{7,5},{8,12},{9,11},{10,... | collective-permute-start | bytes 540680 | tf_op jit(solution)/shard_map/ppermute | solution.py:226
  26.0 3.7 %copy-start.10 = (bf16[704,128]{1,0:T(8,128)(2,1)}, bf16[704,128]{1,0:T(8,128)(2,1)S(1)}, u32[]{:S(2)}) copy-start(bf16[704,128]{1,0:T(8,128)(2,1)S(1)} %collective-permute-done.2.got_first) | copy-start | bytes 540676
  32.1 6.4 %collective-permute-start.5 = (bf16[176,128]{1,0:T(8,128)(2,1)}, bf16[176,128]{1,0:T(8,128)(2,1)S(1)}, u32[]{:S(2)}, u32[]{:S(2)}) collective-permute-start(bf16[176,128]{1,0:T(8,128)(2,1)} %get-tuple-element.27), channel_id=1, source_target_pairs={{0,24},{1,25},{2,26},{3,27},{4,28},{5,29},{6,30},{7,31},{8,16},{9,... | collective-permute-start | bytes 135176 | tf_op jit(solution)/shard_map/ppermute | solution.py:226
  36.3 5.2 %collective-permute-start.6 = (bf16[176,128]{1,0:T(8,128)(2,1)}, bf16[176,128]{1,0:T(8,128)(2,1)S(1)}, u32[]{:S(2)}, u32[]{:S(2)}) collective-permute-start(bf16[176,128]{1,0:T(8,128)(2,1)} %get-tuple-element.28), channel_id=1, source_target_pairs={{0,16},{1,17},{2,18},{3,19},{4,20},{5,21},{6,22},{7,23},{8,24},{9,... | collective-permute-start | bytes 135176 | tf_op jit(solution)/shard_map/ppermute | solution.py:226
  36.3 5.2 %collective-permute-start.7 = (bf16[176,128]{1,0:T(8,128)(2,1)}, bf16[176,128]{1,0:T(8,128)(2,1)S(1)}, u32[]{:S(2)}, u32[]{:S(2)}) collective-permute-start(bf16[176,128]{1,0:T(8,128)(2,1)} %get-tuple-element.29), channel_id=1, source_target_pairs={{0,8},{1,9},{2,10},{3,11},{4,12},{5,13},{6,14},{7,15},{8,0},{9,1},... | collective-permute-start | bytes 135176 | tf_op jit(solution)/shard_map/ppermute | solution.py:226
  38.5 2.9 %copy-start.13 = (bf16[176,128]{1,0:T(8,128)(2,1)}, bf16[176,128]{1,0:T(8,128)(2,1)S(1)}, u32[]{:S(2)}) copy-start(bf16[176,128]{1,0:T(8,128)(2,1)S(1)} %collective-permute-done.5.refs_0_) | copy-start | bytes 135172
  43.6 6.1 %collective-permute-start.10 = (bf16[176,128]{1,0:T(8,128)(2,1)}, bf16[176,128]{1,0:T(8,128)(2,1)S(1)}, u32[]{:S(2)}, u32[]{:S(2)}) collective-permute-start(bf16[176,128]{1,0:T(8,128)(2,1)} %shard_map.89.refs_0_), channel_id=1, source_target_pairs={{0,24},{1,25},{2,26},{3,27},{4,28},{5,29},{6,30},{7,31},{8,16},{9,... | collective-permute-start | bytes 135176 | tf_op jit(solution)/shard_map/ppermute | solution.py:226
  45.1 5.2 %collective-permute-start.9 = (bf16[176,128]{1,0:T(8,128)(2,1)}, bf16[176,128]{1,0:T(8,128)(2,1)S(1)}, u32[]{:S(2)}, u32[]{:S(2)}) collective-permute-start(bf16[176,128]{1,0:T(8,128)(2,1)} %shard_map.89.refs_0_), channel_id=1, source_target_pairs={{0,16},{1,17},{2,18},{3,19},{4,20},{5,21},{6,22},{7,23},{8,24},{9,... | collective-permute-start | bytes 135176 | tf_op jit(solution)/shard_map/ppermute | solution.py:226
  45.6 5.1 %collective-permute-start.8 = (bf16[176,128]{1,0:T(8,128)(2,1)}, bf16[176,128]{1,0:T(8,128)(2,1)S(1)}, u32[]{:S(2)}, u32[]{:S(2)}) collective-permute-start(bf16[176,128]{1,0:T(8,128)(2,1)} %shard_map.89.refs_0_), channel_id=1, source_target_pairs={{0,8},{1,9},{2,10},{3,11},{4,12},{5,13},{6,14},{7,15},{8,0},{9,1},... | collective-permute-start | bytes 135176 | tf_op jit(solution)/shard_map/ppermute | solution.py:226
  49.7 1.0 %copy-start.15 = (bf16[176,128]{1,0:T(8,128)(2,1)}, bf16[176,128]{1,0:T(8,128)(2,1)S(1)}, u32[]{:S(2)}) copy-start(bf16[176,128]{1,0:T(8,128)(2,1)S(1)} %collective-permute-done.10.refs_3_) | copy-start | bytes 135172
  53.0 7.6 %collective-permute-start.11 = (bf16[704,128]{1,0:T(8,128)(2,1)}, bf16[704,128]{1,0:T(8,128)(2,1)S(1)}, u32[]{:S(2)}, u32[]{:S(2)}) collective-permute-start(bf16[704,128]{1,0:T(8,128)(2,1)} %shard_map.90.refs_0_), channel_id=1, source_target_pairs={{0,4},{1,3},{2,6},{3,1},{4,0},{5,7},{6,2},{7,5},{8,12},{9,11},{10,... | collective-permute-start | bytes 540680 | tf_op jit(solution)/shard_map/ppermute | solution.py:226
  54.6 8.0 %collective-permute-start.12 = (bf16[704,128]{1,0:T(8,128)(2,1)}, bf16[704,128]{1,0:T(8,128)(2,1)S(1)}, u32[]{:S(2)}, u32[]{:S(2)}) collective-permute-start(bf16[704,128]{1,0:T(8,128)(2,1)} %shard_map.90.refs_0_), channel_id=1, source_target_pairs={{0,2},{1,5},{2,0},{3,7},{4,6},{5,1},{6,4},{7,3},{8,10},{9,13},{10,... | collective-permute-start | bytes 540680 | tf_op jit(solution)/shard_map/ppermute | solution.py:226
  60.6 7.4 %copy-start.4 = (bf16[704,128]{1,0:T(8,128)(2,1)}, bf16[704,128]{1,0:T(8,128)(2,1)S(1)}, u32[]{:S(2)}) copy-start(bf16[704,128]{1,0:T(8,128)(2,1)S(1)} %collective-permute-done.11.refs_1_) | copy-start | bytes 540676
  60.6 5.5 %collective-permute-start.13 = (bf16[704,128]{1,0:T(8,128)(2,1)S(1)}, bf16[704,128]{1,0:T(8,128)(2,1)S(1)}, u32[]{:S(2)}, u32[]{:S(2)}) collective-permute-start(bf16[704,128]{1,0:T(8,128)(2,1)S(1)} %collective-permute-done.11.refs_1_), channel_id=1, source_target_pairs={{0,2},{1,5},{2,0},{3,7},{4,6},{5,1},{6,4},{7,3},{8,10},{9,13},{10,... | collective-permute-start | bytes 540680 | tf_op jit(solution)/shard_map/ppermute | solution.py:226
  62.1 5.9 %collective-permute-start.14 = (bf16[704,128]{1,0:T(8,128)(2,1)}, bf16[704,128]{1,0:T(8,128)(2,1)S(1)}, u32[]{:S(2)}, u32[]{:S(2)}) collective-permute-start(bf16[704,128]{1,0:T(8,128)(2,1)} %shard_map.90.refs_0_), channel_id=1, source_target_pairs={{0,1},{1,0},{2,3},{3,2},{4,5},{5,4},{6,7},{7,6},{8,9},{9,8},{10,11... | collective-permute-start | bytes 540680 | tf_op jit(solution)/shard_map/ppermute | solution.py:230
  62.1 6.0 %collective-permute-start.15 = (bf16[704,128]{1,0:T(8,128)(2,1)S(1)}, bf16[704,128]{1,0:T(8,128)(2,1)S(1)}, u32[]{:S(2)}, u32[]{:S(2)}) collective-permute-start(bf16[704,128]{1,0:T(8,128)(2,1)S(1)} %collective-permute-done.11.refs_1_), channel_id=1, source_target_pairs={{0,1},{1,0},{2,3},{3,2},{4,5},{5,4},{6,7},{7,6},{8,9},{9,8},{10,11... | collective-permute-start | bytes 540680 | tf_op jit(solution)/shard_map/ppermute | solution.py:230
  62.6 5.4 %copy-start.5 = (bf16[704,128]{1,0:T(8,128)(2,1)}, bf16[704,128]{1,0:T(8,128)(2,1)S(1)}, u32[]{:S(2)}) copy-start(bf16[704,128]{1,0:T(8,128)(2,1)S(1)} %collective-permute-done.12.refs_2_) | copy-start | bytes 540676
  62.6 5.4 %collective-permute-start.16 = (bf16[704,128]{1,0:T(8,128)(2,1)S(1)}, bf16[704,128]{1,0:T(8,128)(2,1)S(1)}, u32[]{:S(2)}, u32[]{:S(2)}) collective-permute-start(bf16[704,128]{1,0:T(8,128)(2,1)S(1)} %collective-permute-done.12.refs_2_), channel_id=1, source_target_pairs={{0,1},{1,0},{2,3},{3,2},{4,5},{5,4},{6,7},{7,6},{8,9},{9,8},{10,11... | collective-permute-start | bytes 540680 | tf_op jit(solution)/shard_map/ppermute | solution.py:230
  66.1 1.9 %copy-start.6 = (bf16[704,128]{1,0:T(8,128)(2,1)}, bf16[704,128]{1,0:T(8,128)(2,1)S(1)}, u32[]{:S(2)}) copy-start(bf16[704,128]{1,0:T(8,128)(2,1)S(1)} %collective-permute-done.13.refs_3_) | copy-start | bytes 540676
  66.1 2.0 %collective-permute-start.17 = (bf16[704,128]{1,0:T(8,128)(2,1)S(1)}, bf16[704,128]{1,0:T(8,128)(2,1)}, u32[]{:S(2)}, u32[]{:S(2)}) collective-permute-start(bf16[704,128]{1,0:T(8,128)(2,1)S(1)} %collective-permute-done.13.refs_3_), channel_id=1, source_target_pairs={{0,1},{1,0},{2,3},{3,2},{4,5},{5,4},{6,7},{7,6},{8,9},{9,8},{10,11... | collective-permute-start | bytes 540680 | tf_op jit(solution)/shard_map/ppermute | solution.py:230
  68.0 0.7 copy-start.7
  68.1 0.7 %copy-start.9 = (bf16[704,128]{1,0:T(8,128)(2,1)}, bf16[704,128]{1,0:T(8,128)(2,1)S(1)}, u32[]{:S(2)}) copy-start(bf16[704,128]{1,0:T(8,128)(2,1)S(1)} %collective-permute-done.16.refs_6_) | copy-start | bytes 540676
  68.1 0.8 %copy-start.8 = (bf16[704,128]{1,0:T(8,128)(2,1)}, bf16[704,128]{1,0:T(8,128)(2,1)S(1)}, u32[]{:S(2)}) copy-start(bf16[704,128]{1,0:T(8,128)(2,1)S(1)} %collective-permute-done.15.refs_5_) | copy-start | bytes 540676
  (5 other events, 3.1 us)

commit v5 on v3

--- a/solution.py
+++ b/solution.py
@@ -45,19 +45,19 @@
     put_shifted(stack, rows + 1, jnp.where(here < peers - 1, after, zero), sign)
 
 
-def grads_kernel(peers, *refs):
-    far, (before, after, merged, grad_top), rest = refs[:5], refs[5:9], refs[9:]
-    outs, stack, near, sems = rest[:-7], rest[-7], rest[-6:-1], rest[-1]
+def merge_kernel(*refs):
+    far, (merged, merged_t, stack), near, sems = refs[:4], refs[4:7], refs[7:11], refs[11]
     copies = [pltpu.make_async_copy(a, b, sems.at[i]) for i, (a, b) in enumerate(zip(far, near))]
     for copy in copies:
         copy.start()
-    feat, lat_w, top, cot, out_w = near
-    for copy in copies[:3]:
+    cot, lat_w, top, feat = near
+    rows, cols, channels = cot.shape
+    half = cols // 2
+    copies[0].wait()
+    for r in range(rows):
+        put_shifted(stack, r, cot[r], 1)
+    for copy in copies[1:]:
         copy.wait()
-    rows, cols, channels = cot.shape
-    cells = rows * cols
-    half = cols // 2
-    in_channels = lat_w.shape[0]
     upper = lax.broadcasted_iota(jnp.int32, (cols, half), 0)
     spread = jnp.where(upper // 2 == lax.broadcasted_iota(jnp.int32, (cols, half), 1), 1.0, 0.0).astype(BF16)
     lateral = jnp.dot(feat[...], lat_w[...], preferred_element_type=F32)
@@ -65,13 +65,28 @@
         lifted = jnp.dot(spread, top[q], preferred_element_type=F32)
         for r in (2 * q, 2 * q + 1):
             merged[r * cols : (r + 1) * cols, :] = (lateral[r * cols : (r + 1) * cols] + lifted).astype(BF16)
-    copies[3].wait()
-    for r in range(rows):
-        put_shifted(stack, r + 1, cot[r], 1)
-    put_halo(stack, before[...], after[...], rows, peers, 1)
+    merged_t[...] = jnp.transpose(merged[...])
+
+
+def grads_kernel(peers, packed, stack, merged, merged_t, before, after, feat_far, taps_far, grad_top, *rest):
+    outs, halo, feat, out_w, sems = rest[:-4], *rest[-4:]
+    copies = [pltpu.make_async_copy(feat_far, feat, sems.at[0]), pltpu.make_async_copy(taps_far, out_w, sems.at[1])]
+    for copy in copies:
+        copy.start()
+    rows, cols, deep = stack.shape
+    channels, cells = merged_t.shape
+    in_channels = feat.shape[1]
+    half = cols // 2
+    put_halo(halo, before[...], after[...], 0, peers, 1)
+    strips = [
+        jnp.concatenate([stack[1:], halo[1:]], axis=0),
+        stack[...],
+        jnp.concatenate([halo[:1], stack[: rows - 1]], axis=0),
+    ]
+    strips = [strip.reshape(cells, deep) for strip in strips]
 
     def put(start, block):
-        if len(outs) == 1:
+        if not packed:
             outs[0][start : start + block.shape[0], :] = block
             return
         here = lax.axis_index("space")
@@ -80,24 +95,22 @@
         mine[start : start + block.shape[0], :] = jnp.where(here == 0, left, right)
         theirs[start : start + block.shape[0], :] = jnp.where(here == 0, right, left).astype(BF16)
 
-    if len(outs) == 2:
+    if packed:
         here = lax.axis_index("space")
         edge = jnp.where(here == 0, merged[cells - cols :, :], merged[:cols, :])
         start = 9 * channels + in_channels
         outs[1][start : start + cols, :] = edge[:, : channels // 2]
         outs[1][start + cols :, :] = edge[:, channels // 2 :]
-    merged_t = jnp.transpose(merged[...])
     for i in range(3):
-        strip = stack[2 - i : 2 - i + rows].reshape(cells, 3 * channels)
-        part = jnp.dot(merged_t, strip, preferred_element_type=F32)
+        part = jnp.dot(merged_t[...], strips[i], preferred_element_type=F32)
         for j in range(3):
             put((3 * i + j) * channels, part[:, j * channels : (j + 1) * channels])
-    copies[4].wait()
+    for copy in copies:
+        copy.wait()
     total = jnp.zeros((cells, channels), F32)
     for i in range(3):
-        strip = stack[2 - i : 2 - i + rows].reshape(cells, 3 * channels)
         taps = jnp.concatenate([out_w[3 * i + j] for j in range(3)], axis=1)
-        total = total + lax.dot_general(strip, taps, (((1,), (1,)), ((), ())), preferred_element_type=F32)
+        total = total + lax.dot_general(strips[i], taps, (((1,), (1,)), ((), ())), preferred_element_type=F32)
     grad = total.astype(BF16)
     lower = lax.broadcasted_iota(jnp.int32, (half, 2 * cols), 1)
     lower = jnp.where(lower >= cols, lower - cols, lower)
@@ -105,12 +118,11 @@
     for q in range(rows // 2):
         pair = grad[2 * q * cols : (2 * q + 2) * cols]
         grad_top[q] = jnp.dot(pool, pair, preferred_element_type=F32).astype(BF16)
-    feat_t = jnp.transpose(feat[...])
-    put(9 * channels, jnp.dot(feat_t, grad, preferred_element_type=F32))
+    put(9 * channels, jnp.dot(jnp.transpose(feat[...]), grad, preferred_element_type=F32))
 
 
 def forward_kernel(peers, merged, out_w, *refs):
-    edges, (out, stack) = refs[:-2], refs[-2:]
+    edges, (out, stack, near, sem) = refs[:-4], refs[-4:]
     rows, cols, channels = merged.shape
     for r in range(rows):
         put_shifted(stack, r + 1, merged[r], -1)
@@ -125,17 +137,27 @@
         strip = stack[i : i + rows].reshape(rows * cols, 3 * channels)
         taps = out_w[3 * i : 3 * i + 3].reshape(3 * channels, channels)
         total = total + jnp.dot(strip, taps, preferred_element_type=F32)
-    out[...] = total.astype(BF16).reshape(out.shape)
-
-
-def place_kernel(mine, other, kernel_out, lateral_out, sems):
-    side = lax.axis_index("space")
-    edge, rest = kernel_out.shape[0], lateral_out.shape[0]
+    near[...] = total.astype(BF16).reshape(out.shape)
+    copy = pltpu.make_async_copy(near, out, sem)
+    copy.start()
+    copy.wait()
+
+
+def place_kernel(gathered, kernel_out, lateral_out, sems):
+    edge, share = kernel_out.shape[0], gathered.shape[1]
     copies = []
-    for columns, half in ((side, mine), (1 - side, other)):
-        lanes = pl.ds(pl.multiple_of(columns * 128, 128), 128)
-        copies.append((half.at[pl.ds(0, edge), :], kernel_out.at[:, lanes]))
-        copies.append((half.at[pl.ds(edge, rest), :], lateral_out.at[:, lanes]))
+    for device in range(gathered.shape[0]):
+        chip, core = device // 2, device % 2
+        index = 4 * (chip % 4) + chip // 4 if core == 0 else chip
+        lanes = pl.ds(core * 128, 128)
+        start, stop = index * share, (index + 1) * share
+        if start < edge:
+            size = min(stop, edge) - start
+            copies.append((gathered.at[device, pl.ds(0, size), :], kernel_out.at[pl.ds(start, size), lanes]))
+        if stop > edge:
+            skip = max(edge - start, 0)
+            rows = pl.ds(start + skip - edge, share - skip)
+            copies.append((gathered.at[device, pl.ds(skip, share - skip), :], lateral_out.at[rows, lanes]))
     copies = [pltpu.make_async_copy(source, to, sems.at[i]) for i, (source, to) in enumerate(copies)]
     for copy in copies:
         copy.start()
@@ -156,20 +178,19 @@
 
 def sum_everywhere(mine, got, scale, edge):
     length, width = mine.shape
-    swap = [(0, 1), (1, 0)]
     first, second = peer_groups()
     pair = (mine + got[:length].astype(F32)).astype(BF16).reshape(4, length // 4, width)
     total = jnp.sum(swap_pieces(pair, first).astype(F32), axis=0).astype(BF16).reshape(4, length // 16, width)
     total = (jnp.sum(swap_pieces(total, second).astype(F32), axis=0) * scale).astype(BF16)
-    total = swap_pieces(jnp.broadcast_to(total[None], (4, *total.shape)), second).reshape(length // 4, width)
-    total = swap_pieces(jnp.broadcast_to(total[None], (4, *total.shape)), first).reshape(length, width)
-    other = lax.ppermute(total, "space", swap)
+    gathered = pltpu.with_memory_space_constraint(lax.all_gather(total, ("dp", "space")), pltpu.HBM)
     return pl.pallas_call(
         place_kernel,
         out_shape=[jax.ShapeDtypeStruct((rows, 2 * width), BF16) for rows in (edge, length - edge)],
+        in_specs=[pl.BlockSpec(memory_space=pltpu.HBM)],
         out_specs=[pl.BlockSpec(memory_space=pltpu.HBM)] * 2,
-        scratch_shapes=[pltpu.SemaphoreType.DMA((4,))],
-    )(total, other)
+        scratch_shapes=[pltpu.SemaphoreType.DMA((34,))],
+        compiler_params=pltpu.CompilerParams(vmem_limit_bytes=8 * 2**20),
+    )(gathered)
 
 
 def local(features, top_down, lateral_weight, out_kernel, cotangent):
@@ -179,7 +200,7 @@
     peers = lax.axis_size("space")
     length = 9 * channels + in_channels
     taps = out_kernel.reshape(9, channels, channels)
-    params = pltpu.CompilerParams(vmem_limit_bytes=48 * 2**20)
+    params = pltpu.CompilerParams(vmem_limit_bytes=32 * 2**20)
     halves = peers == 2 and lax.axis_size("dp") == 16 and images == 1 and (channels, in_channels) == (256, 512)
     if halves:
         sums = [
@@ -192,26 +213,35 @@
     for image in range(images):
         cot = cotangent[image]
         cot_before, cot_after = neighbour_rows(cot)
-        arrays = (features[image].reshape(cells, in_channels), lateral_weight, top_down[image], cot, taps)
+        arrays = (cot, lateral_weight, top_down[image], features[image].reshape(cells, in_channels), taps)
         arrays = [pltpu.with_memory_space_constraint(array, pltpu.HBM) for array in arrays]
-        merged, grad_top, *part = pl.pallas_call(
-            functools.partial(grads_kernel, peers),
+        merged, merged_t, stack = pl.pallas_call(
+            merge_kernel,
             out_shape=[
-                jax.ShapeDtypeStruct((cells, channels), BF16),
-                jax.ShapeDtypeStruct((rows // 2, cols // 2, channels), BF16),
-                *sums,
+                jax.ShapeDtypeStruct(shape, BF16)
+                for shape in ((cells, channels), (channels, cells), (rows, cols, 3 * channels))
             ],
-            in_specs=[pl.BlockSpec(memory_space=pltpu.HBM)] * 5 + [pl.BlockSpec(memory_space=pltpu.VMEM)] * 2,
+            in_specs=[pl.BlockSpec(memory_space=pltpu.HBM)] * 4,
+            scratch_shapes=[*[pltpu.VMEM(array.shape, BF16) for array in arrays[:4]], pltpu.SemaphoreType.DMA((4,))],
+            compiler_params=params,
+            cost_estimate=pl.CostEstimate(
+                flops=2 * cells * channels * 4 * in_channels, bytes_accessed=4 * 2**20, transcendentals=0
+            ),
+        )(*arrays[:4])
+        grad_top, *part = pl.pallas_call(
+            functools.partial(grads_kernel, peers, halves),
+            out_shape=[jax.ShapeDtypeStruct((rows // 2, cols // 2, channels), BF16), *sums],
+            in_specs=[pl.BlockSpec(memory_space=pltpu.VMEM)] * 5 + [pl.BlockSpec(memory_space=pltpu.HBM)] * 2,
             scratch_shapes=[
-                pltpu.VMEM((rows + 2, cols, 3 * channels), BF16),
-                *[pltpu.VMEM(array.shape, BF16) for array in arrays],
-                pltpu.SemaphoreType.DMA((5,)),
+                pltpu.VMEM((2, cols, 3 * channels), BF16),
+                *[pltpu.VMEM(array.shape, BF16) for array in arrays[3:]],
+                pltpu.SemaphoreType.DMA((2,)),
             ],
             compiler_params=params,
             cost_estimate=pl.CostEstimate(
-                flops=2 * cells * channels * (18 * channels + 2 * in_channels), bytes_accessed=6 * 2**20, transcendentals=0
+                flops=2 * cells * channels * (18 * channels + in_channels), bytes_accessed=6 * 2**20, transcendentals=0
             ),
-        )(*arrays, cot_before, cot_after)
+        )(stack, merged, merged_t, cot_before, cot_after, *arrays[3:])
         merged = merged.reshape(rows, cols, channels)
         if halves:
             part[1] = lax.ppermute(part[1], "space", [(0, 1), (1, 0)])
@@ -220,7 +250,12 @@
             pl.pallas_call(
                 functools.partial(forward_kernel, peers),
                 out_shape=jax.ShapeDtypeStruct((rows, cols, channels), BF16),
-                scratch_shapes=[pltpu.VMEM((rows + 2, cols, 3 * channels), BF16)],
+                out_specs=pl.BlockSpec(memory_space=pltpu.HBM),
+                scratch_shapes=[
+                    pltpu.VMEM((rows + 2, cols, 3 * channels), BF16),
+                    pltpu.VMEM((rows, cols, channels), BF16),
+                    pltpu.SemaphoreType.DMA,
+                ],
                 compiler_params=params,
                 cost_estimate=pl.CostEstimate(
                     flops=2 * cells * channels * 9 * channels, bytes_accessed=2 * 2**20, transcendentals=0

time: 61.8 us -> 147 us (2.38)
  waiting for transfers between devices: 2.8 us -> 52.6 us
  Pallas kernels: 9.53 us -> 52.9 us
  blocking collectives: 44.6 us -> 24.6 us
  between operations: 0.69 us -> 14.1 us
    all_gather x0 -> x1, waiting for transfers between devices: none -> 50.3 us  [sum_everywhere(): lax.all_gather(total, ('dp', 'space'))]
    pallas_call x1, Pallas kernels: 2.45 us -> 45.1 us  [sum_everywhere(): pl.pallas_call(place_kernel, out_shape=[jax.ShapeDtypeStruct((rows, 2 * w...]
    all_to_all x4 -> x2, blocking collectives: 44.6 us -> 24.6 us  [swap_pieces(): lax.all_to_all(pieces, ('dp', 'space'), 0, 0, axis_index_groups=groups, t...]
    pallas_call x1 -> x2, Pallas kernels: 5.25 us -> 5.95 us  [the longest x1 4.05 us: local(): pl.pallas_call(functools.partial(grads_kernel, peers, halves), out_shape=...]
where the time goes in v5:
time: 147 us; the launch traced here: 146 us
  Pallas kernels  52.9 us (36%)
  waiting for transfers between devices  52.6 us (36%)
  blocking collectives  24.6 us (17%)
  between operations  14.1 us (10%)
    all_gather x1, waiting for transfers between devices, sum_everywhere(): lax.all_gather(total, ('dp', 'space'))  50.3 us
    pallas_call x1, Pallas kernels, sum_everywhere(): pl.pallas_call(place_kernel, out_shape=[jax.ShapeDtypeStruct((rows, 2 * w...  45.1 us
    all_to_all x2, blocking collectives, swap_pieces(): lax.all_to_all(pieces, ('dp', 'space'), 0, 0, axis_index_groups=groups, t...  24.6 us
    pallas_call x1, Pallas kernels, local(): pl.pallas_call(functools.partial(grads_kernel, peers, halves), out_shape=...  4.05 us
  transfers between devices with their start and end apart: 3, of which 2 were waited for; matrix products, arithmetic and copies ran while one was open for 0% of the time, Pallas kernels for 3%

profile of v5, /device:TPU:0, one launch (start us, length us, event | category | flops | bytes accessed | tf_op | source)
XLA Modules:
  0.0 146.5 jit_solution(13949211998607004525)
XLA Ops:
  7.2 0.0 all-gather.3.cloned.1.call-start
  7.2 0.8 dynamic-slice_bitcast_fusion
  8.0 0.5 collective-permute-start
  8.5 1.9 %shard_map.84 = (bf16[768,256]{1,0:T(8,128)(2,1)S(1)}, bf16[256,768]{1,0:T(8,128)(2,1)S(1)}, bf16[8,96,768]{2,1,0:T(8,128)(2,1)S(1)}) custom-call(bf16[8,96,256]{2,1,0:T(8,128)(2,1)} %bitcast.19, bf16[512,256]{1,0:T(8,128)(2,1)} %refs_1_.1, bf16[4,48,256]{2,1,0:T(8,128)(2,1)} %bitcast.23, bf16[768,512]{1,0:T(8,128)(2,1)} %bitcast.21), custom_call_target="tpu_custom_call" | custom-call | flops 805306368 | bytes 4194304 | tf_op jit(solution)/shard_map/pallas_call | solution.py:218
  10.4 0.0 collective-permute-done.before.after
  10.4 4.1 %shard_map.85 = (bf16[4,48,256]{2,1,0:T(8,128)(2,1)}, f32[2816,128]{1,0:T(8,128)S(1)}, bf16[3008,128]{1,0:T(8,128)(2,1)S(1)}) custom-call(bf16[8,96,768]{2,1,0:T(8,128)(2,1)S(1)} %get-tuple-element.13.stack, bf16[768,256]{1,0:T(8,128)(2,1)S(1)} %get-tuple-element.12.merged, bf16[256,768]{1,0:T(8,128)(2,1)S(1)} %get-tuple-element.14.merged_t, ...), custom_call_target="tpu_custom_call" | custom-call | flops 2013265920 | bytes 6291456 | tf_op jit(solution)/shard_map/pallas_call | solution.py:231
  14.4 0.1 collective-permute-start.1
  14.6 2.2 %collective-permute-done.1.refs_0_ = bf16[3008,128]{1,0:T(8,128)(2,1)S(1)} collective-permute-done((bf16[3008,128]{1,0:T(8,128)(2,1)S(1)}, bf16[3008,128]{1,0:T(8,128)(2,1)S(1)}, u32[]{:S(2)}, u32[]{:S(2)}) %collective-permute-start.1) | collective-permute-done | bytes 770080 | tf_op jit(solution)/shard_map/ppermute | solution.py:247
  16.8 0.1 add_convert_fusion
  16.9 0.0 copy-start
  16.9 13.1 %all_to_all.10 = bf16[4,704,128]{2,1,0:T(8,128)(2,1)S(1)} all-to-all(bf16[4,704,128]{2,1,0:T(8,128)(2,1)S(1)} %bitcast.16), channel_id=1, replica_groups={{0,2,4,6},{8,10,12,14},{16,18,20,22},{24,26,28,30},{1,9,17,25},{3,11,19..., dimensions={0} | all-to-all | bytes 1441792 | tf_op jit(solution)/shard_map/all_to_all | solution.py:176
  30.1 0.1 reduce_sum.21
  30.2 11.4 %all_to_all.11 = bf16[4,176,128]{2,1,0:T(8,128)(2,1)S(1)} all-to-all(bf16[4,176,128]{2,1,0:T(8,128)(2,1)S(1)} %bitcast.18), channel_id=1, replica_groups={{0,8,16,24},{2,10,18,26},{4,12,20,28},{6,14,22,30},{1,3,5,7},{9,11,13,1..., dimensions={0} | all-to-all | bytes 360448 | tf_op jit(solution)/shard_map/all_to_all | solution.py:176
  41.7 0.6 multiply_convert_fusion
  42.3 0.0 all-gather.3.cloned.1.call-update
  42.3 0.0 copy-done
  42.3 1.8 %shard_map.86 = bf16[8,96,256]{2,1,0:T(8,128)(2,1)} custom-call(bf16[8,96,256]{2,1,0:T(8,128)(2,1)S(1)} %bitcast.15, bf16[9,256,256]{2,1,0:T(8,128)(2,1)S(1)} %bitcast.14, bf16[3008,128]{1,0:T(8,128)(2,1)S(1)} %collective-permute-done.1.refs_0_), custom_call_target="tpu_custom_call" | custom-call | flops 905969664 | bytes 2097152 | tf_op jit(solution)/shard_map/pallas_call | solution.py:250
  44.2 50.3 %all-gather.3.cloned.1.call-done = bf16[5632,128]{1,0:T(8,128)(2,1)} async-done(((bf16[176,128]{1,0:T(8,128)(2,1)}), bf16[5632,128]{1,0:T(8,128)(2,1)}) %all-gather.3.cloned.1.call-update) | async-done | bytes 1441808 | tf_op jit(solution)/shard_map/all_gather | solution.py:185
  94.5 45.1 %shard_map.87 = (bf16[2304,256]{1,0:T(8,128)(2,1)}, bf16[512,256]{1,0:T(8,128)(2,1)}) custom-call(bf16[32,176,128]{2,1,0:T(8,128)(2,1)} %bitcast.17), custom_call_target="tpu_custom_call" | custom-call | tf_op jit(solution)/shard_map/pallas_call | solution.py:186
  (1 shorter events, 0.0 us)
Async XLA Ops:
  7.2 87.3 %all-gather.3.cloned.1.call-start = ((), (), s32[]{:S(2)}) async-start(), calls=%async_computation.2 | async-start | bytes 1486848 | tf_op jit(solution)/shard_map/all_gather | solution.py:185
  8.0 2.4 %collective-permute-start = (bf16[96,256]{1,0:T(8,128)(2,1)S(1)}, bf16[96,256]{1,0:T(8,128)(2,1)S(1)}, u32[]{:S(2)}, u32[]{:S(2)}) collective-permute-start(bf16[96,256]{1,0:T(8,128)(2,1)S(1)} %dynamic-slice_bitcast_fusion), channel_id=1, source_target_pairs={{0,1},{1,0},{2,3},{3,2},{4,5},{5,4},{6,7},{7,6},{8,9},{9,8},{10,11... | collective-permute-start | bytes 147464 | tf_op jit(solution)/shard_map/ppermute | solution.py:22
  14.4 2.3 %collective-permute-start.1 = (bf16[3008,128]{1,0:T(8,128)(2,1)S(1)}, bf16[3008,128]{1,0:T(8,128)(2,1)S(1)}, u32[]{:S(2)}, u32[]{:S(2)}) collective-permute-start(bf16[3008,128]{1,0:T(8,128)(2,1)S(1)} %get-tuple-element.15), channel_id=1, source_target_pairs={{0,1},{1,0},{2,3},{3,2},{4,5},{5,4},{6,7},{7,6},{8,9},{9,8},{10,11... | collective-permute-start | bytes 2310152 | tf_op jit(solution)/shard_map/ppermute | solution.py:247
  16.9 25.4 %copy-start = (bf16[3,3,256,256]{3,2,1,0:T(8,128)(2,1)S(1)}, bf16[3,3,256,256]{3,2,1,0:T(8,128)(2,1)}, u32[]{:S(2)}) copy-start(bf16[3,3,256,256]{3,2,1,0:T(8,128)(2,1)} %param.8) | copy-start | bytes 3538948
Sparse Core Ops, SparseCore 0:
  42.4 52.0 all-gather.2

commit v6 on v5

--- a/solution.py
+++ b/solution.py
@@ -68,57 +68,66 @@
     merged_t[...] = jnp.transpose(merged[...])
 
 
-def grads_kernel(peers, packed, stack, merged, merged_t, before, after, feat_far, taps_far, grad_top, *rest):
-    outs, halo, feat, out_w, sems = rest[:-4], *rest[-4:]
-    copies = [pltpu.make_async_copy(feat_far, feat, sems.at[0]), pltpu.make_async_copy(taps_far, out_w, sems.at[1])]
-    for copy in copies:
-        copy.start()
+def strips_of(stack, halo):
     rows, cols, deep = stack.shape
-    channels, cells = merged_t.shape
-    in_channels = feat.shape[1]
-    half = cols // 2
-    put_halo(halo, before[...], after[...], 0, peers, 1)
     strips = [
         jnp.concatenate([stack[1:], halo[1:]], axis=0),
         stack[...],
         jnp.concatenate([halo[:1], stack[: rows - 1]], axis=0),
     ]
-    strips = [strip.reshape(cells, deep) for strip in strips]
-
-    def put(start, block):
-        if not packed:
-            outs[0][start : start + block.shape[0], :] = block
-            return
-        here = lax.axis_index("space")
-        left, right = block[:, : channels // 2], block[:, channels // 2 :]
-        mine, theirs = outs
-        mine[start : start + block.shape[0], :] = jnp.where(here == 0, left, right)
-        theirs[start : start + block.shape[0], :] = jnp.where(here == 0, right, left).astype(BF16)
-
-    if packed:
+    return [strip.reshape(rows * cols, deep) for strip in strips]
+
+
+def put_sums(outs, start, values):
+    rows = slice(start, start + values.shape[0])
+    if len(outs) == 1:
+        outs[0][rows, :] = values
+        return
+    here = lax.axis_index("space")
+    half = values.shape[1] // 2
+    mine, theirs = outs
+    mine[rows, :] = jnp.where(here == 0, values[:, :half], values[:, half:])
+    theirs[rows, :] = jnp.where(here == 0, values[:, half:], values[:, :half]).astype(BF16)
+
+
+def kernel_grad_kernel(peers, stack, merged, merged_t, before, after, halo, *outs):
+    cols = stack.shape[1]
+    channels, cells = merged_t.shape
+    put_halo(halo, before[...], after[...], 0, peers, 1)
+    if len(outs) == 2:
         here = lax.axis_index("space")
         edge = jnp.where(here == 0, merged[cells - cols :, :], merged[:cols, :])
-        start = 9 * channels + in_channels
+        start = 9 * channels
         outs[1][start : start + cols, :] = edge[:, : channels // 2]
         outs[1][start + cols :, :] = edge[:, channels // 2 :]
-    for i in range(3):
-        part = jnp.dot(merged_t[...], strips[i], preferred_element_type=F32)
+    for i, strip in enumerate(strips_of(stack, halo)):
+        part = jnp.dot(merged_t[...], strip, preferred_element_type=F32)
         for j in range(3):
-            put((3 * i + j) * channels, part[:, j * channels : (j + 1) * channels])
+            put_sums(outs, (3 * i + j) * channels, part[:, j * channels : (j + 1) * channels])
+
+
+def data_grad_kernel(stack, halo, feat_far, taps_far, grad_top, *rest):
+    outs, feat, out_w, sems = rest[:-3], *rest[-3:]
+    copies = [pltpu.make_async_copy(taps_far, out_w, sems.at[0]), pltpu.make_async_copy(feat_far, feat, sems.at[1])]
     for copy in copies:
-        copy.wait()
+        copy.start()
+    rows, cols, deep = stack.shape
+    cells, channels, half = rows * cols, deep // 3, cols // 2
+    strips = strips_of(stack, halo)
+    copies[0].wait()
     total = jnp.zeros((cells, channels), F32)
     for i in range(3):
         taps = jnp.concatenate([out_w[3 * i + j] for j in range(3)], axis=1)
         total = total + lax.dot_general(strips[i], taps, (((1,), (1,)), ((), ())), preferred_element_type=F32)
     grad = total.astype(BF16)
+    copies[1].wait()
+    put_sums(outs, 0, jnp.dot(jnp.transpose(feat[...]), grad, preferred_element_type=F32))
     lower = lax.broadcasted_iota(jnp.int32, (half, 2 * cols), 1)
     lower = jnp.where(lower >= cols, lower - cols, lower)
     pool = jnp.where(lower // 2 == lax.broadcasted_iota(jnp.int32, (half, 2 * cols), 0), 1.0, 0.0).astype(BF16)
     for q in range(rows // 2):
         pair = grad[2 * q * cols : (2 * q + 2) * cols]
         grad_top[q] = jnp.dot(pool, pair, preferred_element_type=F32).astype(BF16)
-    put(9 * channels, jnp.dot(jnp.transpose(feat[...]), grad, preferred_element_type=F32))
 
 
 def forward_kernel(peers, merged, out_w, *refs):
@@ -143,21 +152,16 @@
     copy.wait()
 
 
-def place_kernel(gathered, kernel_out, lateral_out, sems):
-    edge, share = kernel_out.shape[0], gathered.shape[1]
+def place_kernel(mine, other, kernel_out, lateral_out, sems):
+    side = lax.axis_index("space")
+    edge, rest = kernel_out.shape[0], lateral_out.shape[0]
     copies = []
-    for device in range(gathered.shape[0]):
-        chip, core = device // 2, device % 2
-        index = 4 * (chip % 4) + chip // 4 if core == 0 else chip
-        lanes = pl.ds(core * 128, 128)
-        start, stop = index * share, (index + 1) * share
-        if start < edge:
-            size = min(stop, edge) - start
-            copies.append((gathered.at[device, pl.ds(0, size), :], kernel_out.at[pl.ds(start, size), lanes]))
-        if stop > edge:
-            skip = max(edge - start, 0)
-            rows = pl.ds(start + skip - edge, share - skip)
-            copies.append((gathered.at[device, pl.ds(skip, share - skip), :], lateral_out.at[rows, lanes]))
+    for columns, half in ((side, mine), (1 - side, other)):
+        lanes = pl.ds(pl.multiple_of(columns * 128, 128), 128)
+        for start in range(0, edge, rest // 2):
+            size = min(rest // 2, edge - start)
+            copies.append((half.at[pl.ds(start, size), :], kernel_out.at[pl.ds(start, size), lanes]))
+        copies.append((half.at[pl.ds(edge, rest), :], lateral_out.at[:, lanes]))
     copies = [pltpu.make_async_copy(source, to, sems.at[i]) for i, (source, to) in enumerate(copies)]
     for copy in copies:
         copy.start()
@@ -176,21 +180,26 @@
     return lax.all_to_all(pieces, ("dp", "space"), 0, 0, axis_index_groups=groups, tiled=True)
 
 
-def sum_everywhere(mine, got, scale, edge):
-    length, width = mine.shape
+def swap(array):
+    return lax.ppermute(array, "space", [(0, 1), (1, 0)])
+
+
+def sum_everywhere(pair, scale, edge):
+    length, width = pair.shape
     first, second = peer_groups()
-    pair = (mine + got[:length].astype(F32)).astype(BF16).reshape(4, length // 4, width)
-    total = jnp.sum(swap_pieces(pair, first).astype(F32), axis=0).astype(BF16).reshape(4, length // 16, width)
-    total = (jnp.sum(swap_pieces(total, second).astype(F32), axis=0) * scale).astype(BF16)
-    gathered = pltpu.with_memory_space_constraint(lax.all_gather(total, ("dp", "space")), pltpu.HBM)
+    quarter = (length // 4, width)
+    copies = lambda array: jnp.broadcast_to(array[None], (4, *array.shape))
+    terms = swap_pieces(pair.reshape(4, *quarter), first)
+    terms = swap_pieces(copies(jnp.sum(terms.astype(F32), axis=0).astype(BF16)), second)
+    total = (jnp.sum(terms.astype(F32), axis=0) * scale).astype(BF16)
+    total = swap_pieces(copies(total), first).reshape(length, width)
     return pl.pallas_call(
         place_kernel,
         out_shape=[jax.ShapeDtypeStruct((rows, 2 * width), BF16) for rows in (edge, length - edge)],
-        in_specs=[pl.BlockSpec(memory_space=pltpu.HBM)],
         out_specs=[pl.BlockSpec(memory_space=pltpu.HBM)] * 2,
-        scratch_shapes=[pltpu.SemaphoreType.DMA((34,))],
+        scratch_shapes=[pltpu.SemaphoreType.DMA((20,))],
         compiler_params=pltpu.CompilerParams(vmem_limit_bytes=8 * 2**20),
-    )(gathered)
+    )(total, swap(total))
 
 
 def local(features, top_down, lateral_weight, out_kernel, cotangent):
@@ -198,17 +207,18 @@
     channels = lateral_weight.shape[1]
     cells = rows * cols
     peers = lax.axis_size("space")
-    length = 9 * channels + in_channels
     taps = out_kernel.reshape(9, channels, channels)
     params = pltpu.CompilerParams(vmem_limit_bytes=32 * 2**20)
     halves = peers == 2 and lax.axis_size("dp") == 16 and images == 1 and (channels, in_channels) == (256, 512)
-    if halves:
-        sums = [
+
+    def sums(length, extra):
+        if not halves:
+            return [jax.ShapeDtypeStruct((length, channels), F32)]
+        return [
             jax.ShapeDtypeStruct((length, channels // 2), F32),
-            jax.ShapeDtypeStruct((length + 2 * cols, channels // 2), BF16),
+            jax.ShapeDtypeStruct((length + extra, channels // 2), BF16),
         ]
-    else:
-        sums = [jax.ShapeDtypeStruct((length, channels), F32)]
+
     outs, tops, parts = [], [], None
     for image in range(images):
         cot = cotangent[image]
@@ -228,24 +238,33 @@
                 flops=2 * cells * channels * 4 * in_channels, bytes_accessed=4 * 2**20, transcendentals=0
             ),
         )(*arrays[:4])
-        grad_top, *part = pl.pallas_call(
-            functools.partial(grads_kernel, peers, halves),
-            out_shape=[jax.ShapeDtypeStruct((rows // 2, cols // 2, channels), BF16), *sums],
-            in_specs=[pl.BlockSpec(memory_space=pltpu.VMEM)] * 5 + [pl.BlockSpec(memory_space=pltpu.HBM)] * 2,
+        halo, *kernel_part = pl.pallas_call(
+            functools.partial(kernel_grad_kernel, peers),
+            out_shape=[jax.ShapeDtypeStruct((2, cols, 3 * channels), BF16), *sums(9 * channels, 2 * cols)],
+            compiler_params=params,
+            cost_estimate=pl.CostEstimate(
+                flops=2 * cells * channels * 9 * channels, bytes_accessed=4 * 2**20, transcendentals=0
+            ),
+        )(stack, merged, merged_t, cot_before, cot_after)
+        if halves:
+            kernel_part[1] = swap(kernel_part[1])
+        grad_top, *lateral_part = pl.pallas_call(
+            data_grad_kernel,
+            out_shape=[jax.ShapeDtypeStruct((rows // 2, cols // 2, channels), BF16), *sums(in_channels, 0)],
+            in_specs=[pl.BlockSpec(memory_space=pltpu.VMEM)] * 2 + [pl.BlockSpec(memory_space=pltpu.HBM)] * 2,
             scratch_shapes=[
-                pltpu.VMEM((2, cols, 3 * channels), BF16),
                 *[pltpu.VMEM(array.shape, BF16) for array in arrays[3:]],
                 pltpu.SemaphoreType.DMA((2,)),
             ],
             compiler_params=params,
             cost_estimate=pl.CostEstimate(
-                flops=2 * cells * channels * (18 * channels + in_channels), bytes_accessed=6 * 2**20, transcendentals=0
+                flops=2 * cells * channels * (9 * channels + in_channels), bytes_accessed=4 * 2**20, transcendentals=0
             ),
-        )(stack, merged, merged_t, cot_before, cot_after, *arrays[3:])
+        )(stack, halo, *arrays[3:])
+        if halves:
+            lateral_part[1] = swap(lateral_part[1])
         merged = merged.reshape(rows, cols, channels)
-        if halves:
-            part[1] = lax.ppermute(part[1], "space", [(0, 1), (1, 0)])
-        edges = (part[1],) if halves else neighbour_rows(merged)
+        edges = kernel_part[1:] if halves else neighbour_rows(merged)
         outs.append(
             pl.pallas_call(
                 functools.partial(forward_kernel, peers),
@@ -263,13 +282,19 @@
             )(merged, taps, *edges)
         )
         tops.append(grad_top)
-        parts = part if parts is None else [a + b for a, b in zip(parts, part)]
+        if halves:
+            parts = [
+                (mine + got[: mine.shape[0]].astype(F32)).astype(BF16) for mine, got in (kernel_part, lateral_part)
+            ]
+        else:
+            parts = [kernel_part[0], lateral_part[0]] if parts is None else [
+                a + b for a, b in zip(parts, (kernel_part[0], lateral_part[0]))
+            ]
     scale = 1.0 / (images * lax.axis_size("dp"))
     if halves:
-        grad_kernel, grad_lateral = sum_everywhere(*parts, scale, 9 * channels)
+        grad_kernel, grad_lateral = sum_everywhere(jnp.concatenate(parts), scale, 9 * channels)
     else:
-        total = (lax.psum(parts[0], ("dp", "space")) * scale).astype(BF16)
-        grad_kernel, grad_lateral = total[: 9 * channels], total[9 * channels :]
+        grad_kernel, grad_lateral = [(total * scale).astype(BF16) for total in lax.psum(parts, ("dp", "space"))]
     return jnp.stack(outs), jnp.stack(tops), grad_kernel.reshape(out_kernel.shape), grad_lateral
 
 

time: 147 us -> 56.3 us (0.38)
  waiting for transfers between devices: 52.6 us -> 0.99 us
  Pallas kernels: 52.9 us -> 10 us
  blocking collectives: 24.6 us -> 41.2 us
  between operations: 14.1 us -> 0.75 us
    all_gather x1 -> x0, waiting for transfers between devices: 50.3 us -> none  [sum_everywhere(): lax.all_gather(total, ('dp', 'space'))]
    pallas_call x1, Pallas kernels: 45.1 us -> 1.26 us  [sum_everywhere(): pl.pallas_call(place_kernel, out_shape=[jax.ShapeDtypeStruct((rows, 2 * w...]
    all_to_all x2 -> x3, blocking collectives: 24.6 us -> 41.2 us  [swap_pieces(): lax.all_to_all(pieces, ('dp', 'space'), 0, 0, axis_index_groups=groups, t...]
    pallas_call x1 -> x2, Pallas kernels: 4.05 us -> 5.05 us  [the longest x1 3.95 us: local(): pl.pallas_call(data_grad_kernel, out_shape=[jax.ShapeDtypeStruct((rows //...]
  transfers between devices with their start and end apart: 3 -> 4, of which waited for: 2 -> 1; matrix products, arithmetic and copies ran while one was open for 0% -> 0% of each run, Pallas kernels for 3% -> 14%
where the time goes in v6:
time: 56.3 us; the launch traced here: 56 us
  blocking collectives  41.2 us (73%)
  Pallas kernels  10 us (18%)
  starting transfers between devices  1.56 us (3%)
  local copies, waits for them, and re-layouts  1 us (2%)
  waiting for transfers between devices  0.99 us (2%)
  between operations  0.75 us (1%)
    all_to_all x3, blocking collectives, swap_pieces(): lax.all_to_all(pieces, ('dp', 'space'), 0, 0, axis_index_groups=groups, t...  41.2 us
    pallas_call x1, Pallas kernels, local(): pl.pallas_call(data_grad_kernel, out_shape=[jax.ShapeDtypeStruct((rows //...  3.95 us
    pallas_call x1, Pallas kernels, local(): pl.pallas_call(merge_kernel, out_shape=[jax.ShapeDtypeStruct(shape, BF16)...  1.89 us
    pallas_call x1, Pallas kernels, local(): pl.pallas_call(functools.partial(forward_kernel, peers), out_shape=jax.Sh...  1.84 us
    pallas_call x1, Pallas kernels, sum_everywhere(): pl.pallas_call(place_kernel, out_shape=[jax.ShapeDtypeStruct((rows, 2 * w...  1.26 us
  transfers between devices with their start and end apart: 4, of which 1 were waited for; matrix products, arithmetic and copies ran while one was open for 0% of the time, Pallas kernels for 14%

profile of v6, /device:TPU:0, one launch (start us, length us, event | category | flops | bytes accessed | tf_op | source)
XLA Modules:
  0.0 56.0 jit_solution(7702852745118988378)
XLA Ops:
  0.6 0.8 %dynamic-slice_bitcast_fusion = bf16[96,256]{1,0:T(8,128)(2,1)S(1)} fusion(bf16[1,8,96,256]{3,2,1,0:T(8,128)(2,1)} %param.9, s32[]{:T(128)S(6)} %select_n.4), kind=kLoop, calls=%fused_computation.5 | loop fusion | bytes 98308 | tf_op jit(solution)/shard_map/jit(dynamic_index_in_dim)/squeeze | solution.py:21
  1.4 0.5 collective-permute-start
  1.9 1.9 %shard_map.84 = (bf16[768,256]{1,0:T(8,128)(2,1)S(1)}, bf16[256,768]{1,0:T(8,128)(2,1)S(1)}, bf16[8,96,768]{2,1,0:T(8,128)(2,1)S(1)}) custom-call(bf16[8,96,256]{2,1,0:T(8,128)(2,1)} %bitcast.18, bf16[512,256]{1,0:T(8,128)(2,1)} %refs_1_.1, bf16[4,48,256]{2,1,0:T(8,128)(2,1)} %bitcast.22, bf16[768,512]{1,0:T(8,128)(2,1)} %bitcast.20), custom_call_target="tpu_custom_call" | custom-call | flops 805306368 | bytes 4194304 | tf_op jit(solution)/shard_map/pallas_call | solution.py:228
  3.8 0.0 collective-permute-done.before.after
  3.8 1.1 %shard_map.85 = (bf16[2,96,768]{2,1,0:T(8,128)(2,1)S(1)}, f32[2304,128]{1,0:T(8,128)S(1)}, bf16[2496,128]{1,0:T(8,128)(2,1)S(1)}) custom-call(bf16[8,96,768]{2,1,0:T(8,128)(2,1)S(1)} %get-tuple-element.16.stack, bf16[768,256]{1,0:T(8,128)(2,1)S(1)} %get-tuple-element.15.merged, bf16[256,768]{1,0:T(8,128)(2,1)S(1)} %get-tuple-element.17.merged_t, ...), custom_call_target="tpu_custom_call" | custom-call | flops 905969664 | bytes 4194304 | tf_op jit(solution)/shard_map/pallas_call | solution.py:241
  4.9 0.1 collective-permute-start.1
  5.0 4.0 %shard_map.87 = (bf16[4,48,256]{2,1,0:T(8,128)(2,1)}, f32[512,128]{1,0:T(8,128)S(1)}, bf16[512,128]{1,0:T(8,128)(2,1)S(1)}) custom-call(bf16[8,96,768]{2,1,0:T(8,128)(2,1)S(1)} %get-tuple-element.16.stack, bf16[2,96,768]{2,1,0:T(8,128)(2,1)S(1)} %get-tuple-element.19.halo, bf16[768,512]{1,0:T(8,128)(2,1)} %bitcast.21, bf16[9,256,256]{2,1,0:T(8,128)(2,1)} %bitcast.14), custom_call_target="tpu_custom_call" | custom-call | flops 1107296256 | bytes 4194304 | tf_op jit(solution)/shard_map/pallas_call | solution.py:251
  9.0 0.5 collective-permute-start.2
  9.5 1.0 %collective-permute-done.2 = bf16[512,128]{1,0:T(8,128)(2,1)S(1)} collective-permute-done((bf16[512,128]{1,0:T(8,128)(2,1)S(1)}, bf16[512,128]{1,0:T(8,128)(2,1)S(1)}, u32[]{:S(2)}, u32[]{:S(2)}) %collective-permute-start.2) | collective-permute-done | bytes 131104 | tf_op jit(solution)/shard_map/ppermute | solution.py:184
  10.5 0.0 collective-permute-done.1.refs_0_
  10.5 0.1 add_convert_fusion
  10.7 13.2 %all_to_all.15 = bf16[4,704,128]{2,1,0:T(8,128)(2,1)S(1)} all-to-all(bf16[4,704,128]{2,1,0:T(8,128)(2,1)S(1)} %bitcast.17), channel_id=1, replica_groups={{0,2,4,6},{8,10,12,14},{16,18,20,22},{24,26,28,30},{1,9,17,25},{3,11,19..., dimensions={0} | all-to-all | bytes 1441792 | tf_op jit(solution)/shard_map/all_to_all | solution.py:180
  24.0 0.1 reduce_sum.21
  24.1 0.1 broadcast_in_dim.4
  24.2 17.1 %all_to_all.16 = bf16[4,704,128]{2,1,0:T(8,128)(2,1)S(1)} all-to-all(bf16[4,704,128]{2,1,0:T(8,128)(2,1)S(1)} %broadcast_in_dim.4), channel_id=1, replica_groups={{0,8,16,24},{2,10,18,26},{4,12,20,28},{6,14,22,30},{1,3,5,7},{9,11,13,1..., dimensions={0} | all-to-all | bytes 1441792 | tf_op jit(solution)/shard_map/all_to_all | solution.py:180
  41.3 0.1 convert_reduce_fusion
  41.4 0.0 copy-start
  41.4 0.1 broadcast_in_dim.5
  41.5 10.9 %all_to_all.17 = bf16[4,704,128]{2,1,0:T(8,128)(2,1)S(1)} all-to-all(bf16[4,704,128]{2,1,0:T(8,128)(2,1)S(1)} %broadcast_in_dim.5), channel_id=1, replica_groups={{0,2,4,6},{8,10,12,14},{16,18,20,22},{24,26,28,30},{1,9,17,25},{3,11,19..., dimensions={0} | all-to-all | bytes 1441792 | tf_op jit(solution)/shard_map/all_to_all | solution.py:180
  52.4 0.5 collective-permute-start.3
  52.9 0.0 copy-done
  52.9 1.8 %shard_map.86 = bf16[8,96,256]{2,1,0:T(8,128)(2,1)} custom-call(bf16[8,96,256]{2,1,0:T(8,128)(2,1)S(1)} %bitcast.16, bf16[9,256,256]{2,1,0:T(8,128)(2,1)S(1)} %bitcast.15, bf16[2496,128]{1,0:T(8,128)(2,1)S(1)} %collective-permute-done.1.refs_0_), custom_call_target="tpu_custom_call" | custom-call | flops 905969664 | bytes 2097152 | tf_op jit(solution)/shard_map/pallas_call | solution.py:269
  54.7 0.0 collective-permute-done.3.other
  54.7 1.3 %shard_map.88 = (bf16[2304,256]{1,0:T(8,128)(2,1)}, bf16[512,256]{1,0:T(8,128)(2,1)}) custom-call(bf16[2816,128]{1,0:T(8,128)(2,1)S(1)} %bitcast.13, bf16[2816,128]{1,0:T(8,128)(2,1)S(1)} %collective-permute-done.3.other), custom_call_target="tpu_custom_call" | custom-call | tf_op jit(solution)/shard_map/pallas_call | solution.py:196
  (3 shorter events, 0.1 us)
Async XLA Ops:
  1.4 2.4 %collective-permute-start = (bf16[96,256]{1,0:T(8,128)(2,1)S(1)}, bf16[96,256]{1,0:T(8,128)(2,1)S(1)}, u32[]{:S(2)}, u32[]{:S(2)}) collective-permute-start(bf16[96,256]{1,0:T(8,128)(2,1)S(1)} %dynamic-slice_bitcast_fusion), channel_id=1, source_target_pairs={{0,1},{1,0},{2,3},{3,2},{4,5},{5,4},{6,7},{7,6},{8,9},{9,8},{10,11... | collective-permute-start | bytes 147464 | tf_op jit(solution)/shard_map/ppermute | solution.py:22
  4.9 5.6 %collective-permute-start.1 = (bf16[2496,128]{1,0:T(8,128)(2,1)S(1)}, bf16[2496,128]{1,0:T(8,128)(2,1)S(1)}, u32[]{:S(2)}, u32[]{:S(2)}) collective-permute-start(bf16[2496,128]{1,0:T(8,128)(2,1)S(1)} %get-tuple-element.18), channel_id=1, source_target_pairs={{0,1},{1,0},{2,3},{3,2},{4,5},{5,4},{6,7},{7,6},{8,9},{9,8},{10,11... | collective-permute-start | bytes 1916936 | tf_op jit(solution)/shard_map/ppermute | solution.py:184
  9.0 1.5 %collective-permute-start.2 = (bf16[512,128]{1,0:T(8,128)(2,1)S(1)}, bf16[512,128]{1,0:T(8,128)(2,1)S(1)}, u32[]{:S(2)}, u32[]{:S(2)}) collective-permute-start(bf16[512,128]{1,0:T(8,128)(2,1)S(1)} %get-tuple-element.23), channel_id=1, source_target_pairs={{0,1},{1,0},{2,3},{3,2},{4,5},{5,4},{6,7},{7,6},{8,9},{9,8},{10,11... | collective-permute-start | bytes 393224 | tf_op jit(solution)/shard_map/ppermute | solution.py:184
  41.4 11.5 %copy-start = (bf16[3,3,256,256]{3,2,1,0:T(8,128)(2,1)S(1)}, bf16[3,3,256,256]{3,2,1,0:T(8,128)(2,1)}, u32[]{:S(2)}) copy-start(bf16[3,3,256,256]{3,2,1,0:T(8,128)(2,1)} %param.8) | copy-start | bytes 3538948
  52.4 2.3 %collective-permute-start.3 = (bf16[2816,128]{1,0:T(8,128)(2,1)S(1)}, bf16[2816,128]{1,0:T(8,128)(2,1)S(1)}, u32[]{:S(2)}, u32[]{:S(2)}) collective-permute-start(bf16[2816,128]{1,0:T(8,128)(2,1)S(1)} %bitcast.12), channel_id=1, source_target_pairs={{0,1},{1,0},{2,3},{3,2},{4,5},{5,4},{6,7},{7,6},{8,9},{9,8},{10,11... | collective-permute-start | bytes 2162696 | tf_op jit(solution)/shard_map/ppermute | solution.py:184

commit v7 on v6

--- a/solution.py
+++ b/solution.py
@@ -46,17 +46,18 @@
 
 
 def merge_kernel(*refs):
-    far, (merged, merged_t, stack), near, sems = refs[:4], refs[4:7], refs[7:11], refs[11]
+    far, (merged, merged_t, stack, feat_t, out_w), near, sems = refs[:5], refs[5:10], refs[10:14], refs[14]
+    near = (*near, out_w)
     copies = [pltpu.make_async_copy(a, b, sems.at[i]) for i, (a, b) in enumerate(zip(far, near))]
     for copy in copies:
         copy.start()
-    cot, lat_w, top, feat = near
+    cot, lat_w, top, feat, _ = near
     rows, cols, channels = cot.shape
     half = cols // 2
     copies[0].wait()
     for r in range(rows):
         put_shifted(stack, r, cot[r], 1)
-    for copy in copies[1:]:
+    for copy in copies[1:4]:
         copy.wait()
     upper = lax.broadcasted_iota(jnp.int32, (cols, half), 0)
     spread = jnp.where(upper // 2 == lax.broadcasted_iota(jnp.int32, (cols, half), 1), 1.0, 0.0).astype(BF16)
@@ -66,6 +67,8 @@
         for r in (2 * q, 2 * q + 1):
             merged[r * cols : (r + 1) * cols, :] = (lateral[r * cols : (r + 1) * cols] + lifted).astype(BF16)
     merged_t[...] = jnp.transpose(merged[...])
+    feat_t[...] = jnp.transpose(feat[...])
+    copies[4].wait()
 
 
 def strips_of(stack, halo):
@@ -106,22 +109,14 @@
             put_sums(outs, (3 * i + j) * channels, part[:, j * channels : (j + 1) * channels])
 
 
-def data_grad_kernel(stack, halo, feat_far, taps_far, grad_top, *rest):
-    outs, feat, out_w, sems = rest[:-3], *rest[-3:]
-    copies = [pltpu.make_async_copy(taps_far, out_w, sems.at[0]), pltpu.make_async_copy(feat_far, feat, sems.at[1])]
-    for copy in copies:
-        copy.start()
+def data_grad_kernel(stack, halo, feat_t, out_w, grad_top, *outs):
     rows, cols, deep = stack.shape
-    cells, channels, half = rows * cols, deep // 3, cols // 2
-    strips = strips_of(stack, halo)
-    copies[0].wait()
-    total = jnp.zeros((cells, channels), F32)
-    for i in range(3):
-        taps = jnp.concatenate([out_w[3 * i + j] for j in range(3)], axis=1)
-        total = total + lax.dot_general(strips[i], taps, (((1,), (1,)), ((), ())), preferred_element_type=F32)
+    channels, half = deep // 3, cols // 2
+    cells = jnp.concatenate(strips_of(stack, halo), axis=1)
+    taps = jnp.concatenate([out_w[tap] for tap in range(9)], axis=1)
+    total = lax.dot_general(cells, taps, (((1,), (1,)), ((), ())), preferred_element_type=F32)
     grad = total.astype(BF16)
-    copies[1].wait()
-    put_sums(outs, 0, jnp.dot(jnp.transpose(feat[...]), grad, preferred_element_type=F32))
+    put_sums(outs, 0, jnp.dot(feat_t[...], grad, preferred_element_type=F32))
     lower = lax.broadcasted_iota(jnp.int32, (half, 2 * cols), 1)
     lower = jnp.where(lower >= cols, lower - cols, lower)
     pool = jnp.where(lower // 2 == lax.broadcasted_iota(jnp.int32, (half, 2 * cols), 0), 1.0, 0.0).astype(BF16)
@@ -141,65 +136,121 @@
         put_halo(stack, edge, edge, rows, peers, -1)
     else:
         put_halo(stack, edges[0][...], edges[1][...], rows, peers, -1)
-    total = jnp.zeros((rows * cols, channels), F32)
-    for i in range(3):
-        strip = stack[i : i + rows].reshape(rows * cols, 3 * channels)
-        taps = out_w[3 * i : 3 * i + 3].reshape(3 * channels, channels)
-        total = total + jnp.dot(strip, taps, preferred_element_type=F32)
+    cells = jnp.concatenate([stack[i : i + rows].reshape(rows * cols, 3 * channels) for i in range(3)], axis=1)
+    total = jnp.dot(cells, out_w[...].reshape(9 * channels, channels), preferred_element_type=F32)
     near[...] = total.astype(BF16).reshape(out.shape)
     copy = pltpu.make_async_copy(near, out, sem)
     copy.start()
     copy.wait()
 
 
-def place_kernel(mine, other, kernel_out, lateral_out, sems):
+def places():
+    chip, core = lax.axis_index("dp"), lax.axis_index("space")
+    plane, line = chip % 4, chip // 4
+    return jnp.where(core == 0, plane, line), jnp.where(core == 0, line, plane)
+
+
+def block(index, length):
+    return pl.ds(pl.multiple_of(index * length, 16), length)
+
+
+def cut_kernel(mine_a, got_a, mine_b, got_b, *refs):
+    outs, total = refs[:4], refs[4]
+    start = 0
+    for mine, got in ((mine_a, got_a), (mine_b, got_b)):
+        rows = mine.shape[0]
+        total[start : start + rows, :] = mine[...] + got[:rows, :].astype(F32)
+        start += rows
+    place, _ = places()
+    for k, out in enumerate(outs):
+        out[...] = total[block(place ^ k, out.shape[0]), :].astype(out.dtype)
+
+
+def add_kernel(own, one, two, three, *refs):
+    refs[-1][...] = (own[...] + one[...].astype(F32) + two[...].astype(F32) + three[...].astype(F32)).astype(BF16)
+
+
+def finish_kernel(scale, own, one, two, three, out):
+    near = own[...].astype(F32) + one[...].astype(F32)
+    far = two[...].astype(F32) + three[...].astype(F32)
+    out[...] = ((near + far) * scale).astype(BF16)
+
+
+def place_kernel(*refs):
+    kernel_out, lateral_out, sems = refs[8:]
     side = lax.axis_index("space")
-    edge, rest = kernel_out.shape[0], lateral_out.shape[0]
-    copies = []
-    for columns, half in ((side, mine), (1 - side, other)):
+    edge, share = kernel_out.shape[0], refs[0].shape[0]
+    inside = edge - 3 * share
+    waits = []
+    for columns, quarters, place in zip((side, 1 - side), (refs[:4], refs[4:8]), places()):
         lanes = pl.ds(pl.multiple_of(columns * 128, 128), 128)
-        for start in range(0, edge, rest // 2):
-            size = min(rest // 2, edge - start)
-            copies.append((half.at[pl.ds(start, size), :], kernel_out.at[pl.ds(start, size), lanes]))
-        copies.append((half.at[pl.ds(edge, rest), :], lateral_out.at[:, lanes]))
-    copies = [pltpu.make_async_copy(source, to, sems.at[i]) for i, (source, to) in enumerate(copies)]
-    for copy in copies:
-        copy.start()
-    for copy in copies:
+        for k, quarter in enumerate(quarters):
+            index = place ^ k
+            base = pl.multiple_of(index * share, 16)
+            head, tail = quarter.at[pl.ds(0, inside), :], quarter.at[pl.ds(inside, share - inside), :]
+            copy = pltpu.make_async_copy(head, kernel_out.at[pl.ds(base, inside), lanes], sems.at[len(waits)])
+            copy.start()
+            waits.append(copy)
+            sem = sems.at[len(waits)]
+
+            @pl.when(index < 3)
+            def _():
+                rows = pl.ds(base + inside, share - inside)
+                pltpu.make_async_copy(tail, kernel_out.at[rows, lanes], sem).start()
+
+            @pl.when(index == 3)
+            def _():
+                pltpu.make_async_copy(tail, lateral_out.at[:, lanes], sem).start()
+
+            waits.append(pltpu.make_async_copy(tail, lateral_out.at[:, lanes], sem))
+    for copy in waits:
         copy.wait()
 
 
-def peer_groups():
-    plane = [[4 * z + q for q in range(4)] for z in range(4)]
-    line = [[4 * z + q for z in range(4)] for q in range(4)]
-    pick = lambda chips, core: [[2 * chip + core for chip in group] for group in chips]
-    return pick(plane, 0) + pick(line, 1), pick(line, 0) + pick(plane, 1)
-
-
-def swap_pieces(pieces, groups):
-    return lax.all_to_all(pieces, ("dp", "space"), 0, 0, axis_index_groups=groups, tiled=True)
+def exchange(pieces, step):
+    came = {}
+    for k in (3, 2, 1):
+        pairs = []
+        for chip in range(16):
+            for core in range(2):
+                flip = k if core == step else 4 * k
+                pairs.append((2 * chip + core, 2 * (chip ^ flip) + core))
+        came[k] = lax.ppermute(pieces[k - 1], ("dp", "space"), pairs)
+    return [came[k] for k in (1, 2, 3)]
 
 
 def swap(array):
     return lax.ppermute(array, "space", [(0, 1), (1, 0)])
 
 
-def sum_everywhere(pair, scale, edge):
-    length, width = pair.shape
-    first, second = peer_groups()
+def call(kernel, *shapes, **more):
+    return pl.pallas_call(
+        kernel,
+        out_shape=[jax.ShapeDtypeStruct(shape, kind) for shape, kind in shapes],
+        compiler_params=pltpu.CompilerParams(vmem_limit_bytes=12 * 2**20),
+        **more,
+    )
+
+
+def sum_everywhere(kernel_part, lateral_part, scale, after):
+    edge, width = kernel_part[0].shape
+    length = edge + lateral_part[0].shape[0]
     quarter = (length // 4, width)
-    copies = lambda array: jnp.broadcast_to(array[None], (4, *array.shape))
-    terms = swap_pieces(pair.reshape(4, *quarter), first)
-    terms = swap_pieces(copies(jnp.sum(terms.astype(F32), axis=0).astype(BF16)), second)
-    total = (jnp.sum(terms.astype(F32), axis=0) * scale).astype(BF16)
-    total = swap_pieces(copies(total), first).reshape(length, width)
-    return pl.pallas_call(
+    own, *pieces = call(
+        cut_kernel, (quarter, F32), *[(quarter, BF16)] * 3, scratch_shapes=[pltpu.VMEM((length, width), F32)]
+    )(*kernel_part, *lateral_part)
+    vmem, far = pl.BlockSpec(memory_space=pltpu.VMEM), pl.BlockSpec(memory_space=pltpu.HBM)
+    after = pltpu.with_memory_space_constraint(after, pltpu.HBM)
+    [total] = call(add_kernel, (quarter, BF16), in_specs=[vmem] * 4 + [far])(own, *exchange(pieces, 0), after)
+    [total] = call(functools.partial(finish_kernel, scale), (quarter, BF16))(total, *exchange([total] * 3, 1))
+    quarters = [total, *exchange([total] * 3, 0)]
+    return call(
         place_kernel,
-        out_shape=[jax.ShapeDtypeStruct((rows, 2 * width), BF16) for rows in (edge, length - edge)],
-        out_specs=[pl.BlockSpec(memory_space=pltpu.HBM)] * 2,
-        scratch_shapes=[pltpu.SemaphoreType.DMA((20,))],
-        compiler_params=pltpu.CompilerParams(vmem_limit_bytes=8 * 2**20),
-    )(total, swap(total))
+        ((edge, 2 * width), BF16),
+        ((length - edge, 2 * width), BF16),
+        out_specs=[far] * 2,
+        scratch_shapes=[pltpu.SemaphoreType.DMA((16,))],
+    )(*quarters, *[swap(one) for one in quarters])
 
 
 def local(features, top_down, lateral_weight, out_kernel, cotangent):
@@ -225,19 +276,25 @@
         cot_before, cot_after = neighbour_rows(cot)
         arrays = (cot, lateral_weight, top_down[image], features[image].reshape(cells, in_channels), taps)
         arrays = [pltpu.with_memory_space_constraint(array, pltpu.HBM) for array in arrays]
-        merged, merged_t, stack = pl.pallas_call(
+        merged, merged_t, stack, feat_t, near_taps = pl.pallas_call(
             merge_kernel,
             out_shape=[
                 jax.ShapeDtypeStruct(shape, BF16)
-                for shape in ((cells, channels), (channels, cells), (rows, cols, 3 * channels))
+                for shape in (
+                    (cells, channels),
+                    (channels, cells),
+                    (rows, cols, 3 * channels),
+                    (in_channels, cells),
+                    taps.shape,
+                )
             ],
-            in_specs=[pl.BlockSpec(memory_space=pltpu.HBM)] * 4,
-            scratch_shapes=[*[pltpu.VMEM(array.shape, BF16) for array in arrays[:4]], pltpu.SemaphoreType.DMA((4,))],
+            in_specs=[pl.BlockSpec(memory_space=pltpu.HBM)] * 5,
+            scratch_shapes=[*[pltpu.VMEM(array.shape, BF16) for array in arrays[:4]], pltpu.SemaphoreType.DMA((5,))],
             compiler_params=params,
             cost_estimate=pl.CostEstimate(
                 flops=2 * cells * channels * 4 * in_channels, bytes_accessed=4 * 2**20, transcendentals=0
             ),
-        )(*arrays[:4])
+        )(*arrays)
         halo, *kernel_part = pl.pallas_call(
             functools.partial(kernel_grad_kernel, peers),
             out_shape=[jax.ShapeDtypeStruct((2, cols, 3 * channels), BF16), *sums(9 * channels, 2 * cols)],
@@ -251,16 +308,11 @@
         grad_top, *lateral_part = pl.pallas_call(
             data_grad_kernel,
             out_shape=[jax.ShapeDtypeStruct((rows // 2, cols // 2, channels), BF16), *sums(in_channels, 0)],
-            in_specs=[pl.BlockSpec(memory_space=pltpu.VMEM)] * 2 + [pl.BlockSpec(memory_space=pltpu.HBM)] * 2,
-            scratch_shapes=[
-                *[pltpu.VMEM(array.shape, BF16) for array in arrays[3:]],
-                pltpu.SemaphoreType.DMA((2,)),
-            ],
             compiler_params=params,
             cost_estimate=pl.CostEstimate(
                 flops=2 * cells * channels * (9 * channels + in_channels), bytes_accessed=4 * 2**20, transcendentals=0
             ),
-        )(stack, halo, *arrays[3:])
+        )(stack, halo, feat_t, near_taps)
         if halves:
             lateral_part[1] = swap(lateral_part[1])
         merged = merged.reshape(rows, cols, channels)
@@ -279,20 +331,15 @@
                 cost_estimate=pl.CostEstimate(
                     flops=2 * cells * channels * 9 * channels, bytes_accessed=2 * 2**20, transcendentals=0
                 ),
-            )(merged, taps, *edges)
+            )(merged, near_taps, *edges)
         )
         tops.append(grad_top)
-        if halves:
-            parts = [
-                (mine + got[: mine.shape[0]].astype(F32)).astype(BF16) for mine, got in (kernel_part, lateral_part)
-            ]
-        else:
-            parts = [kernel_part[0], lateral_part[0]] if parts is None else [
-                a + b for a, b in zip(parts, (kernel_part[0], lateral_part[0]))
-            ]
+        if not halves:
+            part = [kernel_part[0], lateral_part[0]]
+            parts = part if parts is None else [a + b for a, b in zip(parts, part)]
     scale = 1.0 / (images * lax.axis_size("dp"))
     if halves:
-        grad_kernel, grad_lateral = sum_everywhere(jnp.concatenate(parts), scale, 9 * channels)
+        grad_kernel, grad_lateral = sum_everywhere(kernel_part, lateral_part, scale, outs[0])
     else:
         grad_kernel, grad_lateral = [(total * scale).astype(BF16) for total in lax.psum(parts, ("dp", "space"))]
     return jnp.stack(outs), jnp.stack(tops), grad_kernel.reshape(out_kernel.shape), grad_lateral

time: 56.3 us -> 44.1 us (0.78)
  blocking collectives: 41.2 us -> 0 us
  waiting for transfers between devices: 0.99 us -> 19.4 us
  starting transfers between devices: 1.56 us -> 14 us
  Pallas kernels: 10 us -> 8.99 us
    all_to_all x3 -> x0, blocking collectives: 41.2 us -> none  [swap_pieces(): lax.all_to_all(pieces, ('dp', 'space'), 0, 0, axis_index_groups=groups, t...]
    ppermute x0 -> x9, waiting for transfers between devices: none -> 17.3 us  [exchange(): came[k] = lax.ppermute(pieces[k - 1], ('dp', 'space'), pairs)]
    ppermute x0 -> x9, starting transfers between devices: none -> 12.5 us  [exchange(): came[k] = lax.ppermute(pieces[k - 1], ('dp', 'space'), pairs)]
    pallas_call x1, Pallas kernels: 3.95 us -> 2.48 us  [local(): pl.pallas_call(data_grad_kernel, out_shape=[jax.ShapeDtypeStruct((rows //...]
    ppermute x3 -> x6, waiting for transfers between devices: 0.99 us -> 2.15 us  [swap(): return lax.ppermute(array, 'space', [(0, 1), (1, 0)])]
    pallas_call x1 -> x4, Pallas kernels: 1.26 us -> 1.64 us  [the longest x1 1.22 us: sum_everywhere(): call(place_kernel, ((edge, 2 * width), BF16), ((length - edge, 2 * width)...]
  transfers between devices with their start and end apart: 4 -> 16, of which waited for: 1 -> 10; matrix products, arithmetic and copies ran while one was open for 0% -> 0% of each run, Pallas kernels for 14% -> 14%
where the time goes in v7:
time: 44.1 us; the launch traced here: 43.9 us
  waiting for transfers between devices  19.4 us (44%)
  starting transfers between devices  14 us (32%)
  Pallas kernels  8.99 us (20%)
  local copies, waits for them, and re-layouts  0.81 us (2%)
  between operations  0.69 us (2%)
    ppermute x9, waiting for transfers between devices, exchange(): came[k] = lax.ppermute(pieces[k - 1], ('dp', 'space'), pairs)  17.3 us
    ppermute x9, starting transfers between devices, exchange(): came[k] = lax.ppermute(pieces[k - 1], ('dp', 'space'), pairs)  12.5 us
    pallas_call x1, Pallas kernels, local(): pl.pallas_call(data_grad_kernel, out_shape=[jax.ShapeDtypeStruct((rows //...  2.48 us
    ppermute x6, waiting for transfers between devices, swap(): return lax.ppermute(array, 'space', [(0, 1), (1, 0)])  2.15 us
    pallas_call x1, Pallas kernels, local(): pl.pallas_call(merge_kernel, out_shape=[jax.ShapeDtypeStruct(shape, BF16)...  1.94 us
    pallas_call x1, Pallas kernels, local(): pl.pallas_call(functools.partial(forward_kernel, peers), out_shape=jax.Sh...  1.85 us
    pallas_call x1, Pallas kernels, sum_everywhere(): call(place_kernel, ((edge, 2 * width), BF16), ((length - edge, 2 * width)...  1.22 us
    pallas_call x1, Pallas kernels, local(): pl.pallas_call(functools.partial(kernel_grad_kernel, peers), out_shape=[j...  1.09 us
  transfers between devices with their start and end apart: 16, of which 10 were waited for; matrix products, arithmetic and copies ran while one was open for 0% of the time, Pallas kernels for 14%

profile of v7, /device:TPU:0, one launch (start us, length us, event | category | flops | bytes accessed | tf_op | source)
XLA Modules:
  0.0 43.9 jit_solution(9129592712097780043)
XLA Ops:
  0.6 0.8 %dynamic-slice_bitcast_fusion = bf16[96,256]{1,0:T(8,128)(2,1)S(1)} fusion(bf16[1,8,96,256]{3,2,1,0:T(8,128)(2,1)} %param.9, s32[]{:T(128)S(6)} %select_n.4), kind=kLoop, calls=%fused_computation | loop fusion | bytes 98308 | tf_op jit(solution)/shard_map/jit(dynamic_index_in_dim)/squeeze | solution.py:21
  1.4 0.5 %collective-permute-start = (bf16[96,256]{1,0:T(8,128)(2,1)S(1)}, bf16[96,256]{1,0:T(8,128)(2,1)S(1)}, u32[]{:S(2)}, u32[]{:S(2)}) collective-permute-start(bf16[96,256]{1,0:T(8,128)(2,1)S(1)} %dynamic-slice_bitcast_fusion), channel_id=1, source_target_pairs={{0,1},{1,0},{2,3},{3,2},{4,5},{5,4},{6,7},{7,6},{8,9},{9,8},{10,11... | collective-permute-start | bytes 147464 | tf_op jit(solution)/shard_map/ppermute | solution.py:22
  1.9 1.9 %shard_map.84 = (bf16[768,256]{1,0:T(8,128)(2,1)S(1)}, bf16[256,768]{1,0:T(8,128)(2,1)S(1)}, bf16[8,96,768]{2,1,0:T(8,128)(2,1)S(1)}, bf16[512,768]{1,0:T(8,128)(2,1)S(1)}, bf16[9,256,256]{2,1,0:T(8,128)(2,1)S(1)}) custom-call(bf16[8,96,256]{2,1,0:T(8,128)(2,1)} %bitcast.12, bf16[512,256]{1,0:T(8,128)(2,1)} %refs_1_.1, bf16[4,48,256]{2,1,0:T(8,128)(2,1)} %bitcast.16, ...), custom_call_target="tpu_custom_call" | custom-call | flops 805306368 | bytes 4194304 | tf_op jit(solution)/shard_map/pallas_call | solution.py:279
  3.8 1.1 %shard_map.85 = (bf16[2,96,768]{2,1,0:T(8,128)(2,1)S(1)}, f32[2304,128]{1,0:T(8,128)S(1)}, bf16[2496,128]{1,0:T(8,128)(2,1)S(1)}) custom-call(bf16[8,96,768]{2,1,0:T(8,128)(2,1)S(1)} %get-tuple-element.23.stack, bf16[768,256]{1,0:T(8,128)(2,1)S(1)} %get-tuple-element.21.merged, bf16[256,768]{1,0:T(8,128)(2,1)S(1)} %get-tuple-element.24.merged_t, ...), custom_call_target="tpu_custom_call" | custom-call | flops 905969664 | bytes 4194304 | tf_op jit(solution)/shard_map/pallas_call | solution.py:298
  5.0 0.1 collective-permute-start.1
  5.1 2.5 %shard_map.87 = (bf16[4,48,256]{2,1,0:T(8,128)(2,1)}, f32[512,128]{1,0:T(8,128)S(1)}, bf16[512,128]{1,0:T(8,128)(2,1)S(1)}) custom-call(bf16[8,96,768]{2,1,0:T(8,128)(2,1)S(1)} %get-tuple-element.23.stack, bf16[2,96,768]{2,1,0:T(8,128)(2,1)S(1)} %get-tuple-element.26.halo, bf16[512,768]{1,0:T(8,128)(2,1)S(1)} %get-tuple-element.27.feat_t, ...), custom_call_target="tpu_custom_call" | custom-call | flops 1107296256 | bytes 4194304 | tf_op jit(solution)/shard_map/pallas_call | solution.py:308
  7.5 0.5 %collective-permute-start.2 = (bf16[512,128]{1,0:T(8,128)(2,1)S(1)}, bf16[512,128]{1,0:T(8,128)(2,1)S(1)}, u32[]{:S(2)}, u32[]{:S(2)}) collective-permute-start(bf16[512,128]{1,0:T(8,128)(2,1)S(1)} %get-tuple-element.31), channel_id=1, source_target_pairs={{0,1},{1,0},{2,3},{3,2},{4,5},{5,4},{6,7},{7,6},{8,9},{9,8},{10,11... | collective-permute-start | bytes 393224 | tf_op jit(solution)/shard_map/ppermute | solution.py:223
  8.0 1.0 %collective-permute-done.2.got_b = bf16[512,128]{1,0:T(8,128)(2,1)S(1)} collective-permute-done((bf16[512,128]{1,0:T(8,128)(2,1)S(1)}, bf16[512,128]{1,0:T(8,128)(2,1)S(1)}, u32[]{:S(2)}, u32[]{:S(2)}) %collective-permute-start.2) | collective-permute-done | bytes 131104 | tf_op jit(solution)/shard_map/ppermute | solution.py:223
  9.0 0.2 shard_map.88
  9.2 2.9 %collective-permute-start.3 = (bf16[704,128]{1,0:T(8,128)(2,1)S(1)}, bf16[704,128]{1,0:T(8,128)(2,1)S(1)}, u32[]{:S(2)}, u32[]{:S(2)}) collective-permute-start(bf16[704,128]{1,0:T(8,128)(2,1)S(1)} %get-tuple-element.33), channel_id=1, source_target_pairs={{0,2},{1,9},{2,0},{3,11},{4,6},{5,13},{6,4},{7,15},{8,10},{9,1},{1... | collective-permute-start | bytes 540680 | tf_op jit(solution)/shard_map/ppermute | solution.py:218
  12.1 1.5 %collective-permute-start.4 = (bf16[704,128]{1,0:T(8,128)(2,1)S(1)}, bf16[704,128]{1,0:T(8,128)(2,1)S(1)}, u32[]{:S(2)}, u32[]{:S(2)}) collective-permute-start(bf16[704,128]{1,0:T(8,128)(2,1)S(1)} %get-tuple-element.34), channel_id=1, source_target_pairs={{0,4},{1,17},{2,6},{3,19},{4,0},{5,21},{6,2},{7,23},{8,12},{9,25},... | collective-permute-start | bytes 540680 | tf_op jit(solution)/shard_map/ppermute | solution.py:218
  13.7 0.0 collective-permute-start.5
  13.7 1.8 %shard_map.86.refs_0_ = bf16[8,96,256]{2,1,0:T(8,128)(2,1)} custom-call(bf16[8,96,256]{2,1,0:T(8,128)(2,1)S(1)} %bitcast.10, bf16[9,256,256]{2,1,0:T(8,128)(2,1)S(1)} %get-tuple-element.22.out_w, bf16[2496,128]{1,0:T(8,128)(2,1)S(1)} %collective-permute-done.1.refs_0_.got_a), custom_call_target="tpu_custom_call" | custom-call | flops 905969664 | bytes 2097152 | tf_op jit(solution)/shard_map/pallas_call | solution.py:321
  15.5 0.1 collective-permute-done.3.one
  15.6 3.0 %collective-permute-done.4.two = bf16[704,128]{1,0:T(8,128)(2,1)S(1)} collective-permute-done((bf16[704,128]{1,0:T(8,128)(2,1)S(1)}, bf16[704,128]{1,0:T(8,128)(2,1)S(1)}, u32[]{:S(2)}, u32[]{:S(2)}) %collective-permute-start.4) | collective-permute-done | bytes 180256 | tf_op jit(solution)/shard_map/ppermute | solution.py:218
  18.6 1.4 %collective-permute-done.5.three = bf16[704,128]{1,0:T(8,128)(2,1)S(1)} collective-permute-done((bf16[704,128]{1,0:T(8,128)(2,1)S(1)}, bf16[704,128]{1,0:T(8,128)(2,1)S(1)}, u32[]{:S(2)}, u32[]{:S(2)}) %collective-permute-start.5) | collective-permute-done | bytes 180256 | tf_op jit(solution)/shard_map/ppermute | solution.py:218
  20.1 0.1 shard_map.89.own
  20.1 3.7 %collective-permute-start.8 = (bf16[704,128]{1,0:T(8,128)(2,1)S(1)}, bf16[704,128]{1,0:T(8,128)(2,1)S(1)}, u32[]{:S(2)}, u32[]{:S(2)}) collective-permute-start(bf16[704,128]{1,0:T(8,128)(2,1)S(1)} %shard_map.89.own), channel_id=1, source_target_pairs={{0,24},{1,7},{2,26},{3,5},{4,28},{5,3},{6,30},{7,1},{8,16},{9,15},... | collective-permute-start | bytes 540680 | tf_op jit(solution)/shard_map/ppermute | solution.py:218
  23.8 0.8 %collective-permute-start.6 = (bf16[704,128]{1,0:T(8,128)(2,1)S(1)}, bf16[704,128]{1,0:T(8,128)(2,1)S(1)}, u32[]{:S(2)}, u32[]{:S(2)}) collective-permute-start(bf16[704,128]{1,0:T(8,128)(2,1)S(1)} %shard_map.89.own), channel_id=1, source_target_pairs={{0,8},{1,3},{2,10},{3,1},{4,12},{5,7},{6,14},{7,5},{8,0},{9,11},{1... | collective-permute-start | bytes 540680 | tf_op jit(solution)/shard_map/ppermute | solution.py:218
  24.6 3.0 %collective-permute-done.8.three = bf16[704,128]{1,0:T(8,128)(2,1)S(1)} collective-permute-done((bf16[704,128]{1,0:T(8,128)(2,1)S(1)}, bf16[704,128]{1,0:T(8,128)(2,1)S(1)}, u32[]{:S(2)}, u32[]{:S(2)}) %collective-permute-start.8) | collective-permute-done | bytes 180256 | tf_op jit(solution)/shard_map/ppermute | solution.py:218
  27.6 4.9 %collective-permute-done.7.two = bf16[704,128]{1,0:T(8,128)(2,1)S(1)} collective-permute-done((bf16[704,128]{1,0:T(8,128)(2,1)S(1)}, bf16[704,128]{1,0:T(8,128)(2,1)S(1)}, u32[]{:S(2)}, u32[]{:S(2)}) %collective-permute-start.7) | collective-permute-done | bytes 180256 | tf_op jit(solution)/shard_map/ppermute | solution.py:218
  32.5 0.1 shard_map.90.refs_0_
  32.6 1.1 %collective-permute-start.11 = (bf16[704,128]{1,0:T(8,128)(2,1)S(1)}, bf16[704,128]{1,0:T(8,128)(2,1)S(1)}, u32[]{:S(2)}, u32[]{:S(2)}) collective-permute-start(bf16[704,128]{1,0:T(8,128)(2,1)S(1)} %shard_map.90.refs_0_), channel_id=1, source_target_pairs={{0,6},{1,25},{2,4},{3,27},{4,2},{5,29},{6,0},{7,31},{8,14},{9,17},... | collective-permute-start | bytes 540680 | tf_op jit(solution)/shard_map/ppermute | solution.py:218
  33.7 1.0 %collective-permute-start.10 = (bf16[704,128]{1,0:T(8,128)(2,1)S(1)}, bf16[704,128]{1,0:T(8,128)(2,1)S(1)}, u32[]{:S(2)}, u32[]{:S(2)}) collective-permute-start(bf16[704,128]{1,0:T(8,128)(2,1)S(1)} %shard_map.90.refs_0_), channel_id=1, source_target_pairs={{0,4},{1,17},{2,6},{3,19},{4,0},{5,21},{6,2},{7,23},{8,12},{9,25},... | collective-permute-start | bytes 540680 | tf_op jit(solution)/shard_map/ppermute | solution.py:218
  34.7 1.5 %collective-permute-start.9 = (bf16[704,128]{1,0:T(8,128)(2,1)S(1)}, bf16[704,128]{1,0:T(8,128)(2,1)S(1)}, u32[]{:S(2)}, u32[]{:S(2)}) collective-permute-start(bf16[704,128]{1,0:T(8,128)(2,1)S(1)} %shard_map.90.refs_0_), channel_id=1, source_target_pairs={{0,2},{1,9},{2,0},{3,11},{4,6},{5,13},{6,4},{7,15},{8,10},{9,1},{1... | collective-permute-start | bytes 540680 | tf_op jit(solution)/shard_map/ppermute | solution.py:218
  36.2 3.0 %collective-permute-done.11.refs_3_ = bf16[704,128]{1,0:T(8,128)(2,1)S(1)} collective-permute-done((bf16[704,128]{1,0:T(8,128)(2,1)S(1)}, bf16[704,128]{1,0:T(8,128)(2,1)S(1)}, u32[]{:S(2)}, u32[]{:S(2)}) %collective-permute-start.11) | collective-permute-done | bytes 180256 | tf_op jit(solution)/shard_map/ppermute | solution.py:218
  39.2 1.8 %collective-permute-done.10.refs_2_ = bf16[704,128]{1,0:T(8,128)(2,1)S(1)} collective-permute-done((bf16[704,128]{1,0:T(8,128)(2,1)S(1)}, bf16[704,128]{1,0:T(8,128)(2,1)S(1)}, u32[]{:S(2)}, u32[]{:S(2)}) %collective-permute-start.10) | collective-permute-done | bytes 180256 | tf_op jit(solution)/shard_map/ppermute | solution.py:218
  41.0 0.0 collective-permute-start.14
  41.0 0.5 %collective-permute-start.13 = (bf16[704,128]{1,0:T(8,128)(2,1)S(1)}, bf16[704,128]{1,0:T(8,128)(2,1)S(1)}, u32[]{:S(2)}, u32[]{:S(2)}) collective-permute-start(bf16[704,128]{1,0:T(8,128)(2,1)S(1)} %collective-permute-done.9.refs_1_), channel_id=1, source_target_pairs={{0,1},{1,0},{2,3},{3,2},{4,5},{5,4},{6,7},{7,6},{8,9},{9,8},{10,11... | collective-permute-start | bytes 540680 | tf_op jit(solution)/shard_map/ppermute | solution.py:223
  41.5 0.9 %collective-permute-done.14.refs_6_ = bf16[704,128]{1,0:T(8,128)(2,1)S(1)} collective-permute-done((bf16[704,128]{1,0:T(8,128)(2,1)S(1)}, bf16[704,128]{1,0:T(8,128)(2,1)S(1)}, u32[]{:S(2)}, u32[]{:S(2)}) %collective-permute-start.14) | collective-permute-done | bytes 180256 | tf_op jit(solution)/shard_map/ppermute | solution.py:223
  42.4 0.3 collective-permute-done.13.refs_5_
  42.7 1.2 %shard_map.91 = (bf16[2304,256]{1,0:T(8,128)(2,1)}, bf16[512,256]{1,0:T(8,128)(2,1)}) custom-call(bf16[704,128]{1,0:T(8,128)(2,1)S(1)} %shard_map.90.refs_0_, bf16[704,128]{1,0:T(8,128)(2,1)S(1)} %collective-permute-done.9.refs_1_, bf16[704,128]{1,0:T(8,128)(2,1)S(1)} %collective-permute-done.10.refs_2_, ...), custom_call_target="tpu_custom_call" | custom-call | tf_op jit(solution)/shard_map/pallas_call | solution.py:247
  (9 shorter events, 0.0 us)
Async XLA Ops:
  1.4 2.4 %collective-permute-start = (bf16[96,256]{1,0:T(8,128)(2,1)S(1)}, bf16[96,256]{1,0:T(8,128)(2,1)S(1)}, u32[]{:S(2)}, u32[]{:S(2)}) collective-permute-start(bf16[96,256]{1,0:T(8,128)(2,1)S(1)} %dynamic-slice_bitcast_fusion), channel_id=1, source_target_pairs={{0,1},{1,0},{2,3},{3,2},{4,5},{5,4},{6,7},{7,6},{8,9},{9,8},{10,11... | collective-permute-start | bytes 147464 | tf_op jit(solution)/shard_map/ppermute | solution.py:22
  5.0 4.0 %collective-permute-start.1 = (bf16[2496,128]{1,0:T(8,128)(2,1)S(1)}, bf16[2496,128]{1,0:T(8,128)(2,1)S(1)}, u32[]{:S(2)}, u32[]{:S(2)}) collective-permute-start(bf16[2496,128]{1,0:T(8,128)(2,1)S(1)} %get-tuple-element.25), channel_id=1, source_target_pairs={{0,1},{1,0},{2,3},{3,2},{4,5},{5,4},{6,7},{7,6},{8,9},{9,8},{10,11... | collective-permute-start | bytes 1916936 | tf_op jit(solution)/shard_map/ppermute | solution.py:223
  7.5 1.4 %collective-permute-start.2 = (bf16[512,128]{1,0:T(8,128)(2,1)S(1)}, bf16[512,128]{1,0:T(8,128)(2,1)S(1)}, u32[]{:S(2)}, u32[]{:S(2)}) collective-permute-start(bf16[512,128]{1,0:T(8,128)(2,1)S(1)} %get-tuple-element.31), channel_id=1, source_target_pairs={{0,1},{1,0},{2,3},{3,2},{4,5},{5,4},{6,7},{7,6},{8,9},{9,8},{10,11... | collective-permute-start | bytes 393224 | tf_op jit(solution)/shard_map/ppermute | solution.py:223
  9.2 6.4 %collective-permute-start.3 = (bf16[704,128]{1,0:T(8,128)(2,1)S(1)}, bf16[704,128]{1,0:T(8,128)(2,1)S(1)}, u32[]{:S(2)}, u32[]{:S(2)}) collective-permute-start(bf16[704,128]{1,0:T(8,128)(2,1)S(1)} %get-tuple-element.33), channel_id=1, source_target_pairs={{0,2},{1,9},{2,0},{3,11},{4,6},{5,13},{6,4},{7,15},{8,10},{9,1},{1... | collective-permute-start | bytes 540680 | tf_op jit(solution)/shard_map/ppermute | solution.py:218
  12.1 6.5 %collective-permute-start.4 = (bf16[704,128]{1,0:T(8,128)(2,1)S(1)}, bf16[704,128]{1,0:T(8,128)(2,1)S(1)}, u32[]{:S(2)}, u32[]{:S(2)}) collective-permute-start(bf16[704,128]{1,0:T(8,128)(2,1)S(1)} %get-tuple-element.34), channel_id=1, source_target_pairs={{0,4},{1,17},{2,6},{3,19},{4,0},{5,21},{6,2},{7,23},{8,12},{9,25},... | collective-permute-start | bytes 540680 | tf_op jit(solution)/shard_map/ppermute | solution.py:218
  13.7 6.4 %collective-permute-start.5 = (bf16[704,128]{1,0:T(8,128)(2,1)S(1)}, bf16[704,128]{1,0:T(8,128)(2,1)S(1)}, u32[]{:S(2)}, u32[]{:S(2)}) collective-permute-start(bf16[704,128]{1,0:T(8,128)(2,1)S(1)} %get-tuple-element.35), channel_id=1, source_target_pairs={{0,6},{1,25},{2,4},{3,27},{4,2},{5,29},{6,0},{7,31},{8,14},{9,17},... | collective-permute-start | bytes 540680 | tf_op jit(solution)/shard_map/ppermute | solution.py:218
  20.1 7.5 %collective-permute-start.8 = (bf16[704,128]{1,0:T(8,128)(2,1)S(1)}, bf16[704,128]{1,0:T(8,128)(2,1)S(1)}, u32[]{:S(2)}, u32[]{:S(2)}) collective-permute-start(bf16[704,128]{1,0:T(8,128)(2,1)S(1)} %shard_map.89.own), channel_id=1, source_target_pairs={{0,24},{1,7},{2,26},{3,5},{4,28},{5,3},{6,30},{7,1},{8,16},{9,15},... | collective-permute-start | bytes 540680 | tf_op jit(solution)/shard_map/ppermute | solution.py:218
  23.8 8.7 %collective-permute-start.7 = (bf16[704,128]{1,0:T(8,128)(2,1)S(1)}, bf16[704,128]{1,0:T(8,128)(2,1)S(1)}, u32[]{:S(2)}, u32[]{:S(2)}) collective-permute-start(bf16[704,128]{1,0:T(8,128)(2,1)S(1)} %shard_map.89.own), channel_id=1, source_target_pairs={{0,16},{1,5},{2,18},{3,7},{4,20},{5,1},{6,22},{7,3},{8,24},{9,13},... | collective-permute-start | bytes 540680 | tf_op jit(solution)/shard_map/ppermute | solution.py:218
  23.8 8.7 %collective-permute-start.6 = (bf16[704,128]{1,0:T(8,128)(2,1)S(1)}, bf16[704,128]{1,0:T(8,128)(2,1)S(1)}, u32[]{:S(2)}, u32[]{:S(2)}) collective-permute-start(bf16[704,128]{1,0:T(8,128)(2,1)S(1)} %shard_map.89.own), channel_id=1, source_target_pairs={{0,8},{1,3},{2,10},{3,1},{4,12},{5,7},{6,14},{7,5},{8,0},{9,11},{1... | collective-permute-start | bytes 540680 | tf_op jit(solution)/shard_map/ppermute | solution.py:218
  32.6 6.6 %collective-permute-start.11 = (bf16[704,128]{1,0:T(8,128)(2,1)S(1)}, bf16[704,128]{1,0:T(8,128)(2,1)S(1)}, u32[]{:S(2)}, u32[]{:S(2)}) collective-permute-start(bf16[704,128]{1,0:T(8,128)(2,1)S(1)} %shard_map.90.refs_0_), channel_id=1, source_target_pairs={{0,6},{1,25},{2,4},{3,27},{4,2},{5,29},{6,0},{7,31},{8,14},{9,17},... | collective-permute-start | bytes 540680 | tf_op jit(solution)/shard_map/ppermute | solution.py:218
  33.7 7.3 %collective-permute-start.10 = (bf16[704,128]{1,0:T(8,128)(2,1)S(1)}, bf16[704,128]{1,0:T(8,128)(2,1)S(1)}, u32[]{:S(2)}, u32[]{:S(2)}) collective-permute-start(bf16[704,128]{1,0:T(8,128)(2,1)S(1)} %shard_map.90.refs_0_), channel_id=1, source_target_pairs={{0,4},{1,17},{2,6},{3,19},{4,0},{5,21},{6,2},{7,23},{8,12},{9,25},... | collective-permute-start | bytes 540680 | tf_op jit(solution)/shard_map/ppermute | solution.py:218
  34.7 6.3 %collective-permute-start.9 = (bf16[704,128]{1,0:T(8,128)(2,1)S(1)}, bf16[704,128]{1,0:T(8,128)(2,1)S(1)}, u32[]{:S(2)}, u32[]{:S(2)}) collective-permute-start(bf16[704,128]{1,0:T(8,128)(2,1)S(1)} %shard_map.90.refs_0_), channel_id=1, source_target_pairs={{0,2},{1,9},{2,0},{3,11},{4,6},{5,13},{6,4},{7,15},{8,10},{9,1},{1... | collective-permute-start | bytes 540680 | tf_op jit(solution)/shard_map/ppermute | solution.py:218
  36.2 5.4 %collective-permute-start.12 = (bf16[704,128]{1,0:T(8,128)(2,1)S(1)}, bf16[704,128]{1,0:T(8,128)(2,1)S(1)}, u32[]{:S(2)}, u32[]{:S(2)}) collective-permute-start(bf16[704,128]{1,0:T(8,128)(2,1)S(1)} %shard_map.90.refs_0_), channel_id=1, source_target_pairs={{0,1},{1,0},{2,3},{3,2},{4,5},{5,4},{6,7},{7,6},{8,9},{9,8},{10,11... | collective-permute-start | bytes 540680 | tf_op jit(solution)/shard_map/ppermute | solution.py:223
  39.2 2.3 %collective-permute-start.15 = (bf16[704,128]{1,0:T(8,128)(2,1)S(1)}, bf16[704,128]{1,0:T(8,128)(2,1)S(1)}, u32[]{:S(2)}, u32[]{:S(2)}) collective-permute-start(bf16[704,128]{1,0:T(8,128)(2,1)S(1)} %collective-permute-done.11.refs_3_), channel_id=1, source_target_pairs={{0,1},{1,0},{2,3},{3,2},{4,5},{5,4},{6,7},{7,6},{8,9},{9,8},{10,11... | collective-permute-start | bytes 540680 | tf_op jit(solution)/shard_map/ppermute | solution.py:223
  41.0 1.4 %collective-permute-start.14 = (bf16[704,128]{1,0:T(8,128)(2,1)S(1)}, bf16[704,128]{1,0:T(8,128)(2,1)S(1)}, u32[]{:S(2)}, u32[]{:S(2)}) collective-permute-start(bf16[704,128]{1,0:T(8,128)(2,1)S(1)} %collective-permute-done.10.refs_2_), channel_id=1, source_target_pairs={{0,1},{1,0},{2,3},{3,2},{4,5},{5,4},{6,7},{7,6},{8,9},{9,8},{10,11... | collective-permute-start | bytes 540680 | tf_op jit(solution)/shard_map/ppermute | solution.py:223
  41.0 1.7 %collective-permute-start.13 = (bf16[704,128]{1,0:T(8,128)(2,1)S(1)}, bf16[704,128]{1,0:T(8,128)(2,1)S(1)}, u32[]{:S(2)}, u32[]{:S(2)}) collective-permute-start(bf16[704,128]{1,0:T(8,128)(2,1)S(1)} %collective-permute-done.9.refs_1_), channel_id=1, source_target_pairs={{0,1},{1,0},{2,3},{3,2},{4,5},{5,4},{6,7},{7,6},{8,9},{9,8},{10,11... | collective-permute-start | bytes 540680 | tf_op jit(solution)/shard_map/ppermute | solution.py:223

commit v8 on v7

--- a/solution.py
+++ b/solution.py
@@ -46,12 +46,12 @@
 
 
 def merge_kernel(*refs):
-    far, (merged, merged_t, stack, feat_t, out_w), near, sems = refs[:5], refs[5:10], refs[10:14], refs[14]
-    near = (*near, out_w)
+    far, (merged, merged_t, stack, feat, out_w), near, sems = refs[:5], refs[5:10], refs[10:13], refs[13]
+    near = (*near, feat, out_w)
     copies = [pltpu.make_async_copy(a, b, sems.at[i]) for i, (a, b) in enumerate(zip(far, near))]
     for copy in copies:
         copy.start()
-    cot, lat_w, top, feat, _ = near
+    cot, lat_w, top = near[:3]
     rows, cols, channels = cot.shape
     half = cols // 2
     copies[0].wait()
@@ -67,7 +67,6 @@
         for r in (2 * q, 2 * q + 1):
             merged[r * cols : (r + 1) * cols, :] = (lateral[r * cols : (r + 1) * cols] + lifted).astype(BF16)
     merged_t[...] = jnp.transpose(merged[...])
-    feat_t[...] = jnp.transpose(feat[...])
     copies[4].wait()
 
 
@@ -109,25 +108,18 @@
             put_sums(outs, (3 * i + j) * channels, part[:, j * channels : (j + 1) * channels])
 
 
-def data_grad_kernel(stack, halo, feat_t, out_w, grad_top, *outs):
-    rows, cols, deep = stack.shape
-    channels, half = deep // 3, cols // 2
+def data_grad_kernel(stack, halo, feat, out_w, grad, *outs):
     cells = jnp.concatenate(strips_of(stack, halo), axis=1)
     taps = jnp.concatenate([out_w[tap] for tap in range(9)], axis=1)
     total = lax.dot_general(cells, taps, (((1,), (1,)), ((), ())), preferred_element_type=F32)
-    grad = total.astype(BF16)
-    put_sums(outs, 0, jnp.dot(feat_t[...], grad, preferred_element_type=F32))
-    lower = lax.broadcasted_iota(jnp.int32, (half, 2 * cols), 1)
-    lower = jnp.where(lower >= cols, lower - cols, lower)
-    pool = jnp.where(lower // 2 == lax.broadcasted_iota(jnp.int32, (half, 2 * cols), 0), 1.0, 0.0).astype(BF16)
-    for q in range(rows // 2):
-        pair = grad[2 * q * cols : (2 * q + 2) * cols]
-        grad_top[q] = jnp.dot(pool, pair, preferred_element_type=F32).astype(BF16)
-
-
-def forward_kernel(peers, merged, out_w, *refs):
-    edges, (out, stack, near, sem) = refs[:-4], refs[-4:]
+    grad[...] = total.astype(BF16)
+    put_sums(outs, 0, jnp.dot(jnp.transpose(feat[...]), grad[...], preferred_element_type=F32))
+
+
+def forward_kernel(peers, merged, out_w, grad, *refs):
+    edges, (out, grad_top, stack, near, sem) = refs[:-5], refs[-5:]
     rows, cols, channels = merged.shape
+    half = cols // 2
     for r in range(rows):
         put_shifted(stack, r + 1, merged[r], -1)
     if len(edges) == 1:
@@ -141,6 +133,12 @@
     near[...] = total.astype(BF16).reshape(out.shape)
     copy = pltpu.make_async_copy(near, out, sem)
     copy.start()
+    lower = lax.broadcasted_iota(jnp.int32, (half, 2 * cols), 1)
+    lower = jnp.where(lower >= cols, lower - cols, lower)
+    pool = jnp.where(lower // 2 == lax.broadcasted_iota(jnp.int32, (half, 2 * cols), 0), 1.0, 0.0).astype(BF16)
+    for q in range(rows // 2):
+        pair = grad[2 * q * cols : (2 * q + 2) * cols, :]
+        grad_top[q] = jnp.dot(pool, pair, preferred_element_type=F32).astype(BF16)
     copy.wait()
 
 
@@ -154,69 +152,54 @@
     return pl.ds(pl.multiple_of(index * length, 16), length)
 
 
-def cut_kernel(mine_a, got_a, mine_b, got_b, *refs):
-    outs, total = refs[:4], refs[4]
+def cut_kernel(mine, got, *refs):
+    place, _ = places()
+    for k, out in zip((0, 3, 2, 1), refs):
+        rows = block(place ^ k, out.shape[0])
+        out[...] = (mine[rows, :] + got[rows, :].astype(F32)).astype(out.dtype)
+
+
+def add_kernel(own_a, own_b, three_a, two_a, one_a, one_b, two_b, three_b, out):
     start = 0
-    for mine, got in ((mine_a, got_a), (mine_b, got_b)):
-        rows = mine.shape[0]
-        total[start : start + rows, :] = mine[...] + got[:rows, :].astype(F32)
-        start += rows
-    place, _ = places()
-    for k, out in enumerate(outs):
-        out[...] = total[block(place ^ k, out.shape[0]), :].astype(out.dtype)
-
-
-def add_kernel(own, one, two, three, *refs):
-    refs[-1][...] = (own[...] + one[...].astype(F32) + two[...].astype(F32) + three[...].astype(F32)).astype(BF16)
-
-
-def finish_kernel(scale, own, one, two, three, out):
+    for own, one, two, three in ((own_a, one_a, two_a, three_a), (own_b, one_b, two_b, three_b)):
+        rows = slice(start, start + own.shape[0])
+        total = own[...] + one[...].astype(F32) + two[...].astype(F32) + three[...].astype(F32)
+        out[rows, :] = total.astype(BF16)
+        start += own.shape[0]
+
+
+def finish_kernel(scale, own, one, two, three, _, out):
     near = own[...].astype(F32) + one[...].astype(F32)
     far = two[...].astype(F32) + three[...].astype(F32)
     out[...] = ((near + far) * scale).astype(BF16)
 
 
 def place_kernel(*refs):
-    kernel_out, lateral_out, sems = refs[8:]
+    results, sems = refs[8:10], refs[10]
     side = lax.axis_index("space")
-    edge, share = kernel_out.shape[0], refs[0].shape[0]
-    inside = edge - 3 * share
-    waits = []
+    copies = []
     for columns, quarters, place in zip((side, 1 - side), (refs[:4], refs[4:8]), places()):
         lanes = pl.ds(pl.multiple_of(columns * 128, 128), 128)
         for k, quarter in enumerate(quarters):
-            index = place ^ k
-            base = pl.multiple_of(index * share, 16)
-            head, tail = quarter.at[pl.ds(0, inside), :], quarter.at[pl.ds(inside, share - inside), :]
-            copy = pltpu.make_async_copy(head, kernel_out.at[pl.ds(base, inside), lanes], sems.at[len(waits)])
-            copy.start()
-            waits.append(copy)
-            sem = sems.at[len(waits)]
-
-            @pl.when(index < 3)
-            def _():
-                rows = pl.ds(base + inside, share - inside)
-                pltpu.make_async_copy(tail, kernel_out.at[rows, lanes], sem).start()
-
-            @pl.when(index == 3)
-            def _():
-                pltpu.make_async_copy(tail, lateral_out.at[:, lanes], sem).start()
-
-            waits.append(pltpu.make_async_copy(tail, lateral_out.at[:, lanes], sem))
-    for copy in waits:
+            start = 0
+            for result in results:
+                share = result.shape[0] // 4
+                to = result.at[block(place ^ k, share), lanes]
+                copies.append(pltpu.make_async_copy(quarter.at[pl.ds(start, share), :], to, sems.at[len(copies)]))
+                start += share
+    for copy in copies:
+        copy.start()
+    for copy in copies:
         copy.wait()
 
 
-def exchange(pieces, step):
-    came = {}
-    for k in (3, 2, 1):
-        pairs = []
-        for chip in range(16):
-            for core in range(2):
-                flip = k if core == step else 4 * k
-                pairs.append((2 * chip + core, 2 * (chip ^ flip) + core))
-        came[k] = lax.ppermute(pieces[k - 1], ("dp", "space"), pairs)
-    return [came[k] for k in (1, 2, 3)]
+def exchange(array, step, k):
+    pairs = []
+    for chip in range(16):
+        for core in range(2):
+            flip = k if core == step else 4 * k
+            pairs.append((2 * chip + core, 2 * (chip ^ flip) + core))
+    return lax.ppermute(array, ("dp", "space"), pairs)
 
 
 def swap(array):
@@ -232,22 +215,24 @@
     )
 
 
-def sum_everywhere(kernel_part, lateral_part, scale, after):
-    edge, width = kernel_part[0].shape
-    length = edge + lateral_part[0].shape[0]
-    quarter = (length // 4, width)
-    own, *pieces = call(
-        cut_kernel, (quarter, F32), *[(quarter, BF16)] * 3, scratch_shapes=[pltpu.VMEM((length, width), F32)]
-    )(*kernel_part, *lateral_part)
+def sum_everywhere(parts, scale, after):
+    lengths, width = [mine.shape[0] for mine, _ in parts], parts[0][0].shape[1]
     vmem, far = pl.BlockSpec(memory_space=pltpu.VMEM), pl.BlockSpec(memory_space=pltpu.HBM)
     after = pltpu.with_memory_space_constraint(after, pltpu.HBM)
-    [total] = call(add_kernel, (quarter, BF16), in_specs=[vmem] * 4 + [far])(own, *exchange(pieces, 0), after)
-    [total] = call(functools.partial(finish_kernel, scale), (quarter, BF16))(total, *exchange([total] * 3, 1))
-    quarters = [total, *exchange([total] * 3, 0)]
+    share_a, share_b, quarter = [(length // 4, width) for length in (*lengths, sum(lengths))]
+    own_a, *pieces = call(cut_kernel, (share_a, F32), *[(share_a, BF16)] * 3)(*parts[0])
+    three_a, two_a, one_a = [exchange(piece, 0, k) for piece, k in zip(pieces, (3, 2, 1))]
+    own_b, *pieces = call(cut_kernel, (share_b, F32), *[(share_b, BF16)] * 3)(*parts[1])
+    three_b, two_b, one_b = [exchange(piece, 0, k) for piece, k in zip(pieces, (3, 2, 1))]
+    [total] = call(add_kernel, (quarter, BF16))(own_a, own_b, three_a, two_a, one_a, one_b, two_b, three_b)
+    three, two, one = [exchange(total, 1, k) for k in (3, 2, 1)]
+    finish = call(functools.partial(finish_kernel, scale), (quarter, BF16), in_specs=[vmem] * 4 + [far])
+    [total] = finish(total, one, two, three, after)
+    three, two, one = [exchange(total, 0, k) for k in (3, 2, 1)]
+    quarters = [total, one, two, three]
     return call(
         place_kernel,
-        ((edge, 2 * width), BF16),
-        ((length - edge, 2 * width), BF16),
+        *[((length, 2 * width), BF16) for length in lengths],
         out_specs=[far] * 2,
         scratch_shapes=[pltpu.SemaphoreType.DMA((16,))],
     )(*quarters, *[swap(one) for one in quarters])
@@ -276,7 +261,7 @@
         cot_before, cot_after = neighbour_rows(cot)
         arrays = (cot, lateral_weight, top_down[image], features[image].reshape(cells, in_channels), taps)
         arrays = [pltpu.with_memory_space_constraint(array, pltpu.HBM) for array in arrays]
-        merged, merged_t, stack, feat_t, near_taps = pl.pallas_call(
+        merged, merged_t, stack, near_feat, near_taps = pl.pallas_call(
             merge_kernel,
             out_shape=[
                 jax.ShapeDtypeStruct(shape, BF16)
@@ -284,12 +269,12 @@
                     (cells, channels),
                     (channels, cells),
                     (rows, cols, 3 * channels),
-                    (in_channels, cells),
+                    (cells, in_channels),
                     taps.shape,
                 )
             ],
             in_specs=[pl.BlockSpec(memory_space=pltpu.HBM)] * 5,
-            scratch_shapes=[*[pltpu.VMEM(array.shape, BF16) for array in arrays[:4]], pltpu.SemaphoreType.DMA((5,))],
+            scratch_shapes=[*[pltpu.VMEM(array.shape, BF16) for array in arrays[:3]], pltpu.SemaphoreType.DMA((5,))],
             compiler_params=params,
             cost_estimate=pl.CostEstimate(
                 flops=2 * cells * channels * 4 * in_channels, bytes_accessed=4 * 2**20, transcendentals=0
@@ -305,41 +290,43 @@
         )(stack, merged, merged_t, cot_before, cot_after)
         if halves:
             kernel_part[1] = swap(kernel_part[1])
-        grad_top, *lateral_part = pl.pallas_call(
+        grad, *lateral_part = pl.pallas_call(
             data_grad_kernel,
-            out_shape=[jax.ShapeDtypeStruct((rows // 2, cols // 2, channels), BF16), *sums(in_channels, 0)],
+            out_shape=[jax.ShapeDtypeStruct((cells, channels), BF16), *sums(in_channels, 0)],
             compiler_params=params,
             cost_estimate=pl.CostEstimate(
                 flops=2 * cells * channels * (9 * channels + in_channels), bytes_accessed=4 * 2**20, transcendentals=0
             ),
-        )(stack, halo, feat_t, near_taps)
+        )(stack, halo, near_feat, near_taps)
         if halves:
             lateral_part[1] = swap(lateral_part[1])
         merged = merged.reshape(rows, cols, channels)
         edges = kernel_part[1:] if halves else neighbour_rows(merged)
-        outs.append(
-            pl.pallas_call(
-                functools.partial(forward_kernel, peers),
-                out_shape=jax.ShapeDtypeStruct((rows, cols, channels), BF16),
-                out_specs=pl.BlockSpec(memory_space=pltpu.HBM),
-                scratch_shapes=[
-                    pltpu.VMEM((rows + 2, cols, 3 * channels), BF16),
-                    pltpu.VMEM((rows, cols, channels), BF16),
-                    pltpu.SemaphoreType.DMA,
-                ],
-                compiler_params=params,
-                cost_estimate=pl.CostEstimate(
-                    flops=2 * cells * channels * 9 * channels, bytes_accessed=2 * 2**20, transcendentals=0
-                ),
-            )(merged, near_taps, *edges)
-        )
+        out, grad_top = pl.pallas_call(
+            functools.partial(forward_kernel, peers),
+            out_shape=[
+                jax.ShapeDtypeStruct((rows, cols, channels), BF16),
+                jax.ShapeDtypeStruct((rows // 2, cols // 2, channels), BF16),
+            ],
+            out_specs=[pl.BlockSpec(memory_space=pltpu.HBM), pl.BlockSpec(memory_space=pltpu.VMEM)],
+            scratch_shapes=[
+                pltpu.VMEM((rows + 2, cols, 3 * channels), BF16),
+                pltpu.VMEM((rows, cols, channels), BF16),
+                pltpu.SemaphoreType.DMA,
+            ],
+            compiler_params=params,
+            cost_estimate=pl.CostEstimate(
+                flops=2 * cells * channels * 9 * channels, bytes_accessed=2 * 2**20, transcendentals=0
+            ),
+        )(merged, near_taps, grad, *edges)
+        outs.append(out)
         tops.append(grad_top)
         if not halves:
             part = [kernel_part[0], lateral_part[0]]
             parts = part if parts is None else [a + b for a, b in zip(parts, part)]
     scale = 1.0 / (images * lax.axis_size("dp"))
     if halves:
-        grad_kernel, grad_lateral = sum_everywhere(kernel_part, lateral_part, scale, outs[0])
+        grad_kernel, grad_lateral = sum_everywhere((kernel_part, lateral_part), scale, outs[0])
     else:
         grad_kernel, grad_lateral = [(total * scale).astype(BF16) for total in lax.psum(parts, ("dp", "space"))]
     return jnp.stack(outs), jnp.stack(tops), grad_kernel.reshape(out_kernel.shape), grad_lateral

time: 44.1 us -> 50.7 us (1.15)
  starting transfers between devices: 14 us -> 18.3 us
  waiting for transfers between devices: 19.4 us -> 21.9 us
    ppermute x9 -> x12, starting transfers between devices: 12.5 us -> 17.2 us  [exchange(): return lax.ppermute(array, ('dp', 'space'), pairs)]
    ppermute x9 -> x12, waiting for transfers between devices: 17.3 us -> 20.5 us  [exchange(): return lax.ppermute(array, ('dp', 'space'), pairs)]
    ppermute x6, waiting for transfers between devices: 2.15 us -> 1.42 us  [swap(): return lax.ppermute(array, 'space', [(0, 1), (1, 0)])]
    pallas_call x6 -> x7, Pallas kernels: 5.96 us -> 5.77 us  [the longest x1 2.53 us: local(): pl.pallas_call(functools.partial(forward_kernel, peers), out_shape=[jax.S...]
  transfers between devices with their start and end apart: 16 -> 19, of which waited for: 10 -> 9; matrix products, arithmetic and copies ran while one was open for 0% -> 0% of each run, Pallas kernels for 14% -> 12%
where the time goes in v8:
time: 50.7 us; the launch traced here: 50.5 us
  waiting for transfers between devices  21.9 us (43%)
  starting transfers between devices  18.3 us (36%)
  Pallas kernels  8.76 us (17%)
  local copies, waits for them, and re-layouts  0.81 us (2%)
  between operations  0.73 us (1%)
    ppermute x12, waiting for transfers between devices, exchange(): return lax.ppermute(array, ('dp', 'space'), pairs)  20.5 us
    ppermute x12, starting transfers between devices, exchange(): return lax.ppermute(array, ('dp', 'space'), pairs)  17.2 us
    pallas_call x1, Pallas kernels, local(): pl.pallas_call(functools.partial(forward_kernel, peers), out_shape=[jax.S...  2.53 us
    pallas_call x1, Pallas kernels, local(): pl.pallas_call(merge_kernel, out_shape=[jax.ShapeDtypeStruct(shape, BF16)...  1.9 us
    pallas_call x1, Pallas kernels, local(): pl.pallas_call(data_grad_kernel, out_shape=[jax.ShapeDtypeStruct((cells,...  1.71 us
    ppermute x6, waiting for transfers between devices, swap(): return lax.ppermute(array, 'space', [(0, 1), (1, 0)])  1.42 us
    pallas_call x1, Pallas kernels, sum_everywhere(): call(place_kernel, *[((length, 2 * width), BF16) for length in lengths],...  1.22 us
    pallas_call x1, Pallas kernels, local(): pl.pallas_call(functools.partial(kernel_grad_kernel, peers), out_shape=[j...  1.09 us
  transfers between devices with their start and end apart: 19, of which 9 were waited for; matrix products, arithmetic and copies ran while one was open for 0% of the time, Pallas kernels for 12%

profile of v8, /device:TPU:0, one launch (start us, length us, event | category | flops | bytes accessed | tf_op | source)
XLA Modules:
  0.0 50.5 jit_solution(11995249949293081787)
XLA Ops:
  0.6 0.8 %dynamic-slice_bitcast_fusion = bf16[96,256]{1,0:T(8,128)(2,1)S(1)} fusion(bf16[1,8,96,256]{3,2,1,0:T(8,128)(2,1)} %param.9, s32[]{:T(128)S(6)} %select_n.4), kind=kLoop, calls=%fused_computation | loop fusion | bytes 98308 | tf_op jit(solution)/shard_map/jit(dynamic_index_in_dim)/squeeze | solution.py:21
  1.4 0.5 collective-permute-start
  1.9 1.9 %shard_map.84 = (bf16[768,256]{1,0:T(8,128)(2,1)S(1)}, bf16[256,768]{1,0:T(8,128)(2,1)S(1)}, bf16[8,96,768]{2,1,0:T(8,128)(2,1)S(1)}, bf16[768,512]{1,0:T(8,128)(2,1)S(1)}, bf16[9,256,256]{2,1,0:T(8,128)(2,1)S(1)}) custom-call(bf16[8,96,256]{2,1,0:T(8,128)(2,1)} %bitcast.12, bf16[512,256]{1,0:T(8,128)(2,1)} %refs_1_.1, bf16[4,48,256]{2,1,0:T(8,128)(2,1)} %bitcast.16, ...), custom_call_target="tpu_custom_call" | custom-call | flops 805306368 | bytes 4194304 | tf_op jit(solution)/shard_map/pallas_call | solution.py:264
  3.8 1.1 %shard_map.85 = (bf16[2,96,768]{2,1,0:T(8,128)(2,1)S(1)}, f32[2304,128]{1,0:T(8,128)S(1)}, bf16[2496,128]{1,0:T(8,128)(2,1)S(1)}) custom-call(bf16[8,96,768]{2,1,0:T(8,128)(2,1)S(1)} %get-tuple-element.29.stack, bf16[768,256]{1,0:T(8,128)(2,1)S(1)} %get-tuple-element.27.merged, bf16[256,768]{1,0:T(8,128)(2,1)S(1)} %get-tuple-element.30.merged_t, ...), custom_call_target="tpu_custom_call" | custom-call | flops 905969664 | bytes 4194304 | tf_op jit(solution)/shard_map/pallas_call | solution.py:283
  4.9 0.1 collective-permute-start.1
  5.0 1.7 %shard_map.86 = (bf16[768,256]{1,0:T(8,128)(2,1)S(1)}, f32[512,128]{1,0:T(8,128)S(1)}, bf16[512,128]{1,0:T(8,128)(2,1)S(1)}) custom-call(bf16[8,96,768]{2,1,0:T(8,128)(2,1)S(1)} %get-tuple-element.29.stack, bf16[2,96,768]{2,1,0:T(8,128)(2,1)S(1)} %get-tuple-element.31.halo, bf16[768,512]{1,0:T(8,128)(2,1)S(1)} %get-tuple-element.32.feat, ...), custom_call_target="tpu_custom_call" | custom-call | flops 1107296256 | bytes 4194304 | tf_op jit(solution)/shard_map/pallas_call | solution.py:293
  6.8 0.5 %collective-permute-start.2 = (bf16[512,128]{1,0:T(8,128)(2,1)S(1)}, bf16[512,128]{1,0:T(8,128)(2,1)S(1)}, u32[]{:S(2)}, u32[]{:S(2)}) collective-permute-start(bf16[512,128]{1,0:T(8,128)(2,1)S(1)} %get-tuple-element.40), channel_id=1, source_target_pairs={{0,1},{1,0},{2,3},{3,2},{4,5},{5,4},{6,7},{7,6},{8,9},{9,8},{10,11... | collective-permute-start | bytes 393224 | tf_op jit(solution)/shard_map/ppermute | solution.py:206
  7.3 0.1 shard_map.88
  7.4 3.5 %collective-permute-start.3 = (bf16[576,128]{1,0:T(8,128)(2,1)S(1)}, bf16[576,128]{1,0:T(8,128)(2,1)S(1)}, u32[]{:S(2)}, u32[]{:S(2)}) collective-permute-start(bf16[576,128]{1,0:T(8,128)(2,1)S(1)} %get-tuple-element.42), channel_id=1, source_target_pairs={{0,6},{1,25},{2,4},{3,27},{4,2},{5,29},{6,0},{7,31},{8,14},{9,17},... | collective-permute-start | bytes 442376 | tf_op jit(solution)/shard_map/ppermute | solution.py:202
  10.9 0.5 %collective-permute-start.4 = (bf16[576,128]{1,0:T(8,128)(2,1)S(1)}, bf16[576,128]{1,0:T(8,128)(2,1)S(1)}, u32[]{:S(2)}, u32[]{:S(2)}) collective-permute-start(bf16[576,128]{1,0:T(8,128)(2,1)S(1)} %get-tuple-element.43), channel_id=1, source_target_pairs={{0,4},{1,17},{2,6},{3,19},{4,0},{5,21},{6,2},{7,23},{8,12},{9,25},... | collective-permute-start | bytes 442376 | tf_op jit(solution)/shard_map/ppermute | solution.py:202
  11.4 0.1 collective-permute-start.5
  11.6 2.0 %collective-permute-start.6 = (bf16[128,128]{1,0:T(8,128)(2,1)S(1)}, bf16[128,128]{1,0:T(8,128)(2,1)S(1)}, u32[]{:S(2)}, u32[]{:S(2)}) collective-permute-start(bf16[128,128]{1,0:T(8,128)(2,1)S(1)} %get-tuple-element.45), channel_id=1, source_target_pairs={{0,2},{1,9},{2,0},{3,11},{4,6},{5,13},{6,4},{7,15},{8,10},{9,1},{1... | collective-permute-start | bytes 98312 | tf_op jit(solution)/shard_map/ppermute | solution.py:202
  13.6 1.5 %collective-permute-start.7 = (bf16[128,128]{1,0:T(8,128)(2,1)S(1)}, bf16[128,128]{1,0:T(8,128)(2,1)S(1)}, u32[]{:S(2)}, u32[]{:S(2)}) collective-permute-start(bf16[128,128]{1,0:T(8,128)(2,1)S(1)} %get-tuple-element.46), channel_id=1, source_target_pairs={{0,4},{1,17},{2,6},{3,19},{4,0},{5,21},{6,2},{7,23},{8,12},{9,25},... | collective-permute-start | bytes 98312 | tf_op jit(solution)/shard_map/ppermute | solution.py:202
  15.1 1.9 %collective-permute-done.6.one_b = bf16[128,128]{1,0:T(8,128)(2,1)S(1)} collective-permute-done((bf16[128,128]{1,0:T(8,128)(2,1)S(1)}, bf16[128,128]{1,0:T(8,128)(2,1)S(1)}, u32[]{:S(2)}, u32[]{:S(2)}) %collective-permute-start.6) | collective-permute-done | bytes 32800 | tf_op jit(solution)/shard_map/ppermute | solution.py:202
  16.9 1.5 %collective-permute-start.8 = (bf16[128,128]{1,0:T(8,128)(2,1)S(1)}, bf16[128,128]{1,0:T(8,128)(2,1)S(1)}, u32[]{:S(2)}, u32[]{:S(2)}) collective-permute-start(bf16[128,128]{1,0:T(8,128)(2,1)S(1)} %get-tuple-element.47), channel_id=1, source_target_pairs={{0,6},{1,25},{2,4},{3,27},{4,2},{5,29},{6,0},{7,31},{8,14},{9,17},... | collective-permute-start | bytes 98312 | tf_op jit(solution)/shard_map/ppermute | solution.py:202
  18.4 3.3 %collective-permute-done.8.three_b = bf16[128,128]{1,0:T(8,128)(2,1)S(1)} collective-permute-done((bf16[128,128]{1,0:T(8,128)(2,1)S(1)}, bf16[128,128]{1,0:T(8,128)(2,1)S(1)}, u32[]{:S(2)}, u32[]{:S(2)}) %collective-permute-start.8) | collective-permute-done | bytes 32800 | tf_op jit(solution)/shard_map/ppermute | solution.py:202
  21.8 0.1 shard_map.90.own
  21.8 3.7 %collective-permute-start.11 = (bf16[704,128]{1,0:T(8,128)(2,1)S(1)}, bf16[704,128]{1,0:T(8,128)(2,1)S(1)}, u32[]{:S(2)}, u32[]{:S(2)}) collective-permute-start(bf16[704,128]{1,0:T(8,128)(2,1)S(1)} %shard_map.90.own), channel_id=1, source_target_pairs={{0,24},{1,7},{2,26},{3,5},{4,28},{5,3},{6,30},{7,1},{8,16},{9,15},... | collective-permute-start | bytes 540680 | tf_op jit(solution)/shard_map/ppermute | solution.py:202
  25.5 0.8 %collective-permute-start.9 = (bf16[704,128]{1,0:T(8,128)(2,1)S(1)}, bf16[704,128]{1,0:T(8,128)(2,1)S(1)}, u32[]{:S(2)}, u32[]{:S(2)}) collective-permute-start(bf16[704,128]{1,0:T(8,128)(2,1)S(1)} %shard_map.90.own), channel_id=1, source_target_pairs={{0,8},{1,3},{2,10},{3,1},{4,12},{5,7},{6,14},{7,5},{8,0},{9,11},{1... | collective-permute-start | bytes 540680 | tf_op jit(solution)/shard_map/ppermute | solution.py:202
  26.3 2.5 %shard_map.87 = (bf16[8,96,256]{2,1,0:T(8,128)(2,1)}, bf16[4,48,256]{2,1,0:T(8,128)(2,1)}) custom-call(bf16[8,96,256]{2,1,0:T(8,128)(2,1)S(1)} %bitcast.10, bf16[9,256,256]{2,1,0:T(8,128)(2,1)S(1)} %get-tuple-element.28.out_w, bf16[768,256]{1,0:T(8,128)(2,1)S(1)} %get-tuple-element.33.grad, bf16[2496,128]{1,0:T(8,128)(2,1)S(1)} %collective-permute-done.1.refs_0_.got), custom_call_target="tpu_custom_call" | custom-call | flops 905969664 | bytes 2097152 | tf_op jit(solution)/shard_map/pallas_call | solution.py:305
  28.8 0.5 collective-permute-done.11.three
  29.3 9.8 %collective-permute-done.10.two = bf16[704,128]{1,0:T(8,128)(2,1)S(1)} collective-permute-done((bf16[704,128]{1,0:T(8,128)(2,1)S(1)}, bf16[704,128]{1,0:T(8,128)(2,1)S(1)}, u32[]{:S(2)}, u32[]{:S(2)}) %collective-permute-start.10) | collective-permute-done | bytes 180256 | tf_op jit(solution)/shard_map/ppermute | solution.py:202
  39.1 0.1 shard_map.91.refs_0_
  39.3 0.1 collective-permute-start.14
  39.3 1.7 %collective-permute-start.13 = (bf16[704,128]{1,0:T(8,128)(2,1)S(1)}, bf16[704,128]{1,0:T(8,128)(2,1)S(1)}, u32[]{:S(2)}, u32[]{:S(2)}) collective-permute-start(bf16[704,128]{1,0:T(8,128)(2,1)S(1)} %shard_map.91.refs_0_), channel_id=1, source_target_pairs={{0,4},{1,17},{2,6},{3,19},{4,0},{5,21},{6,2},{7,23},{8,12},{9,25},... | collective-permute-start | bytes 540680 | tf_op jit(solution)/shard_map/ppermute | solution.py:202
  41.0 1.8 %collective-permute-start.12 = (bf16[704,128]{1,0:T(8,128)(2,1)S(1)}, bf16[704,128]{1,0:T(8,128)(2,1)S(1)}, u32[]{:S(2)}, u32[]{:S(2)}) collective-permute-start(bf16[704,128]{1,0:T(8,128)(2,1)S(1)} %shard_map.91.refs_0_), channel_id=1, source_target_pairs={{0,2},{1,9},{2,0},{3,11},{4,6},{5,13},{6,4},{7,15},{8,10},{9,1},{1... | collective-permute-start | bytes 540680 | tf_op jit(solution)/shard_map/ppermute | solution.py:202
  42.8 3.0 %collective-permute-done.14.refs_3_ = bf16[704,128]{1,0:T(8,128)(2,1)S(1)} collective-permute-done((bf16[704,128]{1,0:T(8,128)(2,1)S(1)}, bf16[704,128]{1,0:T(8,128)(2,1)S(1)}, u32[]{:S(2)}, u32[]{:S(2)}) %collective-permute-start.14) | collective-permute-done | bytes 180256 | tf_op jit(solution)/shard_map/ppermute | solution.py:202
  45.8 1.0 %collective-permute-done.13.refs_2_ = bf16[704,128]{1,0:T(8,128)(2,1)S(1)} collective-permute-done((bf16[704,128]{1,0:T(8,128)(2,1)S(1)}, bf16[704,128]{1,0:T(8,128)(2,1)S(1)}, u32[]{:S(2)}, u32[]{:S(2)}) %collective-permute-start.13) | collective-permute-done | bytes 180256 | tf_op jit(solution)/shard_map/ppermute | solution.py:202
  46.8 1.0 %collective-permute-done.12.refs_1_ = bf16[704,128]{1,0:T(8,128)(2,1)S(1)} collective-permute-done((bf16[704,128]{1,0:T(8,128)(2,1)S(1)}, bf16[704,128]{1,0:T(8,128)(2,1)S(1)}, u32[]{:S(2)}, u32[]{:S(2)}) %collective-permute-start.12) | collective-permute-done | bytes 180256 | tf_op jit(solution)/shard_map/ppermute | solution.py:202
  47.8 0.4 collective-permute-done.17.refs_6_
  48.2 1.0 %collective-permute-done.16.refs_5_ = bf16[704,128]{1,0:T(8,128)(2,1)S(1)} collective-permute-done((bf16[704,128]{1,0:T(8,128)(2,1)S(1)}, bf16[704,128]{1,0:T(8,128)(2,1)S(1)}, u32[]{:S(2)}, u32[]{:S(2)}) %collective-permute-start.16) | collective-permute-done | bytes 180256 | tf_op jit(solution)/shard_map/ppermute | solution.py:206
  49.2 1.2 %shard_map.92 = (bf16[2304,256]{1,0:T(8,128)(2,1)}, bf16[512,256]{1,0:T(8,128)(2,1)}) custom-call(bf16[704,128]{1,0:T(8,128)(2,1)S(1)} %shard_map.91.refs_0_, bf16[704,128]{1,0:T(8,128)(2,1)S(1)} %collective-permute-done.12.refs_1_, bf16[704,128]{1,0:T(8,128)(2,1)S(1)} %collective-permute-done.13.refs_2_, ...), custom_call_target="tpu_custom_call" | custom-call | tf_op jit(solution)/shard_map/pallas_call | solution.py:233
  (16 shorter events, 0.1 us)
Async XLA Ops:
  1.4 2.4 %collective-permute-start = (bf16[96,256]{1,0:T(8,128)(2,1)S(1)}, bf16[96,256]{1,0:T(8,128)(2,1)S(1)}, u32[]{:S(2)}, u32[]{:S(2)}) collective-permute-start(bf16[96,256]{1,0:T(8,128)(2,1)S(1)} %dynamic-slice_bitcast_fusion), channel_id=1, source_target_pairs={{0,1},{1,0},{2,3},{3,2},{4,5},{5,4},{6,7},{7,6},{8,9},{9,8},{10,11... | collective-permute-start | bytes 147464 | tf_op jit(solution)/shard_map/ppermute | solution.py:22
  4.9 2.4 %collective-permute-start.1 = (bf16[2496,128]{1,0:T(8,128)(2,1)S(1)}, bf16[2496,128]{1,0:T(8,128)(2,1)S(1)}, u32[]{:S(2)}, u32[]{:S(2)}) collective-permute-start(bf16[2496,128]{1,0:T(8,128)(2,1)S(1)} %get-tuple-element.34), channel_id=1, source_target_pairs={{0,1},{1,0},{2,3},{3,2},{4,5},{5,4},{6,7},{7,6},{8,9},{9,8},{10,11... | collective-permute-start | bytes 1916936 | tf_op jit(solution)/shard_map/ppermute | solution.py:206
  6.8 4.8 %collective-permute-start.2 = (bf16[512,128]{1,0:T(8,128)(2,1)S(1)}, bf16[512,128]{1,0:T(8,128)(2,1)S(1)}, u32[]{:S(2)}, u32[]{:S(2)}) collective-permute-start(bf16[512,128]{1,0:T(8,128)(2,1)S(1)} %get-tuple-element.40), channel_id=1, source_target_pairs={{0,1},{1,0},{2,3},{3,2},{4,5},{5,4},{6,7},{7,6},{8,9},{9,8},{10,11... | collective-permute-start | bytes 393224 | tf_op jit(solution)/shard_map/ppermute | solution.py:206
  7.4 14.4 %collective-permute-start.3 = (bf16[576,128]{1,0:T(8,128)(2,1)S(1)}, bf16[576,128]{1,0:T(8,128)(2,1)S(1)}, u32[]{:S(2)}, u32[]{:S(2)}) collective-permute-start(bf16[576,128]{1,0:T(8,128)(2,1)S(1)} %get-tuple-element.42), channel_id=1, source_target_pairs={{0,6},{1,25},{2,4},{3,27},{4,2},{5,29},{6,0},{7,31},{8,14},{9,17},... | collective-permute-start | bytes 442376 | tf_op jit(solution)/shard_map/ppermute | solution.py:202
  10.9 10.8 %collective-permute-start.4 = (bf16[576,128]{1,0:T(8,128)(2,1)S(1)}, bf16[576,128]{1,0:T(8,128)(2,1)S(1)}, u32[]{:S(2)}, u32[]{:S(2)}) collective-permute-start(bf16[576,128]{1,0:T(8,128)(2,1)S(1)} %get-tuple-element.43), channel_id=1, source_target_pairs={{0,4},{1,17},{2,6},{3,19},{4,0},{5,21},{6,2},{7,23},{8,12},{9,25},... | collective-permute-start | bytes 442376 | tf_op jit(solution)/shard_map/ppermute | solution.py:202
  11.4 10.3 %collective-permute-start.5 = (bf16[576,128]{1,0:T(8,128)(2,1)S(1)}, bf16[576,128]{1,0:T(8,128)(2,1)S(1)}, u32[]{:S(2)}, u32[]{:S(2)}) collective-permute-start(bf16[576,128]{1,0:T(8,128)(2,1)S(1)} %get-tuple-element.44), channel_id=1, source_target_pairs={{0,2},{1,9},{2,0},{3,11},{4,6},{5,13},{6,4},{7,15},{8,10},{9,1},{1... | collective-permute-start | bytes 442376 | tf_op jit(solution)/shard_map/ppermute | solution.py:202
  11.6 5.3 %collective-permute-start.6 = (bf16[128,128]{1,0:T(8,128)(2,1)S(1)}, bf16[128,128]{1,0:T(8,128)(2,1)S(1)}, u32[]{:S(2)}, u32[]{:S(2)}) collective-permute-start(bf16[128,128]{1,0:T(8,128)(2,1)S(1)} %get-tuple-element.45), channel_id=1, source_target_pairs={{0,2},{1,9},{2,0},{3,11},{4,6},{5,13},{6,4},{7,15},{8,10},{9,1},{1... | collective-permute-start | bytes 98312 | tf_op jit(solution)/shard_map/ppermute | solution.py:202
  13.6 4.9 %collective-permute-start.7 = (bf16[128,128]{1,0:T(8,128)(2,1)S(1)}, bf16[128,128]{1,0:T(8,128)(2,1)S(1)}, u32[]{:S(2)}, u32[]{:S(2)}) collective-permute-start(bf16[128,128]{1,0:T(8,128)(2,1)S(1)} %get-tuple-element.46), channel_id=1, source_target_pairs={{0,4},{1,17},{2,6},{3,19},{4,0},{5,21},{6,2},{7,23},{8,12},{9,25},... | collective-permute-start | bytes 98312 | tf_op jit(solution)/shard_map/ppermute | solution.py:202
  16.9 4.8 %collective-permute-start.8 = (bf16[128,128]{1,0:T(8,128)(2,1)S(1)}, bf16[128,128]{1,0:T(8,128)(2,1)S(1)}, u32[]{:S(2)}, u32[]{:S(2)}) collective-permute-start(bf16[128,128]{1,0:T(8,128)(2,1)S(1)} %get-tuple-element.47), channel_id=1, source_target_pairs={{0,6},{1,25},{2,4},{3,27},{4,2},{5,29},{6,0},{7,31},{8,14},{9,17},... | collective-permute-start | bytes 98312 | tf_op jit(solution)/shard_map/ppermute | solution.py:202
  21.8 7.5 %collective-permute-start.11 = (bf16[704,128]{1,0:T(8,128)(2,1)S(1)}, bf16[704,128]{1,0:T(8,128)(2,1)S(1)}, u32[]{:S(2)}, u32[]{:S(2)}) collective-permute-start(bf16[704,128]{1,0:T(8,128)(2,1)S(1)} %shard_map.90.own), channel_id=1, source_target_pairs={{0,24},{1,7},{2,26},{3,5},{4,28},{5,3},{6,30},{7,1},{8,16},{9,15},... | collective-permute-start | bytes 540680 | tf_op jit(solution)/shard_map/ppermute | solution.py:202
  25.5 13.6 %collective-permute-start.10 = (bf16[704,128]{1,0:T(8,128)(2,1)S(1)}, bf16[704,128]{1,0:T(8,128)(2,1)S(1)}, u32[]{:S(2)}, u32[]{:S(2)}) collective-permute-start(bf16[704,128]{1,0:T(8,128)(2,1)S(1)} %shard_map.90.own), channel_id=1, source_target_pairs={{0,16},{1,5},{2,18},{3,7},{4,20},{5,1},{6,22},{7,3},{8,24},{9,13},... | collective-permute-start | bytes 540680 | tf_op jit(solution)/shard_map/ppermute | solution.py:202
  25.5 13.6 %collective-permute-start.9 = (bf16[704,128]{1,0:T(8,128)(2,1)S(1)}, bf16[704,128]{1,0:T(8,128)(2,1)S(1)}, u32[]{:S(2)}, u32[]{:S(2)}) collective-permute-start(bf16[704,128]{1,0:T(8,128)(2,1)S(1)} %shard_map.90.own), channel_id=1, source_target_pairs={{0,8},{1,3},{2,10},{3,1},{4,12},{5,7},{6,14},{7,5},{8,0},{9,11},{1... | collective-permute-start | bytes 540680 | tf_op jit(solution)/shard_map/ppermute | solution.py:202
  39.3 6.6 %collective-permute-start.14 = (bf16[704,128]{1,0:T(8,128)(2,1)S(1)}, bf16[704,128]{1,0:T(8,128)(2,1)S(1)}, u32[]{:S(2)}, u32[]{:S(2)}) collective-permute-start(bf16[704,128]{1,0:T(8,128)(2,1)S(1)} %shard_map.91.refs_0_), channel_id=1, source_target_pairs={{0,6},{1,25},{2,4},{3,27},{4,2},{5,29},{6,0},{7,31},{8,14},{9,17},... | collective-permute-start | bytes 540680 | tf_op jit(solution)/shard_map/ppermute | solution.py:202
  39.3 7.5 %collective-permute-start.13 = (bf16[704,128]{1,0:T(8,128)(2,1)S(1)}, bf16[704,128]{1,0:T(8,128)(2,1)S(1)}, u32[]{:S(2)}, u32[]{:S(2)}) collective-permute-start(bf16[704,128]{1,0:T(8,128)(2,1)S(1)} %shard_map.91.refs_0_), channel_id=1, source_target_pairs={{0,4},{1,17},{2,6},{3,19},{4,0},{5,21},{6,2},{7,23},{8,12},{9,25},... | collective-permute-start | bytes 540680 | tf_op jit(solution)/shard_map/ppermute | solution.py:202
  41.0 6.8 %collective-permute-start.12 = (bf16[704,128]{1,0:T(8,128)(2,1)S(1)}, bf16[704,128]{1,0:T(8,128)(2,1)S(1)}, u32[]{:S(2)}, u32[]{:S(2)}) collective-permute-start(bf16[704,128]{1,0:T(8,128)(2,1)S(1)} %shard_map.91.refs_0_), channel_id=1, source_target_pairs={{0,2},{1,9},{2,0},{3,11},{4,6},{5,13},{6,4},{7,15},{8,10},{9,1},{1... | collective-permute-start | bytes 540680 | tf_op jit(solution)/shard_map/ppermute | solution.py:202
  42.8 5.0 %collective-permute-start.15 = (bf16[704,128]{1,0:T(8,128)(2,1)S(1)}, bf16[704,128]{1,0:T(8,128)(2,1)S(1)}, u32[]{:S(2)}, u32[]{:S(2)}) collective-permute-start(bf16[704,128]{1,0:T(8,128)(2,1)S(1)} %shard_map.91.refs_0_), channel_id=1, source_target_pairs={{0,1},{1,0},{2,3},{3,2},{4,5},{5,4},{6,7},{7,6},{8,9},{9,8},{10,11... | collective-permute-start | bytes 540680 | tf_op jit(solution)/shard_map/ppermute | solution.py:206
  45.8 2.0 %collective-permute-start.18 = (bf16[704,128]{1,0:T(8,128)(2,1)S(1)}, bf16[704,128]{1,0:T(8,128)(2,1)S(1)}, u32[]{:S(2)}, u32[]{:S(2)}) collective-permute-start(bf16[704,128]{1,0:T(8,128)(2,1)S(1)} %collective-permute-done.14.refs_3_), channel_id=1, source_target_pairs={{0,1},{1,0},{2,3},{3,2},{4,5},{5,4},{6,7},{7,6},{8,9},{9,8},{10,11... | collective-permute-start | bytes 540680 | tf_op jit(solution)/shard_map/ppermute | solution.py:206
  46.8 1.4 %collective-permute-start.17 = (bf16[704,128]{1,0:T(8,128)(2,1)S(1)}, bf16[704,128]{1,0:T(8,128)(2,1)S(1)}, u32[]{:S(2)}, u32[]{:S(2)}) collective-permute-start(bf16[704,128]{1,0:T(8,128)(2,1)S(1)} %collective-permute-done.13.refs_2_), channel_id=1, source_target_pairs={{0,1},{1,0},{2,3},{3,2},{4,5},{5,4},{6,7},{7,6},{8,9},{9,8},{10,11... | collective-permute-start | bytes 540680 | tf_op jit(solution)/shard_map/ppermute | solution.py:206
  47.8 1.4 %collective-permute-start.16 = (bf16[704,128]{1,0:T(8,128)(2,1)S(1)}, bf16[704,128]{1,0:T(8,128)(2,1)S(1)}, u32[]{:S(2)}, u32[]{:S(2)}) collective-permute-start(bf16[704,128]{1,0:T(8,128)(2,1)S(1)} %collective-permute-done.12.refs_1_), channel_id=1, source_target_pairs={{0,1},{1,0},{2,3},{3,2},{4,5},{5,4},{6,7},{7,6},{8,9},{9,8},{10,11... | collective-permute-start | bytes 540680 | tf_op jit(solution)/shard_map/ppermute | solution.py:206

commit v9 on v8

--- a/solution.py
+++ b/solution.py
@@ -13,17 +13,14 @@
 
 def neighbour_rows(array):
     peers = lax.axis_size("space")
-    rows = array.shape[0]
     if peers == 1:
-        return array[0], array[0]
+        return array[-1:], array[:1]
     if peers == 2:
-        here = lax.axis_index("space")
-        edge = lax.dynamic_index_in_dim(array, (1 - here) * (rows - 1), 0, keepdims=False)
-        got = lax.ppermute(edge, "space", [(0, 1), (1, 0)])
+        got = lax.ppermute(array, "space", [(0, 1), (1, 0)])
         return got, got
     up = [(i, i + 1) for i in range(peers - 1)]
     down = [(j, i) for i, j in up]
-    return lax.ppermute(array[-1], "space", up), lax.ppermute(array[0], "space", down)
+    return lax.ppermute(array[-1:], "space", up), lax.ppermute(array[:1], "space", down)
 
 
 def put_shifted(stack, slot, row, sign):
@@ -95,7 +92,7 @@
 def kernel_grad_kernel(peers, stack, merged, merged_t, before, after, halo, *outs):
     cols = stack.shape[1]
     channels, cells = merged_t.shape
-    put_halo(halo, before[...], after[...], 0, peers, 1)
+    put_halo(halo, before[before.shape[0] - 1], after[0], 0, peers, 1)
     if len(outs) == 2:
         here = lax.axis_index("space")
         edge = jnp.where(here == 0, merged[cells - cols :, :], merged[:cols, :])
@@ -127,7 +124,7 @@
         edge = jnp.concatenate([edges[0][start : start + cols, :], edges[0][start + cols :, :]], axis=1)
         put_halo(stack, edge, edge, rows, peers, -1)
     else:
-        put_halo(stack, edges[0][...], edges[1][...], rows, peers, -1)
+        put_halo(stack, edges[0][edges[0].shape[0] - 1], edges[1][0], rows, peers, -1)
     cells = jnp.concatenate([stack[i : i + rows].reshape(rows * cols, 3 * channels) for i in range(3)], axis=1)
     total = jnp.dot(cells, out_w[...].reshape(9 * channels, channels), preferred_element_type=F32)
     near[...] = total.astype(BF16).reshape(out.shape)
@@ -154,18 +151,24 @@
 
 def cut_kernel(mine, got, *refs):
     place, _ = places()
-    for k, out in zip((0, 3, 2, 1), refs):
-        rows = block(place ^ k, out.shape[0])
-        out[...] = (mine[rows, :] + got[rows, :].astype(F32)).astype(out.dtype)
-
-
-def add_kernel(own_a, own_b, three_a, two_a, one_a, one_b, two_b, three_b, out):
-    start = 0
-    for own, one, two, three in ((own_a, one_a, two_a, three_a), (own_b, one_b, two_b, three_b)):
-        rows = slice(start, start + own.shape[0])
-        total = own[...] + one[...].astype(F32) + two[...].astype(F32) + three[...].astype(F32)
-        out[rows, :] = total.astype(BF16)
-        start += own.shape[0]
+    share = mine.shape[0] // 4
+    for k, out in zip((0, 3, 2, 1), refs[-4:]):
+        rows = block(place ^ k, share)
+        start = out.shape[0] - share
+        if start:
+            out[:start, :] = refs[0][...]
+        out[start:, :] = (mine[rows, :] + got[rows, :].astype(F32)).astype(out.dtype)
+
+
+def add_early_kernel(own, three, two, out):
+    out[...] = own[...] + three[...].astype(F32) + two[...].astype(F32)
+
+
+def add_kernel(part_a, own_b, one, three_b, two_b, out):
+    edge = part_a.shape[0]
+    out[:edge, :] = (part_a[...] + one[:edge, :].astype(F32)).astype(BF16)
+    total = own_b[...] + one[edge:, :].astype(F32) + two_b[...].astype(F32) + three_b[...].astype(F32)
+    out[edge:, :] = total.astype(BF16)
 
 
 def finish_kernel(scale, own, one, two, three, _, out):
@@ -220,11 +223,13 @@
     vmem, far = pl.BlockSpec(memory_space=pltpu.VMEM), pl.BlockSpec(memory_space=pltpu.HBM)
     after = pltpu.with_memory_space_constraint(after, pltpu.HBM)
     share_a, share_b, quarter = [(length // 4, width) for length in (*lengths, sum(lengths))]
-    own_a, *pieces = call(cut_kernel, (share_a, F32), *[(share_a, BF16)] * 3)(*parts[0])
-    three_a, two_a, one_a = [exchange(piece, 0, k) for piece, k in zip(pieces, (3, 2, 1))]
-    own_b, *pieces = call(cut_kernel, (share_b, F32), *[(share_b, BF16)] * 3)(*parts[1])
-    three_b, two_b, one_b = [exchange(piece, 0, k) for piece, k in zip(pieces, (3, 2, 1))]
-    [total] = call(add_kernel, (quarter, BF16))(own_a, own_b, three_a, two_a, one_a, one_b, two_b, three_b)
+    own_a, three, two, one_a = call(cut_kernel, (share_a, F32), *[(share_a, BF16)] * 3)(*parts[0])
+    three, two = exchange(three, 0, 3), exchange(two, 0, 2)
+    slow = pl.CostEstimate(flops=3 * 2**28, bytes_accessed=2**10, transcendentals=0)
+    [part_a] = call(add_early_kernel, (share_a, F32), cost_estimate=slow)(own_a, three, two)
+    own_b, three, two, one = call(cut_kernel, (share_b, F32), *[(share_b, BF16)] * 2, (quarter, BF16))(*parts[1], one_a)
+    one, three, two = exchange(one, 0, 1), exchange(three, 0, 3), exchange(two, 0, 2)
+    [total] = call(add_kernel, (quarter, BF16))(part_a, own_b, one, three, two)
     three, two, one = [exchange(total, 1, k) for k in (3, 2, 1)]
     finish = call(functools.partial(finish_kernel, scale), (quarter, BF16), in_specs=[vmem] * 4 + [far])
     [total] = finish(total, one, two, three, after)

time: 50.7 us -> 41.7 us (0.82)
  waiting for transfers between devices: 21.9 us -> 14.8 us
  starting transfers between devices: 18.3 us -> 17.3 us
  local copies, waits for them, and re-layouts: 0.81 us -> 0 us
    ppermute x12 -> x11, waiting for transfers between devices: 20.5 us -> 13.6 us  [exchange(): return lax.ppermute(array, ('dp', 'space'), pairs)]
    ppermute x12 -> x11, starting transfers between devices: 17.2 us -> 15.6 us  [exchange(): return lax.ppermute(array, ('dp', 'space'), pairs)]
    squeeze x1 -> x0, local copies, waits for them, and re-layouts: 0.81 us -> none  [neighbour_rows(): lax.dynamic_index_in_dim(array, (1 - here) * (rows - 1), 0, keepdims=False)]
    ppermute x6, starting transfers between devices: 0.65 us -> 1.17 us  [swap(): return lax.ppermute(array, 'space', [(0, 1), (1, 0)])]
  transfers between devices with their start and end apart: 19 -> 18, of which waited for: 9 -> 9; matrix products, arithmetic and copies ran while one was open for 0% -> 0% of each run, Pallas kernels for 12% -> 15%
where the time goes in v9:
time: 41.7 us; the launch traced here: 41.6 us
  starting transfers between devices  17.3 us (41%)
  waiting for transfers between devices  14.8 us (35%)
  Pallas kernels  8.77 us (21%)
  between operations  0.71 us (2%)
    ppermute x11, starting transfers between devices, exchange(): return lax.ppermute(array, ('dp', 'space'), pairs)  15.6 us
    ppermute x11, waiting for transfers between devices, exchange(): return lax.ppermute(array, ('dp', 'space'), pairs)  13.6 us
    pallas_call x1, Pallas kernels, local(): pl.pallas_call(functools.partial(forward_kernel, peers), out_shape=[jax.S...  2.53 us
    pallas_call x1, Pallas kernels, local(): pl.pallas_call(merge_kernel, out_shape=[jax.ShapeDtypeStruct(shape, BF16)...  1.9 us
    pallas_call x1, Pallas kernels, local(): pl.pallas_call(data_grad_kernel, out_shape=[jax.ShapeDtypeStruct((cells,...  1.7 us
    pallas_call x1, Pallas kernels, sum_everywhere(): call(place_kernel, *[((length, 2 * width), BF16) for length in lengths],...  1.22 us
    ppermute x6, starting transfers between devices, swap(): return lax.ppermute(array, 'space', [(0, 1), (1, 0)])  1.17 us
    ppermute x6, waiting for transfers between devices, swap(): return lax.ppermute(array, 'space', [(0, 1), (1, 0)])  1.17 us
  transfers between devices with their start and end apart: 18, of which 9 were waited for; matrix products, arithmetic and copies ran while one was open for 0% of the time, Pallas kernels for 15%

profile of v9, /device:TPU:0, one launch (start us, length us, event | category | flops | bytes accessed | tf_op | source)
XLA Modules:
  0.0 41.6 jit_solution(10013354486431767452)
XLA Ops:
  0.6 0.5 %collective-permute-start = (bf16[8,96,256]{2,1,0:T(8,128)(2,1)}, bf16[8,96,256]{2,1,0:T(8,128)(2,1)S(1)}, u32[]{:S(2)}, u32[]{:S(2)}) collective-permute-start(bf16[8,96,256]{2,1,0:T(8,128)(2,1)} %bitcast.13), channel_id=1, source_target_pairs={{0,1},{1,0},{2,3},{3,2},{4,5},{5,4},{6,7},{7,6},{8,9},{9,8},{10,11... | collective-permute-start | bytes 1179656 | tf_op jit(solution)/shard_map/ppermute | solution.py:19
  1.1 1.9 %shard_map.84 = (bf16[768,256]{1,0:T(8,128)(2,1)S(1)}, bf16[256,768]{1,0:T(8,128)(2,1)S(1)}, bf16[8,96,768]{2,1,0:T(8,128)(2,1)S(1)}, bf16[768,512]{1,0:T(8,128)(2,1)S(1)}, bf16[9,256,256]{2,1,0:T(8,128)(2,1)S(1)}) custom-call(bf16[8,96,256]{2,1,0:T(8,128)(2,1)} %bitcast.14, bf16[512,256]{1,0:T(8,128)(2,1)} %refs_1_.1, bf16[4,48,256]{2,1,0:T(8,128)(2,1)} %bitcast.15, ...), custom_call_target="tpu_custom_call" | custom-call | flops 805306368 | bytes 4194304 | tf_op jit(solution)/shard_map/pallas_call | solution.py:269
  3.1 1.1 %shard_map.85 = (bf16[2,96,768]{2,1,0:T(8,128)(2,1)S(1)}, f32[2304,128]{1,0:T(8,128)S(1)}, bf16[2496,128]{1,0:T(8,128)(2,1)S(1)}) custom-call(bf16[8,96,768]{2,1,0:T(8,128)(2,1)S(1)} %get-tuple-element.29.stack, bf16[768,256]{1,0:T(8,128)(2,1)S(1)} %get-tuple-element.27.merged, bf16[256,768]{1,0:T(8,128)(2,1)S(1)} %get-tuple-element.30.merged_t, ...), custom_call_target="tpu_custom_call" | custom-call | flops 905969664 | bytes 4194304 | tf_op jit(solution)/shard_map/pallas_call | solution.py:288
  4.2 0.1 collective-permute-start.1
  4.3 1.7 %shard_map.86 = (bf16[768,256]{1,0:T(8,128)(2,1)S(1)}, f32[512,128]{1,0:T(8,128)S(1)}, bf16[512,128]{1,0:T(8,128)(2,1)S(1)}) custom-call(bf16[8,96,768]{2,1,0:T(8,128)(2,1)S(1)} %get-tuple-element.29.stack, bf16[2,96,768]{2,1,0:T(8,128)(2,1)S(1)} %get-tuple-element.31.halo, bf16[768,512]{1,0:T(8,128)(2,1)S(1)} %get-tuple-element.32.feat, ...), custom_call_target="tpu_custom_call" | custom-call | flops 1107296256 | bytes 4194304 | tf_op jit(solution)/shard_map/pallas_call | solution.py:298
  6.0 0.5 %collective-permute-start.4 = (bf16[512,128]{1,0:T(8,128)(2,1)S(1)}, bf16[512,128]{1,0:T(8,128)(2,1)S(1)}, u32[]{:S(2)}, u32[]{:S(2)}) collective-permute-start(bf16[512,128]{1,0:T(8,128)(2,1)S(1)} %get-tuple-element.42), channel_id=1, source_target_pairs={{0,1},{1,0},{2,3},{3,2},{4,5},{5,4},{6,7},{7,6},{8,9},{9,8},{10,11... | collective-permute-start | bytes 393224 | tf_op jit(solution)/shard_map/ppermute | solution.py:209
  6.5 0.1 shard_map.88
  6.6 3.5 %collective-permute-start.2 = (bf16[576,128]{1,0:T(8,128)(2,1)S(1)}, bf16[576,128]{1,0:T(8,128)(2,1)S(1)}, u32[]{:S(2)}, u32[]{:S(2)}) collective-permute-start(bf16[576,128]{1,0:T(8,128)(2,1)S(1)} %get-tuple-element.39), channel_id=1, source_target_pairs={{0,6},{1,25},{2,4},{3,27},{4,2},{5,29},{6,0},{7,31},{8,14},{9,17},... | collective-permute-start | bytes 442376 | tf_op jit(solution)/shard_map/ppermute | solution.py:205
  10.2 0.5 %collective-permute-start.3 = (bf16[576,128]{1,0:T(8,128)(2,1)S(1)}, bf16[576,128]{1,0:T(8,128)(2,1)S(1)}, u32[]{:S(2)}, u32[]{:S(2)}) collective-permute-start(bf16[576,128]{1,0:T(8,128)(2,1)S(1)} %get-tuple-element.40), channel_id=1, source_target_pairs={{0,4},{1,17},{2,6},{3,19},{4,0},{5,21},{6,2},{7,23},{8,12},{9,25},... | collective-permute-start | bytes 442376 | tf_op jit(solution)/shard_map/ppermute | solution.py:205
  10.7 0.0 collective-permute-done.4.got
  10.7 0.2 collective-permute-start.5
  10.9 2.8 %collective-permute-start.6 = (bf16[128,128]{1,0:T(8,128)(2,1)S(1)}, bf16[128,128]{1,0:T(8,128)(2,1)S(1)}, u32[]{:S(2)}, u32[]{:S(2)}) collective-permute-start(bf16[128,128]{1,0:T(8,128)(2,1)S(1)} %get-tuple-element.46), channel_id=1, source_target_pairs={{0,6},{1,25},{2,4},{3,27},{4,2},{5,29},{6,0},{7,31},{8,14},{9,17},... | collective-permute-start | bytes 98312 | tf_op jit(solution)/shard_map/ppermute | solution.py:205
  13.8 0.5 %collective-permute-start.7 = (bf16[128,128]{1,0:T(8,128)(2,1)S(1)}, bf16[128,128]{1,0:T(8,128)(2,1)S(1)}, u32[]{:S(2)}, u32[]{:S(2)}) collective-permute-start(bf16[128,128]{1,0:T(8,128)(2,1)S(1)} %get-tuple-element.47), channel_id=1, source_target_pairs={{0,4},{1,17},{2,6},{3,19},{4,0},{5,21},{6,2},{7,23},{8,12},{9,25},... | collective-permute-start | bytes 98312 | tf_op jit(solution)/shard_map/ppermute | solution.py:205
  14.3 0.0 collective-permute-done.2.three
  14.3 1.0 %collective-permute-done.3.two = bf16[576,128]{1,0:T(8,128)(2,1)S(1)} collective-permute-done((bf16[576,128]{1,0:T(8,128)(2,1)S(1)}, bf16[576,128]{1,0:T(8,128)(2,1)S(1)}, u32[]{:S(2)}, u32[]{:S(2)}) %collective-permute-start.3) | collective-permute-done | bytes 147488 | tf_op jit(solution)/shard_map/ppermute | solution.py:205
  15.4 2.3 %collective-permute-done.6.three_b = bf16[128,128]{1,0:T(8,128)(2,1)S(1)} collective-permute-done((bf16[128,128]{1,0:T(8,128)(2,1)S(1)}, bf16[128,128]{1,0:T(8,128)(2,1)S(1)}, u32[]{:S(2)}, u32[]{:S(2)}) %collective-permute-start.6) | collective-permute-done | bytes 32800 | tf_op jit(solution)/shard_map/ppermute | solution.py:205
  17.6 0.3 collective-permute-done.7.two_b
  18.0 3.7 %collective-permute-start.10 = (bf16[704,128]{1,0:T(8,128)(2,1)S(1)}, bf16[704,128]{1,0:T(8,128)(2,1)S(1)}, u32[]{:S(2)}, u32[]{:S(2)}) collective-permute-start(bf16[704,128]{1,0:T(8,128)(2,1)S(1)} %shard_map.91.own), channel_id=1, source_target_pairs={{0,24},{1,7},{2,26},{3,5},{4,28},{5,3},{6,30},{7,1},{8,16},{9,15},... | collective-permute-start | bytes 540680 | tf_op jit(solution)/shard_map/ppermute | solution.py:205
  21.7 0.8 %collective-permute-start.8 = (bf16[704,128]{1,0:T(8,128)(2,1)S(1)}, bf16[704,128]{1,0:T(8,128)(2,1)S(1)}, u32[]{:S(2)}, u32[]{:S(2)}) collective-permute-start(bf16[704,128]{1,0:T(8,128)(2,1)S(1)} %shard_map.91.own), channel_id=1, source_target_pairs={{0,8},{1,3},{2,10},{3,1},{4,12},{5,7},{6,14},{7,5},{8,0},{9,11},{1... | collective-permute-start | bytes 540680 | tf_op jit(solution)/shard_map/ppermute | solution.py:205
  22.5 2.5 %shard_map.87 = (bf16[8,96,256]{2,1,0:T(8,128)(2,1)}, bf16[4,48,256]{2,1,0:T(8,128)(2,1)}) custom-call(bf16[8,96,256]{2,1,0:T(8,128)(2,1)S(1)} %bitcast.8, bf16[9,256,256]{2,1,0:T(8,128)(2,1)S(1)} %get-tuple-element.28.out_w, bf16[768,256]{1,0:T(8,128)(2,1)S(1)} %get-tuple-element.33.grad, bf16[2496,128]{1,0:T(8,128)(2,1)S(1)} %collective-permute-done.1.refs_0_.got), custom_call_target="tpu_custom_call" | custom-call | flops 905969664 | bytes 2097152 | tf_op jit(solution)/shard_map/pallas_call | solution.py:310
  25.0 0.5 %collective-permute-done.10.three = bf16[704,128]{1,0:T(8,128)(2,1)S(1)} collective-permute-done((bf16[704,128]{1,0:T(8,128)(2,1)S(1)}, bf16[704,128]{1,0:T(8,128)(2,1)S(1)}, u32[]{:S(2)}, u32[]{:S(2)}) %collective-permute-start.10) | collective-permute-done | bytes 180256 | tf_op jit(solution)/shard_map/ppermute | solution.py:205
  25.5 5.5 %collective-permute-done.9.two = bf16[704,128]{1,0:T(8,128)(2,1)S(1)} collective-permute-done((bf16[704,128]{1,0:T(8,128)(2,1)S(1)}, bf16[704,128]{1,0:T(8,128)(2,1)S(1)}, u32[]{:S(2)}, u32[]{:S(2)}) %collective-permute-start.9) | collective-permute-done | bytes 180256 | tf_op jit(solution)/shard_map/ppermute | solution.py:205
  31.0 0.1 shard_map.92.refs_0_
  31.1 0.1 collective-permute-start.13
  31.2 1.4 %collective-permute-start.12 = (bf16[704,128]{1,0:T(8,128)(2,1)S(1)}, bf16[704,128]{1,0:T(8,128)(2,1)S(1)}, u32[]{:S(2)}, u32[]{:S(2)}) collective-permute-start(bf16[704,128]{1,0:T(8,128)(2,1)S(1)} %shard_map.92.refs_0_), channel_id=1, source_target_pairs={{0,4},{1,17},{2,6},{3,19},{4,0},{5,21},{6,2},{7,23},{8,12},{9,25},... | collective-permute-start | bytes 540680 | tf_op jit(solution)/shard_map/ppermute | solution.py:205
  32.5 2.1 %collective-permute-start.11 = (bf16[704,128]{1,0:T(8,128)(2,1)S(1)}, bf16[704,128]{1,0:T(8,128)(2,1)S(1)}, u32[]{:S(2)}, u32[]{:S(2)}) collective-permute-start(bf16[704,128]{1,0:T(8,128)(2,1)S(1)} %shard_map.92.refs_0_), channel_id=1, source_target_pairs={{0,2},{1,9},{2,0},{3,11},{4,6},{5,13},{6,4},{7,15},{8,10},{9,1},{1... | collective-permute-start | bytes 540680 | tf_op jit(solution)/shard_map/ppermute | solution.py:205
  34.7 3.0 %collective-permute-done.13.refs_3_ = bf16[704,128]{1,0:T(8,128)(2,1)S(1)} collective-permute-done((bf16[704,128]{1,0:T(8,128)(2,1)S(1)}, bf16[704,128]{1,0:T(8,128)(2,1)S(1)}, u32[]{:S(2)}, u32[]{:S(2)}) %collective-permute-start.13) | collective-permute-done | bytes 180256 | tf_op jit(solution)/shard_map/ppermute | solution.py:205
  37.7 1.0 %collective-permute-done.12.refs_2_ = bf16[704,128]{1,0:T(8,128)(2,1)S(1)} collective-permute-done((bf16[704,128]{1,0:T(8,128)(2,1)S(1)}, bf16[704,128]{1,0:T(8,128)(2,1)S(1)}, u32[]{:S(2)}, u32[]{:S(2)}) %collective-permute-start.12) | collective-permute-done | bytes 180256 | tf_op jit(solution)/shard_map/ppermute | solution.py:205
  38.7 0.5 %collective-permute-start.15 = (bf16[704,128]{1,0:T(8,128)(2,1)S(1)}, bf16[704,128]{1,0:T(8,128)(2,1)S(1)}, u32[]{:S(2)}, u32[]{:S(2)}) collective-permute-start(bf16[704,128]{1,0:T(8,128)(2,1)S(1)} %collective-permute-done.11.refs_1_), channel_id=1, source_target_pairs={{0,1},{1,0},{2,3},{3,2},{4,5},{5,4},{6,7},{7,6},{8,9},{9,8},{10,11... | collective-permute-start | bytes 540680 | tf_op jit(solution)/shard_map/ppermute | solution.py:209
  39.2 0.9 %collective-permute-done.16.refs_6_ = bf16[704,128]{1,0:T(8,128)(2,1)S(1)} collective-permute-done((bf16[704,128]{1,0:T(8,128)(2,1)S(1)}, bf16[704,128]{1,0:T(8,128)(2,1)S(1)}, u32[]{:S(2)}, u32[]{:S(2)}) %collective-permute-start.16) | collective-permute-done | bytes 180256 | tf_op jit(solution)/shard_map/ppermute | solution.py:209
  40.1 0.3 collective-permute-done.15.refs_5_
  40.4 1.2 %shard_map.93 = (bf16[2304,256]{1,0:T(8,128)(2,1)}, bf16[512,256]{1,0:T(8,128)(2,1)}) custom-call(bf16[704,128]{1,0:T(8,128)(2,1)S(1)} %shard_map.92.refs_0_, bf16[704,128]{1,0:T(8,128)(2,1)S(1)} %collective-permute-done.11.refs_1_, bf16[704,128]{1,0:T(8,128)(2,1)S(1)} %collective-permute-done.12.refs_2_, ...), custom_call_target="tpu_custom_call" | custom-call | tf_op jit(solution)/shard_map/pallas_call | solution.py:238
  (14 shorter events, 0.2 us)
Async XLA Ops:
  0.6 2.4 %collective-permute-start = (bf16[8,96,256]{2,1,0:T(8,128)(2,1)}, bf16[8,96,256]{2,1,0:T(8,128)(2,1)S(1)}, u32[]{:S(2)}, u32[]{:S(2)}) collective-permute-start(bf16[8,96,256]{2,1,0:T(8,128)(2,1)} %bitcast.13), channel_id=1, source_target_pairs={{0,1},{1,0},{2,3},{3,2},{4,5},{5,4},{6,7},{7,6},{8,9},{9,8},{10,11... | collective-permute-start | bytes 1179656 | tf_op jit(solution)/shard_map/ppermute | solution.py:19
  4.2 2.4 %collective-permute-start.1 = (bf16[2496,128]{1,0:T(8,128)(2,1)S(1)}, bf16[2496,128]{1,0:T(8,128)(2,1)S(1)}, u32[]{:S(2)}, u32[]{:S(2)}) collective-permute-start(bf16[2496,128]{1,0:T(8,128)(2,1)S(1)} %get-tuple-element.34), channel_id=1, source_target_pairs={{0,1},{1,0},{2,3},{3,2},{4,5},{5,4},{6,7},{7,6},{8,9},{9,8},{10,11... | collective-permute-start | bytes 1916936 | tf_op jit(solution)/shard_map/ppermute | solution.py:209
  6.0 4.7 %collective-permute-start.4 = (bf16[512,128]{1,0:T(8,128)(2,1)S(1)}, bf16[512,128]{1,0:T(8,128)(2,1)S(1)}, u32[]{:S(2)}, u32[]{:S(2)}) collective-permute-start(bf16[512,128]{1,0:T(8,128)(2,1)S(1)} %get-tuple-element.42), channel_id=1, source_target_pairs={{0,1},{1,0},{2,3},{3,2},{4,5},{5,4},{6,7},{7,6},{8,9},{9,8},{10,11... | collective-permute-start | bytes 393224 | tf_op jit(solution)/shard_map/ppermute | solution.py:209
  6.6 7.7 %collective-permute-start.2 = (bf16[576,128]{1,0:T(8,128)(2,1)S(1)}, bf16[576,128]{1,0:T(8,128)(2,1)S(1)}, u32[]{:S(2)}, u32[]{:S(2)}) collective-permute-start(bf16[576,128]{1,0:T(8,128)(2,1)S(1)} %get-tuple-element.39), channel_id=1, source_target_pairs={{0,6},{1,25},{2,4},{3,27},{4,2},{5,29},{6,0},{7,31},{8,14},{9,17},... | collective-permute-start | bytes 442376 | tf_op jit(solution)/shard_map/ppermute | solution.py:205
  10.2 5.1 %collective-permute-start.3 = (bf16[576,128]{1,0:T(8,128)(2,1)S(1)}, bf16[576,128]{1,0:T(8,128)(2,1)S(1)}, u32[]{:S(2)}, u32[]{:S(2)}) collective-permute-start(bf16[576,128]{1,0:T(8,128)(2,1)S(1)} %get-tuple-element.40), channel_id=1, source_target_pairs={{0,4},{1,17},{2,6},{3,19},{4,0},{5,21},{6,2},{7,23},{8,12},{9,25},... | collective-permute-start | bytes 442376 | tf_op jit(solution)/shard_map/ppermute | solution.py:205
  10.7 7.2 %collective-permute-start.5 = (bf16[704,128]{1,0:T(8,128)(2,1)S(1)}, bf16[704,128]{1,0:T(8,128)(2,1)S(1)}, u32[]{:S(2)}, u32[]{:S(2)}) collective-permute-start(bf16[704,128]{1,0:T(8,128)(2,1)S(1)} %get-tuple-element.45), channel_id=1, source_target_pairs={{0,2},{1,9},{2,0},{3,11},{4,6},{5,13},{6,4},{7,15},{8,10},{9,1},{1... | collective-permute-start | bytes 540680 | tf_op jit(solution)/shard_map/ppermute | solution.py:205
  10.9 6.7 %collective-permute-start.6 = (bf16[128,128]{1,0:T(8,128)(2,1)S(1)}, bf16[128,128]{1,0:T(8,128)(2,1)S(1)}, u32[]{:S(2)}, u32[]{:S(2)}) collective-permute-start(bf16[128,128]{1,0:T(8,128)(2,1)S(1)} %get-tuple-element.46), channel_id=1, source_target_pairs={{0,6},{1,25},{2,4},{3,27},{4,2},{5,29},{6,0},{7,31},{8,14},{9,17},... | collective-permute-start | bytes 98312 | tf_op jit(solution)/shard_map/ppermute | solution.py:205
  13.8 4.2 %collective-permute-start.7 = (bf16[128,128]{1,0:T(8,128)(2,1)S(1)}, bf16[128,128]{1,0:T(8,128)(2,1)S(1)}, u32[]{:S(2)}, u32[]{:S(2)}) collective-permute-start(bf16[128,128]{1,0:T(8,128)(2,1)S(1)} %get-tuple-element.47), channel_id=1, source_target_pairs={{0,4},{1,17},{2,6},{3,19},{4,0},{5,21},{6,2},{7,23},{8,12},{9,25},... | collective-permute-start | bytes 98312 | tf_op jit(solution)/shard_map/ppermute | solution.py:205
  18.0 7.5 %collective-permute-start.10 = (bf16[704,128]{1,0:T(8,128)(2,1)S(1)}, bf16[704,128]{1,0:T(8,128)(2,1)S(1)}, u32[]{:S(2)}, u32[]{:S(2)}) collective-permute-start(bf16[704,128]{1,0:T(8,128)(2,1)S(1)} %shard_map.91.own), channel_id=1, source_target_pairs={{0,24},{1,7},{2,26},{3,5},{4,28},{5,3},{6,30},{7,1},{8,16},{9,15},... | collective-permute-start | bytes 540680 | tf_op jit(solution)/shard_map/ppermute | solution.py:205
  21.7 9.3 %collective-permute-start.9 = (bf16[704,128]{1,0:T(8,128)(2,1)S(1)}, bf16[704,128]{1,0:T(8,128)(2,1)S(1)}, u32[]{:S(2)}, u32[]{:S(2)}) collective-permute-start(bf16[704,128]{1,0:T(8,128)(2,1)S(1)} %shard_map.91.own), channel_id=1, source_target_pairs={{0,16},{1,5},{2,18},{3,7},{4,20},{5,1},{6,22},{7,3},{8,24},{9,13},... | collective-permute-start | bytes 540680 | tf_op jit(solution)/shard_map/ppermute | solution.py:205
  21.7 9.3 %collective-permute-start.8 = (bf16[704,128]{1,0:T(8,128)(2,1)S(1)}, bf16[704,128]{1,0:T(8,128)(2,1)S(1)}, u32[]{:S(2)}, u32[]{:S(2)}) collective-permute-start(bf16[704,128]{1,0:T(8,128)(2,1)S(1)} %shard_map.91.own), channel_id=1, source_target_pairs={{0,8},{1,3},{2,10},{3,1},{4,12},{5,7},{6,14},{7,5},{8,0},{9,11},{1... | collective-permute-start | bytes 540680 | tf_op jit(solution)/shard_map/ppermute | solution.py:205
  31.1 6.6 %collective-permute-start.13 = (bf16[704,128]{1,0:T(8,128)(2,1)S(1)}, bf16[704,128]{1,0:T(8,128)(2,1)S(1)}, u32[]{:S(2)}, u32[]{:S(2)}) collective-permute-start(bf16[704,128]{1,0:T(8,128)(2,1)S(1)} %shard_map.92.refs_0_), channel_id=1, source_target_pairs={{0,6},{1,25},{2,4},{3,27},{4,2},{5,29},{6,0},{7,31},{8,14},{9,17},... | collective-permute-start | bytes 540680 | tf_op jit(solution)/shard_map/ppermute | solution.py:205
  31.2 7.5 %collective-permute-start.12 = (bf16[704,128]{1,0:T(8,128)(2,1)S(1)}, bf16[704,128]{1,0:T(8,128)(2,1)S(1)}, u32[]{:S(2)}, u32[]{:S(2)}) collective-permute-start(bf16[704,128]{1,0:T(8,128)(2,1)S(1)} %shard_map.92.refs_0_), channel_id=1, source_target_pairs={{0,4},{1,17},{2,6},{3,19},{4,0},{5,21},{6,2},{7,23},{8,12},{9,25},... | collective-permute-start | bytes 540680 | tf_op jit(solution)/shard_map/ppermute | solution.py:205
  32.5 6.1 %collective-permute-start.11 = (bf16[704,128]{1,0:T(8,128)(2,1)S(1)}, bf16[704,128]{1,0:T(8,128)(2,1)S(1)}, u32[]{:S(2)}, u32[]{:S(2)}) collective-permute-start(bf16[704,128]{1,0:T(8,128)(2,1)S(1)} %shard_map.92.refs_0_), channel_id=1, source_target_pairs={{0,2},{1,9},{2,0},{3,11},{4,6},{5,13},{6,4},{7,15},{8,10},{9,1},{1... | collective-permute-start | bytes 540680 | tf_op jit(solution)/shard_map/ppermute | solution.py:205
  34.7 4.5 %collective-permute-start.14 = (bf16[704,128]{1,0:T(8,128)(2,1)S(1)}, bf16[704,128]{1,0:T(8,128)(2,1)S(1)}, u32[]{:S(2)}, u32[]{:S(2)}) collective-permute-start(bf16[704,128]{1,0:T(8,128)(2,1)S(1)} %shard_map.92.refs_0_), channel_id=1, source_target_pairs={{0,1},{1,0},{2,3},{3,2},{4,5},{5,4},{6,7},{7,6},{8,9},{9,8},{10,11... | collective-permute-start | bytes 540680 | tf_op jit(solution)/shard_map/ppermute | solution.py:209
  37.7 1.5 %collective-permute-start.17 = (bf16[704,128]{1,0:T(8,128)(2,1)S(1)}, bf16[704,128]{1,0:T(8,128)(2,1)S(1)}, u32[]{:S(2)}, u32[]{:S(2)}) collective-permute-start(bf16[704,128]{1,0:T(8,128)(2,1)S(1)} %collective-permute-done.13.refs_3_), channel_id=1, source_target_pairs={{0,1},{1,0},{2,3},{3,2},{4,5},{5,4},{6,7},{7,6},{8,9},{9,8},{10,11... | collective-permute-start | bytes 540680 | tf_op jit(solution)/shard_map/ppermute | solution.py:209
  38.7 1.4 %collective-permute-start.16 = (bf16[704,128]{1,0:T(8,128)(2,1)S(1)}, bf16[704,128]{1,0:T(8,128)(2,1)S(1)}, u32[]{:S(2)}, u32[]{:S(2)}) collective-permute-start(bf16[704,128]{1,0:T(8,128)(2,1)S(1)} %collective-permute-done.12.refs_2_), channel_id=1, source_target_pairs={{0,1},{1,0},{2,3},{3,2},{4,5},{5,4},{6,7},{7,6},{8,9},{9,8},{10,11... | collective-permute-start | bytes 540680 | tf_op jit(solution)/shard_map/ppermute | solution.py:209
  38.7 1.7 %collective-permute-start.15 = (bf16[704,128]{1,0:T(8,128)(2,1)S(1)}, bf16[704,128]{1,0:T(8,128)(2,1)S(1)}, u32[]{:S(2)}, u32[]{:S(2)}) collective-permute-start(bf16[704,128]{1,0:T(8,128)(2,1)S(1)} %collective-permute-done.11.refs_1_), channel_id=1, source_target_pairs={{0,1},{1,0},{2,3},{3,2},{4,5},{5,4},{6,7},{7,6},{8,9},{9,8},{10,11... | collective-permute-start | bytes 540680 | tf_op jit(solution)/shard_map/ppermute | solution.py:209

commit v10 on v9

--- a/solution.py
+++ b/solution.py
@@ -89,28 +89,37 @@
     theirs[rows, :] = jnp.where(here == 0, values[:, half:], values[:, :half]).astype(BF16)
 
 
-def kernel_grad_kernel(peers, stack, merged, merged_t, before, after, halo, *outs):
+def put_taps(outs, start, merged_t, strip):
+    channels = merged_t.shape[0]
+    part = jnp.dot(merged_t[...], strip, preferred_element_type=F32)
+    for j in range(3):
+        put_sums(outs, start + j * channels, part[:, j * channels : (j + 1) * channels])
+
+
+def first_grads_kernel(peers, stack, merged, merged_t, before, after, halo, *outs):
     cols = stack.shape[1]
     channels, cells = merged_t.shape
     put_halo(halo, before[before.shape[0] - 1], after[0], 0, peers, 1)
     if len(outs) == 2:
         here = lax.axis_index("space")
         edge = jnp.where(here == 0, merged[cells - cols :, :], merged[:cols, :])
-        start = 9 * channels
+        start = 6 * channels
         outs[1][start : start + cols, :] = edge[:, : channels // 2]
         outs[1][start + cols :, :] = edge[:, channels // 2 :]
-    for i, strip in enumerate(strips_of(stack, halo)):
-        part = jnp.dot(merged_t[...], strip, preferred_element_type=F32)
-        for j in range(3):
-            put_sums(outs, (3 * i + j) * channels, part[:, j * channels : (j + 1) * channels])
-
-
-def data_grad_kernel(stack, halo, feat, out_w, grad, *outs):
-    cells = jnp.concatenate(strips_of(stack, halo), axis=1)
+    strips = strips_of(stack, halo)
+    for i in range(2):
+        put_taps(outs, 3 * i * channels, merged_t, strips[i])
+
+
+def last_grads_kernel(stack, merged_t, halo, feat, out_w, grad, *outs):
+    channels = merged_t.shape[0]
+    strips = strips_of(stack, halo)
+    put_taps(outs, 0, merged_t, strips[2])
+    cells = jnp.concatenate(strips, axis=1)
     taps = jnp.concatenate([out_w[tap] for tap in range(9)], axis=1)
     total = lax.dot_general(cells, taps, (((1,), (1,)), ((), ())), preferred_element_type=F32)
     grad[...] = total.astype(BF16)
-    put_sums(outs, 0, jnp.dot(jnp.transpose(feat[...]), grad[...], preferred_element_type=F32))
+    put_sums(outs, 3 * channels, jnp.dot(jnp.transpose(feat[...]), grad[...], preferred_element_type=F32))
 
 
 def forward_kernel(peers, merged, out_w, grad, *refs):
@@ -149,35 +158,34 @@
     return pl.ds(pl.multiple_of(index * length, 16), length)
 
 
-def cut_kernel(mine, got, *refs):
+def cut_kernel(segments, mine, got, *refs):
     place, _ = places()
-    share = mine.shape[0] // 4
-    for k, out in zip((0, 3, 2, 1), refs[-4:]):
-        rows = block(place ^ k, share)
-        start = out.shape[0] - share
-        if start:
-            out[:start, :] = refs[0][...]
-        out[start:, :] = (mine[rows, :] + got[rows, :].astype(F32)).astype(out.dtype)
-
-
-def add_early_kernel(own, three, two, out):
-    out[...] = own[...] + three[...].astype(F32) + two[...].astype(F32)
-
-
-def add_kernel(part_a, own_b, one, three_b, two_b, out):
-    edge = part_a.shape[0]
-    out[:edge, :] = (part_a[...] + one[:edge, :].astype(F32)).astype(BF16)
-    total = own_b[...] + one[edge:, :].astype(F32) + two_b[...].astype(F32) + three_b[...].astype(F32)
-    out[edge:, :] = total.astype(BF16)
-
-
-def finish_kernel(scale, own, one, two, three, _, out):
+    for k, out in zip((0, 3, 2, 1), refs):
+        start, to = 0, 0
+        for length in segments:
+            share = length // 4
+            rows = pl.ds(pl.multiple_of(start + (place ^ k) * share, 16), share)
+            out[to : to + share, :] = (mine[rows, :] + got[rows, :].astype(F32)).astype(out.dtype)
+            start, to = start + length, to + share
+
+
+def add_kernel(own, three, two, one, *refs):
+    out = refs[-1]
+    total = own[...] + one[...].astype(F32) + two[...].astype(F32) + three[...].astype(F32)
+    out[...] = total.astype(BF16)
+
+
+def finish_kernel(scale, own, one, two, three, *refs):
     near = own[...].astype(F32) + one[...].astype(F32)
     far = two[...].astype(F32) + three[...].astype(F32)
-    out[...] = ((near + far) * scale).astype(BF16)
-
-
-def place_kernel(*refs):
+    out = refs[-1]
+    start = out.shape[0] - own.shape[0]
+    if start:
+        out[:start, :] = refs[0][...]
+    out[start:, :] = ((near + far) * scale).astype(BF16)
+
+
+def place_kernel(segments, *refs):
     results, sems = refs[8:10], refs[10]
     side = lax.axis_index("space")
     copies = []
@@ -185,9 +193,10 @@
         lanes = pl.ds(pl.multiple_of(columns * 128, 128), 128)
         for k, quarter in enumerate(quarters):
             start = 0
-            for result in results:
-                share = result.shape[0] // 4
-                to = result.at[block(place ^ k, share), lanes]
+            for result, first, length in segments:
+                share = length // 4
+                rows = pl.ds(pl.multiple_of(first + (place ^ k) * share, 16), share)
+                to = results[result].at[rows, lanes]
                 copies.append(pltpu.make_async_copy(quarter.at[pl.ds(start, share), :], to, sems.at[len(copies)]))
                 start += share
     for copy in copies:
@@ -218,28 +227,36 @@
     )
 
 
-def sum_everywhere(parts, scale, after):
-    lengths, width = [mine.shape[0] for mine, _ in parts], parts[0][0].shape[1]
+def sum_everywhere(parts, splits, scale, after):
+    width = parts[0][0].shape[1]
     vmem, far = pl.BlockSpec(memory_space=pltpu.VMEM), pl.BlockSpec(memory_space=pltpu.HBM)
     after = pltpu.with_memory_space_constraint(after, pltpu.HBM)
-    share_a, share_b, quarter = [(length // 4, width) for length in (*lengths, sum(lengths))]
-    own_a, three, two, one_a = call(cut_kernel, (share_a, F32), *[(share_a, BF16)] * 3)(*parts[0])
-    three, two = exchange(three, 0, 3), exchange(two, 0, 2)
-    slow = pl.CostEstimate(flops=3 * 2**28, bytes_accessed=2**10, transcendentals=0)
-    [part_a] = call(add_early_kernel, (share_a, F32), cost_estimate=slow)(own_a, three, two)
-    own_b, three, two, one = call(cut_kernel, (share_b, F32), *[(share_b, BF16)] * 2, (quarter, BF16))(*parts[1], one_a)
-    one, three, two = exchange(one, 0, 1), exchange(three, 0, 3), exchange(two, 0, 2)
-    [total] = call(add_kernel, (quarter, BF16))(part_a, own_b, one, three, two)
-    three, two, one = [exchange(total, 1, k) for k in (3, 2, 1)]
-    finish = call(functools.partial(finish_kernel, scale), (quarter, BF16), in_specs=[vmem] * 4 + [far])
-    [total] = finish(total, one, two, three, after)
-    three, two, one = [exchange(total, 0, k) for k in (3, 2, 1)]
-    quarters = [total, one, two, three]
+    slow = pl.CostEstimate(flops=2**30, bytes_accessed=2**10, transcendentals=0)
+    shares = [(sum(split) // 4, width) for split in splits]
+    terms = []
+    for part, split, share in zip(parts, splits, shares):
+        own, *pieces = call(functools.partial(cut_kernel, split), (share, F32), *[(share, BF16)] * 3)(*part)
+        terms.append([own] + [exchange(piece, 0, k) for piece, k in zip(pieces, (3, 2, 1))])
+    sums = []
+    for number, share in enumerate(shares):
+        extra = [after] if number == 0 else []
+        [total] = call(
+            add_kernel, (share, BF16), in_specs=[vmem] * 4 + [far] * len(extra), cost_estimate=slow
+        )(*terms[number], *extra)
+        three, two, one = [exchange(total, 1, k) for k in (3, 2, 1)]
+        sums.append((total, one, two, three))
+    finish = functools.partial(finish_kernel, scale)
+    [first] = call(finish, (shares[0], BF16), cost_estimate=slow)(*sums[0])
+    [joint] = call(finish, ((sum(rows for rows, _ in shares), width), BF16))(*sums[1], first)
+    three, two, one = [exchange(joint, 0, k) for k in (3, 2, 1)]
+    quarters = [joint, one, two, three]
+    (length_a,), (length_b, length_c) = splits
     return call(
-        place_kernel,
-        *[((length, 2 * width), BF16) for length in lengths],
+        functools.partial(place_kernel, ((0, 0, length_a), (0, length_a, length_b), (1, 0, length_c))),
+        ((length_a + length_b, 2 * width), BF16),
+        ((length_c, 2 * width), BF16),
         out_specs=[far] * 2,
-        scratch_shapes=[pltpu.SemaphoreType.DMA((16,))],
+        scratch_shapes=[pltpu.SemaphoreType.DMA((24,))],
     )(*quarters, *[swap(one) for one in quarters])
 
 
@@ -285,28 +302,28 @@
                 flops=2 * cells * channels * 4 * in_channels, bytes_accessed=4 * 2**20, transcendentals=0
             ),
         )(*arrays)
-        halo, *kernel_part = pl.pallas_call(
-            functools.partial(kernel_grad_kernel, peers),
-            out_shape=[jax.ShapeDtypeStruct((2, cols, 3 * channels), BF16), *sums(9 * channels, 2 * cols)],
+        halo, *first_part = pl.pallas_call(
+            functools.partial(first_grads_kernel, peers),
+            out_shape=[jax.ShapeDtypeStruct((2, cols, 3 * channels), BF16), *sums(6 * channels, 2 * cols)],
             compiler_params=params,
             cost_estimate=pl.CostEstimate(
-                flops=2 * cells * channels * 9 * channels, bytes_accessed=4 * 2**20, transcendentals=0
+                flops=2 * cells * channels * 6 * channels, bytes_accessed=4 * 2**20, transcendentals=0
             ),
         )(stack, merged, merged_t, cot_before, cot_after)
         if halves:
-            kernel_part[1] = swap(kernel_part[1])
-        grad, *lateral_part = pl.pallas_call(
-            data_grad_kernel,
-            out_shape=[jax.ShapeDtypeStruct((cells, channels), BF16), *sums(in_channels, 0)],
+            first_part[1] = swap(first_part[1])
+        grad, *last_part = pl.pallas_call(
+            last_grads_kernel,
+            out_shape=[jax.ShapeDtypeStruct((cells, channels), BF16), *sums(3 * channels + in_channels, 0)],
             compiler_params=params,
             cost_estimate=pl.CostEstimate(
-                flops=2 * cells * channels * (9 * channels + in_channels), bytes_accessed=4 * 2**20, transcendentals=0
+                flops=2 * cells * channels * (12 * channels + in_channels), bytes_accessed=4 * 2**20, transcendentals=0
             ),
-        )(stack, halo, near_feat, near_taps)
+        )(stack, merged_t, halo, near_feat, near_taps)
         if halves:
-            lateral_part[1] = swap(lateral_part[1])
+            last_part[1] = swap(last_part[1])
         merged = merged.reshape(rows, cols, channels)
-        edges = kernel_part[1:] if halves else neighbour_rows(merged)
+        edges = first_part[1:] if halves else neighbour_rows(merged)
         out, grad_top = pl.pallas_call(
             functools.partial(forward_kernel, peers),
             out_shape=[
@@ -327,13 +344,16 @@
         outs.append(out)
         tops.append(grad_top)
         if not halves:
-            part = [kernel_part[0], lateral_part[0]]
+            part = [first_part[0], last_part[0]]
             parts = part if parts is None else [a + b for a, b in zip(parts, part)]
     scale = 1.0 / (images * lax.axis_size("dp"))
     if halves:
-        grad_kernel, grad_lateral = sum_everywhere((kernel_part, lateral_part), scale, outs[0])
+        splits = (6 * channels,), (3 * channels, in_channels)
+        grad_kernel, grad_lateral = sum_everywhere((first_part, last_part), splits, scale, outs[0])
     else:
-        grad_kernel, grad_lateral = [(total * scale).astype(BF16) for total in lax.psum(parts, ("dp", "space"))]
+        total = jnp.concatenate(lax.psum(parts, ("dp", "space")))
+        total = (total * scale).astype(BF16)
+        grad_kernel, grad_lateral = total[: 9 * channels], total[9 * channels :]
     return jnp.stack(outs), jnp.stack(tops), grad_kernel.reshape(out_kernel.shape), grad_lateral
 
 

time: 41.7 us -> 43.9 us (1.053)
  starting transfers between devices: 17.3 us -> 23.6 us
  waiting for transfers between devices: 14.8 us -> 10.7 us
    ppermute x11 -> x15, starting transfers between devices: 15.6 us -> 21.9 us  [exchange(): return lax.ppermute(array, ('dp', 'space'), pairs)]
    ppermute x11 -> x15, waiting for transfers between devices: 13.6 us -> 9.5 us  [exchange(): return lax.ppermute(array, ('dp', 'space'), pairs)]
    pallas_call x8 -> x9, Pallas kernels: 4.33 us -> 4.37 us  [the longest x1 1.97 us: local(): pl.pallas_call(last_grads_kernel, out_shape=[jax.ShapeDtypeStruct((cells,...]
  transfers between devices with their start and end apart: 18 -> 22, of which waited for: 9 -> 7; matrix products, arithmetic and copies ran while one was open for 0% -> 0% of each run, Pallas kernels for 15% -> 15%
where the time goes in v10:
time: 43.9 us; the launch traced here: 43.8 us
  starting transfers between devices  23.6 us (54%)
  waiting for transfers between devices  10.7 us (24%)
  Pallas kernels  8.81 us (20%)
  between operations  0.72 us (2%)
    ppermute x15, starting transfers between devices, exchange(): return lax.ppermute(array, ('dp', 'space'), pairs)  21.9 us
    ppermute x15, waiting for transfers between devices, exchange(): return lax.ppermute(array, ('dp', 'space'), pairs)  9.5 us
    pallas_call x1, Pallas kernels, local(): pl.pallas_call(functools.partial(forward_kernel, peers), out_shape=[jax.S...  2.53 us
    pallas_call x1, Pallas kernels, local(): pl.pallas_call(last_grads_kernel, out_shape=[jax.ShapeDtypeStruct((cells,...  1.97 us
    pallas_call x1, Pallas kernels, local(): pl.pallas_call(merge_kernel, out_shape=[jax.ShapeDtypeStruct(shape, BF16)...  1.9 us
    pallas_call x1, Pallas kernels, sum_everywhere(): call(functools.partial(place_kernel, ((0, 0, length_a), (0, length_a, len...  1.28 us
    ppermute x6, waiting for transfers between devices, swap(): return lax.ppermute(array, 'space', [(0, 1), (1, 0)])  1.17 us
    ppermute x6, starting transfers between devices, swap(): return lax.ppermute(array, 'space', [(0, 1), (1, 0)])  1.16 us
  transfers between devices with their start and end apart: 22, of which 7 were waited for; matrix products, arithmetic and copies ran while one was open for 0% of the time, Pallas kernels for 15%

profile of v10, /device:TPU:0, one launch (start us, length us, event | category | flops | bytes accessed | tf_op | source)
XLA Modules:
  0.0 43.8 jit_solution(1016165198164131845)
XLA Ops:
  0.6 0.5 %collective-permute-start = (bf16[8,96,256]{2,1,0:T(8,128)(2,1)}, bf16[8,96,256]{2,1,0:T(8,128)(2,1)S(1)}, u32[]{:S(2)}, u32[]{:S(2)}) collective-permute-start(bf16[8,96,256]{2,1,0:T(8,128)(2,1)} %bitcast.12), channel_id=1, source_target_pairs={{0,1},{1,0},{2,3},{3,2},{4,5},{5,4},{6,7},{7,6},{8,9},{9,8},{10,11... | collective-permute-start | bytes 1179656 | tf_op jit(solution)/shard_map/ppermute | solution.py:19
  1.1 1.9 %shard_map.84 = (bf16[768,256]{1,0:T(8,128)(2,1)S(1)}, bf16[256,768]{1,0:T(8,128)(2,1)S(1)}, bf16[8,96,768]{2,1,0:T(8,128)(2,1)S(1)}, bf16[768,512]{1,0:T(8,128)(2,1)S(1)}, bf16[9,256,256]{2,1,0:T(8,128)(2,1)S(1)}) custom-call(bf16[8,96,256]{2,1,0:T(8,128)(2,1)} %bitcast.13, bf16[512,256]{1,0:T(8,128)(2,1)} %refs_1_.1, bf16[4,48,256]{2,1,0:T(8,128)(2,1)} %bitcast.14, ...), custom_call_target="tpu_custom_call" | custom-call | flops 805306368 | bytes 4194304 | tf_op jit(solution)/shard_map/pallas_call | solution.py:286
  3.1 0.8 %shard_map.85 = (bf16[2,96,768]{2,1,0:T(8,128)(2,1)S(1)}, f32[1536,128]{1,0:T(8,128)S(1)}, bf16[1728,128]{1,0:T(8,128)(2,1)S(1)}) custom-call(bf16[8,96,768]{2,1,0:T(8,128)(2,1)S(1)} %get-tuple-element.29.stack, bf16[768,256]{1,0:T(8,128)(2,1)S(1)} %get-tuple-element.27.merged, bf16[256,768]{1,0:T(8,128)(2,1)S(1)} %get-tuple-element.30.merged_t, ...), custom_call_target="tpu_custom_call" | custom-call | flops 603979776 | bytes 4194304 | tf_op jit(solution)/shard_map/pallas_call | solution.py:305
  3.9 0.1 collective-permute-start.1
  4.0 2.0 %shard_map.86 = (bf16[768,256]{1,0:T(8,128)(2,1)S(1)}, f32[1280,128]{1,0:T(8,128)S(1)}, bf16[1280,128]{1,0:T(8,128)(2,1)S(1)}) custom-call(bf16[8,96,768]{2,1,0:T(8,128)(2,1)S(1)} %get-tuple-element.29.stack, bf16[256,768]{1,0:T(8,128)(2,1)S(1)} %get-tuple-element.30.merged_t, bf16[2,96,768]{2,1,0:T(8,128)(2,1)S(1)} %get-tuple-element.31.halo, ...), custom_call_target="tpu_custom_call" | custom-call | flops 1409286144 | bytes 4194304 | tf_op jit(solution)/shard_map/pallas_call | solution.py:315
  6.0 0.5 %collective-permute-start.2 = (bf16[1280,128]{1,0:T(8,128)(2,1)S(1)}, bf16[1280,128]{1,0:T(8,128)(2,1)S(1)}, u32[]{:S(2)}, u32[]{:S(2)}) collective-permute-start(bf16[1280,128]{1,0:T(8,128)(2,1)S(1)} %get-tuple-element.38), channel_id=1, source_target_pairs={{0,1},{1,0},{2,3},{3,2},{4,5},{5,4},{6,7},{7,6},{8,9},{9,8},{10,11... | collective-permute-start | bytes 983048 | tf_op jit(solution)/shard_map/ppermute | solution.py:218
  6.5 0.1 shard_map.90
  6.6 3.5 %collective-permute-start.9 = (bf16[384,128]{1,0:T(8,128)(2,1)S(1)}, bf16[384,128]{1,0:T(8,128)(2,1)S(1)}, u32[]{:S(2)}, u32[]{:S(2)}) collective-permute-start(bf16[384,128]{1,0:T(8,128)(2,1)S(1)} %get-tuple-element.45), channel_id=1, source_target_pairs={{0,6},{1,25},{2,4},{3,27},{4,2},{5,29},{6,0},{7,31},{8,14},{9,17},... | collective-permute-start | bytes 294920 | tf_op jit(solution)/shard_map/ppermute | solution.py:214
  10.1 0.5 %collective-permute-start.10 = (bf16[384,128]{1,0:T(8,128)(2,1)S(1)}, bf16[384,128]{1,0:T(8,128)(2,1)S(1)}, u32[]{:S(2)}, u32[]{:S(2)}) collective-permute-start(bf16[384,128]{1,0:T(8,128)(2,1)S(1)} %get-tuple-element.46), channel_id=1, source_target_pairs={{0,4},{1,17},{2,6},{3,19},{4,0},{5,21},{6,2},{7,23},{8,12},{9,25},... | collective-permute-start | bytes 294920 | tf_op jit(solution)/shard_map/ppermute | solution.py:214
  10.6 0.1 collective-permute-start.11
  10.8 0.1 shard_map.88
  10.8 2.9 %collective-permute-start.3 = (bf16[320,128]{1,0:T(8,128)(2,1)S(1)}, bf16[320,128]{1,0:T(8,128)(2,1)S(1)}, u32[]{:S(2)}, u32[]{:S(2)}) collective-permute-start(bf16[320,128]{1,0:T(8,128)(2,1)S(1)} %get-tuple-element.40), channel_id=1, source_target_pairs={{0,6},{1,25},{2,4},{3,27},{4,2},{5,29},{6,0},{7,31},{8,14},{9,17},... | collective-permute-start | bytes 245768 | tf_op jit(solution)/shard_map/ppermute | solution.py:214
  13.7 0.5 %collective-permute-start.4 = (bf16[320,128]{1,0:T(8,128)(2,1)S(1)}, bf16[320,128]{1,0:T(8,128)(2,1)S(1)}, u32[]{:S(2)}, u32[]{:S(2)}) collective-permute-start(bf16[320,128]{1,0:T(8,128)(2,1)S(1)} %get-tuple-element.41), channel_id=1, source_target_pairs={{0,4},{1,17},{2,6},{3,19},{4,0},{5,21},{6,2},{7,23},{8,12},{9,25},... | collective-permute-start | bytes 245768 | tf_op jit(solution)/shard_map/ppermute | solution.py:214
  14.2 2.5 %shard_map.87 = (bf16[8,96,256]{2,1,0:T(8,128)(2,1)}, bf16[4,48,256]{2,1,0:T(8,128)(2,1)}) custom-call(bf16[8,96,256]{2,1,0:T(8,128)(2,1)S(1)} %bitcast.8, bf16[9,256,256]{2,1,0:T(8,128)(2,1)S(1)} %get-tuple-element.28.out_w, bf16[768,256]{1,0:T(8,128)(2,1)S(1)} %get-tuple-element.33.grad, bf16[1728,128]{1,0:T(8,128)(2,1)S(1)} %collective-permute-done.1.refs_0_.got), custom_call_target="tpu_custom_call" | custom-call | flops 905969664 | bytes 2097152 | tf_op jit(solution)/shard_map/pallas_call | solution.py:327
  16.8 0.2 collective-permute-start.5
  17.0 4.1 %collective-permute-start.14 = (bf16[384,128]{1,0:T(8,128)(2,1)S(1)}, bf16[384,128]{1,0:T(8,128)(2,1)S(1)}, u32[]{:S(2)}, u32[]{:S(2)}) collective-permute-start(bf16[384,128]{1,0:T(8,128)(2,1)S(1)} %shard_map.91.own), channel_id=1, source_target_pairs={{0,24},{1,7},{2,26},{3,5},{4,28},{5,3},{6,30},{7,1},{8,16},{9,15},... | collective-permute-start | bytes 294920 | tf_op jit(solution)/shard_map/ppermute | solution.py:214
  21.1 0.6 %collective-permute-start.12 = (bf16[384,128]{1,0:T(8,128)(2,1)S(1)}, bf16[384,128]{1,0:T(8,128)(2,1)S(1)}, u32[]{:S(2)}, u32[]{:S(2)}) collective-permute-start(bf16[384,128]{1,0:T(8,128)(2,1)S(1)} %shard_map.91.own), channel_id=1, source_target_pairs={{0,8},{1,3},{2,10},{3,1},{4,12},{5,7},{6,14},{7,5},{8,0},{9,11},{1... | collective-permute-start | bytes 294920 | tf_op jit(solution)/shard_map/ppermute | solution.py:214
  21.8 3.8 %collective-permute-start.8 = (bf16[320,128]{1,0:T(8,128)(2,1)S(1)}, bf16[320,128]{1,0:T(8,128)(2,1)S(1)}, u32[]{:S(2)}, u32[]{:S(2)}) collective-permute-start(bf16[320,128]{1,0:T(8,128)(2,1)S(1)} %shard_map.89.own), channel_id=1, source_target_pairs={{0,24},{1,7},{2,26},{3,5},{4,28},{5,3},{6,30},{7,1},{8,16},{9,15},... | collective-permute-start | bytes 245768 | tf_op jit(solution)/shard_map/ppermute | solution.py:214
  25.6 0.6 %collective-permute-start.6 = (bf16[320,128]{1,0:T(8,128)(2,1)S(1)}, bf16[320,128]{1,0:T(8,128)(2,1)S(1)}, u32[]{:S(2)}, u32[]{:S(2)}) collective-permute-start(bf16[320,128]{1,0:T(8,128)(2,1)S(1)} %shard_map.89.own), channel_id=1, source_target_pairs={{0,8},{1,3},{2,10},{3,1},{4,12},{5,7},{6,14},{7,5},{8,0},{9,11},{1... | collective-permute-start | bytes 245768 | tf_op jit(solution)/shard_map/ppermute | solution.py:214
  26.3 0.5 %collective-permute-done.13.two = bf16[384,128]{1,0:T(8,128)(2,1)S(1)} collective-permute-done((bf16[384,128]{1,0:T(8,128)(2,1)S(1)}, bf16[384,128]{1,0:T(8,128)(2,1)S(1)}, u32[]{:S(2)}, u32[]{:S(2)}) %collective-permute-start.13) | collective-permute-done | bytes 98336 | tf_op jit(solution)/shard_map/ppermute | solution.py:214
  26.8 0.1 shard_map.92.refs_0_
  26.9 2.1 %collective-permute-done.8.three = bf16[320,128]{1,0:T(8,128)(2,1)S(1)} collective-permute-done((bf16[320,128]{1,0:T(8,128)(2,1)S(1)}, bf16[320,128]{1,0:T(8,128)(2,1)S(1)}, u32[]{:S(2)}, u32[]{:S(2)}) %collective-permute-start.8) | collective-permute-done | bytes 81952 | tf_op jit(solution)/shard_map/ppermute | solution.py:214
  29.0 2.0 %collective-permute-done.7.two = bf16[320,128]{1,0:T(8,128)(2,1)S(1)} collective-permute-done((bf16[320,128]{1,0:T(8,128)(2,1)S(1)}, bf16[320,128]{1,0:T(8,128)(2,1)S(1)}, u32[]{:S(2)}, u32[]{:S(2)}) %collective-permute-start.7) | collective-permute-done | bytes 81952 | tf_op jit(solution)/shard_map/ppermute | solution.py:214
  31.0 0.1 shard_map.93.refs_0_
  31.0 4.3 %collective-permute-start.17 = (bf16[704,128]{1,0:T(8,128)(2,1)S(1)}, bf16[704,128]{1,0:T(8,128)(2,1)S(1)}, u32[]{:S(2)}, u32[]{:S(2)}) collective-permute-start(bf16[704,128]{1,0:T(8,128)(2,1)S(1)} %shard_map.93.refs_0_), channel_id=1, source_target_pairs={{0,6},{1,25},{2,4},{3,27},{4,2},{5,29},{6,0},{7,31},{8,14},{9,17},... | collective-permute-start | bytes 540680 | tf_op jit(solution)/shard_map/ppermute | solution.py:214
  35.3 0.6 %collective-permute-start.15 = (bf16[704,128]{1,0:T(8,128)(2,1)S(1)}, bf16[704,128]{1,0:T(8,128)(2,1)S(1)}, u32[]{:S(2)}, u32[]{:S(2)}) collective-permute-start(bf16[704,128]{1,0:T(8,128)(2,1)S(1)} %shard_map.93.refs_0_), channel_id=1, source_target_pairs={{0,2},{1,9},{2,0},{3,11},{4,6},{5,13},{6,4},{7,15},{8,10},{9,1},{1... | collective-permute-start | bytes 540680 | tf_op jit(solution)/shard_map/ppermute | solution.py:214
  36.0 2.8 %collective-permute-done.17.refs_3_ = bf16[704,128]{1,0:T(8,128)(2,1)S(1)} collective-permute-done((bf16[704,128]{1,0:T(8,128)(2,1)S(1)}, bf16[704,128]{1,0:T(8,128)(2,1)S(1)}, u32[]{:S(2)}, u32[]{:S(2)}) %collective-permute-start.17) | collective-permute-done | bytes 180256 | tf_op jit(solution)/shard_map/ppermute | solution.py:214
  38.8 2.0 %collective-permute-done.16.refs_2_ = bf16[704,128]{1,0:T(8,128)(2,1)S(1)} collective-permute-done((bf16[704,128]{1,0:T(8,128)(2,1)S(1)}, bf16[704,128]{1,0:T(8,128)(2,1)S(1)}, u32[]{:S(2)}, u32[]{:S(2)}) %collective-permute-start.16) | collective-permute-done | bytes 180256 | tf_op jit(solution)/shard_map/ppermute | solution.py:214
  40.8 0.5 %collective-permute-start.19 = (bf16[704,128]{1,0:T(8,128)(2,1)S(1)}, bf16[704,128]{1,0:T(8,128)(2,1)S(1)}, u32[]{:S(2)}, u32[]{:S(2)}) collective-permute-start(bf16[704,128]{1,0:T(8,128)(2,1)S(1)} %collective-permute-done.15.refs_1_), channel_id=1, source_target_pairs={{0,1},{1,0},{2,3},{3,2},{4,5},{5,4},{6,7},{7,6},{8,9},{9,8},{10,11... | collective-permute-start | bytes 540680 | tf_op jit(solution)/shard_map/ppermute | solution.py:218
  41.3 0.9 %collective-permute-done.20.refs_6_ = bf16[704,128]{1,0:T(8,128)(2,1)S(1)} collective-permute-done((bf16[704,128]{1,0:T(8,128)(2,1)S(1)}, bf16[704,128]{1,0:T(8,128)(2,1)S(1)}, u32[]{:S(2)}, u32[]{:S(2)}) %collective-permute-start.20) | collective-permute-done | bytes 180256 | tf_op jit(solution)/shard_map/ppermute | solution.py:218
  42.2 0.3 collective-permute-done.19.refs_5_
  42.5 1.3 %shard_map.94 = (bf16[2304,256]{1,0:T(8,128)(2,1)}, bf16[512,256]{1,0:T(8,128)(2,1)}) custom-call(bf16[704,128]{1,0:T(8,128)(2,1)S(1)} %shard_map.93.refs_0_, bf16[704,128]{1,0:T(8,128)(2,1)S(1)} %collective-permute-done.15.refs_1_, bf16[704,128]{1,0:T(8,128)(2,1)S(1)} %collective-permute-done.16.refs_2_, ...), custom_call_target="tpu_custom_call" | custom-call | tf_op jit(solution)/shard_map/pallas_call | solution.py:254
  (23 shorter events, 0.1 us)
Async XLA Ops:
  0.6 2.4 %collective-permute-start = (bf16[8,96,256]{2,1,0:T(8,128)(2,1)}, bf16[8,96,256]{2,1,0:T(8,128)(2,1)S(1)}, u32[]{:S(2)}, u32[]{:S(2)}) collective-permute-start(bf16[8,96,256]{2,1,0:T(8,128)(2,1)} %bitcast.12), channel_id=1, source_target_pairs={{0,1},{1,0},{2,3},{3,2},{4,5},{5,4},{6,7},{7,6},{8,9},{9,8},{10,11... | collective-permute-start | bytes 1179656 | tf_op jit(solution)/shard_map/ppermute | solution.py:19
  3.9 2.6 %collective-permute-start.1 = (bf16[1728,128]{1,0:T(8,128)(2,1)S(1)}, bf16[1728,128]{1,0:T(8,128)(2,1)S(1)}, u32[]{:S(2)}, u32[]{:S(2)}) collective-permute-start(bf16[1728,128]{1,0:T(8,128)(2,1)S(1)} %get-tuple-element.34), channel_id=1, source_target_pairs={{0,1},{1,0},{2,3},{3,2},{4,5},{5,4},{6,7},{7,6},{8,9},{9,8},{10,11... | collective-permute-start | bytes 1327112 | tf_op jit(solution)/shard_map/ppermute | solution.py:218
  6.0 4.8 %collective-permute-start.2 = (bf16[1280,128]{1,0:T(8,128)(2,1)S(1)}, bf16[1280,128]{1,0:T(8,128)(2,1)S(1)}, u32[]{:S(2)}, u32[]{:S(2)}) collective-permute-start(bf16[1280,128]{1,0:T(8,128)(2,1)S(1)} %get-tuple-element.38), channel_id=1, source_target_pairs={{0,1},{1,0},{2,3},{3,2},{4,5},{5,4},{6,7},{7,6},{8,9},{9,8},{10,11... | collective-permute-start | bytes 983048 | tf_op jit(solution)/shard_map/ppermute | solution.py:218
  6.6 10.2 %collective-permute-start.9 = (bf16[384,128]{1,0:T(8,128)(2,1)S(1)}, bf16[384,128]{1,0:T(8,128)(2,1)S(1)}, u32[]{:S(2)}, u32[]{:S(2)}) collective-permute-start(bf16[384,128]{1,0:T(8,128)(2,1)S(1)} %get-tuple-element.45), channel_id=1, source_target_pairs={{0,6},{1,25},{2,4},{3,27},{4,2},{5,29},{6,0},{7,31},{8,14},{9,17},... | collective-permute-start | bytes 294920 | tf_op jit(solution)/shard_map/ppermute | solution.py:214
  10.1 6.9 %collective-permute-start.10 = (bf16[384,128]{1,0:T(8,128)(2,1)S(1)}, bf16[384,128]{1,0:T(8,128)(2,1)S(1)}, u32[]{:S(2)}, u32[]{:S(2)}) collective-permute-start(bf16[384,128]{1,0:T(8,128)(2,1)S(1)} %get-tuple-element.46), channel_id=1, source_target_pairs={{0,4},{1,17},{2,6},{3,19},{4,0},{5,21},{6,2},{7,23},{8,12},{9,25},... | collective-permute-start | bytes 294920 | tf_op jit(solution)/shard_map/ppermute | solution.py:214
  10.6 6.4 %collective-permute-start.11 = (bf16[384,128]{1,0:T(8,128)(2,1)S(1)}, bf16[384,128]{1,0:T(8,128)(2,1)S(1)}, u32[]{:S(2)}, u32[]{:S(2)}) collective-permute-start(bf16[384,128]{1,0:T(8,128)(2,1)S(1)} %get-tuple-element.47), channel_id=1, source_target_pairs={{0,2},{1,9},{2,0},{3,11},{4,6},{5,13},{6,4},{7,15},{8,10},{9,1},{1... | collective-permute-start | bytes 294920 | tf_op jit(solution)/shard_map/ppermute | solution.py:214
  10.8 10.3 %collective-permute-start.3 = (bf16[320,128]{1,0:T(8,128)(2,1)S(1)}, bf16[320,128]{1,0:T(8,128)(2,1)S(1)}, u32[]{:S(2)}, u32[]{:S(2)}) collective-permute-start(bf16[320,128]{1,0:T(8,128)(2,1)S(1)} %get-tuple-element.40), channel_id=1, source_target_pairs={{0,6},{1,25},{2,4},{3,27},{4,2},{5,29},{6,0},{7,31},{8,14},{9,17},... | collective-permute-start | bytes 245768 | tf_op jit(solution)/shard_map/ppermute | solution.py:214
  13.7 8.0 %collective-permute-start.4 = (bf16[320,128]{1,0:T(8,128)(2,1)S(1)}, bf16[320,128]{1,0:T(8,128)(2,1)S(1)}, u32[]{:S(2)}, u32[]{:S(2)}) collective-permute-start(bf16[320,128]{1,0:T(8,128)(2,1)S(1)} %get-tuple-element.41), channel_id=1, source_target_pairs={{0,4},{1,17},{2,6},{3,19},{4,0},{5,21},{6,2},{7,23},{8,12},{9,25},... | collective-permute-start | bytes 245768 | tf_op jit(solution)/shard_map/ppermute | solution.py:214
  16.8 5.0 %collective-permute-start.5 = (bf16[320,128]{1,0:T(8,128)(2,1)S(1)}, bf16[320,128]{1,0:T(8,128)(2,1)S(1)}, u32[]{:S(2)}, u32[]{:S(2)}) collective-permute-start(bf16[320,128]{1,0:T(8,128)(2,1)S(1)} %get-tuple-element.42), channel_id=1, source_target_pairs={{0,2},{1,9},{2,0},{3,11},{4,6},{5,13},{6,4},{7,15},{8,10},{9,1},{1... | collective-permute-start | bytes 245768 | tf_op jit(solution)/shard_map/ppermute | solution.py:214
  17.0 8.6 %collective-permute-start.14 = (bf16[384,128]{1,0:T(8,128)(2,1)S(1)}, bf16[384,128]{1,0:T(8,128)(2,1)S(1)}, u32[]{:S(2)}, u32[]{:S(2)}) collective-permute-start(bf16[384,128]{1,0:T(8,128)(2,1)S(1)} %shard_map.91.own), channel_id=1, source_target_pairs={{0,24},{1,7},{2,26},{3,5},{4,28},{5,3},{6,30},{7,1},{8,16},{9,15},... | collective-permute-start | bytes 294920 | tf_op jit(solution)/shard_map/ppermute | solution.py:214
  21.1 5.7 %collective-permute-start.13 = (bf16[384,128]{1,0:T(8,128)(2,1)S(1)}, bf16[384,128]{1,0:T(8,128)(2,1)S(1)}, u32[]{:S(2)}, u32[]{:S(2)}) collective-permute-start(bf16[384,128]{1,0:T(8,128)(2,1)S(1)} %shard_map.91.own), channel_id=1, source_target_pairs={{0,16},{1,5},{2,18},{3,7},{4,20},{5,1},{6,22},{7,3},{8,24},{9,13},... | collective-permute-start | bytes 294920 | tf_op jit(solution)/shard_map/ppermute | solution.py:214
  21.1 5.7 %collective-permute-start.12 = (bf16[384,128]{1,0:T(8,128)(2,1)S(1)}, bf16[384,128]{1,0:T(8,128)(2,1)S(1)}, u32[]{:S(2)}, u32[]{:S(2)}) collective-permute-start(bf16[384,128]{1,0:T(8,128)(2,1)S(1)} %shard_map.91.own), channel_id=1, source_target_pairs={{0,8},{1,3},{2,10},{3,1},{4,12},{5,7},{6,14},{7,5},{8,0},{9,11},{1... | collective-permute-start | bytes 294920 | tf_op jit(solution)/shard_map/ppermute | solution.py:214
  21.8 7.2 %collective-permute-start.8 = (bf16[320,128]{1,0:T(8,128)(2,1)S(1)}, bf16[320,128]{1,0:T(8,128)(2,1)S(1)}, u32[]{:S(2)}, u32[]{:S(2)}) collective-permute-start(bf16[320,128]{1,0:T(8,128)(2,1)S(1)} %shard_map.89.own), channel_id=1, source_target_pairs={{0,24},{1,7},{2,26},{3,5},{4,28},{5,3},{6,30},{7,1},{8,16},{9,15},... | collective-permute-start | bytes 245768 | tf_op jit(solution)/shard_map/ppermute | solution.py:214
  25.6 5.3 %collective-permute-start.7 = (bf16[320,128]{1,0:T(8,128)(2,1)S(1)}, bf16[320,128]{1,0:T(8,128)(2,1)S(1)}, u32[]{:S(2)}, u32[]{:S(2)}) collective-permute-start(bf16[320,128]{1,0:T(8,128)(2,1)S(1)} %shard_map.89.own), channel_id=1, source_target_pairs={{0,16},{1,5},{2,18},{3,7},{4,20},{5,1},{6,22},{7,3},{8,24},{9,13},... | collective-permute-start | bytes 245768 | tf_op jit(solution)/shard_map/ppermute | solution.py:214
  25.6 5.3 %collective-permute-start.6 = (bf16[320,128]{1,0:T(8,128)(2,1)S(1)}, bf16[320,128]{1,0:T(8,128)(2,1)S(1)}, u32[]{:S(2)}, u32[]{:S(2)}) collective-permute-start(bf16[320,128]{1,0:T(8,128)(2,1)S(1)} %shard_map.89.own), channel_id=1, source_target_pairs={{0,8},{1,3},{2,10},{3,1},{4,12},{5,7},{6,14},{7,5},{8,0},{9,11},{1... | collective-permute-start | bytes 245768 | tf_op jit(solution)/shard_map/ppermute | solution.py:214
  31.0 7.8 %collective-permute-start.17 = (bf16[704,128]{1,0:T(8,128)(2,1)S(1)}, bf16[704,128]{1,0:T(8,128)(2,1)S(1)}, u32[]{:S(2)}, u32[]{:S(2)}) collective-permute-start(bf16[704,128]{1,0:T(8,128)(2,1)S(1)} %shard_map.93.refs_0_), channel_id=1, source_target_pairs={{0,6},{1,25},{2,4},{3,27},{4,2},{5,29},{6,0},{7,31},{8,14},{9,17},... | collective-permute-start | bytes 540680 | tf_op jit(solution)/shard_map/ppermute | solution.py:214
  35.3 5.5 %collective-permute-start.16 = (bf16[704,128]{1,0:T(8,128)(2,1)S(1)}, bf16[704,128]{1,0:T(8,128)(2,1)S(1)}, u32[]{:S(2)}, u32[]{:S(2)}) collective-permute-start(bf16[704,128]{1,0:T(8,128)(2,1)S(1)} %shard_map.93.refs_0_), channel_id=1, source_target_pairs={{0,4},{1,17},{2,6},{3,19},{4,0},{5,21},{6,2},{7,23},{8,12},{9,25},... | collective-permute-start | bytes 540680 | tf_op jit(solution)/shard_map/ppermute | solution.py:214
  35.3 5.5 %collective-permute-start.15 = (bf16[704,128]{1,0:T(8,128)(2,1)S(1)}, bf16[704,128]{1,0:T(8,128)(2,1)S(1)}, u32[]{:S(2)}, u32[]{:S(2)}) collective-permute-start(bf16[704,128]{1,0:T(8,128)(2,1)S(1)} %shard_map.93.refs_0_), channel_id=1, source_target_pairs={{0,2},{1,9},{2,0},{3,11},{4,6},{5,13},{6,4},{7,15},{8,10},{9,1},{1... | collective-permute-start | bytes 540680 | tf_op jit(solution)/shard_map/ppermute | solution.py:214
  36.0 5.4 %collective-permute-start.18 = (bf16[704,128]{1,0:T(8,128)(2,1)S(1)}, bf16[704,128]{1,0:T(8,128)(2,1)S(1)}, u32[]{:S(2)}, u32[]{:S(2)}) collective-permute-start(bf16[704,128]{1,0:T(8,128)(2,1)S(1)} %shard_map.93.refs_0_), channel_id=1, source_target_pairs={{0,1},{1,0},{2,3},{3,2},{4,5},{5,4},{6,7},{7,6},{8,9},{9,8},{10,11... | collective-permute-start | bytes 540680 | tf_op jit(solution)/shard_map/ppermute | solution.py:218
  38.8 2.5 %collective-permute-start.21 = (bf16[704,128]{1,0:T(8,128)(2,1)S(1)}, bf16[704,128]{1,0:T(8,128)(2,1)S(1)}, u32[]{:S(2)}, u32[]{:S(2)}) collective-permute-start(bf16[704,128]{1,0:T(8,128)(2,1)S(1)} %collective-permute-done.17.refs_3_), channel_id=1, source_target_pairs={{0,1},{1,0},{2,3},{3,2},{4,5},{5,4},{6,7},{7,6},{8,9},{9,8},{10,11... | collective-permute-start | bytes 540680 | tf_op jit(solution)/shard_map/ppermute | solution.py:218
  40.8 1.4 %collective-permute-start.20 = (bf16[704,128]{1,0:T(8,128)(2,1)S(1)}, bf16[704,128]{1,0:T(8,128)(2,1)S(1)}, u32[]{:S(2)}, u32[]{:S(2)}) collective-permute-start(bf16[704,128]{1,0:T(8,128)(2,1)S(1)} %collective-permute-done.16.refs_2_), channel_id=1, source_target_pairs={{0,1},{1,0},{2,3},{3,2},{4,5},{5,4},{6,7},{7,6},{8,9},{9,8},{10,11... | collective-permute-start | bytes 540680 | tf_op jit(solution)/shard_map/ppermute | solution.py:218
  40.8 1.7 %collective-permute-start.19 = (bf16[704,128]{1,0:T(8,128)(2,1)S(1)}, bf16[704,128]{1,0:T(8,128)(2,1)S(1)}, u32[]{:S(2)}, u32[]{:S(2)}) collective-permute-start(bf16[704,128]{1,0:T(8,128)(2,1)S(1)} %collective-permute-done.15.refs_1_), channel_id=1, source_target_pairs={{0,1},{1,0},{2,3},{3,2},{4,5},{5,4},{6,7},{7,6},{8,9},{9,8},{10,11... | collective-permute-start | bytes 540680 | tf_op jit(solution)/shard_map/ppermute | solution.py:218

commit v11 on v9

--- a/solution.py
+++ b/solution.py
@@ -43,8 +43,8 @@
 
 
 def merge_kernel(*refs):
-    far, (merged, merged_t, stack, feat, out_w), near, sems = refs[:5], refs[5:10], refs[10:13], refs[13]
-    near = (*near, feat, out_w)
+    far, (merged, merged_t, stack, feat), near, sems = refs[:4], refs[4:8], refs[8:11], refs[11]
+    near = (*near, feat)
     copies = [pltpu.make_async_copy(a, b, sems.at[i]) for i, (a, b) in enumerate(zip(far, near))]
     for copy in copies:
         copy.start()
@@ -54,7 +54,7 @@
     copies[0].wait()
     for r in range(rows):
         put_shifted(stack, r, cot[r], 1)
-    for copy in copies[1:4]:
+    for copy in copies[1:]:
         copy.wait()
     upper = lax.broadcasted_iota(jnp.int32, (cols, half), 0)
     spread = jnp.where(upper // 2 == lax.broadcasted_iota(jnp.int32, (cols, half), 1), 1.0, 0.0).astype(BF16)
@@ -64,7 +64,6 @@
         for r in (2 * q, 2 * q + 1):
             merged[r * cols : (r + 1) * cols, :] = (lateral[r * cols : (r + 1) * cols] + lifted).astype(BF16)
     merged_t[...] = jnp.transpose(merged[...])
-    copies[4].wait()
 
 
 def strips_of(stack, halo):
@@ -89,7 +88,10 @@
     theirs[rows, :] = jnp.where(here == 0, values[:, half:], values[:, :half]).astype(BF16)
 
 
-def kernel_grad_kernel(peers, stack, merged, merged_t, before, after, halo, *outs):
+def kernel_grad_kernel(peers, stack, merged, merged_t, before, after, taps_far, out_w, halo, *refs):
+    outs, sem = refs[:-1], refs[-1]
+    copy = pltpu.make_async_copy(taps_far, out_w, sem)
+    copy.start()
     cols = stack.shape[1]
     channels, cells = merged_t.shape
     put_halo(halo, before[before.shape[0] - 1], after[0], 0, peers, 1)
@@ -103,6 +105,7 @@
         part = jnp.dot(merged_t[...], strip, preferred_element_type=F32)
         for j in range(3):
             put_sums(outs, (3 * i + j) * channels, part[:, j * channels : (j + 1) * channels])
+    copy.wait()
 
 
 def data_grad_kernel(stack, halo, feat, out_w, grad, *outs):
@@ -152,7 +155,7 @@
 def cut_kernel(mine, got, *refs):
     place, _ = places()
     share = mine.shape[0] // 4
-    for k, out in zip((0, 3, 2, 1), refs[-4:]):
+    for k, out in zip((0, 2, 3, 1), refs[-4:]):
         rows = block(place ^ k, share)
         start = out.shape[0] - share
         if start:
@@ -160,36 +163,36 @@
         out[start:, :] = (mine[rows, :] + got[rows, :].astype(F32)).astype(out.dtype)
 
 
-def add_early_kernel(own, three, two, out):
+def add_early_kernel(own, two, three, out):
     out[...] = own[...] + three[...].astype(F32) + two[...].astype(F32)
 
 
-def add_kernel(part_a, own_b, one, three_b, two_b, out):
+def add_kernel(part_a, own_b, one, two_b, three_b, out):
     edge = part_a.shape[0]
     out[:edge, :] = (part_a[...] + one[:edge, :].astype(F32)).astype(BF16)
     total = own_b[...] + one[edge:, :].astype(F32) + two_b[...].astype(F32) + three_b[...].astype(F32)
     out[edge:, :] = total.astype(BF16)
 
 
-def finish_kernel(scale, own, one, two, three, _, out):
+def finish_kernel(scale, own, one, three, two, _, out):
     near = own[...].astype(F32) + one[...].astype(F32)
     far = two[...].astype(F32) + three[...].astype(F32)
     out[...] = ((near + far) * scale).astype(BF16)
 
 
-def place_kernel(*refs):
-    results, sems = refs[8:10], refs[10]
+def place_kernel(pair, *refs):
+    results, sems = refs[-3:-1], refs[-1]
     side = lax.axis_index("space")
+    columns, place = (1 - side, places()[1]) if pair else (side, places()[0])
+    lanes = pl.ds(pl.multiple_of(columns * 128, 128), 128)
     copies = []
-    for columns, quarters, place in zip((side, 1 - side), (refs[:4], refs[4:8]), places()):
-        lanes = pl.ds(pl.multiple_of(columns * 128, 128), 128)
-        for k, quarter in enumerate(quarters):
-            start = 0
-            for result in results:
-                share = result.shape[0] // 4
-                to = result.at[block(place ^ k, share), lanes]
-                copies.append(pltpu.make_async_copy(quarter.at[pl.ds(start, share), :], to, sems.at[len(copies)]))
-                start += share
+    for k, quarter in zip((0, 1, 3, 2), refs):
+        start = 0
+        for result in results:
+            share = result.shape[0] // 4
+            to = result.at[block(place ^ k, share), lanes]
+            copies.append(pltpu.make_async_copy(quarter.at[pl.ds(start, share), :], to, sems.at[len(copies)]))
+            start += share
     for copy in copies:
         copy.start()
     for copy in copies:
@@ -223,24 +226,23 @@
     vmem, far = pl.BlockSpec(memory_space=pltpu.VMEM), pl.BlockSpec(memory_space=pltpu.HBM)
     after = pltpu.with_memory_space_constraint(after, pltpu.HBM)
     share_a, share_b, quarter = [(length // 4, width) for length in (*lengths, sum(lengths))]
-    own_a, three, two, one_a = call(cut_kernel, (share_a, F32), *[(share_a, BF16)] * 3)(*parts[0])
-    three, two = exchange(three, 0, 3), exchange(two, 0, 2)
+    own_a, two, three, one_a = call(cut_kernel, (share_a, F32), *[(share_a, BF16)] * 3)(*parts[0])
+    two, three = exchange(two, 0, 2), exchange(three, 0, 3)
     slow = pl.CostEstimate(flops=3 * 2**28, bytes_accessed=2**10, transcendentals=0)
-    [part_a] = call(add_early_kernel, (share_a, F32), cost_estimate=slow)(own_a, three, two)
-    own_b, three, two, one = call(cut_kernel, (share_b, F32), *[(share_b, BF16)] * 2, (quarter, BF16))(*parts[1], one_a)
-    one, three, two = exchange(one, 0, 1), exchange(three, 0, 3), exchange(two, 0, 2)
-    [total] = call(add_kernel, (quarter, BF16))(part_a, own_b, one, three, two)
-    three, two, one = [exchange(total, 1, k) for k in (3, 2, 1)]
+    [part_a] = call(add_early_kernel, (share_a, F32), cost_estimate=slow)(own_a, two, three)
+    own_b, two, three, one = call(cut_kernel, (share_b, F32), *[(share_b, BF16)] * 2, (quarter, BF16))(*parts[1], one_a)
+    one, two, three = exchange(one, 0, 1), exchange(two, 0, 2), exchange(three, 0, 3)
+    [total] = call(add_kernel, (quarter, BF16))(part_a, own_b, one, two, three)
+    two, three, one = [exchange(total, 1, k) for k in (2, 3, 1)]
     finish = call(functools.partial(finish_kernel, scale), (quarter, BF16), in_specs=[vmem] * 4 + [far])
-    [total] = finish(total, one, two, three, after)
-    three, two, one = [exchange(total, 0, k) for k in (3, 2, 1)]
-    quarters = [total, one, two, three]
-    return call(
-        place_kernel,
-        *[((length, 2 * width), BF16) for length in lengths],
-        out_specs=[far] * 2,
-        scratch_shapes=[pltpu.SemaphoreType.DMA((16,))],
-    )(*quarters, *[swap(one) for one in quarters])
+    [total] = finish(total, one, three, two, after)
+    two, three, one = [exchange(total, 0, k) for k in (2, 3, 1)]
+    quarters = [total, one, three, two]
+    results = [((length, 2 * width), BF16) for length in lengths]
+    place = dict(out_specs=[far] * 2, scratch_shapes=[pltpu.SemaphoreType.DMA((8,))])
+    half = call(functools.partial(place_kernel, False), *results, **place)(*quarters)
+    place.update(in_specs=[vmem] * 4 + [far] * 2, input_output_aliases={4: 0, 5: 1})
+    return call(functools.partial(place_kernel, True), *results, **place)(*[swap(one) for one in quarters], *half)
 
 
 def local(features, top_down, lateral_weight, out_kernel, cotangent):
@@ -266,7 +268,7 @@
         cot_before, cot_after = neighbour_rows(cot)
         arrays = (cot, lateral_weight, top_down[image], features[image].reshape(cells, in_channels), taps)
         arrays = [pltpu.with_memory_space_constraint(array, pltpu.HBM) for array in arrays]
-        merged, merged_t, stack, near_feat, near_taps = pl.pallas_call(
+        merged, merged_t, stack, near_feat = pl.pallas_call(
             merge_kernel,
             out_shape=[
                 jax.ShapeDtypeStruct(shape, BF16)
@@ -275,24 +277,29 @@
                     (channels, cells),
                     (rows, cols, 3 * channels),
                     (cells, in_channels),
-                    taps.shape,
                 )
             ],
-            in_specs=[pl.BlockSpec(memory_space=pltpu.HBM)] * 5,
-            scratch_shapes=[*[pltpu.VMEM(array.shape, BF16) for array in arrays[:3]], pltpu.SemaphoreType.DMA((5,))],
+            in_specs=[pl.BlockSpec(memory_space=pltpu.HBM)] * 4,
+            scratch_shapes=[*[pltpu.VMEM(array.shape, BF16) for array in arrays[:3]], pltpu.SemaphoreType.DMA((4,))],
             compiler_params=params,
             cost_estimate=pl.CostEstimate(
                 flops=2 * cells * channels * 4 * in_channels, bytes_accessed=4 * 2**20, transcendentals=0
             ),
-        )(*arrays)
-        halo, *kernel_part = pl.pallas_call(
+        )(*arrays[:4])
+        near_taps, halo, *kernel_part = pl.pallas_call(
             functools.partial(kernel_grad_kernel, peers),
-            out_shape=[jax.ShapeDtypeStruct((2, cols, 3 * channels), BF16), *sums(9 * channels, 2 * cols)],
+            out_shape=[
+                jax.ShapeDtypeStruct(taps.shape, BF16),
+                jax.ShapeDtypeStruct((2, cols, 3 * channels), BF16),
+                *sums(9 * channels, 2 * cols),
+            ],
+            in_specs=[pl.BlockSpec(memory_space=pltpu.VMEM)] * 5 + [pl.BlockSpec(memory_space=pltpu.HBM)],
+            scratch_shapes=[pltpu.SemaphoreType.DMA],
             compiler_params=params,
             cost_estimate=pl.CostEstimate(
                 flops=2 * cells * channels * 9 * channels, bytes_accessed=4 * 2**20, transcendentals=0
             ),
-        )(stack, merged, merged_t, cot_before, cot_after)
+        )(stack, merged, merged_t, cot_before, cot_after, arrays[4])
         if halves:
             kernel_part[1] = swap(kernel_part[1])
         grad, *lateral_part = pl.pallas_call(

time: 41.7 us -> 41.7 us (level)
  Pallas kernels: 8.77 us -> 9.57 us
  waiting for transfers between devices: 14.8 us -> 14.2 us
    ppermute x6, waiting for transfers between devices: 1.17 us -> 0.48 us  [swap(): return lax.ppermute(array, 'space', [(0, 1), (1, 0)])]
    pallas_call x3 -> x4, Pallas kernels: 1.36 us -> 1.97 us  [the longest x1 0.91 us: sum_everywhere(): call(functools.partial(place_kernel, False), *results, **place)(*quarters)]
  transfers between devices with their start and end apart: 18 -> 18, of which waited for: 9 -> 8; matrix products, arithmetic and copies ran while one was open for 0% -> 0% of each run, Pallas kernels for 15% -> 17%
where the time goes in v11:
time: 41.7 us; the launch traced here: 41.5 us
  starting transfers between devices  17.1 us (41%)
  waiting for transfers between devices  14.2 us (34%)
  Pallas kernels  9.57 us (23%)
  between operations  0.74 us (2%)
    ppermute x11, starting transfers between devices, exchange(): return lax.ppermute(array, ('dp', 'space'), pairs)  15.4 us
    ppermute x11, waiting for transfers between devices, exchange(): return lax.ppermute(array, ('dp', 'space'), pairs)  13.7 us
    pallas_call x1, Pallas kernels, local(): pl.pallas_call(functools.partial(forward_kernel, peers), out_shape=[jax.S...  2.53 us
    pallas_call x1, Pallas kernels, local(): pl.pallas_call(merge_kernel, out_shape=[jax.ShapeDtypeStruct(shape, BF16)...  1.89 us
    pallas_call x1, Pallas kernels, local(): pl.pallas_call(data_grad_kernel, out_shape=[jax.ShapeDtypeStruct((cells,...  1.7 us
    pallas_call x1, Pallas kernels, local(): pl.pallas_call(functools.partial(kernel_grad_kernel, peers), out_shape=[j...  1.3 us
    ppermute x6, starting transfers between devices, swap(): return lax.ppermute(array, 'space', [(0, 1), (1, 0)])  1.16 us
    pallas_call x1, Pallas kernels, sum_everywhere(): call(functools.partial(place_kernel, False), *results, **place)(*quarters)  0.91 us
  transfers between devices with their start and end apart: 18, of which 8 were waited for; matrix products, arithmetic and copies ran while one was open for 0% of the time, Pallas kernels for 17%

profile of v11, /device:TPU:0, one launch (start us, length us, event | category | flops | bytes accessed | tf_op | source)
XLA Modules:
  0.0 41.5 jit_solution(17475819924491340694)
XLA Ops:
  0.6 0.5 %collective-permute-start = (bf16[8,96,256]{2,1,0:T(8,128)(2,1)}, bf16[8,96,256]{2,1,0:T(8,128)(2,1)S(1)}, u32[]{:S(2)}, u32[]{:S(2)}) collective-permute-start(bf16[8,96,256]{2,1,0:T(8,128)(2,1)} %bitcast.13), channel_id=1, source_target_pairs={{0,1},{1,0},{2,3},{3,2},{4,5},{5,4},{6,7},{7,6},{8,9},{9,8},{10,11... | collective-permute-start | bytes 1179656 | tf_op jit(solution)/shard_map/ppermute | solution.py:19
  1.1 1.9 %shard_map.84 = (bf16[768,256]{1,0:T(8,128)(2,1)S(1)}, bf16[256,768]{1,0:T(8,128)(2,1)S(1)}, bf16[8,96,768]{2,1,0:T(8,128)(2,1)S(1)}, bf16[768,512]{1,0:T(8,128)(2,1)S(1)}) custom-call(bf16[8,96,256]{2,1,0:T(8,128)(2,1)} %bitcast.14, bf16[512,256]{1,0:T(8,128)(2,1)} %refs_1_.1, bf16[4,48,256]{2,1,0:T(8,128)(2,1)} %bitcast.15, bf16[768,512]{1,0:T(8,128)(2,1)} %bitcast.12), custom_call_target="tpu_custom_call" | custom-call | flops 805306368 | bytes 4194304 | tf_op jit(solution)/shard_map/pallas_call | solution.py:271
  3.1 0.0 collective-permute-done.before.after
  3.1 1.3 %shard_map.85 = (bf16[9,256,256]{2,1,0:T(8,128)(2,1)S(1)}, bf16[2,96,768]{2,1,0:T(8,128)(2,1)S(1)}, f32[2304,128]{1,0:T(8,128)S(1)}, bf16[2496,128]{1,0:T(8,128)(2,1)S(1)}) custom-call(bf16[8,96,768]{2,1,0:T(8,128)(2,1)S(1)} %get-tuple-element.30.stack, bf16[768,256]{1,0:T(8,128)(2,1)S(1)} %get-tuple-element.29.merged, ...), custom_call_target="tpu_custom_call" | custom-call | flops 905969664 | bytes 4194304 | tf_op jit(solution)/shard_map/pallas_call | solution.py:289
  4.4 0.1 collective-permute-start.1
  4.5 1.7 %shard_map.86 = (bf16[768,256]{1,0:T(8,128)(2,1)S(1)}, f32[512,128]{1,0:T(8,128)S(1)}, bf16[512,128]{1,0:T(8,128)(2,1)S(1)}) custom-call(bf16[8,96,768]{2,1,0:T(8,128)(2,1)S(1)} %get-tuple-element.30.stack, bf16[2,96,768]{2,1,0:T(8,128)(2,1)S(1)} %get-tuple-element.33.halo, bf16[768,512]{1,0:T(8,128)(2,1)S(1)} %get-tuple-element.34.feat, ...), custom_call_target="tpu_custom_call" | custom-call | flops 1107296256 | bytes 4194304 | tf_op jit(solution)/shard_map/pallas_call | solution.py:305
  6.2 0.5 %collective-permute-start.4 = (bf16[512,128]{1,0:T(8,128)(2,1)S(1)}, bf16[512,128]{1,0:T(8,128)(2,1)S(1)}, u32[]{:S(2)}, u32[]{:S(2)}) collective-permute-start(bf16[512,128]{1,0:T(8,128)(2,1)S(1)} %get-tuple-element.44), channel_id=1, source_target_pairs={{0,1},{1,0},{2,3},{3,2},{4,5},{5,4},{6,7},{7,6},{8,9},{9,8},{10,11... | collective-permute-start | bytes 393224 | tf_op jit(solution)/shard_map/ppermute | solution.py:212
  6.7 0.1 shard_map.88
  6.8 2.6 %collective-permute-start.2 = (bf16[576,128]{1,0:T(8,128)(2,1)S(1)}, bf16[576,128]{1,0:T(8,128)(2,1)S(1)}, u32[]{:S(2)}, u32[]{:S(2)}) collective-permute-start(bf16[576,128]{1,0:T(8,128)(2,1)S(1)} %get-tuple-element.41), channel_id=1, source_target_pairs={{0,4},{1,17},{2,6},{3,19},{4,0},{5,21},{6,2},{7,23},{8,12},{9,25},... | collective-permute-start | bytes 442376 | tf_op jit(solution)/shard_map/ppermute | solution.py:208
  9.4 1.4 %collective-permute-start.3 = (bf16[576,128]{1,0:T(8,128)(2,1)S(1)}, bf16[576,128]{1,0:T(8,128)(2,1)S(1)}, u32[]{:S(2)}, u32[]{:S(2)}) collective-permute-start(bf16[576,128]{1,0:T(8,128)(2,1)S(1)} %get-tuple-element.42), channel_id=1, source_target_pairs={{0,6},{1,25},{2,4},{3,27},{4,2},{5,29},{6,0},{7,31},{8,14},{9,17},... | collective-permute-start | bytes 442376 | tf_op jit(solution)/shard_map/ppermute | solution.py:208
  10.9 0.2 collective-permute-start.5
  11.1 1.9 %collective-permute-start.6 = (bf16[128,128]{1,0:T(8,128)(2,1)S(1)}, bf16[128,128]{1,0:T(8,128)(2,1)S(1)}, u32[]{:S(2)}, u32[]{:S(2)}) collective-permute-start(bf16[128,128]{1,0:T(8,128)(2,1)S(1)} %get-tuple-element.48), channel_id=1, source_target_pairs={{0,4},{1,17},{2,6},{3,19},{4,0},{5,21},{6,2},{7,23},{8,12},{9,25},... | collective-permute-start | bytes 98312 | tf_op jit(solution)/shard_map/ppermute | solution.py:208
  13.0 1.4 %collective-permute-start.7 = (bf16[128,128]{1,0:T(8,128)(2,1)S(1)}, bf16[128,128]{1,0:T(8,128)(2,1)S(1)}, u32[]{:S(2)}, u32[]{:S(2)}) collective-permute-start(bf16[128,128]{1,0:T(8,128)(2,1)S(1)} %get-tuple-element.49), channel_id=1, source_target_pairs={{0,6},{1,25},{2,4},{3,27},{4,2},{5,29},{6,0},{7,31},{8,14},{9,17},... | collective-permute-start | bytes 98312 | tf_op jit(solution)/shard_map/ppermute | solution.py:208
  14.5 1.1 %collective-permute-done.3.three = bf16[576,128]{1,0:T(8,128)(2,1)S(1)} collective-permute-done((bf16[576,128]{1,0:T(8,128)(2,1)S(1)}, bf16[576,128]{1,0:T(8,128)(2,1)S(1)}, u32[]{:S(2)}, u32[]{:S(2)}) %collective-permute-start.3) | collective-permute-done | bytes 147488 | tf_op jit(solution)/shard_map/ppermute | solution.py:208
  15.6 0.2 collective-permute-done.6.two_b
  15.8 2.0 %collective-permute-done.7.three_b = bf16[128,128]{1,0:T(8,128)(2,1)S(1)} collective-permute-done((bf16[128,128]{1,0:T(8,128)(2,1)S(1)}, bf16[128,128]{1,0:T(8,128)(2,1)S(1)}, u32[]{:S(2)}, u32[]{:S(2)}) %collective-permute-start.7) | collective-permute-done | bytes 32800 | tf_op jit(solution)/shard_map/ppermute | solution.py:208
  17.9 2.7 %collective-permute-start.10 = (bf16[704,128]{1,0:T(8,128)(2,1)S(1)}, bf16[704,128]{1,0:T(8,128)(2,1)S(1)}, u32[]{:S(2)}, u32[]{:S(2)}) collective-permute-start(bf16[704,128]{1,0:T(8,128)(2,1)S(1)} %shard_map.91.own), channel_id=1, source_target_pairs={{0,16},{1,5},{2,18},{3,7},{4,20},{5,1},{6,22},{7,3},{8,24},{9,13},... | collective-permute-start | bytes 540680 | tf_op jit(solution)/shard_map/ppermute | solution.py:208
  20.6 1.3 %collective-permute-start.9 = (bf16[704,128]{1,0:T(8,128)(2,1)S(1)}, bf16[704,128]{1,0:T(8,128)(2,1)S(1)}, u32[]{:S(2)}, u32[]{:S(2)}) collective-permute-start(bf16[704,128]{1,0:T(8,128)(2,1)S(1)} %shard_map.91.own), channel_id=1, source_target_pairs={{0,24},{1,7},{2,26},{3,5},{4,28},{5,3},{6,30},{7,1},{8,16},{9,15},... | collective-permute-start | bytes 540680 | tf_op jit(solution)/shard_map/ppermute | solution.py:208
  21.9 0.2 collective-permute-start.8
  22.1 2.5 %shard_map.87 = (bf16[8,96,256]{2,1,0:T(8,128)(2,1)}, bf16[4,48,256]{2,1,0:T(8,128)(2,1)}) custom-call(bf16[8,96,256]{2,1,0:T(8,128)(2,1)S(1)} %bitcast.8, bf16[9,256,256]{2,1,0:T(8,128)(2,1)S(1)} %get-tuple-element.32.out_w, bf16[768,256]{1,0:T(8,128)(2,1)S(1)} %get-tuple-element.35.grad, bf16[2496,128]{1,0:T(8,128)(2,1)S(1)} %collective-permute-done.1.refs_0_.got), custom_call_target="tpu_custom_call" | custom-call | flops 905969664 | bytes 2097152 | tf_op jit(solution)/shard_map/pallas_call | solution.py:317
  24.7 3.6 %collective-permute-done.10.two = bf16[704,128]{1,0:T(8,128)(2,1)S(1)} collective-permute-done((bf16[704,128]{1,0:T(8,128)(2,1)S(1)}, bf16[704,128]{1,0:T(8,128)(2,1)S(1)}, u32[]{:S(2)}, u32[]{:S(2)}) %collective-permute-start.10) | collective-permute-done | bytes 180256 | tf_op jit(solution)/shard_map/ppermute | solution.py:208
  28.3 1.8 %collective-permute-done.8.one = bf16[704,128]{1,0:T(8,128)(2,1)S(1)} collective-permute-done((bf16[704,128]{1,0:T(8,128)(2,1)S(1)}, bf16[704,128]{1,0:T(8,128)(2,1)S(1)}, u32[]{:S(2)}, u32[]{:S(2)}) %collective-permute-start.8) | collective-permute-done | bytes 180256 | tf_op jit(solution)/shard_map/ppermute | solution.py:208
  30.2 0.1 shard_map.92.refs_0_
  30.3 0.5 %collective-permute-start.16 = (bf16[704,128]{1,0:T(8,128)(2,1)S(1)}, bf16[704,128]{1,0:T(8,128)(2,1)S(1)}, u32[]{:S(2)}, u32[]{:S(2)}) collective-permute-start(bf16[704,128]{1,0:T(8,128)(2,1)S(1)} %shard_map.92.refs_0_), channel_id=1, source_target_pairs={{0,4},{1,17},{2,6},{3,19},{4,0},{5,21},{6,2},{7,23},{8,12},{9,25},... | collective-permute-start | bytes 540680 | tf_op jit(solution)/shard_map/ppermute | solution.py:208
  30.8 2.5 %collective-permute-start.14 = (bf16[704,128]{1,0:T(8,128)(2,1)S(1)}, bf16[704,128]{1,0:T(8,128)(2,1)S(1)}, u32[]{:S(2)}, u32[]{:S(2)}) collective-permute-start(bf16[704,128]{1,0:T(8,128)(2,1)S(1)} %shard_map.92.refs_0_), channel_id=1, source_target_pairs={{0,6},{1,25},{2,4},{3,27},{4,2},{5,29},{6,0},{7,31},{8,14},{9,17},... | collective-permute-start | bytes 540680 | tf_op jit(solution)/shard_map/ppermute | solution.py:208
  33.3 0.5 %collective-permute-start.12 = (bf16[704,128]{1,0:T(8,128)(2,1)S(1)}, bf16[704,128]{1,0:T(8,128)(2,1)S(1)}, u32[]{:S(2)}, u32[]{:S(2)}) collective-permute-start(bf16[704,128]{1,0:T(8,128)(2,1)S(1)} %shard_map.92.refs_0_), channel_id=1, source_target_pairs={{0,2},{1,9},{2,0},{3,11},{4,6},{5,13},{6,4},{7,15},{8,10},{9,1},{1... | collective-permute-start | bytes 540680 | tf_op jit(solution)/shard_map/ppermute | solution.py:208
  33.8 3.9 %collective-permute-done.16.refs_3_ = bf16[704,128]{1,0:T(8,128)(2,1)S(1)} collective-permute-done((bf16[704,128]{1,0:T(8,128)(2,1)S(1)}, bf16[704,128]{1,0:T(8,128)(2,1)S(1)}, u32[]{:S(2)}, u32[]{:S(2)}) %collective-permute-start.16) | collective-permute-done | bytes 180256 | tf_op jit(solution)/shard_map/ppermute | solution.py:208
  37.8 0.5 %collective-permute-start.15 = (bf16[704,128]{1,0:T(8,128)(2,1)S(1)}, bf16[704,128]{1,0:T(8,128)(2,1)S(1)}, u32[]{:S(2)}, u32[]{:S(2)}) collective-permute-start(bf16[704,128]{1,0:T(8,128)(2,1)S(1)} %collective-permute-done.14.refs_2_), channel_id=1, source_target_pairs={{0,1},{1,0},{2,3},{3,2},{4,5},{5,4},{6,7},{7,6},{8,9},{9,8},{10,11... | collective-permute-start | bytes 540680 | tf_op jit(solution)/shard_map/ppermute | solution.py:212
  38.3 0.9 %collective-permute-done.12.refs_1_ = bf16[704,128]{1,0:T(8,128)(2,1)S(1)} collective-permute-done((bf16[704,128]{1,0:T(8,128)(2,1)S(1)}, bf16[704,128]{1,0:T(8,128)(2,1)S(1)}, u32[]{:S(2)}, u32[]{:S(2)}) %collective-permute-start.12) | collective-permute-done | bytes 180256 | tf_op jit(solution)/shard_map/ppermute | solution.py:208
  39.2 0.9 %shard_map.93 = (bf16[2304,256]{1,0:T(8,128)(2,1)}, bf16[512,256]{1,0:T(8,128)(2,1)}) custom-call(bf16[704,128]{1,0:T(8,128)(2,1)S(1)} %shard_map.92.refs_0_, bf16[704,128]{1,0:T(8,128)(2,1)S(1)} %collective-permute-done.12.refs_1_, bf16[704,128]{1,0:T(8,128)(2,1)S(1)} %collective-permute-done.14.refs_2_, bf16[704,128]{1,0:T(8,128)(2,1)S(1)} %collective-permute-done.16.refs_3_), custom_call_target="tpu_custom_call" | custom-call | tf_op jit(solution)/shard_map/pallas_call | solution.py:243
  40.2 0.5 %collective-permute-done.13.refs_1_ = bf16[704,128]{1,0:T(8,128)(2,1)S(1)} collective-permute-done((bf16[704,128]{1,0:T(8,128)(2,1)S(1)}, bf16[704,128]{1,0:T(8,128)(2,1)S(1)}, u32[]{:S(2)}, u32[]{:S(2)}) %collective-permute-start.13) | collective-permute-done | bytes 180256 | tf_op jit(solution)/shard_map/ppermute | solution.py:212
  40.6 0.9 %shard_map.94 = (bf16[2304,256]{1,0:T(8,128)(2,1)}, bf16[512,256]{1,0:T(8,128)(2,1)}) custom-call(bf16[704,128]{1,0:T(8,128)(2,1)S(1)} %collective-permute-done.11.refs_0_, bf16[704,128]{1,0:T(8,128)(2,1)S(1)} %collective-permute-done.13.refs_1_, bf16[704,128]{1,0:T(8,128)(2,1)S(1)} %collective-permute-done.15.refs_2_, ...), custom_call_target="tpu_custom_call", output_to_operand_aliasing={{0}: (4, {}), {1}: (5, {})} | custom-call | tf_op jit(solution)/shard_map/pallas_call | solution.py:245
  (15 shorter events, 0.2 us)
Async XLA Ops:
  0.6 2.4 %collective-permute-start = (bf16[8,96,256]{2,1,0:T(8,128)(2,1)}, bf16[8,96,256]{2,1,0:T(8,128)(2,1)S(1)}, u32[]{:S(2)}, u32[]{:S(2)}) collective-permute-start(bf16[8,96,256]{2,1,0:T(8,128)(2,1)} %bitcast.13), channel_id=1, source_target_pairs={{0,1},{1,0},{2,3},{3,2},{4,5},{5,4},{6,7},{7,6},{8,9},{9,8},{10,11... | collective-permute-start | bytes 1179656 | tf_op jit(solution)/shard_map/ppermute | solution.py:19
  4.4 2.3 %collective-permute-start.1 = (bf16[2496,128]{1,0:T(8,128)(2,1)S(1)}, bf16[2496,128]{1,0:T(8,128)(2,1)S(1)}, u32[]{:S(2)}, u32[]{:S(2)}) collective-permute-start(bf16[2496,128]{1,0:T(8,128)(2,1)S(1)} %get-tuple-element.36), channel_id=1, source_target_pairs={{0,1},{1,0},{2,3},{3,2},{4,5},{5,4},{6,7},{7,6},{8,9},{9,8},{10,11... | collective-permute-start | bytes 1916936 | tf_op jit(solution)/shard_map/ppermute | solution.py:212
  6.2 4.7 %collective-permute-start.4 = (bf16[512,128]{1,0:T(8,128)(2,1)S(1)}, bf16[512,128]{1,0:T(8,128)(2,1)S(1)}, u32[]{:S(2)}, u32[]{:S(2)}) collective-permute-start(bf16[512,128]{1,0:T(8,128)(2,1)S(1)} %get-tuple-element.44), channel_id=1, source_target_pairs={{0,1},{1,0},{2,3},{3,2},{4,5},{5,4},{6,7},{7,6},{8,9},{9,8},{10,11... | collective-permute-start | bytes 393224 | tf_op jit(solution)/shard_map/ppermute | solution.py:212
  6.8 7.7 %collective-permute-start.2 = (bf16[576,128]{1,0:T(8,128)(2,1)S(1)}, bf16[576,128]{1,0:T(8,128)(2,1)S(1)}, u32[]{:S(2)}, u32[]{:S(2)}) collective-permute-start(bf16[576,128]{1,0:T(8,128)(2,1)S(1)} %get-tuple-element.41), channel_id=1, source_target_pairs={{0,4},{1,17},{2,6},{3,19},{4,0},{5,21},{6,2},{7,23},{8,12},{9,25},... | collective-permute-start | bytes 442376 | tf_op jit(solution)/shard_map/ppermute | solution.py:208
  9.4 6.1 %collective-permute-start.3 = (bf16[576,128]{1,0:T(8,128)(2,1)S(1)}, bf16[576,128]{1,0:T(8,128)(2,1)S(1)}, u32[]{:S(2)}, u32[]{:S(2)}) collective-permute-start(bf16[576,128]{1,0:T(8,128)(2,1)S(1)} %get-tuple-element.42), channel_id=1, source_target_pairs={{0,6},{1,25},{2,4},{3,27},{4,2},{5,29},{6,0},{7,31},{8,14},{9,17},... | collective-permute-start | bytes 442376 | tf_op jit(solution)/shard_map/ppermute | solution.py:208
  10.9 6.9 %collective-permute-start.5 = (bf16[704,128]{1,0:T(8,128)(2,1)S(1)}, bf16[704,128]{1,0:T(8,128)(2,1)S(1)}, u32[]{:S(2)}, u32[]{:S(2)}) collective-permute-start(bf16[704,128]{1,0:T(8,128)(2,1)S(1)} %get-tuple-element.47), channel_id=1, source_target_pairs={{0,2},{1,9},{2,0},{3,11},{4,6},{5,13},{6,4},{7,15},{8,10},{9,1},{1... | collective-permute-start | bytes 540680 | tf_op jit(solution)/shard_map/ppermute | solution.py:208
  11.1 4.7 %collective-permute-start.6 = (bf16[128,128]{1,0:T(8,128)(2,1)S(1)}, bf16[128,128]{1,0:T(8,128)(2,1)S(1)}, u32[]{:S(2)}, u32[]{:S(2)}) collective-permute-start(bf16[128,128]{1,0:T(8,128)(2,1)S(1)} %get-tuple-element.48), channel_id=1, source_target_pairs={{0,4},{1,17},{2,6},{3,19},{4,0},{5,21},{6,2},{7,23},{8,12},{9,25},... | collective-permute-start | bytes 98312 | tf_op jit(solution)/shard_map/ppermute | solution.py:208
  13.0 4.8 %collective-permute-start.7 = (bf16[128,128]{1,0:T(8,128)(2,1)S(1)}, bf16[128,128]{1,0:T(8,128)(2,1)S(1)}, u32[]{:S(2)}, u32[]{:S(2)}) collective-permute-start(bf16[128,128]{1,0:T(8,128)(2,1)S(1)} %get-tuple-element.49), channel_id=1, source_target_pairs={{0,6},{1,25},{2,4},{3,27},{4,2},{5,29},{6,0},{7,31},{8,14},{9,17},... | collective-permute-start | bytes 98312 | tf_op jit(solution)/shard_map/ppermute | solution.py:208
  17.9 10.4 %collective-permute-start.10 = (bf16[704,128]{1,0:T(8,128)(2,1)S(1)}, bf16[704,128]{1,0:T(8,128)(2,1)S(1)}, u32[]{:S(2)}, u32[]{:S(2)}) collective-permute-start(bf16[704,128]{1,0:T(8,128)(2,1)S(1)} %shard_map.91.own), channel_id=1, source_target_pairs={{0,16},{1,5},{2,18},{3,7},{4,20},{5,1},{6,22},{7,3},{8,24},{9,13},... | collective-permute-start | bytes 540680 | tf_op jit(solution)/shard_map/ppermute | solution.py:208
  20.6 7.8 %collective-permute-start.9 = (bf16[704,128]{1,0:T(8,128)(2,1)S(1)}, bf16[704,128]{1,0:T(8,128)(2,1)S(1)}, u32[]{:S(2)}, u32[]{:S(2)}) collective-permute-start(bf16[704,128]{1,0:T(8,128)(2,1)S(1)} %shard_map.91.own), channel_id=1, source_target_pairs={{0,24},{1,7},{2,26},{3,5},{4,28},{5,3},{6,30},{7,1},{8,16},{9,15},... | collective-permute-start | bytes 540680 | tf_op jit(solution)/shard_map/ppermute | solution.py:208
  21.9 8.2 %collective-permute-start.8 = (bf16[704,128]{1,0:T(8,128)(2,1)S(1)}, bf16[704,128]{1,0:T(8,128)(2,1)S(1)}, u32[]{:S(2)}, u32[]{:S(2)}) collective-permute-start(bf16[704,128]{1,0:T(8,128)(2,1)S(1)} %shard_map.91.own), channel_id=1, source_target_pairs={{0,8},{1,3},{2,10},{3,1},{4,12},{5,7},{6,14},{7,5},{8,0},{9,11},{1... | collective-permute-start | bytes 540680 | tf_op jit(solution)/shard_map/ppermute | solution.py:208
  30.3 7.5 %collective-permute-start.16 = (bf16[704,128]{1,0:T(8,128)(2,1)S(1)}, bf16[704,128]{1,0:T(8,128)(2,1)S(1)}, u32[]{:S(2)}, u32[]{:S(2)}) collective-permute-start(bf16[704,128]{1,0:T(8,128)(2,1)S(1)} %shard_map.92.refs_0_), channel_id=1, source_target_pairs={{0,4},{1,17},{2,6},{3,19},{4,0},{5,21},{6,2},{7,23},{8,12},{9,25},... | collective-permute-start | bytes 540680 | tf_op jit(solution)/shard_map/ppermute | solution.py:208
  30.8 7.0 %collective-permute-start.14 = (bf16[704,128]{1,0:T(8,128)(2,1)S(1)}, bf16[704,128]{1,0:T(8,128)(2,1)S(1)}, u32[]{:S(2)}, u32[]{:S(2)}) collective-permute-start(bf16[704,128]{1,0:T(8,128)(2,1)S(1)} %shard_map.92.refs_0_), channel_id=1, source_target_pairs={{0,6},{1,25},{2,4},{3,27},{4,2},{5,29},{6,0},{7,31},{8,14},{9,17},... | collective-permute-start | bytes 540680 | tf_op jit(solution)/shard_map/ppermute | solution.py:208
  33.3 5.9 %collective-permute-start.12 = (bf16[704,128]{1,0:T(8,128)(2,1)S(1)}, bf16[704,128]{1,0:T(8,128)(2,1)S(1)}, u32[]{:S(2)}, u32[]{:S(2)}) collective-permute-start(bf16[704,128]{1,0:T(8,128)(2,1)S(1)} %shard_map.92.refs_0_), channel_id=1, source_target_pairs={{0,2},{1,9},{2,0},{3,11},{4,6},{5,13},{6,4},{7,15},{8,10},{9,1},{1... | collective-permute-start | bytes 540680 | tf_op jit(solution)/shard_map/ppermute | solution.py:208
  33.8 6.3 %collective-permute-start.11 = (bf16[704,128]{1,0:T(8,128)(2,1)S(1)}, bf16[704,128]{1,0:T(8,128)(2,1)S(1)}, u32[]{:S(2)}, u32[]{:S(2)}) collective-permute-start(bf16[704,128]{1,0:T(8,128)(2,1)S(1)} %shard_map.92.refs_0_), channel_id=1, source_target_pairs={{0,1},{1,0},{2,3},{3,2},{4,5},{5,4},{6,7},{7,6},{8,9},{9,8},{10,11... | collective-permute-start | bytes 540680 | tf_op jit(solution)/shard_map/ppermute | solution.py:212
  37.8 2.4 %collective-permute-start.17 = (bf16[704,128]{1,0:T(8,128)(2,1)S(1)}, bf16[704,128]{1,0:T(8,128)(2,1)S(1)}, u32[]{:S(2)}, u32[]{:S(2)}) collective-permute-start(bf16[704,128]{1,0:T(8,128)(2,1)S(1)} %collective-permute-done.16.refs_3_), channel_id=1, source_target_pairs={{0,1},{1,0},{2,3},{3,2},{4,5},{5,4},{6,7},{7,6},{8,9},{9,8},{10,11... | collective-permute-start | bytes 540680 | tf_op jit(solution)/shard_map/ppermute | solution.py:212
  37.8 2.4 %collective-permute-start.15 = (bf16[704,128]{1,0:T(8,128)(2,1)S(1)}, bf16[704,128]{1,0:T(8,128)(2,1)S(1)}, u32[]{:S(2)}, u32[]{:S(2)}) collective-permute-start(bf16[704,128]{1,0:T(8,128)(2,1)S(1)} %collective-permute-done.14.refs_2_), channel_id=1, source_target_pairs={{0,1},{1,0},{2,3},{3,2},{4,5},{5,4},{6,7},{7,6},{8,9},{9,8},{10,11... | collective-permute-start | bytes 540680 | tf_op jit(solution)/shard_map/ppermute | solution.py:212
  39.2 1.4 %collective-permute-start.13 = (bf16[704,128]{1,0:T(8,128)(2,1)S(1)}, bf16[704,128]{1,0:T(8,128)(2,1)S(1)}, u32[]{:S(2)}, u32[]{:S(2)}) collective-permute-start(bf16[704,128]{1,0:T(8,128)(2,1)S(1)} %collective-permute-done.12.refs_1_), channel_id=1, source_target_pairs={{0,1},{1,0},{2,3},{3,2},{4,5},{5,4},{6,7},{7,6},{8,9},{9,8},{10,11... | collective-permute-start | bytes 540680 | tf_op jit(solution)/shard_map/ppermute | solution.py:212

commit v12 on v11

--- a/solution.py
+++ b/solution.py
@@ -43,8 +43,8 @@
 
 
 def merge_kernel(*refs):
-    far, (merged, merged_t, stack, feat), near, sems = refs[:4], refs[4:8], refs[8:11], refs[11]
-    near = (*near, feat)
+    far, (merged, merged_t, stack, feat, out_w), near, sems = refs[:5], refs[5:10], refs[10:13], refs[13]
+    near = (*near, feat, out_w)
     copies = [pltpu.make_async_copy(a, b, sems.at[i]) for i, (a, b) in enumerate(zip(far, near))]
     for copy in copies:
         copy.start()
@@ -54,7 +54,7 @@
     copies[0].wait()
     for r in range(rows):
         put_shifted(stack, r, cot[r], 1)
-    for copy in copies[1:]:
+    for copy in copies[1:4]:
         copy.wait()
     upper = lax.broadcasted_iota(jnp.int32, (cols, half), 0)
     spread = jnp.where(upper // 2 == lax.broadcasted_iota(jnp.int32, (cols, half), 1), 1.0, 0.0).astype(BF16)
@@ -64,6 +64,7 @@
         for r in (2 * q, 2 * q + 1):
             merged[r * cols : (r + 1) * cols, :] = (lateral[r * cols : (r + 1) * cols] + lifted).astype(BF16)
     merged_t[...] = jnp.transpose(merged[...])
+    copies[4].wait()
 
 
 def strips_of(stack, halo):
@@ -88,27 +89,42 @@
     theirs[rows, :] = jnp.where(here == 0, values[:, half:], values[:, :half]).astype(BF16)
 
 
-def kernel_grad_kernel(peers, stack, merged, merged_t, before, after, taps_far, out_w, halo, *refs):
-    outs, sem = refs[:-1], refs[-1]
-    copy = pltpu.make_async_copy(taps_far, out_w, sem)
-    copy.start()
-    cols = stack.shape[1]
-    channels, cells = merged_t.shape
-    put_halo(halo, before[before.shape[0] - 1], after[0], 0, peers, 1)
-    if len(outs) == 2:
-        here = lax.axis_index("space")
-        edge = jnp.where(here == 0, merged[cells - cols :, :], merged[:cols, :])
-        start = 9 * channels
-        outs[1][start : start + cols, :] = edge[:, : channels // 2]
-        outs[1][start + cols :, :] = edge[:, channels // 2 :]
+def kernel_grad_kernel(stack, halo, merged_t, out):
+    channels = merged_t.shape[0]
     for i, strip in enumerate(strips_of(stack, halo)):
         part = jnp.dot(merged_t[...], strip, preferred_element_type=F32)
         for j in range(3):
-            put_sums(outs, (3 * i + j) * channels, part[:, j * channels : (j + 1) * channels])
-    copy.wait()
-
-
-def data_grad_kernel(stack, halo, feat, out_w, grad, *outs):
+            start = (3 * i + j) * channels
+            out[start : start + channels, :] = part[:, j * channels : (j + 1) * channels]
+
+
+def pair_kernel_grad_kernel(stack, merged_t, cot, merged, out, image):
+    here = lax.axis_index("space")
+    rows, cols, channels = cot.shape
+    half = channels // 2
+    zero = jnp.zeros((1, cols, 3 * half), BF16)
+    image[0:1] = zero
+    image[2 * rows + 1 :] = zero
+    own, other = 1 + rows * here, 1 + rows * (1 - here)
+    for r in range(rows):
+        row = cot[r]
+        put_shifted(image, other + r, jnp.where(here == 0, row[:, :half], row[:, half:]), 1)
+        for j in range(3):
+            start = j * channels
+            left, right = stack[r, :, start : start + half], stack[r, :, start + half : start + channels]
+            image[own + r, :, j * half : (j + 1) * half] = jnp.where(here == 0, left, right)
+    cells = []
+    for first in (own, other):
+        strips = [image[pl.ds(first + 1 - i, rows)].reshape(rows * cols, 3 * half) for i in range(3)]
+        cells.append(jnp.concatenate(strips, axis=1))
+    left = jnp.concatenate([merged_t[...], jnp.transpose(merged[...])], axis=1)
+    part = jnp.dot(left, jnp.concatenate(cells, axis=0), preferred_element_type=F32)
+    for tap in range(9):
+        out[tap * channels : (tap + 1) * channels, :] = part[:, tap * half : (tap + 1) * half]
+
+
+def data_grad_kernel(peers, stack, before, after, feat, out_w, grad, halo, *outs):
+    put_halo(halo, before[before.shape[0] - 1], after[0], 0, peers, 1)
     cells = jnp.concatenate(strips_of(stack, halo), axis=1)
     taps = jnp.concatenate([out_w[tap] for tap in range(9)], axis=1)
     total = lax.dot_general(cells, taps, (((1,), (1,)), ((), ())), preferred_element_type=F32)
@@ -122,12 +138,7 @@
     half = cols // 2
     for r in range(rows):
         put_shifted(stack, r + 1, merged[r], -1)
-    if len(edges) == 1:
-        start = edges[0].shape[0] - 2 * cols
-        edge = jnp.concatenate([edges[0][start : start + cols, :], edges[0][start + cols :, :]], axis=1)
-        put_halo(stack, edge, edge, rows, peers, -1)
-    else:
-        put_halo(stack, edges[0][edges[0].shape[0] - 1], edges[1][0], rows, peers, -1)
+    put_halo(stack, edges[0][edges[0].shape[0] - 1], edges[1][0], rows, peers, -1)
     cells = jnp.concatenate([stack[i : i + rows].reshape(rows * cols, 3 * channels) for i in range(3)], axis=1)
     total = jnp.dot(cells, out_w[...].reshape(9 * channels, channels), preferred_element_type=F32)
     near[...] = total.astype(BF16).reshape(out.shape)
@@ -152,29 +163,21 @@
     return pl.ds(pl.multiple_of(index * length, 16), length)
 
 
-def cut_kernel(mine, got, *refs):
+def cut_kernel(kernel_sums, mine, got, *refs):
     place, _ = places()
-    share = mine.shape[0] // 4
-    for k, out in zip((0, 2, 3, 1), refs[-4:]):
+    edge, share = kernel_sums.shape[0] // 4, mine.shape[0] // 4
+    for k, out in zip((0, 3, 2, 1), refs):
+        out[:edge, :] = kernel_sums[block(place ^ k, edge), :].astype(out.dtype)
         rows = block(place ^ k, share)
-        start = out.shape[0] - share
-        if start:
-            out[:start, :] = refs[0][...]
-        out[start:, :] = (mine[rows, :] + got[rows, :].astype(F32)).astype(out.dtype)
-
-
-def add_early_kernel(own, two, three, out):
-    out[...] = own[...] + three[...].astype(F32) + two[...].astype(F32)
-
-
-def add_kernel(part_a, own_b, one, two_b, three_b, out):
-    edge = part_a.shape[0]
-    out[:edge, :] = (part_a[...] + one[:edge, :].astype(F32)).astype(BF16)
-    total = own_b[...] + one[edge:, :].astype(F32) + two_b[...].astype(F32) + three_b[...].astype(F32)
-    out[edge:, :] = total.astype(BF16)
-
-
-def finish_kernel(scale, own, one, three, two, _, out):
+        out[edge:, :] = (mine[rows, :] + got[rows, :].astype(F32)).astype(out.dtype)
+
+
+def add_kernel(own, three, two, one, out):
+    total = own[...] + one[...].astype(F32) + two[...].astype(F32) + three[...].astype(F32)
+    out[...] = total.astype(BF16)
+
+
+def finish_kernel(scale, own, three, two, one, _, out):
     near = own[...].astype(F32) + one[...].astype(F32)
     far = two[...].astype(F32) + three[...].astype(F32)
     out[...] = ((near + far) * scale).astype(BF16)
@@ -186,7 +189,7 @@
     columns, place = (1 - side, places()[1]) if pair else (side, places()[0])
     lanes = pl.ds(pl.multiple_of(columns * 128, 128), 128)
     copies = []
-    for k, quarter in zip((0, 1, 3, 2), refs):
+    for k, quarter in zip((0, 3, 2, 1), refs):
         start = 0
         for result in results:
             share = result.shape[0] // 4
@@ -221,23 +224,19 @@
     )
 
 
-def sum_everywhere(parts, scale, after):
-    lengths, width = [mine.shape[0] for mine, _ in parts], parts[0][0].shape[1]
+def sum_everywhere(kernel_sums, lateral_part, scale, after):
+    lengths, width = [kernel_sums.shape[0], lateral_part[0].shape[0]], kernel_sums.shape[1]
     vmem, far = pl.BlockSpec(memory_space=pltpu.VMEM), pl.BlockSpec(memory_space=pltpu.HBM)
     after = pltpu.with_memory_space_constraint(after, pltpu.HBM)
-    share_a, share_b, quarter = [(length // 4, width) for length in (*lengths, sum(lengths))]
-    own_a, two, three, one_a = call(cut_kernel, (share_a, F32), *[(share_a, BF16)] * 3)(*parts[0])
-    two, three = exchange(two, 0, 2), exchange(three, 0, 3)
-    slow = pl.CostEstimate(flops=3 * 2**28, bytes_accessed=2**10, transcendentals=0)
-    [part_a] = call(add_early_kernel, (share_a, F32), cost_estimate=slow)(own_a, two, three)
-    own_b, two, three, one = call(cut_kernel, (share_b, F32), *[(share_b, BF16)] * 2, (quarter, BF16))(*parts[1], one_a)
-    one, two, three = exchange(one, 0, 1), exchange(two, 0, 2), exchange(three, 0, 3)
-    [total] = call(add_kernel, (quarter, BF16))(part_a, own_b, one, two, three)
-    two, three, one = [exchange(total, 1, k) for k in (2, 3, 1)]
+    quarter = (sum(lengths) // 4, width)
+    own, *pieces = call(cut_kernel, (quarter, F32), *[(quarter, BF16)] * 3)(kernel_sums, *lateral_part)
+    three, two, one = [exchange(piece, 0, k) for piece, k in zip(pieces, (3, 2, 1))]
+    [total] = call(add_kernel, (quarter, BF16))(own, three, two, one)
+    three, two, one = [exchange(total, 1, k) for k in (3, 2, 1)]
     finish = call(functools.partial(finish_kernel, scale), (quarter, BF16), in_specs=[vmem] * 4 + [far])
-    [total] = finish(total, one, three, two, after)
-    two, three, one = [exchange(total, 0, k) for k in (2, 3, 1)]
-    quarters = [total, one, three, two]
+    [total] = finish(total, three, two, one, after)
+    three, two, one = [exchange(total, 0, k) for k in (3, 2, 1)]
+    quarters = [total, three, two, one]
     results = [((length, 2 * width), BF16) for length in lengths]
     place = dict(out_specs=[far] * 2, scratch_shapes=[pltpu.SemaphoreType.DMA((8,))])
     half = call(functools.partial(place_kernel, False), *results, **place)(*quarters)
@@ -254,13 +253,10 @@
     params = pltpu.CompilerParams(vmem_limit_bytes=32 * 2**20)
     halves = peers == 2 and lax.axis_size("dp") == 16 and images == 1 and (channels, in_channels) == (256, 512)
 
-    def sums(length, extra):
+    def sums(length):
         if not halves:
             return [jax.ShapeDtypeStruct((length, channels), F32)]
-        return [
-            jax.ShapeDtypeStruct((length, channels // 2), F32),
-            jax.ShapeDtypeStruct((length + extra, channels // 2), BF16),
-        ]
+        return [jax.ShapeDtypeStruct((length, channels // 2), kind) for kind in (F32, BF16)]
 
     outs, tops, parts = [], [], None
     for image in range(images):
@@ -268,7 +264,7 @@
         cot_before, cot_after = neighbour_rows(cot)
         arrays = (cot, lateral_weight, top_down[image], features[image].reshape(cells, in_channels), taps)
         arrays = [pltpu.with_memory_space_constraint(array, pltpu.HBM) for array in arrays]
-        merged, merged_t, stack, near_feat = pl.pallas_call(
+        merged, merged_t, stack, near_feat, near_taps = pl.pallas_call(
             merge_kernel,
             out_shape=[
                 jax.ShapeDtypeStruct(shape, BF16)
@@ -277,43 +273,49 @@
                     (channels, cells),
                     (rows, cols, 3 * channels),
                     (cells, in_channels),
+                    taps.shape,
                 )
             ],
-            in_specs=[pl.BlockSpec(memory_space=pltpu.HBM)] * 4,
-            scratch_shapes=[*[pltpu.VMEM(array.shape, BF16) for array in arrays[:3]], pltpu.SemaphoreType.DMA((4,))],
+            in_specs=[pl.BlockSpec(memory_space=pltpu.HBM)] * 5,
+            scratch_shapes=[*[pltpu.VMEM(array.shape, BF16) for array in arrays[:3]], pltpu.SemaphoreType.DMA((5,))],
             compiler_params=params,
             cost_estimate=pl.CostEstimate(
                 flops=2 * cells * channels * 4 * in_channels, bytes_accessed=4 * 2**20, transcendentals=0
             ),
-        )(*arrays[:4])
-        near_taps, halo, *kernel_part = pl.pallas_call(
-            functools.partial(kernel_grad_kernel, peers),
+        )(*arrays)
+        merged = merged.reshape(rows, cols, channels)
+        edges = neighbour_rows(merged)
+        grad, halo, *lateral_part = pl.pallas_call(
+            functools.partial(data_grad_kernel, peers),
             out_shape=[
-                jax.ShapeDtypeStruct(taps.shape, BF16),
+                jax.ShapeDtypeStruct((cells, channels), BF16),
                 jax.ShapeDtypeStruct((2, cols, 3 * channels), BF16),
-                *sums(9 * channels, 2 * cols),
+                *sums(in_channels),
             ],
-            in_specs=[pl.BlockSpec(memory_space=pltpu.VMEM)] * 5 + [pl.BlockSpec(memory_space=pltpu.HBM)],
-            scratch_shapes=[pltpu.SemaphoreType.DMA],
-            compiler_params=params,
-            cost_estimate=pl.CostEstimate(
-                flops=2 * cells * channels * 9 * channels, bytes_accessed=4 * 2**20, transcendentals=0
-            ),
-        )(stack, merged, merged_t, cot_before, cot_after, arrays[4])
-        if halves:
-            kernel_part[1] = swap(kernel_part[1])
-        grad, *lateral_part = pl.pallas_call(
-            data_grad_kernel,
-            out_shape=[jax.ShapeDtypeStruct((cells, channels), BF16), *sums(in_channels, 0)],
             compiler_params=params,
             cost_estimate=pl.CostEstimate(
                 flops=2 * cells * channels * (9 * channels + in_channels), bytes_accessed=4 * 2**20, transcendentals=0
             ),
-        )(stack, halo, near_feat, near_taps)
+        )(stack, cot_before, cot_after, near_feat, near_taps)
+        kernel_cost = pl.CostEstimate(
+            flops=2 * cells * channels * 9 * channels, bytes_accessed=4 * 2**20, transcendentals=0
+        )
         if halves:
             lateral_part[1] = swap(lateral_part[1])
-        merged = merged.reshape(rows, cols, channels)
-        edges = kernel_part[1:] if halves else neighbour_rows(merged)
+            kernel_sums = pl.pallas_call(
+                pair_kernel_grad_kernel,
+                out_shape=jax.ShapeDtypeStruct((9 * channels, channels // 2), F32),
+                scratch_shapes=[pltpu.VMEM((2 * rows + 2, cols, 3 * channels // 2), BF16)],
+                compiler_params=params,
+                cost_estimate=kernel_cost,
+            )(stack, merged_t, cot_after, edges[0].reshape(cells, channels))
+        else:
+            kernel_sums = pl.pallas_call(
+                kernel_grad_kernel,
+                out_shape=jax.ShapeDtypeStruct((9 * channels, channels), F32),
+                compiler_params=params,
+                cost_estimate=kernel_cost,
+            )(stack, halo, merged_t)
         out, grad_top = pl.pallas_call(
             functools.partial(forward_kernel, peers),
             out_shape=[
@@ -334,11 +336,11 @@
         outs.append(out)
         tops.append(grad_top)
         if not halves:
-            part = [kernel_part[0], lateral_part[0]]
+            part = [kernel_sums, lateral_part[0]]
             parts = part if parts is None else [a + b for a, b in zip(parts, part)]
     scale = 1.0 / (images * lax.axis_size("dp"))
     if halves:
-        grad_kernel, grad_lateral = sum_everywhere((kernel_part, lateral_part), scale, outs[0])
+        grad_kernel, grad_lateral = sum_everywhere(kernel_sums, lateral_part, scale, outs[0])
     else:
         grad_kernel, grad_lateral = [(total * scale).astype(BF16) for total in lax.psum(parts, ("dp", "space"))]
     return jnp.stack(outs), jnp.stack(tops), grad_kernel.reshape(out_kernel.shape), grad_lateral

time: 41.7 us -> 40.4 us (0.969)
  starting transfers between devices: 17.1 us -> 13.8 us
  waiting for transfers between devices: 14.2 us -> 16 us
    ppermute x11 -> x9, starting transfers between devices: 15.4 us -> 12.2 us  [exchange(): return lax.ppermute(array, ('dp', 'space'), pairs)]
    ppermute x11 -> x9, waiting for transfers between devices: 13.7 us -> 15.6 us  [exchange(): return lax.ppermute(array, ('dp', 'space'), pairs)]
    ppermute x6 -> x5, starting transfers between devices: 1.16 us -> 1.03 us  [swap(): return lax.ppermute(array, 'space', [(0, 1), (1, 0)])]
    pallas_call x7 -> x5, Pallas kernels: 3.32 us -> 3.43 us  [the longest x1 1.71 us: local(): pl.pallas_call(functools.partial(data_grad_kernel, peers), out_shape=[jax...]
  transfers between devices with their start and end apart: 18 -> 16, of which waited for: 8 -> 8; matrix products, arithmetic and copies ran while one was open for 0% -> 0% of each run, Pallas kernels for 17% -> 21%
where the time goes in v12:
time: 40.4 us; the launch traced here: 40.2 us
  waiting for transfers between devices  16 us (40%)
  starting transfers between devices  13.8 us (34%)
  Pallas kernels  9.68 us (24%)
  between operations  0.72 us (2%)
    ppermute x9, waiting for transfers between devices, exchange(): return lax.ppermute(array, ('dp', 'space'), pairs)  15.6 us
    ppermute x9, starting transfers between devices, exchange(): return lax.ppermute(array, ('dp', 'space'), pairs)  12.2 us
    pallas_call x1, Pallas kernels, local(): pl.pallas_call(functools.partial(forward_kernel, peers), out_shape=[jax.S...  2.53 us
    pallas_call x1, Pallas kernels, local(): pl.pallas_call(merge_kernel, out_shape=[jax.ShapeDtypeStruct(shape, BF16)...  1.9 us
    pallas_call x1, Pallas kernels, local(): pl.pallas_call(functools.partial(data_grad_kernel, peers), out_shape=[jax...  1.71 us
    pallas_call x1, Pallas kernels, local(): pl.pallas_call(pair_kernel_grad_kernel, out_shape=jax.ShapeDtypeStruct((9...  1.43 us
    ppermute x5, starting transfers between devices, swap(): return lax.ppermute(array, 'space', [(0, 1), (1, 0)])  1.03 us
    pallas_call x1, Pallas kernels, sum_everywhere(): call(functools.partial(place_kernel, True), *results, **place)  0.91 us
  transfers between devices with their start and end apart: 16, of which 8 were waited for; matrix products, arithmetic and copies ran while one was open for 0% of the time, Pallas kernels for 21%

profile of v12, /device:TPU:0, one launch (start us, length us, event | category | flops | bytes accessed | tf_op | source)
XLA Modules:
  0.0 40.2 jit_solution(18095924096539511765)
XLA Ops:
  0.6 0.5 %collective-permute-start = (bf16[8,96,256]{2,1,0:T(8,128)(2,1)}, bf16[8,96,256]{2,1,0:T(8,128)(2,1)S(1)}, u32[]{:S(2)}, u32[]{:S(2)}) collective-permute-start(bf16[8,96,256]{2,1,0:T(8,128)(2,1)} %bitcast.16), channel_id=1, source_target_pairs={{0,1},{1,0},{2,3},{3,2},{4,5},{5,4},{6,7},{7,6},{8,9},{9,8},{10,11... | collective-permute-start | bytes 1179656 | tf_op jit(solution)/shard_map/ppermute | solution.py:19
  1.1 1.9 %shard_map.84 = (bf16[768,256]{1,0:T(8,128)(2,1)S(1)}, bf16[256,768]{1,0:T(8,128)(2,1)S(1)}, bf16[8,96,768]{2,1,0:T(8,128)(2,1)S(1)}, bf16[768,512]{1,0:T(8,128)(2,1)S(1)}, bf16[9,256,256]{2,1,0:T(8,128)(2,1)S(1)}) custom-call(bf16[8,96,256]{2,1,0:T(8,128)(2,1)} %bitcast.17, bf16[512,256]{1,0:T(8,128)(2,1)} %refs_1_.1, bf16[4,48,256]{2,1,0:T(8,128)(2,1)} %bitcast.18, ...), custom_call_target="tpu_custom_call" | custom-call | flops 805306368 | bytes 4194304 | tf_op jit(solution)/shard_map/pallas_call | solution.py:267
  3.1 0.1 collective-permute-start.1
  3.2 1.7 %shard_map.85 = (bf16[768,256]{1,0:T(8,128)(2,1)S(1)}, bf16[2,96,768]{2,1,0:T(8,128)(2,1)}, f32[512,128]{1,0:T(8,128)S(1)}, bf16[512,128]{1,0:T(8,128)(2,1)S(1)}) custom-call(bf16[8,96,768]{2,1,0:T(8,128)(2,1)S(1)} %get-tuple-element.24.stack, bf16[8,96,256]{2,1,0:T(8,128)(2,1)S(1)} %collective-permute-done.before.after.cot, ...), custom_call_target="tpu_custom_call" | custom-call | flops 1107296256 | bytes 4194304 | tf_op jit(solution)/shard_map/pallas_call | solution.py:288
  4.9 0.5 %collective-permute-start.2 = (bf16[512,128]{1,0:T(8,128)(2,1)S(1)}, bf16[512,128]{1,0:T(8,128)(2,1)S(1)}, u32[]{:S(2)}, u32[]{:S(2)}) collective-permute-start(bf16[512,128]{1,0:T(8,128)(2,1)S(1)} %get-tuple-element.31), channel_id=1, source_target_pairs={{0,1},{1,0},{2,3},{3,2},{4,5},{5,4},{6,7},{7,6},{8,9},{9,8},{10,11... | collective-permute-start | bytes 393224 | tf_op jit(solution)/shard_map/ppermute | solution.py:215
  5.4 1.4 %shard_map.87.kernel_sums = f32[2304,128]{1,0:T(8,128)S(1)} custom-call(bf16[8,96,768]{2,1,0:T(8,128)(2,1)S(1)} %get-tuple-element.24.stack, bf16[256,768]{1,0:T(8,128)(2,1)S(1)} %get-tuple-element.29.merged_t, bf16[8,96,256]{2,1,0:T(8,128)(2,1)S(1)} %collective-permute-done.before.after.cot, bf16[768,256]{1,0:T(8,128)(2,1)S(1)} %bitcast.9), custom_call_target="tpu_custom_call" | custom-call | flops 905969664 | bytes 4194304 | tf_op jit(solution)/shard_map/pallas_call | solution.py:305
  6.9 0.0 collective-permute-done.2.got
  6.9 0.1 shard_map.88
  7.0 3.5 %collective-permute-start.3 = (bf16[704,128]{1,0:T(8,128)(2,1)S(1)}, bf16[704,128]{1,0:T(8,128)(2,1)S(1)}, u32[]{:S(2)}, u32[]{:S(2)}) collective-permute-start(bf16[704,128]{1,0:T(8,128)(2,1)S(1)} %get-tuple-element.33), channel_id=1, source_target_pairs={{0,6},{1,25},{2,4},{3,27},{4,2},{5,29},{6,0},{7,31},{8,14},{9,17},... | collective-permute-start | bytes 540680 | tf_op jit(solution)/shard_map/ppermute | solution.py:211
  10.5 0.5 %collective-permute-start.4 = (bf16[704,128]{1,0:T(8,128)(2,1)S(1)}, bf16[704,128]{1,0:T(8,128)(2,1)S(1)}, u32[]{:S(2)}, u32[]{:S(2)}) collective-permute-start(bf16[704,128]{1,0:T(8,128)(2,1)S(1)} %get-tuple-element.34), channel_id=1, source_target_pairs={{0,4},{1,17},{2,6},{3,19},{4,0},{5,21},{6,2},{7,23},{8,12},{9,25},... | collective-permute-start | bytes 540680 | tf_op jit(solution)/shard_map/ppermute | solution.py:211
  11.0 0.1 collective-permute-start.5
  11.2 2.8 %collective-permute-done.3.three = bf16[704,128]{1,0:T(8,128)(2,1)S(1)} collective-permute-done((bf16[704,128]{1,0:T(8,128)(2,1)S(1)}, bf16[704,128]{1,0:T(8,128)(2,1)S(1)}, u32[]{:S(2)}, u32[]{:S(2)}) %collective-permute-start.3) | collective-permute-done | bytes 180256 | tf_op jit(solution)/shard_map/ppermute | solution.py:211
  14.0 2.0 %collective-permute-done.4.two = bf16[704,128]{1,0:T(8,128)(2,1)S(1)} collective-permute-done((bf16[704,128]{1,0:T(8,128)(2,1)S(1)}, bf16[704,128]{1,0:T(8,128)(2,1)S(1)}, u32[]{:S(2)}, u32[]{:S(2)}) %collective-permute-start.4) | collective-permute-done | bytes 180256 | tf_op jit(solution)/shard_map/ppermute | solution.py:211
  16.0 0.5 %collective-permute-done.5.one = bf16[704,128]{1,0:T(8,128)(2,1)S(1)} collective-permute-done((bf16[704,128]{1,0:T(8,128)(2,1)S(1)}, bf16[704,128]{1,0:T(8,128)(2,1)S(1)}, u32[]{:S(2)}, u32[]{:S(2)}) %collective-permute-start.5) | collective-permute-done | bytes 180256 | tf_op jit(solution)/shard_map/ppermute | solution.py:211
  16.5 0.1 shard_map.89.own
  16.6 3.7 %collective-permute-start.6 = (bf16[704,128]{1,0:T(8,128)(2,1)S(1)}, bf16[704,128]{1,0:T(8,128)(2,1)S(1)}, u32[]{:S(2)}, u32[]{:S(2)}) collective-permute-start(bf16[704,128]{1,0:T(8,128)(2,1)S(1)} %shard_map.89.own), channel_id=1, source_target_pairs={{0,24},{1,7},{2,26},{3,5},{4,28},{5,3},{6,30},{7,1},{8,16},{9,15},... | collective-permute-start | bytes 540680 | tf_op jit(solution)/shard_map/ppermute | solution.py:211
  20.3 0.8 %collective-permute-start.8 = (bf16[704,128]{1,0:T(8,128)(2,1)S(1)}, bf16[704,128]{1,0:T(8,128)(2,1)S(1)}, u32[]{:S(2)}, u32[]{:S(2)}) collective-permute-start(bf16[704,128]{1,0:T(8,128)(2,1)S(1)} %shard_map.89.own), channel_id=1, source_target_pairs={{0,8},{1,3},{2,10},{3,1},{4,12},{5,7},{6,14},{7,5},{8,0},{9,11},{1... | collective-permute-start | bytes 540680 | tf_op jit(solution)/shard_map/ppermute | solution.py:211
  21.1 2.5 %shard_map.86 = (bf16[8,96,256]{2,1,0:T(8,128)(2,1)}, bf16[4,48,256]{2,1,0:T(8,128)(2,1)}) custom-call(bf16[8,96,256]{2,1,0:T(8,128)(2,1)S(1)} %bitcast.11, bf16[9,256,256]{2,1,0:T(8,128)(2,1)S(1)} %get-tuple-element.23.out_w, bf16[768,256]{1,0:T(8,128)(2,1)S(1)} %get-tuple-element.26.grad, bf16[8,96,256]{2,1,0:T(8,128)(2,1)S(1)} %collective-permute-done.1.refs_0_.refs_1_, ...), custom_call_target="tpu_custom_call" | custom-call | flops 905969664 | bytes 2097152 | tf_op jit(solution)/shard_map/pallas_call | solution.py:319
  23.6 0.5 %collective-permute-done.6.three = bf16[704,128]{1,0:T(8,128)(2,1)S(1)} collective-permute-done((bf16[704,128]{1,0:T(8,128)(2,1)S(1)}, bf16[704,128]{1,0:T(8,128)(2,1)S(1)}, u32[]{:S(2)}, u32[]{:S(2)}) %collective-permute-start.6) | collective-permute-done | bytes 180256 | tf_op jit(solution)/shard_map/ppermute | solution.py:211
  24.1 4.9 %collective-permute-done.7.two = bf16[704,128]{1,0:T(8,128)(2,1)S(1)} collective-permute-done((bf16[704,128]{1,0:T(8,128)(2,1)S(1)}, bf16[704,128]{1,0:T(8,128)(2,1)S(1)}, u32[]{:S(2)}, u32[]{:S(2)}) %collective-permute-start.7) | collective-permute-done | bytes 180256 | tf_op jit(solution)/shard_map/ppermute | solution.py:211
  29.0 0.1 shard_map.90.refs_0_
  29.1 2.0 %collective-permute-start.10 = (bf16[704,128]{1,0:T(8,128)(2,1)S(1)}, bf16[704,128]{1,0:T(8,128)(2,1)S(1)}, u32[]{:S(2)}, u32[]{:S(2)}) collective-permute-start(bf16[704,128]{1,0:T(8,128)(2,1)S(1)} %shard_map.90.refs_0_), channel_id=1, source_target_pairs={{0,6},{1,25},{2,4},{3,27},{4,2},{5,29},{6,0},{7,31},{8,14},{9,17},... | collective-permute-start | bytes 540680 | tf_op jit(solution)/shard_map/ppermute | solution.py:211
  31.1 1.0 %collective-permute-start.12 = (bf16[704,128]{1,0:T(8,128)(2,1)S(1)}, bf16[704,128]{1,0:T(8,128)(2,1)S(1)}, u32[]{:S(2)}, u32[]{:S(2)}) collective-permute-start(bf16[704,128]{1,0:T(8,128)(2,1)S(1)} %shard_map.90.refs_0_), channel_id=1, source_target_pairs={{0,4},{1,17},{2,6},{3,19},{4,0},{5,21},{6,2},{7,23},{8,12},{9,25},... | collective-permute-start | bytes 540680 | tf_op jit(solution)/shard_map/ppermute | solution.py:211
  32.1 0.6 %collective-permute-start.14 = (bf16[704,128]{1,0:T(8,128)(2,1)S(1)}, bf16[704,128]{1,0:T(8,128)(2,1)S(1)}, u32[]{:S(2)}, u32[]{:S(2)}) collective-permute-start(bf16[704,128]{1,0:T(8,128)(2,1)S(1)} %shard_map.90.refs_0_), channel_id=1, source_target_pairs={{0,2},{1,9},{2,0},{3,11},{4,6},{5,13},{6,4},{7,15},{8,10},{9,1},{1... | collective-permute-start | bytes 540680 | tf_op jit(solution)/shard_map/ppermute | solution.py:211
  32.6 3.0 %collective-permute-done.10.refs_1_ = bf16[704,128]{1,0:T(8,128)(2,1)S(1)} collective-permute-done((bf16[704,128]{1,0:T(8,128)(2,1)S(1)}, bf16[704,128]{1,0:T(8,128)(2,1)S(1)}, u32[]{:S(2)}, u32[]{:S(2)}) %collective-permute-start.10) | collective-permute-done | bytes 180256 | tf_op jit(solution)/shard_map/ppermute | solution.py:211
  35.6 1.8 %collective-permute-done.12.refs_2_ = bf16[704,128]{1,0:T(8,128)(2,1)S(1)} collective-permute-done((bf16[704,128]{1,0:T(8,128)(2,1)S(1)}, bf16[704,128]{1,0:T(8,128)(2,1)S(1)}, u32[]{:S(2)}, u32[]{:S(2)}) %collective-permute-start.12) | collective-permute-done | bytes 180256 | tf_op jit(solution)/shard_map/ppermute | solution.py:211
  37.5 0.4 %collective-permute-start.13 = (bf16[704,128]{1,0:T(8,128)(2,1)S(1)}, bf16[704,128]{1,0:T(8,128)(2,1)S(1)}, u32[]{:S(2)}, u32[]{:S(2)}) collective-permute-start(bf16[704,128]{1,0:T(8,128)(2,1)S(1)} %collective-permute-done.12.refs_2_), channel_id=1, source_target_pairs={{0,1},{1,0},{2,3},{3,2},{4,5},{5,4},{6,7},{7,6},{8,9},{9,8},{10,11... | collective-permute-start | bytes 540680 | tf_op jit(solution)/shard_map/ppermute | solution.py:215
  37.9 0.1 collective-permute-start.15
  38.0 0.9 %shard_map.91 = (bf16[2304,256]{1,0:T(8,128)(2,1)}, bf16[512,256]{1,0:T(8,128)(2,1)}) custom-call(bf16[704,128]{1,0:T(8,128)(2,1)S(1)} %shard_map.90.refs_0_, bf16[704,128]{1,0:T(8,128)(2,1)S(1)} %collective-permute-done.10.refs_1_, bf16[704,128]{1,0:T(8,128)(2,1)S(1)} %collective-permute-done.12.refs_2_, bf16[704,128]{1,0:T(8,128)(2,1)S(1)} %collective-permute-done.14.refs_3_), custom_call_target="tpu_custom_call" | custom-call | tf_op jit(solution)/shard_map/pallas_call | solution.py:242
  38.9 0.0 collective-permute-done.13.refs_2_
  38.9 0.4 collective-permute-done.15.refs_3_
  39.3 0.9 %shard_map.92 = (bf16[2304,256]{1,0:T(8,128)(2,1)}, bf16[512,256]{1,0:T(8,128)(2,1)}) custom-call(bf16[704,128]{1,0:T(8,128)(2,1)S(1)} %collective-permute-done.9.refs_0_, bf16[704,128]{1,0:T(8,128)(2,1)S(1)} %collective-permute-done.11.refs_1_, bf16[704,128]{1,0:T(8,128)(2,1)S(1)} %collective-permute-done.13.refs_2_, ...), custom_call_target="tpu_custom_call", output_to_operand_aliasing={{0}: (4, {}), {1}: (5, {})} | custom-call | tf_op jit(solution)/shard_map/pallas_call | solution.py:244
  (9 shorter events, 0.0 us)
Async XLA Ops:
  0.6 2.6 %collective-permute-start = (bf16[8,96,256]{2,1,0:T(8,128)(2,1)}, bf16[8,96,256]{2,1,0:T(8,128)(2,1)S(1)}, u32[]{:S(2)}, u32[]{:S(2)}) collective-permute-start(bf16[8,96,256]{2,1,0:T(8,128)(2,1)} %bitcast.16), channel_id=1, source_target_pairs={{0,1},{1,0},{2,3},{3,2},{4,5},{5,4},{6,7},{7,6},{8,9},{9,8},{10,11... | collective-permute-start | bytes 1179656 | tf_op jit(solution)/shard_map/ppermute | solution.py:19
  3.1 2.4 %collective-permute-start.1 = (bf16[8,96,256]{2,1,0:T(8,128)(2,1)S(1)}, bf16[8,96,256]{2,1,0:T(8,128)(2,1)S(1)}, u32[]{:S(2)}, u32[]{:S(2)}) collective-permute-start(bf16[8,96,256]{2,1,0:T(8,128)(2,1)S(1)} %bitcast.10), channel_id=1, source_target_pairs={{0,1},{1,0},{2,3},{3,2},{4,5},{5,4},{6,7},{7,6},{8,9},{9,8},{10,11... | collective-permute-start | bytes 1179656 | tf_op jit(solution)/shard_map/ppermute | solution.py:19
  4.9 2.0 %collective-permute-start.2 = (bf16[512,128]{1,0:T(8,128)(2,1)S(1)}, bf16[512,128]{1,0:T(8,128)(2,1)S(1)}, u32[]{:S(2)}, u32[]{:S(2)}) collective-permute-start(bf16[512,128]{1,0:T(8,128)(2,1)S(1)} %get-tuple-element.31), channel_id=1, source_target_pairs={{0,1},{1,0},{2,3},{3,2},{4,5},{5,4},{6,7},{7,6},{8,9},{9,8},{10,11... | collective-permute-start | bytes 393224 | tf_op jit(solution)/shard_map/ppermute | solution.py:215
  7.0 7.0 %collective-permute-start.3 = (bf16[704,128]{1,0:T(8,128)(2,1)S(1)}, bf16[704,128]{1,0:T(8,128)(2,1)S(1)}, u32[]{:S(2)}, u32[]{:S(2)}) collective-permute-start(bf16[704,128]{1,0:T(8,128)(2,1)S(1)} %get-tuple-element.33), channel_id=1, source_target_pairs={{0,6},{1,25},{2,4},{3,27},{4,2},{5,29},{6,0},{7,31},{8,14},{9,17},... | collective-permute-start | bytes 540680 | tf_op jit(solution)/shard_map/ppermute | solution.py:211
  10.5 5.5 %collective-permute-start.4 = (bf16[704,128]{1,0:T(8,128)(2,1)S(1)}, bf16[704,128]{1,0:T(8,128)(2,1)S(1)}, u32[]{:S(2)}, u32[]{:S(2)}) collective-permute-start(bf16[704,128]{1,0:T(8,128)(2,1)S(1)} %get-tuple-element.34), channel_id=1, source_target_pairs={{0,4},{1,17},{2,6},{3,19},{4,0},{5,21},{6,2},{7,23},{8,12},{9,25},... | collective-permute-start | bytes 540680 | tf_op jit(solution)/shard_map/ppermute | solution.py:211
  11.0 5.5 %collective-permute-start.5 = (bf16[704,128]{1,0:T(8,128)(2,1)S(1)}, bf16[704,128]{1,0:T(8,128)(2,1)S(1)}, u32[]{:S(2)}, u32[]{:S(2)}) collective-permute-start(bf16[704,128]{1,0:T(8,128)(2,1)S(1)} %get-tuple-element.35), channel_id=1, source_target_pairs={{0,2},{1,9},{2,0},{3,11},{4,6},{5,13},{6,4},{7,15},{8,10},{9,1},{1... | collective-permute-start | bytes 540680 | tf_op jit(solution)/shard_map/ppermute | solution.py:211
  16.6 7.5 %collective-permute-start.6 = (bf16[704,128]{1,0:T(8,128)(2,1)S(1)}, bf16[704,128]{1,0:T(8,128)(2,1)S(1)}, u32[]{:S(2)}, u32[]{:S(2)}) collective-permute-start(bf16[704,128]{1,0:T(8,128)(2,1)S(1)} %shard_map.89.own), channel_id=1, source_target_pairs={{0,24},{1,7},{2,26},{3,5},{4,28},{5,3},{6,30},{7,1},{8,16},{9,15},... | collective-permute-start | bytes 540680 | tf_op jit(solution)/shard_map/ppermute | solution.py:211
  20.3 8.7 %collective-permute-start.7 = (bf16[704,128]{1,0:T(8,128)(2,1)S(1)}, bf16[704,128]{1,0:T(8,128)(2,1)S(1)}, u32[]{:S(2)}, u32[]{:S(2)}) collective-permute-start(bf16[704,128]{1,0:T(8,128)(2,1)S(1)} %shard_map.89.own), channel_id=1, source_target_pairs={{0,16},{1,5},{2,18},{3,7},{4,20},{5,1},{6,22},{7,3},{8,24},{9,13},... | collective-permute-start | bytes 540680 | tf_op jit(solution)/shard_map/ppermute | solution.py:211
  20.3 8.7 %collective-permute-start.8 = (bf16[704,128]{1,0:T(8,128)(2,1)S(1)}, bf16[704,128]{1,0:T(8,128)(2,1)S(1)}, u32[]{:S(2)}, u32[]{:S(2)}) collective-permute-start(bf16[704,128]{1,0:T(8,128)(2,1)S(1)} %shard_map.89.own), channel_id=1, source_target_pairs={{0,8},{1,3},{2,10},{3,1},{4,12},{5,7},{6,14},{7,5},{8,0},{9,11},{1... | collective-permute-start | bytes 540680 | tf_op jit(solution)/shard_map/ppermute | solution.py:211
  29.1 6.6 %collective-permute-start.10 = (bf16[704,128]{1,0:T(8,128)(2,1)S(1)}, bf16[704,128]{1,0:T(8,128)(2,1)S(1)}, u32[]{:S(2)}, u32[]{:S(2)}) collective-permute-start(bf16[704,128]{1,0:T(8,128)(2,1)S(1)} %shard_map.90.refs_0_), channel_id=1, source_target_pairs={{0,6},{1,25},{2,4},{3,27},{4,2},{5,29},{6,0},{7,31},{8,14},{9,17},... | collective-permute-start | bytes 540680 | tf_op jit(solution)/shard_map/ppermute | solution.py:211
  31.1 6.4 %collective-permute-start.12 = (bf16[704,128]{1,0:T(8,128)(2,1)S(1)}, bf16[704,128]{1,0:T(8,128)(2,1)S(1)}, u32[]{:S(2)}, u32[]{:S(2)}) collective-permute-start(bf16[704,128]{1,0:T(8,128)(2,1)S(1)} %shard_map.90.refs_0_), channel_id=1, source_target_pairs={{0,4},{1,17},{2,6},{3,19},{4,0},{5,21},{6,2},{7,23},{8,12},{9,25},... | collective-permute-start | bytes 540680 | tf_op jit(solution)/shard_map/ppermute | solution.py:211
  32.1 5.8 %collective-permute-start.14 = (bf16[704,128]{1,0:T(8,128)(2,1)S(1)}, bf16[704,128]{1,0:T(8,128)(2,1)S(1)}, u32[]{:S(2)}, u32[]{:S(2)}) collective-permute-start(bf16[704,128]{1,0:T(8,128)(2,1)S(1)} %shard_map.90.refs_0_), channel_id=1, source_target_pairs={{0,2},{1,9},{2,0},{3,11},{4,6},{5,13},{6,4},{7,15},{8,10},{9,1},{1... | collective-permute-start | bytes 540680 | tf_op jit(solution)/shard_map/ppermute | solution.py:211
  32.6 6.3 %collective-permute-start.9 = (bf16[704,128]{1,0:T(8,128)(2,1)S(1)}, bf16[704,128]{1,0:T(8,128)(2,1)S(1)}, u32[]{:S(2)}, u32[]{:S(2)}) collective-permute-start(bf16[704,128]{1,0:T(8,128)(2,1)S(1)} %shard_map.90.refs_0_), channel_id=1, source_target_pairs={{0,1},{1,0},{2,3},{3,2},{4,5},{5,4},{6,7},{7,6},{8,9},{9,8},{10,11... | collective-permute-start | bytes 540680 | tf_op jit(solution)/shard_map/ppermute | solution.py:215
  35.6 3.3 %collective-permute-start.11 = (bf16[704,128]{1,0:T(8,128)(2,1)S(1)}, bf16[704,128]{1,0:T(8,128)(2,1)S(1)}, u32[]{:S(2)}, u32[]{:S(2)}) collective-permute-start(bf16[704,128]{1,0:T(8,128)(2,1)S(1)} %collective-permute-done.10.refs_1_), channel_id=1, source_target_pairs={{0,1},{1,0},{2,3},{3,2},{4,5},{5,4},{6,7},{7,6},{8,9},{9,8},{10,11... | collective-permute-start | bytes 540680 | tf_op jit(solution)/shard_map/ppermute | solution.py:215
  37.5 1.5 %collective-permute-start.13 = (bf16[704,128]{1,0:T(8,128)(2,1)S(1)}, bf16[704,128]{1,0:T(8,128)(2,1)S(1)}, u32[]{:S(2)}, u32[]{:S(2)}) collective-permute-start(bf16[704,128]{1,0:T(8,128)(2,1)S(1)} %collective-permute-done.12.refs_2_), channel_id=1, source_target_pairs={{0,1},{1,0},{2,3},{3,2},{4,5},{5,4},{6,7},{7,6},{8,9},{9,8},{10,11... | collective-permute-start | bytes 540680 | tf_op jit(solution)/shard_map/ppermute | solution.py:215
  37.9 1.4 %collective-permute-start.15 = (bf16[704,128]{1,0:T(8,128)(2,1)S(1)}, bf16[704,128]{1,0:T(8,128)(2,1)S(1)}, u32[]{:S(2)}, u32[]{:S(2)}) collective-permute-start(bf16[704,128]{1,0:T(8,128)(2,1)S(1)} %collective-permute-done.14.refs_3_), channel_id=1, source_target_pairs={{0,1},{1,0},{2,3},{3,2},{4,5},{5,4},{6,7},{7,6},{8,9},{9,8},{10,11... | collective-permute-start | bytes 540680 | tf_op jit(solution)/shard_map/ppermute | solution.py:215

commit v13 on v12

--- a/solution.py
+++ b/solution.py
@@ -23,48 +23,62 @@
     return lax.ppermute(array[-1:], "space", up), lax.ppermute(array[:1], "space", down)
 
 
-def put_shifted(stack, slot, row, sign):
+def put_shifted(stack, slot, row, sign, pad):
     cols, channels = row.shape
-    wide = row.astype(F32)
-    place = lax.broadcasted_iota(jnp.int32, (cols, channels), 0)
-    later = jnp.where(place == cols - 1, 0.0, pltpu.roll(wide, cols - 1, 0)).astype(BF16)
-    earlier = jnp.where(place == 0, 0.0, pltpu.roll(wide, 1, 0)).astype(BF16)
+    zero = jnp.zeros((8, channels), F32)
+    pad[0:8, :] = zero
+    pad[8 + cols :, :] = zero
+    pad[8 : 8 + cols, :] = row.astype(F32)
+    earlier, later = pad[7 : 7 + cols, :].astype(BF16), pad[9 : 9 + cols, :].astype(BF16)
     first, last = (earlier, later) if sign < 0 else (later, earlier)
     stack[slot, :, 0:channels] = first
     stack[slot, :, channels : 2 * channels] = row
     stack[slot, :, 2 * channels :] = last
 
 
-def put_halo(stack, before, after, rows, peers, sign):
+def put_halo(stack, before, after, rows, peers, sign, pads):
     here = lax.axis_index("space")
     zero = jnp.zeros(before.shape, BF16)
-    put_shifted(stack, 0, jnp.where(here > 0, before, zero), sign)
-    put_shifted(stack, rows + 1, jnp.where(here < peers - 1, after, zero), sign)
+    put_shifted(stack, 0, jnp.where(here > 0, before, zero), sign, pads.at[0])
+    put_shifted(stack, rows + 1, jnp.where(here < peers - 1, after, zero), sign, pads.at[1])
 
 
 def merge_kernel(*refs):
-    far, (merged, merged_t, stack, feat, out_w), near, sems = refs[:5], refs[5:10], refs[10:13], refs[13]
-    near = (*near, feat, out_w)
-    copies = [pltpu.make_async_copy(a, b, sems.at[i]) for i, (a, b) in enumerate(zip(far, near))]
+    far, (merged, merged_t, stack, feat, out_w), near, pads, sems = refs[:5], refs[5:10], refs[10:13], refs[13], refs[14]
+    cot_far, lat_far, top_far, feat_far, taps_far = far
+    cot, lat_w, top = near
+    rows, cols, channels = cot.shape
+    half, cells = cols // 2, rows * cols
+    upper_cells, lower_cells = pl.ds(0, cells // 2), pl.ds(cells // 2, cells // 2)
+    moves = [
+        (cot_far, cot),
+        (lat_far, lat_w),
+        (feat_far.at[upper_cells, :], feat.at[upper_cells, :]),
+        (top_far, top),
+        (feat_far.at[lower_cells, :], feat.at[lower_cells, :]),
+        (taps_far, out_w),
+    ]
+    copies = [pltpu.make_async_copy(a, b, sems.at[i]) for i, (a, b) in enumerate(moves)]
     for copy in copies:
         copy.start()
-    cot, lat_w, top = near[:3]
-    rows, cols, channels = cot.shape
-    half = cols // 2
+    upper = lax.broadcasted_iota(jnp.int32, (cols, half), 0)
+    spread = jnp.where(upper // 2 == lax.broadcasted_iota(jnp.int32, (cols, half), 1), 1.0, 0.0).astype(BF16)
     copies[0].wait()
     for r in range(rows):
-        put_shifted(stack, r, cot[r], 1)
-    for copy in copies[1:4]:
-        copy.wait()
-    upper = lax.broadcasted_iota(jnp.int32, (cols, half), 0)
-    spread = jnp.where(upper // 2 == lax.broadcasted_iota(jnp.int32, (cols, half), 1), 1.0, 0.0).astype(BF16)
-    lateral = jnp.dot(feat[...], lat_w[...], preferred_element_type=F32)
-    for q in range(rows // 2):
-        lifted = jnp.dot(spread, top[q], preferred_element_type=F32)
-        for r in (2 * q, 2 * q + 1):
-            merged[r * cols : (r + 1) * cols, :] = (lateral[r * cols : (r + 1) * cols] + lifted).astype(BF16)
-    merged_t[...] = jnp.transpose(merged[...])
-    copies[4].wait()
+        put_shifted(stack, r, cot[r], 1, pads.at[r])
+    for part, needed in ((0, copies[1:4]), (1, copies[4:5])):
+        for copy in needed:
+            copy.wait()
+        start = part * cells // 2
+        lateral = jnp.dot(feat[start : start + cells // 2, :], lat_w[...], preferred_element_type=F32)
+        for q in range(rows // 4):
+            lifted = jnp.dot(spread, top[part * rows // 4 + q], preferred_element_type=F32)
+            for r in (2 * q, 2 * q + 1):
+                merged[start + r * cols : start + (r + 1) * cols, :] = (
+                    lateral[r * cols : (r + 1) * cols] + lifted
+                ).astype(BF16)
+        merged_t[:, start : start + cells // 2] = jnp.transpose(merged[start : start + cells // 2, :])
+    copies[5].wait()
 
 
 def strips_of(stack, halo):
@@ -98,7 +112,7 @@
             out[start : start + channels, :] = part[:, j * channels : (j + 1) * channels]
 
 
-def pair_kernel_grad_kernel(stack, merged_t, cot, merged, out, image):
+def pair_kernel_grad_kernel(stack, merged_t, cot, merged, out, image, pads):
     here = lax.axis_index("space")
     rows, cols, channels = cot.shape
     half = channels // 2
@@ -108,7 +122,7 @@
     own, other = 1 + rows * here, 1 + rows * (1 - here)
     for r in range(rows):
         row = cot[r]
-        put_shifted(image, other + r, jnp.where(here == 0, row[:, :half], row[:, half:]), 1)
+        put_shifted(image, other + r, jnp.where(here == 0, row[:, :half], row[:, half:]), 1, pads.at[r])
         for j in range(3):
             start = j * channels
             left, right = stack[r, :, start : start + half], stack[r, :, start + half : start + channels]
@@ -123,8 +137,9 @@
         out[tap * channels : (tap + 1) * channels, :] = part[:, tap * half : (tap + 1) * half]
 
 
-def data_grad_kernel(peers, stack, before, after, feat, out_w, grad, halo, *outs):
-    put_halo(halo, before[before.shape[0] - 1], after[0], 0, peers, 1)
+def data_grad_kernel(peers, stack, before, after, feat, out_w, grad, halo, *refs):
+    outs, edge_pads = refs[:-1], refs[-1]
+    put_halo(halo, before[before.shape[0] - 1], after[0], 0, peers, 1, edge_pads)
     cells = jnp.concatenate(strips_of(stack, halo), axis=1)
     taps = jnp.concatenate([out_w[tap] for tap in range(9)], axis=1)
     total = lax.dot_general(cells, taps, (((1,), (1,)), ((), ())), preferred_element_type=F32)
@@ -133,12 +148,12 @@
 
 
 def forward_kernel(peers, merged, out_w, grad, *refs):
-    edges, (out, grad_top, stack, near, sem) = refs[:-5], refs[-5:]
+    edges, (out, grad_top, stack, near, row_pads, sem) = refs[:-6], refs[-6:]
     rows, cols, channels = merged.shape
     half = cols // 2
     for r in range(rows):
-        put_shifted(stack, r + 1, merged[r], -1)
-    put_halo(stack, edges[0][edges[0].shape[0] - 1], edges[1][0], rows, peers, -1)
+        put_shifted(stack, r + 1, merged[r], -1, row_pads.at[r])
+    put_halo(stack, edges[0][edges[0].shape[0] - 1], edges[1][0], rows, peers, -1, row_pads.at[pl.ds(rows, 2)])
     cells = jnp.concatenate([stack[i : i + rows].reshape(rows * cols, 3 * channels) for i in range(3)], axis=1)
     total = jnp.dot(cells, out_w[...].reshape(9 * channels, channels), preferred_element_type=F32)
     near[...] = total.astype(BF16).reshape(out.shape)
@@ -257,6 +272,9 @@
         if not halves:
             return [jax.ShapeDtypeStruct((length, channels), F32)]
         return [jax.ShapeDtypeStruct((length, channels // 2), kind) for kind in (F32, BF16)]
+
+    def pads(count, width):
+        return pltpu.VMEM((count, cols + 16, width), F32)
 
     outs, tops, parts = [], [], None
     for image in range(images):
@@ -277,7 +295,7 @@
                 )
             ],
             in_specs=[pl.BlockSpec(memory_space=pltpu.HBM)] * 5,
-            scratch_shapes=[*[pltpu.VMEM(array.shape, BF16) for array in arrays[:3]], pltpu.SemaphoreType.DMA((5,))],
+            scratch_shapes=[*[pltpu.VMEM(array.shape, BF16) for array in arrays[:3]], pads(rows, channels), pltpu.SemaphoreType.DMA((6,))],
             compiler_params=params,
             cost_estimate=pl.CostEstimate(
                 flops=2 * cells * channels * 4 * in_channels, bytes_accessed=4 * 2**20, transcendentals=0
@@ -292,6 +310,7 @@
                 jax.ShapeDtypeStruct((2, cols, 3 * channels), BF16),
                 *sums(in_channels),
             ],
+            scratch_shapes=[pads(2, channels)],
             compiler_params=params,
             cost_estimate=pl.CostEstimate(
                 flops=2 * cells * channels * (9 * channels + in_channels), bytes_accessed=4 * 2**20, transcendentals=0
@@ -305,7 +324,10 @@
             kernel_sums = pl.pallas_call(
                 pair_kernel_grad_kernel,
                 out_shape=jax.ShapeDtypeStruct((9 * channels, channels // 2), F32),
-                scratch_shapes=[pltpu.VMEM((2 * rows + 2, cols, 3 * channels // 2), BF16)],
+                scratch_shapes=[
+                    pltpu.VMEM((2 * rows + 2, cols, 3 * channels // 2), BF16),
+                    pads(rows, channels // 2),
+                ],
                 compiler_params=params,
                 cost_estimate=kernel_cost,
             )(stack, merged_t, cot_after, edges[0].reshape(cells, channels))
@@ -326,6 +348,7 @@
             scratch_shapes=[
                 pltpu.VMEM((rows + 2, cols, 3 * channels), BF16),
                 pltpu.VMEM((rows, cols, channels), BF16),
+                pads(rows + 2, channels),
                 pltpu.SemaphoreType.DMA,
             ],
             compiler_params=params,

time: 40.4 us -> 40.7 us (level)
  transfers between devices with their start and end apart: 16 -> 16, of which waited for: 8 -> 8; matrix products, arithmetic and copies ran while one was open for 0% -> 0% of each run, Pallas kernels for 21% -> 22%
where the time goes in v13:
time: 40.7 us; the launch traced here: 40.6 us
  waiting for transfers between devices  15.9 us (39%)
  starting transfers between devices  13.9 us (34%)
  Pallas kernels  10 us (25%)
  between operations  0.73 us (2%)
    ppermute x9, waiting for transfers between devices, exchange(): return lax.ppermute(array, ('dp', 'space'), pairs)  15.6 us
    ppermute x9, starting transfers between devices, exchange(): return lax.ppermute(array, ('dp', 'space'), pairs)  12.2 us
    pallas_call x1, Pallas kernels, local(): pl.pallas_call(functools.partial(forward_kernel, peers), out_shape=[jax.S...  2.53 us
    pallas_call x1, Pallas kernels, local(): pl.pallas_call(merge_kernel, out_shape=[jax.ShapeDtypeStruct(shape, BF16)...  2.15 us
    pallas_call x1, Pallas kernels, local(): pl.pallas_call(functools.partial(data_grad_kernel, peers), out_shape=[jax...  1.71 us
    pallas_call x1, Pallas kernels, local(): pl.pallas_call(pair_kernel_grad_kernel, out_shape=jax.ShapeDtypeStruct((9...  1.55 us
    ppermute x5, starting transfers between devices, swap(): return lax.ppermute(array, 'space', [(0, 1), (1, 0)])  1.03 us
    pallas_call x1, Pallas kernels, sum_everywhere(): call(functools.partial(place_kernel, True), *results, **place)  0.91 us
  transfers between devices with their start and end apart: 16, of which 8 were waited for; matrix products, arithmetic and copies ran while one was open for 0% of the time, Pallas kernels for 22%

profile of v13, /device:TPU:0, one launch (start us, length us, event | category | flops | bytes accessed | tf_op | source)
XLA Modules:
  0.0 40.6 jit_solution(7305170558867507446)
XLA Ops:
  0.6 0.5 %collective-permute-start = (bf16[8,96,256]{2,1,0:T(8,128)(2,1)}, bf16[8,96,256]{2,1,0:T(8,128)(2,1)S(1)}, u32[]{:S(2)}, u32[]{:S(2)}) collective-permute-start(bf16[8,96,256]{2,1,0:T(8,128)(2,1)} %bitcast.16), channel_id=1, source_target_pairs={{0,1},{1,0},{2,3},{3,2},{4,5},{5,4},{6,7},{7,6},{8,9},{9,8},{10,11... | collective-permute-start | bytes 1179656 | tf_op jit(solution)/shard_map/ppermute | solution.py:19
  1.1 2.2 %shard_map.84 = (bf16[768,256]{1,0:T(8,128)(2,1)S(1)}, bf16[256,768]{1,0:T(8,128)(2,1)S(1)}, bf16[8,96,768]{2,1,0:T(8,128)(2,1)S(1)}, bf16[768,512]{1,0:T(8,128)(2,1)S(1)}, bf16[9,256,256]{2,1,0:T(8,128)(2,1)S(1)}) custom-call(bf16[8,96,256]{2,1,0:T(8,128)(2,1)} %bitcast.17, bf16[512,256]{1,0:T(8,128)(2,1)} %refs_1_.1, bf16[4,48,256]{2,1,0:T(8,128)(2,1)} %bitcast.18, ...), custom_call_target="tpu_custom_call" | custom-call | flops 805306368 | bytes 4194304 | tf_op jit(solution)/shard_map/pallas_call | solution.py:285
  3.3 0.1 collective-permute-start.1
  3.4 0.0 collective-permute-done.before.after.cot
  3.4 1.7 %shard_map.85 = (bf16[768,256]{1,0:T(8,128)(2,1)S(1)}, bf16[2,96,768]{2,1,0:T(8,128)(2,1)}, f32[512,128]{1,0:T(8,128)S(1)}, bf16[512,128]{1,0:T(8,128)(2,1)S(1)}) custom-call(bf16[8,96,768]{2,1,0:T(8,128)(2,1)S(1)} %get-tuple-element.24.stack, bf16[8,96,256]{2,1,0:T(8,128)(2,1)S(1)} %collective-permute-done.before.after.cot, ...), custom_call_target="tpu_custom_call" | custom-call | flops 1107296256 | bytes 4194304 | tf_op jit(solution)/shard_map/pallas_call | solution.py:306
  5.2 0.5 %collective-permute-start.2 = (bf16[512,128]{1,0:T(8,128)(2,1)S(1)}, bf16[512,128]{1,0:T(8,128)(2,1)S(1)}, u32[]{:S(2)}, u32[]{:S(2)}) collective-permute-start(bf16[512,128]{1,0:T(8,128)(2,1)S(1)} %get-tuple-element.31), channel_id=1, source_target_pairs={{0,1},{1,0},{2,3},{3,2},{4,5},{5,4},{6,7},{7,6},{8,9},{9,8},{10,11... | collective-permute-start | bytes 393224 | tf_op jit(solution)/shard_map/ppermute | solution.py:230
  5.7 0.0 collective-permute-done.1.refs_0_.refs_1_
  5.7 1.5 %shard_map.87.kernel_sums = f32[2304,128]{1,0:T(8,128)S(1)} custom-call(bf16[8,96,768]{2,1,0:T(8,128)(2,1)S(1)} %get-tuple-element.24.stack, bf16[256,768]{1,0:T(8,128)(2,1)S(1)} %get-tuple-element.29.merged_t, bf16[8,96,256]{2,1,0:T(8,128)(2,1)S(1)} %collective-permute-done.before.after.cot, bf16[768,256]{1,0:T(8,128)(2,1)S(1)} %bitcast.9), custom_call_target="tpu_custom_call" | custom-call | flops 905969664 | bytes 4194304 | tf_op jit(solution)/shard_map/pallas_call | solution.py:324
  7.2 0.1 shard_map.88
  7.4 3.5 %collective-permute-start.3 = (bf16[704,128]{1,0:T(8,128)(2,1)S(1)}, bf16[704,128]{1,0:T(8,128)(2,1)S(1)}, u32[]{:S(2)}, u32[]{:S(2)}) collective-permute-start(bf16[704,128]{1,0:T(8,128)(2,1)S(1)} %get-tuple-element.33), channel_id=1, source_target_pairs={{0,6},{1,25},{2,4},{3,27},{4,2},{5,29},{6,0},{7,31},{8,14},{9,17},... | collective-permute-start | bytes 540680 | tf_op jit(solution)/shard_map/ppermute | solution.py:226
  10.9 0.5 %collective-permute-start.4 = (bf16[704,128]{1,0:T(8,128)(2,1)S(1)}, bf16[704,128]{1,0:T(8,128)(2,1)S(1)}, u32[]{:S(2)}, u32[]{:S(2)}) collective-permute-start(bf16[704,128]{1,0:T(8,128)(2,1)S(1)} %get-tuple-element.34), channel_id=1, source_target_pairs={{0,4},{1,17},{2,6},{3,19},{4,0},{5,21},{6,2},{7,23},{8,12},{9,25},... | collective-permute-start | bytes 540680 | tf_op jit(solution)/shard_map/ppermute | solution.py:226
  11.4 0.1 collective-permute-start.5
  11.5 2.8 %collective-permute-done.3.three = bf16[704,128]{1,0:T(8,128)(2,1)S(1)} collective-permute-done((bf16[704,128]{1,0:T(8,128)(2,1)S(1)}, bf16[704,128]{1,0:T(8,128)(2,1)S(1)}, u32[]{:S(2)}, u32[]{:S(2)}) %collective-permute-start.3) | collective-permute-done | bytes 180256 | tf_op jit(solution)/shard_map/ppermute | solution.py:226
  14.4 2.0 %collective-permute-done.4.two = bf16[704,128]{1,0:T(8,128)(2,1)S(1)} collective-permute-done((bf16[704,128]{1,0:T(8,128)(2,1)S(1)}, bf16[704,128]{1,0:T(8,128)(2,1)S(1)}, u32[]{:S(2)}, u32[]{:S(2)}) %collective-permute-start.4) | collective-permute-done | bytes 180256 | tf_op jit(solution)/shard_map/ppermute | solution.py:226
  16.4 0.5 %collective-permute-done.5.one = bf16[704,128]{1,0:T(8,128)(2,1)S(1)} collective-permute-done((bf16[704,128]{1,0:T(8,128)(2,1)S(1)}, bf16[704,128]{1,0:T(8,128)(2,1)S(1)}, u32[]{:S(2)}, u32[]{:S(2)}) %collective-permute-start.5) | collective-permute-done | bytes 180256 | tf_op jit(solution)/shard_map/ppermute | solution.py:226
  16.9 0.1 shard_map.89.own
  17.0 3.7 %collective-permute-start.6 = (bf16[704,128]{1,0:T(8,128)(2,1)S(1)}, bf16[704,128]{1,0:T(8,128)(2,1)S(1)}, u32[]{:S(2)}, u32[]{:S(2)}) collective-permute-start(bf16[704,128]{1,0:T(8,128)(2,1)S(1)} %shard_map.89.own), channel_id=1, source_target_pairs={{0,24},{1,7},{2,26},{3,5},{4,28},{5,3},{6,30},{7,1},{8,16},{9,15},... | collective-permute-start | bytes 540680 | tf_op jit(solution)/shard_map/ppermute | solution.py:226
  20.6 0.8 %collective-permute-start.8 = (bf16[704,128]{1,0:T(8,128)(2,1)S(1)}, bf16[704,128]{1,0:T(8,128)(2,1)S(1)}, u32[]{:S(2)}, u32[]{:S(2)}) collective-permute-start(bf16[704,128]{1,0:T(8,128)(2,1)S(1)} %shard_map.89.own), channel_id=1, source_target_pairs={{0,8},{1,3},{2,10},{3,1},{4,12},{5,7},{6,14},{7,5},{8,0},{9,11},{1... | collective-permute-start | bytes 540680 | tf_op jit(solution)/shard_map/ppermute | solution.py:226
  21.4 2.5 %shard_map.86 = (bf16[8,96,256]{2,1,0:T(8,128)(2,1)}, bf16[4,48,256]{2,1,0:T(8,128)(2,1)}) custom-call(bf16[8,96,256]{2,1,0:T(8,128)(2,1)S(1)} %bitcast.11, bf16[9,256,256]{2,1,0:T(8,128)(2,1)S(1)} %get-tuple-element.23.out_w, bf16[768,256]{1,0:T(8,128)(2,1)S(1)} %get-tuple-element.26.grad, bf16[8,96,256]{2,1,0:T(8,128)(2,1)S(1)} %collective-permute-done.1.refs_0_.refs_1_, ...), custom_call_target="tpu_custom_call" | custom-call | flops 905969664 | bytes 2097152 | tf_op jit(solution)/shard_map/pallas_call | solution.py:341
  24.0 0.5 %collective-permute-done.6.three = bf16[704,128]{1,0:T(8,128)(2,1)S(1)} collective-permute-done((bf16[704,128]{1,0:T(8,128)(2,1)S(1)}, bf16[704,128]{1,0:T(8,128)(2,1)S(1)}, u32[]{:S(2)}, u32[]{:S(2)}) %collective-permute-start.6) | collective-permute-done | bytes 180256 | tf_op jit(solution)/shard_map/ppermute | solution.py:226
  24.4 4.9 %collective-permute-done.7.two = bf16[704,128]{1,0:T(8,128)(2,1)S(1)} collective-permute-done((bf16[704,128]{1,0:T(8,128)(2,1)S(1)}, bf16[704,128]{1,0:T(8,128)(2,1)S(1)}, u32[]{:S(2)}, u32[]{:S(2)}) %collective-permute-start.7) | collective-permute-done | bytes 180256 | tf_op jit(solution)/shard_map/ppermute | solution.py:226
  29.3 0.1 shard_map.90.refs_0_
  29.4 2.0 %collective-permute-start.10 = (bf16[704,128]{1,0:T(8,128)(2,1)S(1)}, bf16[704,128]{1,0:T(8,128)(2,1)S(1)}, u32[]{:S(2)}, u32[]{:S(2)}) collective-permute-start(bf16[704,128]{1,0:T(8,128)(2,1)S(1)} %shard_map.90.refs_0_), channel_id=1, source_target_pairs={{0,6},{1,25},{2,4},{3,27},{4,2},{5,29},{6,0},{7,31},{8,14},{9,17},... | collective-permute-start | bytes 540680 | tf_op jit(solution)/shard_map/ppermute | solution.py:226
  31.4 1.0 %collective-permute-start.12 = (bf16[704,128]{1,0:T(8,128)(2,1)S(1)}, bf16[704,128]{1,0:T(8,128)(2,1)S(1)}, u32[]{:S(2)}, u32[]{:S(2)}) collective-permute-start(bf16[704,128]{1,0:T(8,128)(2,1)S(1)} %shard_map.90.refs_0_), channel_id=1, source_target_pairs={{0,4},{1,17},{2,6},{3,19},{4,0},{5,21},{6,2},{7,23},{8,12},{9,25},... | collective-permute-start | bytes 540680 | tf_op jit(solution)/shard_map/ppermute | solution.py:226
  32.4 0.6 %collective-permute-start.14 = (bf16[704,128]{1,0:T(8,128)(2,1)S(1)}, bf16[704,128]{1,0:T(8,128)(2,1)S(1)}, u32[]{:S(2)}, u32[]{:S(2)}) collective-permute-start(bf16[704,128]{1,0:T(8,128)(2,1)S(1)} %shard_map.90.refs_0_), channel_id=1, source_target_pairs={{0,2},{1,9},{2,0},{3,11},{4,6},{5,13},{6,4},{7,15},{8,10},{9,1},{1... | collective-permute-start | bytes 540680 | tf_op jit(solution)/shard_map/ppermute | solution.py:226
  33.0 3.0 %collective-permute-done.10.refs_1_ = bf16[704,128]{1,0:T(8,128)(2,1)S(1)} collective-permute-done((bf16[704,128]{1,0:T(8,128)(2,1)S(1)}, bf16[704,128]{1,0:T(8,128)(2,1)S(1)}, u32[]{:S(2)}, u32[]{:S(2)}) %collective-permute-start.10) | collective-permute-done | bytes 180256 | tf_op jit(solution)/shard_map/ppermute | solution.py:226
  36.0 1.8 %collective-permute-done.12.refs_2_ = bf16[704,128]{1,0:T(8,128)(2,1)S(1)} collective-permute-done((bf16[704,128]{1,0:T(8,128)(2,1)S(1)}, bf16[704,128]{1,0:T(8,128)(2,1)S(1)}, u32[]{:S(2)}, u32[]{:S(2)}) %collective-permute-start.12) | collective-permute-done | bytes 180256 | tf_op jit(solution)/shard_map/ppermute | solution.py:226
  37.8 0.4 collective-permute-start.13
  38.2 0.1 collective-permute-start.15
  38.4 0.9 %shard_map.91 = (bf16[2304,256]{1,0:T(8,128)(2,1)}, bf16[512,256]{1,0:T(8,128)(2,1)}) custom-call(bf16[704,128]{1,0:T(8,128)(2,1)S(1)} %shard_map.90.refs_0_, bf16[704,128]{1,0:T(8,128)(2,1)S(1)} %collective-permute-done.10.refs_1_, bf16[704,128]{1,0:T(8,128)(2,1)S(1)} %collective-permute-done.12.refs_2_, bf16[704,128]{1,0:T(8,128)(2,1)S(1)} %collective-permute-done.14.refs_3_), custom_call_target="tpu_custom_call" | custom-call | tf_op jit(solution)/shard_map/pallas_call | solution.py:257
  39.3 0.4 collective-permute-done.15.refs_3_
  39.7 0.9 %shard_map.92 = (bf16[2304,256]{1,0:T(8,128)(2,1)}, bf16[512,256]{1,0:T(8,128)(2,1)}) custom-call(bf16[704,128]{1,0:T(8,128)(2,1)S(1)} %collective-permute-done.9.refs_0_, bf16[704,128]{1,0:T(8,128)(2,1)S(1)} %collective-permute-done.11.refs_1_, bf16[704,128]{1,0:T(8,128)(2,1)S(1)} %collective-permute-done.13.refs_2_, ...), custom_call_target="tpu_custom_call", output_to_operand_aliasing={{0}: (4, {}), {1}: (5, {})} | custom-call | tf_op jit(solution)/shard_map/pallas_call | solution.py:259
  (9 shorter events, 0.0 us)
Async XLA Ops:
  0.6 2.8 %collective-permute-start = (bf16[8,96,256]{2,1,0:T(8,128)(2,1)}, bf16[8,96,256]{2,1,0:T(8,128)(2,1)S(1)}, u32[]{:S(2)}, u32[]{:S(2)}) collective-permute-start(bf16[8,96,256]{2,1,0:T(8,128)(2,1)} %bitcast.16), channel_id=1, source_target_pairs={{0,1},{1,0},{2,3},{3,2},{4,5},{5,4},{6,7},{7,6},{8,9},{9,8},{10,11... | collective-permute-start | bytes 1179656 | tf_op jit(solution)/shard_map/ppermute | solution.py:19
  3.3 2.4 %collective-permute-start.1 = (bf16[8,96,256]{2,1,0:T(8,128)(2,1)S(1)}, bf16[8,96,256]{2,1,0:T(8,128)(2,1)S(1)}, u32[]{:S(2)}, u32[]{:S(2)}) collective-permute-start(bf16[8,96,256]{2,1,0:T(8,128)(2,1)S(1)} %bitcast.10), channel_id=1, source_target_pairs={{0,1},{1,0},{2,3},{3,2},{4,5},{5,4},{6,7},{7,6},{8,9},{9,8},{10,11... | collective-permute-start | bytes 1179656 | tf_op jit(solution)/shard_map/ppermute | solution.py:19
  5.2 2.1 %collective-permute-start.2 = (bf16[512,128]{1,0:T(8,128)(2,1)S(1)}, bf16[512,128]{1,0:T(8,128)(2,1)S(1)}, u32[]{:S(2)}, u32[]{:S(2)}) collective-permute-start(bf16[512,128]{1,0:T(8,128)(2,1)S(1)} %get-tuple-element.31), channel_id=1, source_target_pairs={{0,1},{1,0},{2,3},{3,2},{4,5},{5,4},{6,7},{7,6},{8,9},{9,8},{10,11... | collective-permute-start | bytes 393224 | tf_op jit(solution)/shard_map/ppermute | solution.py:230
  7.4 7.0 %collective-permute-start.3 = (bf16[704,128]{1,0:T(8,128)(2,1)S(1)}, bf16[704,128]{1,0:T(8,128)(2,1)S(1)}, u32[]{:S(2)}, u32[]{:S(2)}) collective-permute-start(bf16[704,128]{1,0:T(8,128)(2,1)S(1)} %get-tuple-element.33), channel_id=1, source_target_pairs={{0,6},{1,25},{2,4},{3,27},{4,2},{5,29},{6,0},{7,31},{8,14},{9,17},... | collective-permute-start | bytes 540680 | tf_op jit(solution)/shard_map/ppermute | solution.py:226
  10.9 5.5 %collective-permute-start.4 = (bf16[704,128]{1,0:T(8,128)(2,1)S(1)}, bf16[704,128]{1,0:T(8,128)(2,1)S(1)}, u32[]{:S(2)}, u32[]{:S(2)}) collective-permute-start(bf16[704,128]{1,0:T(8,128)(2,1)S(1)} %get-tuple-element.34), channel_id=1, source_target_pairs={{0,4},{1,17},{2,6},{3,19},{4,0},{5,21},{6,2},{7,23},{8,12},{9,25},... | collective-permute-start | bytes 540680 | tf_op jit(solution)/shard_map/ppermute | solution.py:226
  11.4 5.5 %collective-permute-start.5 = (bf16[704,128]{1,0:T(8,128)(2,1)S(1)}, bf16[704,128]{1,0:T(8,128)(2,1)S(1)}, u32[]{:S(2)}, u32[]{:S(2)}) collective-permute-start(bf16[704,128]{1,0:T(8,128)(2,1)S(1)} %get-tuple-element.35), channel_id=1, source_target_pairs={{0,2},{1,9},{2,0},{3,11},{4,6},{5,13},{6,4},{7,15},{8,10},{9,1},{1... | collective-permute-start | bytes 540680 | tf_op jit(solution)/shard_map/ppermute | solution.py:226
  17.0 7.5 %collective-permute-start.6 = (bf16[704,128]{1,0:T(8,128)(2,1)S(1)}, bf16[704,128]{1,0:T(8,128)(2,1)S(1)}, u32[]{:S(2)}, u32[]{:S(2)}) collective-permute-start(bf16[704,128]{1,0:T(8,128)(2,1)S(1)} %shard_map.89.own), channel_id=1, source_target_pairs={{0,24},{1,7},{2,26},{3,5},{4,28},{5,3},{6,30},{7,1},{8,16},{9,15},... | collective-permute-start | bytes 540680 | tf_op jit(solution)/shard_map/ppermute | solution.py:226
  20.6 8.7 %collective-permute-start.7 = (bf16[704,128]{1,0:T(8,128)(2,1)S(1)}, bf16[704,128]{1,0:T(8,128)(2,1)S(1)}, u32[]{:S(2)}, u32[]{:S(2)}) collective-permute-start(bf16[704,128]{1,0:T(8,128)(2,1)S(1)} %shard_map.89.own), channel_id=1, source_target_pairs={{0,16},{1,5},{2,18},{3,7},{4,20},{5,1},{6,22},{7,3},{8,24},{9,13},... | collective-permute-start | bytes 540680 | tf_op jit(solution)/shard_map/ppermute | solution.py:226
  20.6 8.7 %collective-permute-start.8 = (bf16[704,128]{1,0:T(8,128)(2,1)S(1)}, bf16[704,128]{1,0:T(8,128)(2,1)S(1)}, u32[]{:S(2)}, u32[]{:S(2)}) collective-permute-start(bf16[704,128]{1,0:T(8,128)(2,1)S(1)} %shard_map.89.own), channel_id=1, source_target_pairs={{0,8},{1,3},{2,10},{3,1},{4,12},{5,7},{6,14},{7,5},{8,0},{9,11},{1... | collective-permute-start | bytes 540680 | tf_op jit(solution)/shard_map/ppermute | solution.py:226
  29.4 6.6 %collective-permute-start.10 = (bf16[704,128]{1,0:T(8,128)(2,1)S(1)}, bf16[704,128]{1,0:T(8,128)(2,1)S(1)}, u32[]{:S(2)}, u32[]{:S(2)}) collective-permute-start(bf16[704,128]{1,0:T(8,128)(2,1)S(1)} %shard_map.90.refs_0_), channel_id=1, source_target_pairs={{0,6},{1,25},{2,4},{3,27},{4,2},{5,29},{6,0},{7,31},{8,14},{9,17},... | collective-permute-start | bytes 540680 | tf_op jit(solution)/shard_map/ppermute | solution.py:226
  31.4 6.4 %collective-permute-start.12 = (bf16[704,128]{1,0:T(8,128)(2,1)S(1)}, bf16[704,128]{1,0:T(8,128)(2,1)S(1)}, u32[]{:S(2)}, u32[]{:S(2)}) collective-permute-start(bf16[704,128]{1,0:T(8,128)(2,1)S(1)} %shard_map.90.refs_0_), channel_id=1, source_target_pairs={{0,4},{1,17},{2,6},{3,19},{4,0},{5,21},{6,2},{7,23},{8,12},{9,25},... | collective-permute-start | bytes 540680 | tf_op jit(solution)/shard_map/ppermute | solution.py:226
  32.4 5.8 %collective-permute-start.14 = (bf16[704,128]{1,0:T(8,128)(2,1)S(1)}, bf16[704,128]{1,0:T(8,128)(2,1)S(1)}, u32[]{:S(2)}, u32[]{:S(2)}) collective-permute-start(bf16[704,128]{1,0:T(8,128)(2,1)S(1)} %shard_map.90.refs_0_), channel_id=1, source_target_pairs={{0,2},{1,9},{2,0},{3,11},{4,6},{5,13},{6,4},{7,15},{8,10},{9,1},{1... | collective-permute-start | bytes 540680 | tf_op jit(solution)/shard_map/ppermute | solution.py:226
  33.0 6.3 %collective-permute-start.9 = (bf16[704,128]{1,0:T(8,128)(2,1)S(1)}, bf16[704,128]{1,0:T(8,128)(2,1)S(1)}, u32[]{:S(2)}, u32[]{:S(2)}) collective-permute-start(bf16[704,128]{1,0:T(8,128)(2,1)S(1)} %shard_map.90.refs_0_), channel_id=1, source_target_pairs={{0,1},{1,0},{2,3},{3,2},{4,5},{5,4},{6,7},{7,6},{8,9},{9,8},{10,11... | collective-permute-start | bytes 540680 | tf_op jit(solution)/shard_map/ppermute | solution.py:230
  36.0 3.3 %collective-permute-start.11 = (bf16[704,128]{1,0:T(8,128)(2,1)S(1)}, bf16[704,128]{1,0:T(8,128)(2,1)S(1)}, u32[]{:S(2)}, u32[]{:S(2)}) collective-permute-start(bf16[704,128]{1,0:T(8,128)(2,1)S(1)} %collective-permute-done.10.refs_1_), channel_id=1, source_target_pairs={{0,1},{1,0},{2,3},{3,2},{4,5},{5,4},{6,7},{7,6},{8,9},{9,8},{10,11... | collective-permute-start | bytes 540680 | tf_op jit(solution)/shard_map/ppermute | solution.py:230
  37.8 1.5 %collective-permute-start.13 = (bf16[704,128]{1,0:T(8,128)(2,1)S(1)}, bf16[704,128]{1,0:T(8,128)(2,1)S(1)}, u32[]{:S(2)}, u32[]{:S(2)}) collective-permute-start(bf16[704,128]{1,0:T(8,128)(2,1)S(1)} %collective-permute-done.12.refs_2_), channel_id=1, source_target_pairs={{0,1},{1,0},{2,3},{3,2},{4,5},{5,4},{6,7},{7,6},{8,9},{9,8},{10,11... | collective-permute-start | bytes 540680 | tf_op jit(solution)/shard_map/ppermute | solution.py:230
  38.2 1.4 %collective-permute-start.15 = (bf16[704,128]{1,0:T(8,128)(2,1)S(1)}, bf16[704,128]{1,0:T(8,128)(2,1)S(1)}, u32[]{:S(2)}, u32[]{:S(2)}) collective-permute-start(bf16[704,128]{1,0:T(8,128)(2,1)S(1)} %collective-permute-done.14.refs_3_), channel_id=1, source_target_pairs={{0,1},{1,0},{2,3},{3,2},{4,5},{5,4},{6,7},{7,6},{8,9},{9,8},{10,11... | collective-permute-start | bytes 540680 | tf_op jit(solution)/shard_map/ppermute | solution.py:230

commit v14 on v12

--- a/solution.py
+++ b/solution.py
@@ -98,7 +98,12 @@
             out[start : start + channels, :] = part[:, j * channels : (j + 1) * channels]
 
 
-def pair_kernel_grad_kernel(stack, merged_t, cot, merged, out, image):
+def cells_of(image, first, rows):
+    strips = [image[pl.ds(first + 1 - i, rows)] for i in range(3)]
+    return jnp.concatenate([strip.reshape(-1, strip.shape[-1]) for strip in strips], axis=1)
+
+
+def own_kernel_grad_kernel(stack, merged_t, cot, image, sums):
     here = lax.axis_index("space")
     rows, cols, channels = cot.shape
     half = channels // 2
@@ -113,17 +118,24 @@
             start = j * channels
             left, right = stack[r, :, start : start + half], stack[r, :, start + half : start + channels]
             image[own + r, :, j * half : (j + 1) * half] = jnp.where(here == 0, left, right)
-    cells = []
-    for first in (own, other):
-        strips = [image[pl.ds(first + 1 - i, rows)].reshape(rows * cols, 3 * half) for i in range(3)]
-        cells.append(jnp.concatenate(strips, axis=1))
-    left = jnp.concatenate([merged_t[...], jnp.transpose(merged[...])], axis=1)
-    part = jnp.dot(left, jnp.concatenate(cells, axis=0), preferred_element_type=F32)
+    sums[...] = jnp.dot(merged_t[...], cells_of(image, own, rows), preferred_element_type=F32)
+
+
+def rest_kernel_grad_kernel(image, sums, merged, *refs):
+    outs, total = refs[:4], refs[4]
+    here, (place, _) = lax.axis_index("space"), places()
+    channels, half = merged.shape[1], total.shape[1]
+    rows = (image.shape[0] - 2) // 2
+    cells = cells_of(image, 1 + rows * (1 - here), rows)
+    part = sums[...] + jnp.dot(jnp.transpose(merged[...]), cells, preferred_element_type=F32)
     for tap in range(9):
-        out[tap * channels : (tap + 1) * channels, :] = part[:, tap * half : (tap + 1) * half]
-
-
-def data_grad_kernel(peers, stack, before, after, feat, out_w, grad, halo, *outs):
+        total[tap * channels : (tap + 1) * channels, :] = part[:, tap * half : (tap + 1) * half]
+    for k, out in zip((0, 3, 2, 1), outs):
+        out[...] = total[block(place ^ k, out.shape[0]), :].astype(out.dtype)
+
+
+def data_grad_kernel(peers, waits, stack, before, after, feat, out_w, *refs):
+    grad, halo, *outs = refs[waits:]
     put_halo(halo, before[before.shape[0] - 1], after[0], 0, peers, 1)
     cells = jnp.concatenate(strips_of(stack, halo), axis=1)
     taps = jnp.concatenate([out_w[tap] for tap in range(9)], axis=1)
@@ -163,15 +175,6 @@
     return pl.ds(pl.multiple_of(index * length, 16), length)
 
 
-def cut_kernel(kernel_sums, mine, got, *refs):
-    place, _ = places()
-    edge, share = kernel_sums.shape[0] // 4, mine.shape[0] // 4
-    for k, out in zip((0, 3, 2, 1), refs):
-        out[:edge, :] = kernel_sums[block(place ^ k, edge), :].astype(out.dtype)
-        rows = block(place ^ k, share)
-        out[edge:, :] = (mine[rows, :] + got[rows, :].astype(F32)).astype(out.dtype)
-
-
 def add_kernel(own, three, two, one, out):
     total = own[...] + one[...].astype(F32) + two[...].astype(F32) + three[...].astype(F32)
     out[...] = total.astype(BF16)
@@ -184,18 +187,28 @@
 
 
 def place_kernel(pair, *refs):
-    results, sems = refs[-3:-1], refs[-1]
+    result, sems = refs[-2:]
     side = lax.axis_index("space")
     columns, place = (1 - side, places()[1]) if pair else (side, places()[0])
     lanes = pl.ds(pl.multiple_of(columns * 128, 128), 128)
+    share = result.shape[0] // 8
     copies = []
     for k, quarter in zip((0, 3, 2, 1), refs):
-        start = 0
-        for result in results:
-            share = result.shape[0] // 4
-            to = result.at[block(place ^ k, share), lanes]
-            copies.append(pltpu.make_async_copy(quarter.at[pl.ds(start, share), :], to, sems.at[len(copies)]))
-            start += share
+        for part in range(2):
+            to = result.at[block(2 * (place ^ k) + part, share), lanes]
+            copies.append(pltpu.make_async_copy(quarter.at[pl.ds(part * share, share), :], to, sems.at[len(copies)]))
+    for copy in copies:
+        copy.start()
+    for copy in copies:
+        copy.wait()
+
+
+def place_lateral_kernel(mine, other, result, sems):
+    side = lax.axis_index("space")
+    copies = []
+    for columns, half in ((side, mine), (1 - side, other)):
+        lanes = pl.ds(pl.multiple_of(columns * 128, 128), 128)
+        copies.append(pltpu.make_async_copy(half, result.at[:, lanes], sems.at[len(copies)]))
     for copy in copies:
         copy.start()
     for copy in copies:
@@ -224,24 +237,42 @@
     )
 
 
-def sum_everywhere(kernel_sums, lateral_part, scale, after):
-    lengths, width = [kernel_sums.shape[0], lateral_part[0].shape[0]], kernel_sums.shape[1]
+def sum_lateral(mine, got, scale):
+    length, width = mine.shape
+    plane = [[2 * (4 * z + q) + core for q in range(4)] for z in range(4) for core in range(2)]
+    line = [[2 * (4 * z + q) + core for z in range(4)] for q in range(4) for core in range(2)]
+    total = mine + got.astype(F32)
+    for groups in (plane, line):
+        total = lax.psum(total, ("dp", "space"), axis_index_groups=groups)
+    total = (total * scale).astype(BF16)
+    [result] = call(
+        place_lateral_kernel,
+        ((length, 2 * width), BF16),
+        out_specs=[pl.BlockSpec(memory_space=pltpu.HBM)],
+        scratch_shapes=[pltpu.SemaphoreType.DMA((2,))],
+    )(total, swap(total))
+    return result
+
+
+def sum_kernel(pieces, scale, after):
+    own, *pieces = pieces
+    quarter = own.shape
     vmem, far = pl.BlockSpec(memory_space=pltpu.VMEM), pl.BlockSpec(memory_space=pltpu.HBM)
     after = pltpu.with_memory_space_constraint(after, pltpu.HBM)
-    quarter = (sum(lengths) // 4, width)
-    own, *pieces = call(cut_kernel, (quarter, F32), *[(quarter, BF16)] * 3)(kernel_sums, *lateral_part)
     three, two, one = [exchange(piece, 0, k) for piece, k in zip(pieces, (3, 2, 1))]
-    [total] = call(add_kernel, (quarter, BF16))(own, three, two, one)
+    slow = pl.CostEstimate(flops=2**32, bytes_accessed=2**10, transcendentals=0)
+    [total] = call(add_kernel, (quarter, BF16), cost_estimate=slow)(own, three, two, one)
     three, two, one = [exchange(total, 1, k) for k in (3, 2, 1)]
     finish = call(functools.partial(finish_kernel, scale), (quarter, BF16), in_specs=[vmem] * 4 + [far])
     [total] = finish(total, three, two, one, after)
     three, two, one = [exchange(total, 0, k) for k in (3, 2, 1)]
     quarters = [total, three, two, one]
-    results = [((length, 2 * width), BF16) for length in lengths]
-    place = dict(out_specs=[far] * 2, scratch_shapes=[pltpu.SemaphoreType.DMA((8,))])
-    half = call(functools.partial(place_kernel, False), *results, **place)(*quarters)
-    place.update(in_specs=[vmem] * 4 + [far] * 2, input_output_aliases={4: 0, 5: 1})
-    return call(functools.partial(place_kernel, True), *results, **place)(*[swap(one) for one in quarters], *half)
+    result = ((4 * quarter[0], 2 * quarter[1]), BF16)
+    place = dict(out_specs=[far], scratch_shapes=[pltpu.SemaphoreType.DMA((8,))])
+    [half] = call(functools.partial(place_kernel, False), result, **place)(*quarters)
+    place.update(in_specs=[vmem] * 4 + [far], input_output_aliases={4: 0})
+    [whole] = call(functools.partial(place_kernel, True), result, **place)(*[swap(one) for one in quarters], half)
+    return whole
 
 
 def local(features, top_down, lateral_weight, out_kernel, cotangent):
@@ -285,8 +316,31 @@
         )(*arrays)
         merged = merged.reshape(rows, cols, channels)
         edges = neighbour_rows(merged)
+        kernel_flops = 2 * cells * channels * 9 * channels
+        waited = []
+        if halves:
+            half, quarter = channels // 2, (9 * channels // 4, channels // 2)
+            image_shape = (2 * rows + 2, cols, 3 * half)
+            cost = pl.CostEstimate(flops=kernel_flops // 2, bytes_accessed=2**20, transcendentals=0)
+            image, first_sums = pl.pallas_call(
+                own_kernel_grad_kernel,
+                out_shape=[
+                    jax.ShapeDtypeStruct(image_shape, BF16),
+                    jax.ShapeDtypeStruct((channels, 9 * half), F32),
+                ],
+                compiler_params=params,
+                cost_estimate=cost,
+            )(stack, merged_t, cot_after)
+            pieces = pl.pallas_call(
+                rest_kernel_grad_kernel,
+                out_shape=[jax.ShapeDtypeStruct(quarter, F32), *[jax.ShapeDtypeStruct(quarter, BF16)] * 3],
+                scratch_shapes=[pltpu.VMEM((9 * channels, half), F32)],
+                compiler_params=params,
+                cost_estimate=cost,
+            )(image, first_sums, edges[0].reshape(cells, channels))
+            waited = [pieces[0]]
         grad, halo, *lateral_part = pl.pallas_call(
-            functools.partial(data_grad_kernel, peers),
+            functools.partial(data_grad_kernel, peers, len(waited)),
             out_shape=[
                 jax.ShapeDtypeStruct((cells, channels), BF16),
                 jax.ShapeDtypeStruct((2, cols, 3 * channels), BF16),
@@ -296,25 +350,15 @@
             cost_estimate=pl.CostEstimate(
                 flops=2 * cells * channels * (9 * channels + in_channels), bytes_accessed=4 * 2**20, transcendentals=0
             ),
-        )(stack, cot_before, cot_after, near_feat, near_taps)
-        kernel_cost = pl.CostEstimate(
-            flops=2 * cells * channels * 9 * channels, bytes_accessed=4 * 2**20, transcendentals=0
-        )
+        )(stack, cot_before, cot_after, near_feat, near_taps, *waited)
         if halves:
             lateral_part[1] = swap(lateral_part[1])
-            kernel_sums = pl.pallas_call(
-                pair_kernel_grad_kernel,
-                out_shape=jax.ShapeDtypeStruct((9 * channels, channels // 2), F32),
-                scratch_shapes=[pltpu.VMEM((2 * rows + 2, cols, 3 * channels // 2), BF16)],
-                compiler_params=params,
-                cost_estimate=kernel_cost,
-            )(stack, merged_t, cot_after, edges[0].reshape(cells, channels))
         else:
             kernel_sums = pl.pallas_call(
                 kernel_grad_kernel,
                 out_shape=jax.ShapeDtypeStruct((9 * channels, channels), F32),
                 compiler_params=params,
-                cost_estimate=kernel_cost,
+                cost_estimate=pl.CostEstimate(flops=kernel_flops, bytes_accessed=4 * 2**20, transcendentals=0),
             )(stack, halo, merged_t)
         out, grad_top = pl.pallas_call(
             functools.partial(forward_kernel, peers),
@@ -340,7 +384,8 @@
             parts = part if parts is None else [a + b for a, b in zip(parts, part)]
     scale = 1.0 / (images * lax.axis_size("dp"))
     if halves:
-        grad_kernel, grad_lateral = sum_everywhere(kernel_sums, lateral_part, scale, outs[0])
+        grad_kernel = sum_kernel(pieces, scale, outs[0])
+        grad_lateral = sum_lateral(*lateral_part, scale)
     else:
         grad_kernel, grad_lateral = [(total * scale).astype(BF16) for total in lax.psum(parts, ("dp", "space"))]
     return jnp.stack(outs), jnp.stack(tops), grad_kernel.reshape(out_kernel.shape), grad_lateral

time: 40.4 us -> 114 us (2.82)
  waiting for transfers between devices: 16 us -> 72.9 us
  between operations: 0.72 us -> 14.2 us
  other arithmetic: 0 us -> 1.69 us
    psum x0 -> x2, waiting for transfers between devices: none -> 63.2 us  [sum_lateral(): total = lax.psum(total, ('dp', 'space'), axis_index_groups=groups)]
    ppermute x9, waiting for transfers between devices: 15.6 us -> 8.97 us  [exchange(): return lax.ppermute(array, ('dp', 'space'), pairs)]
    pallas_call x7 -> x8, Pallas kernels: 5.25 us -> 6.1 us  [the longest x1 1.71 us: local(): pl.pallas_call(functools.partial(data_grad_kernel, peers, len(waited)), o...]
  transfers between devices with their start and end apart: 16 -> 19, of which waited for: 8 -> 8; matrix products, arithmetic and copies ran while one was open for 0% -> 1% of each run, Pallas kernels for 21% -> 6%
where the time goes in v14:
time: 114 us
  waiting for transfers between devices  72.9 us (64%)
  starting transfers between devices  14.6 us (13%)
  between operations  14.2 us (12%)
  Pallas kernels  10.5 us (9%)
  other arithmetic  1.69 us (1%)
    psum x2, waiting for transfers between devices, sum_lateral(): total = lax.psum(total, ('dp', 'space'), axis_index_groups=groups)  63.2 us
    ppermute x9, starting transfers between devices, exchange(): return lax.ppermute(array, ('dp', 'space'), pairs)  12.4 us
    ppermute x9, waiting for transfers between devices, exchange(): return lax.ppermute(array, ('dp', 'space'), pairs)  8.97 us
    pallas_call x1, Pallas kernels, local(): pl.pallas_call(functools.partial(forward_kernel, peers), out_shape=[jax.S...  2.54 us
  transfers between devices with their start and end apart: 19, of which 8 were waited for; matrix products, arithmetic and copies ran while one was open for 1% of the time, Pallas kernels for 6%

profile of v14, /device:TPU:0, one launch (start us, length us, event | category | flops | bytes accessed | tf_op | source)
XLA Modules:
  0.0 114.0 jit_solution(13965617450766955619)
XLA Ops:
  7.2 0.5 collective-permute-start
  7.7 1.9 %shard_map.84 = (bf16[768,256]{1,0:T(8,128)(2,1)S(1)}, bf16[256,768]{1,0:T(8,128)(2,1)S(1)}, bf16[8,96,768]{2,1,0:T(8,128)(2,1)S(1)}, bf16[768,512]{1,0:T(8,128)(2,1)S(1)}, bf16[9,256,256]{2,1,0:T(8,128)(2,1)S(1)}) custom-call(bf16[8,96,256]{2,1,0:T(8,128)(2,1)} %bitcast.17, bf16[512,256]{1,0:T(8,128)(2,1)} %refs_1_.1, bf16[4,48,256]{2,1,0:T(8,128)(2,1)} %bitcast.18, ...), custom_call_target="tpu_custom_call" | custom-call | flops 805306368 | bytes 4194304 | tf_op jit(solution)/shard_map/pallas_call | solution.py:298
  9.6 0.1 collective-permute-start.1
  9.8 1.0 shard_map.85
  10.7 0.7 collective-permute-done.1.refs_0_.refs_1_
  11.4 0.8 shard_map.86
  12.2 1.7 %shard_map.87 = (bf16[768,256]{1,0:T(8,128)(2,1)S(1)}, bf16[2,96,768]{2,1,0:T(8,128)(2,1)}, f32[512,128]{1,0:T(8,128)S(1)}, bf16[512,128]{1,0:T(8,128)(2,1)S(1)}) custom-call(bf16[8,96,768]{2,1,0:T(8,128)(2,1)S(1)} %get-tuple-element.22.stack, bf16[8,96,256]{2,1,0:T(8,128)(2,1)S(1)} %collective-permute-done.cot.before.after, ...), custom_call_target="tpu_custom_call" | custom-call | flops 1107296256 | bytes 4194304 | tf_op jit(solution)/shard_map/pallas_call | solution.py:342
  13.9 0.2 collective-permute-start.15
  14.1 3.8 %collective-permute-start.2 = (bf16[576,128]{1,0:T(8,128)(2,1)S(1)}, bf16[576,128]{1,0:T(8,128)(2,1)S(1)}, u32[]{:S(2)}, u32[]{:S(2)}) collective-permute-start(bf16[576,128]{1,0:T(8,128)(2,1)S(1)} %get-tuple-element.31), channel_id=1, source_target_pairs={{0,6},{1,25},{2,4},{3,27},{4,2},{5,29},{6,0},{7,31},{8,14},{9,17},... | collective-permute-start | bytes 442376 | tf_op jit(solution)/shard_map/ppermute | solution.py:224
  17.9 0.5 collective-permute-start.3
  18.5 0.7 convert_add_fusion
  19.3 1.7 %collective-permute-done.2.three = bf16[576,128]{1,0:T(8,128)(2,1)S(1)} collective-permute-done((bf16[576,128]{1,0:T(8,128)(2,1)S(1)}, bf16[576,128]{1,0:T(8,128)(2,1)S(1)}, u32[]{:S(2)}, u32[]{:S(2)}) %collective-permute-start.2) | collective-permute-done | bytes 147488 | tf_op jit(solution)/shard_map/ppermute | solution.py:224
  21.1 2.0 %collective-permute-done.3.two = bf16[576,128]{1,0:T(8,128)(2,1)S(1)} collective-permute-done((bf16[576,128]{1,0:T(8,128)(2,1)S(1)}, bf16[576,128]{1,0:T(8,128)(2,1)S(1)}, u32[]{:S(2)}, u32[]{:S(2)}) %collective-permute-start.3) | collective-permute-done | bytes 147488 | tf_op jit(solution)/shard_map/ppermute | solution.py:224
  23.1 0.5 collective-permute-done.4.one
  23.7 1.6 %collective-permute-start.7 = (bf16[576,128]{1,0:T(8,128)(2,1)S(1)}, bf16[576,128]{1,0:T(8,128)(2,1)S(1)}, u32[]{:S(2)}, u32[]{:S(2)}) collective-permute-start(bf16[576,128]{1,0:T(8,128)(2,1)S(1)} %shard_map.89.own), channel_id=1, source_target_pairs={{0,8},{1,3},{2,10},{3,1},{4,12},{5,7},{6,14},{7,5},{8,0},{9,11},{1... | collective-permute-start | bytes 442376 | tf_op jit(solution)/shard_map/ppermute | solution.py:224
  25.3 2.6 %collective-permute-start.6 = (bf16[576,128]{1,0:T(8,128)(2,1)S(1)}, bf16[576,128]{1,0:T(8,128)(2,1)S(1)}, u32[]{:S(2)}, u32[]{:S(2)}) collective-permute-start(bf16[576,128]{1,0:T(8,128)(2,1)S(1)} %shard_map.89.own), channel_id=1, source_target_pairs={{0,16},{1,5},{2,18},{3,7},{4,20},{5,1},{6,22},{7,3},{8,24},{9,13},... | collective-permute-start | bytes 442376 | tf_op jit(solution)/shard_map/ppermute | solution.py:224
  27.9 0.2 collective-permute-start.5
  28.1 37.0 %all-reduce.3.cloned.1.call-done = f32[512,128]{1,0:T(8,128)} async-done(((f32[512,128]{1,0:T(8,128)}), f32[512,128]{1,0:T(8,128)}) %all-reduce.3.cloned.1.call-update) | async-done | bytes 262160 | tf_op jit(solution)/shard_map/psum | solution.py:246
  65.2 2.5 %shard_map.88 = (bf16[8,96,256]{2,1,0:T(8,128)(2,1)}, bf16[4,48,256]{2,1,0:T(8,128)(2,1)}) custom-call(bf16[8,96,256]{2,1,0:T(8,128)(2,1)S(1)} %bitcast.11, bf16[9,256,256]{2,1,0:T(8,128)(2,1)S(1)} %get-tuple-element.21.out_w, bf16[768,256]{1,0:T(8,128)(2,1)S(1)} %get-tuple-element.28.grad, bf16[8,96,256]{2,1,0:T(8,128)(2,1)S(1)} %collective-permute-done.1.refs_0_.refs_1_, ...), custom_call_target="tpu_custom_call" | custom-call | flops 905969664 | bytes 2097152 | tf_op jit(solution)/shard_map/pallas_call | solution.py:363
  67.7 0.1 shard_map.90.refs_0_
  67.8 1.5 %collective-permute-start.13 = (bf16[576,128]{1,0:T(8,128)(2,1)S(1)}, bf16[576,128]{1,0:T(8,128)(2,1)S(1)}, u32[]{:S(2)}, u32[]{:S(2)}) collective-permute-start(bf16[576,128]{1,0:T(8,128)(2,1)S(1)} %shard_map.90.refs_0_), channel_id=1, source_target_pairs={{0,2},{1,9},{2,0},{3,11},{4,6},{5,13},{6,4},{7,15},{8,10},{9,1},{1... | collective-permute-start | bytes 442376 | tf_op jit(solution)/shard_map/ppermute | solution.py:224
  69.3 0.6 collective-permute-start.11
  69.9 1.5 %collective-permute-start.9 = (bf16[576,128]{1,0:T(8,128)(2,1)S(1)}, bf16[576,128]{1,0:T(8,128)(2,1)S(1)}, u32[]{:S(2)}, u32[]{:S(2)}) collective-permute-start(bf16[576,128]{1,0:T(8,128)(2,1)S(1)} %shard_map.90.refs_0_), channel_id=1, source_target_pairs={{0,6},{1,25},{2,4},{3,27},{4,2},{5,29},{6,0},{7,31},{8,14},{9,17},... | collective-permute-start | bytes 442376 | tf_op jit(solution)/shard_map/ppermute | solution.py:224
  71.4 1.7 %collective-permute-done.13.refs_3_ = bf16[576,128]{1,0:T(8,128)(2,1)S(1)} collective-permute-done((bf16[576,128]{1,0:T(8,128)(2,1)S(1)}, bf16[576,128]{1,0:T(8,128)(2,1)S(1)}, u32[]{:S(2)}, u32[]{:S(2)}) %collective-permute-start.13) | collective-permute-done | bytes 147488 | tf_op jit(solution)/shard_map/ppermute | solution.py:224
  73.0 3.0 %collective-permute-done.11.refs_2_ = bf16[576,128]{1,0:T(8,128)(2,1)S(1)} collective-permute-done((bf16[576,128]{1,0:T(8,128)(2,1)S(1)}, bf16[576,128]{1,0:T(8,128)(2,1)S(1)}, u32[]{:S(2)}, u32[]{:S(2)}) %collective-permute-start.11) | collective-permute-done | bytes 147488 | tf_op jit(solution)/shard_map/ppermute | solution.py:224
  76.1 1.2 %collective-permute-start.12 = (bf16[576,128]{1,0:T(8,128)(2,1)S(1)}, bf16[576,128]{1,0:T(8,128)(2,1)S(1)}, u32[]{:S(2)}, u32[]{:S(2)}) collective-permute-start(bf16[576,128]{1,0:T(8,128)(2,1)S(1)} %collective-permute-done.11.refs_2_), channel_id=1, source_target_pairs={{0,1},{1,0},{2,3},{3,2},{4,5},{5,4},{6,7},{7,6},{8,9},{9,8},{10,11... | collective-permute-start | bytes 442376 | tf_op jit(solution)/shard_map/ppermute | solution.py:228
  77.3 26.2 %all-reduce.5.cloned.1.call-done = f32[512,128]{1,0:T(8,128)} async-done(((f32[512,128]{1,0:T(8,128)}), f32[512,128]{1,0:T(8,128)}) %all-reduce.5.cloned.1.call-update) | async-done | bytes 262160 | tf_op jit(solution)/shard_map/psum | solution.py:246
  103.5 1.0 multiply_convert_fusion.mine
  104.5 0.1 collective-permute-start.16
  104.5 0.9 shard_map.91.refs_4_
  105.5 0.9 shard_map.92
  106.4 0.7 shard_map.93
  (20 shorter events, 0.3 us)
Async XLA Ops:
  7.2 58.0 %all-reduce.3.cloned.1.call-start = ((), (), s32[]{:S(2)}) async-start(), calls=%async_computation | async-start | bytes 524288 | tf_op jit(solution)/shard_map/psum | solution.py:246
  7.2 2.6 %collective-permute-start = (bf16[8,96,256]{2,1,0:T(8,128)(2,1)}, bf16[8,96,256]{2,1,0:T(8,128)(2,1)S(1)}, u32[]{:S(2)}, u32[]{:S(2)}) collective-permute-start(bf16[8,96,256]{2,1,0:T(8,128)(2,1)} %bitcast.16), channel_id=1, source_target_pairs={{0,1},{1,0},{2,3},{3,2},{4,5},{5,4},{6,7},{7,6},{8,9},{9,8},{10,11... | collective-permute-start | bytes 1179656 | tf_op jit(solution)/shard_map/ppermute | solution.py:19
  9.6 1.8 %collective-permute-start.1 = (bf16[8,96,256]{2,1,0:T(8,128)(2,1)S(1)}, bf16[8,96,256]{2,1,0:T(8,128)(2,1)S(1)}, u32[]{:S(2)}, u32[]{:S(2)}) collective-permute-start(bf16[8,96,256]{2,1,0:T(8,128)(2,1)S(1)} %bitcast.10), channel_id=1, source_target_pairs={{0,1},{1,0},{2,3},{3,2},{4,5},{5,4},{6,7},{7,6},{8,9},{9,8},{10,11... | collective-permute-start | bytes 1179656 | tf_op jit(solution)/shard_map/ppermute | solution.py:19
  13.9 4.6 %collective-permute-start.15 = (bf16[512,128]{1,0:T(8,128)(2,1)S(1)}, bf16[512,128]{1,0:T(8,128)(2,1)S(1)}, u32[]{:S(2)}, u32[]{:S(2)}) collective-permute-start(bf16[512,128]{1,0:T(8,128)(2,1)S(1)} %get-tuple-element.35), channel_id=1, source_target_pairs={{0,1},{1,0},{2,3},{3,2},{4,5},{5,4},{6,7},{7,6},{8,9},{9,8},{10,11... | collective-permute-start | bytes 393224 | tf_op jit(solution)/shard_map/ppermute | solution.py:228
  14.1 6.9 %collective-permute-start.2 = (bf16[576,128]{1,0:T(8,128)(2,1)S(1)}, bf16[576,128]{1,0:T(8,128)(2,1)S(1)}, u32[]{:S(2)}, u32[]{:S(2)}) collective-permute-start(bf16[576,128]{1,0:T(8,128)(2,1)S(1)} %get-tuple-element.31), channel_id=1, source_target_pairs={{0,6},{1,25},{2,4},{3,27},{4,2},{5,29},{6,0},{7,31},{8,14},{9,17},... | collective-permute-start | bytes 442376 | tf_op jit(solution)/shard_map/ppermute | solution.py:224
  17.9 5.1 %collective-permute-start.3 = (bf16[576,128]{1,0:T(8,128)(2,1)S(1)}, bf16[576,128]{1,0:T(8,128)(2,1)S(1)}, u32[]{:S(2)}, u32[]{:S(2)}) collective-permute-start(bf16[576,128]{1,0:T(8,128)(2,1)S(1)} %get-tuple-element.32), channel_id=1, source_target_pairs={{0,4},{1,17},{2,6},{3,19},{4,0},{5,21},{6,2},{7,23},{8,12},{9,25},... | collective-permute-start | bytes 442376 | tf_op jit(solution)/shard_map/ppermute | solution.py:224
  18.5 5.1 %collective-permute-start.4 = (bf16[576,128]{1,0:T(8,128)(2,1)S(1)}, bf16[576,128]{1,0:T(8,128)(2,1)S(1)}, u32[]{:S(2)}, u32[]{:S(2)}) collective-permute-start(bf16[576,128]{1,0:T(8,128)(2,1)S(1)} %get-tuple-element.33), channel_id=1, source_target_pairs={{0,2},{1,9},{2,0},{3,11},{4,6},{5,13},{6,4},{7,15},{8,10},{9,1},{1... | collective-permute-start | bytes 442376 | tf_op jit(solution)/shard_map/ppermute | solution.py:224
  19.3 84.2 %all-reduce.5.cloned.1.call-start = ((), (), s32[]{:S(2)}) async-start(), calls=%async_computation.1 | async-start | bytes 524288 | tf_op jit(solution)/shard_map/psum | solution.py:246
  23.7 44.0 %collective-permute-start.7 = (bf16[576,128]{1,0:T(8,128)(2,1)S(1)}, bf16[576,128]{1,0:T(8,128)(2,1)S(1)}, u32[]{:S(2)}, u32[]{:S(2)}) collective-permute-start(bf16[576,128]{1,0:T(8,128)(2,1)S(1)} %shard_map.89.own), channel_id=1, source_target_pairs={{0,8},{1,3},{2,10},{3,1},{4,12},{5,7},{6,14},{7,5},{8,0},{9,11},{1... | collective-permute-start | bytes 442376 | tf_op jit(solution)/shard_map/ppermute | solution.py:224
  25.3 42.4 %collective-permute-start.6 = (bf16[576,128]{1,0:T(8,128)(2,1)S(1)}, bf16[576,128]{1,0:T(8,128)(2,1)S(1)}, u32[]{:S(2)}, u32[]{:S(2)}) collective-permute-start(bf16[576,128]{1,0:T(8,128)(2,1)S(1)} %shard_map.89.own), channel_id=1, source_target_pairs={{0,16},{1,5},{2,18},{3,7},{4,20},{5,1},{6,22},{7,3},{8,24},{9,13},... | collective-permute-start | bytes 442376 | tf_op jit(solution)/shard_map/ppermute | solution.py:224
  27.9 39.8 %collective-permute-start.5 = (bf16[576,128]{1,0:T(8,128)(2,1)S(1)}, bf16[576,128]{1,0:T(8,128)(2,1)S(1)}, u32[]{:S(2)}, u32[]{:S(2)}) collective-permute-start(bf16[576,128]{1,0:T(8,128)(2,1)S(1)} %shard_map.89.own), channel_id=1, source_target_pairs={{0,24},{1,7},{2,26},{3,5},{4,28},{5,3},{6,30},{7,1},{8,16},{9,15},... | collective-permute-start | bytes 442376 | tf_op jit(solution)/shard_map/ppermute | solution.py:224
  67.8 5.2 %collective-permute-start.13 = (bf16[576,128]{1,0:T(8,128)(2,1)S(1)}, bf16[576,128]{1,0:T(8,128)(2,1)S(1)}, u32[]{:S(2)}, u32[]{:S(2)}) collective-permute-start(bf16[576,128]{1,0:T(8,128)(2,1)S(1)} %shard_map.90.refs_0_), channel_id=1, source_target_pairs={{0,2},{1,9},{2,0},{3,11},{4,6},{5,13},{6,4},{7,15},{8,10},{9,1},{1... | collective-permute-start | bytes 442376 | tf_op jit(solution)/shard_map/ppermute | solution.py:224
  69.3 6.7 %collective-permute-start.11 = (bf16[576,128]{1,0:T(8,128)(2,1)S(1)}, bf16[576,128]{1,0:T(8,128)(2,1)S(1)}, u32[]{:S(2)}, u32[]{:S(2)}) collective-permute-start(bf16[576,128]{1,0:T(8,128)(2,1)S(1)} %shard_map.90.refs_0_), channel_id=1, source_target_pairs={{0,4},{1,17},{2,6},{3,19},{4,0},{5,21},{6,2},{7,23},{8,12},{9,25},... | collective-permute-start | bytes 442376 | tf_op jit(solution)/shard_map/ppermute | solution.py:224
  69.9 7.4 %collective-permute-start.9 = (bf16[576,128]{1,0:T(8,128)(2,1)S(1)}, bf16[576,128]{1,0:T(8,128)(2,1)S(1)}, u32[]{:S(2)}, u32[]{:S(2)}) collective-permute-start(bf16[576,128]{1,0:T(8,128)(2,1)S(1)} %shard_map.90.refs_0_), channel_id=1, source_target_pairs={{0,6},{1,25},{2,4},{3,27},{4,2},{5,29},{6,0},{7,31},{8,14},{9,17},... | collective-permute-start | bytes 442376 | tf_op jit(solution)/shard_map/ppermute | solution.py:224
  71.4 34.1 %collective-permute-start.8 = (bf16[576,128]{1,0:T(8,128)(2,1)S(1)}, bf16[576,128]{1,0:T(8,128)(2,1)S(1)}, u32[]{:S(2)}, u32[]{:S(2)}) collective-permute-start(bf16[576,128]{1,0:T(8,128)(2,1)S(1)} %shard_map.90.refs_0_), channel_id=1, source_target_pairs={{0,1},{1,0},{2,3},{3,2},{4,5},{5,4},{6,7},{7,6},{8,9},{9,8},{10,11... | collective-permute-start | bytes 442376 | tf_op jit(solution)/shard_map/ppermute | solution.py:228
  73.0 32.4 %collective-permute-start.14 = (bf16[576,128]{1,0:T(8,128)(2,1)S(1)}, bf16[576,128]{1,0:T(8,128)(2,1)S(1)}, u32[]{:S(2)}, u32[]{:S(2)}) collective-permute-start(bf16[576,128]{1,0:T(8,128)(2,1)S(1)} %collective-permute-done.13.refs_3_), channel_id=1, source_target_pairs={{0,1},{1,0},{2,3},{3,2},{4,5},{5,4},{6,7},{7,6},{8,9},{9,8},{10,11... | collective-permute-start | bytes 442376 | tf_op jit(solution)/shard_map/ppermute | solution.py:228
  76.1 29.4 %collective-permute-start.12 = (bf16[576,128]{1,0:T(8,128)(2,1)S(1)}, bf16[576,128]{1,0:T(8,128)(2,1)S(1)}, u32[]{:S(2)}, u32[]{:S(2)}) collective-permute-start(bf16[576,128]{1,0:T(8,128)(2,1)S(1)} %collective-permute-done.11.refs_2_), channel_id=1, source_target_pairs={{0,1},{1,0},{2,3},{3,2},{4,5},{5,4},{6,7},{7,6},{8,9},{9,8},{10,11... | collective-permute-start | bytes 442376 | tf_op jit(solution)/shard_map/ppermute | solution.py:228
  77.3 28.1 %collective-permute-start.10 = (bf16[576,128]{1,0:T(8,128)(2,1)S(1)}, bf16[576,128]{1,0:T(8,128)(2,1)S(1)}, u32[]{:S(2)}, u32[]{:S(2)}) collective-permute-start(bf16[576,128]{1,0:T(8,128)(2,1)S(1)} %collective-permute-done.9.refs_1_), channel_id=1, source_target_pairs={{0,1},{1,0},{2,3},{3,2},{4,5},{5,4},{6,7},{7,6},{8,9},{9,8},{10,11... | collective-permute-start | bytes 442376 | tf_op jit(solution)/shard_map/ppermute | solution.py:228
  104.5 1.9 %collective-permute-start.16 = (bf16[512,128]{1,0:T(8,128)(2,1)S(1)}, bf16[512,128]{1,0:T(8,128)(2,1)S(1)}, u32[]{:S(2)}, u32[]{:S(2)}) collective-permute-start(bf16[512,128]{1,0:T(8,128)(2,1)S(1)} %multiply_convert_fusion.mine), channel_id=1, source_target_pairs={{0,1},{1,0},{2,3},{3,2},{4,5},{5,4},{6,7},{7,6},{8,9},{9,8},{10,11... | collective-permute-start | bytes 393224 | tf_op jit(solution)/shard_map/ppermute | solution.py:228
Sparse Core Ops, SparseCore 0:
  19.4 45.6 all-reduce.2
  67.6 35.8 all-reduce.4

commit v15 on v14

--- a/solution.py
+++ b/solution.py
@@ -175,40 +175,45 @@
     return pl.ds(pl.multiple_of(index * length, 16), length)
 
 
+def cut_kernel(mine, got, *refs):
+    place, _ = places()
+    for k, out in zip((0, 3, 2, 1), refs):
+        rows = block(place ^ k, out.shape[0])
+        out[...] = (mine[rows, :] + got[rows, :].astype(F32)).astype(out.dtype)
+
+
 def add_kernel(own, three, two, one, out):
     total = own[...] + one[...].astype(F32) + two[...].astype(F32) + three[...].astype(F32)
     out[...] = total.astype(BF16)
 
 
-def finish_kernel(scale, own, three, two, one, _, out):
+def finish_kernel(scale, own, one, two, three, *refs):
     near = own[...].astype(F32) + one[...].astype(F32)
     far = two[...].astype(F32) + three[...].astype(F32)
-    out[...] = ((near + far) * scale).astype(BF16)
+    out = refs[-1]
+    start = out.shape[0] - own.shape[0]
+    if start:
+        out[:start, :] = refs[0][...]
+    out[start:, :] = ((near + far) * scale).astype(BF16)
+
+
+def copy_kernel(array, _, out):
+    out[...] = array[...]
 
 
 def place_kernel(pair, *refs):
-    result, sems = refs[-2:]
+    results, sems = refs[-3:-1], refs[-1]
     side = lax.axis_index("space")
     columns, place = (1 - side, places()[1]) if pair else (side, places()[0])
     lanes = pl.ds(pl.multiple_of(columns * 128, 128), 128)
-    share = result.shape[0] // 8
     copies = []
-    for k, quarter in zip((0, 3, 2, 1), refs):
-        for part in range(2):
-            to = result.at[block(2 * (place ^ k) + part, share), lanes]
-            copies.append(pltpu.make_async_copy(quarter.at[pl.ds(part * share, share), :], to, sems.at[len(copies)]))
-    for copy in copies:
-        copy.start()
-    for copy in copies:
-        copy.wait()
-
-
-def place_lateral_kernel(mine, other, result, sems):
-    side = lax.axis_index("space")
-    copies = []
-    for columns, half in ((side, mine), (1 - side, other)):
-        lanes = pl.ds(pl.multiple_of(columns * 128, 128), 128)
-        copies.append(pltpu.make_async_copy(half, result.at[:, lanes], sems.at[len(copies)]))
+    for k, quarter in enumerate(refs[:4]):
+        start = 0
+        for result in results:
+            share = result.shape[0] // 4
+            to = result.at[block(place ^ k, share), lanes]
+            copies.append(pltpu.make_async_copy(quarter.at[pl.ds(start, share), :], to, sems.at[len(copies)]))
+            start += share
     for copy in copies:
         copy.start()
     for copy in copies:
@@ -237,42 +242,30 @@
     )
 
 
-def sum_lateral(mine, got, scale):
-    length, width = mine.shape
-    plane = [[2 * (4 * z + q) + core for q in range(4)] for z in range(4) for core in range(2)]
-    line = [[2 * (4 * z + q) + core for z in range(4)] for q in range(4) for core in range(2)]
-    total = mine + got.astype(F32)
-    for groups in (plane, line):
-        total = lax.psum(total, ("dp", "space"), axis_index_groups=groups)
-    total = (total * scale).astype(BF16)
-    [result] = call(
-        place_lateral_kernel,
-        ((length, 2 * width), BF16),
-        out_specs=[pl.BlockSpec(memory_space=pltpu.HBM)],
-        scratch_shapes=[pltpu.SemaphoreType.DMA((2,))],
-    )(total, swap(total))
-    return result
-
-
-def sum_kernel(pieces, scale, after):
-    own, *pieces = pieces
-    quarter = own.shape
+def sum_everywhere(pieces, lateral_part, scale, after):
     vmem, far = pl.BlockSpec(memory_space=pltpu.VMEM), pl.BlockSpec(memory_space=pltpu.HBM)
     after = pltpu.with_memory_space_constraint(after, pltpu.HBM)
-    three, two, one = [exchange(piece, 0, k) for piece, k in zip(pieces, (3, 2, 1))]
-    slow = pl.CostEstimate(flops=2**32, bytes_accessed=2**10, transcendentals=0)
-    [total] = call(add_kernel, (quarter, BF16), cost_estimate=slow)(own, three, two, one)
-    three, two, one = [exchange(total, 1, k) for k in (3, 2, 1)]
-    finish = call(functools.partial(finish_kernel, scale), (quarter, BF16), in_specs=[vmem] * 4 + [far])
-    [total] = finish(total, three, two, one, after)
+    slow = [pl.CostEstimate(flops=flops, bytes_accessed=2**10, transcendentals=0) for flops in (2**30, 2**31)]
+    lateral = lateral_part[0].shape
+    share = (lateral[0] // 4, lateral[1])
+    lateral_pieces = call(cut_kernel, (share, F32), *[(share, BF16)] * 3)(*lateral_part)
+    sums = []
+    for (own, *others), cost in zip((pieces, lateral_pieces), slow):
+        came = [exchange(piece, 0, k) for piece, k in zip(others, (3, 2, 1))]
+        [total] = call(add_kernel, (own.shape, BF16), cost_estimate=cost)(own, *came)
+        sums.append([total] + [exchange(total, 1, k) for k in (3, 2, 1)][::-1])
+    finish = functools.partial(finish_kernel, scale)
+    [first] = call(finish, (pieces[0].shape, BF16), cost_estimate=slow[0])(*sums[0])
+    joint = (first.shape[0] + share[0], share[1])
+    [total] = call(finish, (joint, BF16))(*sums[1], first)
     three, two, one = [exchange(total, 0, k) for k in (3, 2, 1)]
-    quarters = [total, three, two, one]
-    result = ((4 * quarter[0], 2 * quarter[1]), BF16)
-    place = dict(out_specs=[far], scratch_shapes=[pltpu.SemaphoreType.DMA((8,))])
-    [half] = call(functools.partial(place_kernel, False), result, **place)(*quarters)
-    place.update(in_specs=[vmem] * 4 + [far], input_output_aliases={4: 0})
-    [whole] = call(functools.partial(place_kernel, True), result, **place)(*[swap(one) for one in quarters], half)
-    return whole
+    quarters = [total, one, two, three]
+    [ready] = call(copy_kernel, (joint, BF16), in_specs=[vmem, far])(total, after)
+    results = [((4 * rows, 2 * share[1]), BF16) for rows in (first.shape[0], share[0])]
+    place = dict(out_specs=[far] * 2, scratch_shapes=[pltpu.SemaphoreType.DMA((8,))])
+    half = call(functools.partial(place_kernel, False), *results, **place)(*quarters)
+    place.update(in_specs=[vmem] * 4 + [far] * 2, input_output_aliases={4: 0, 5: 1})
+    return call(functools.partial(place_kernel, True), *results, **place)(*[swap(one) for one in (ready, *quarters[1:])], *half)
 
 
 def local(features, top_down, lateral_weight, out_kernel, cotangent):
@@ -384,8 +377,7 @@
             parts = part if parts is None else [a + b for a, b in zip(parts, part)]
     scale = 1.0 / (images * lax.axis_size("dp"))
     if halves:
-        grad_kernel = sum_kernel(pieces, scale, outs[0])
-        grad_lateral = sum_lateral(*lateral_part, scale)
+        grad_kernel, grad_lateral = sum_everywhere(pieces, lateral_part, scale, outs[0])
     else:
         grad_kernel, grad_lateral = [(total * scale).astype(BF16) for total in lax.psum(parts, ("dp", "space"))]
     return jnp.stack(outs), jnp.stack(tops), grad_kernel.reshape(out_kernel.shape), grad_lateral

time: 114 us -> 41.6 us (0.36)
  waiting for transfers between devices: 72.9 us -> 7.3 us
  between operations: 14.2 us -> 0.76 us
  starting transfers between devices: 14.6 us -> 23.4 us
  other arithmetic: 1.69 us -> 0 us
    psum x2 -> x0, waiting for transfers between devices: 63.2 us -> none  [sum_lateral(): total = lax.psum(total, ('dp', 'space'), axis_index_groups=groups)]
    ppermute x9 -> x15, starting transfers between devices: 12.4 us -> 21.1 us  [exchange(): return lax.ppermute(array, ('dp', 'space'), pairs)]
    ppermute x9 -> x15, waiting for transfers between devices: 8.97 us -> 5.39 us  [exchange(): return lax.ppermute(array, ('dp', 'space'), pairs)]
    ppermute x6 -> x5, waiting for transfers between devices: 0.02 us -> 1.21 us  [swap(): return lax.ppermute(array, 'space', [(0, 1), (1, 0)])]
    pallas_call x5 -> x8, Pallas kernels: 2.67 us -> 2.06 us  [the longest x1 0.91 us: sum_everywhere(): call(functools.partial(place_kernel, True), *results, **place)]
  transfers between devices with their start and end apart: 19 -> 22, of which waited for: 8 -> 9; matrix products, arithmetic and copies ran while one was open for 1% -> 0% of each run, Pallas kernels for 6% -> 20%
where the time goes in v15:
time: 41.6 us; the launch traced here: 41.4 us
  starting transfers between devices  23.4 us (56%)
  Pallas kernels  9.93 us (24%)
  waiting for transfers between devices  7.3 us (18%)
  between operations  0.76 us (2%)
    ppermute x15, starting transfers between devices, exchange(): return lax.ppermute(array, ('dp', 'space'), pairs)  21.1 us
    ppermute x15, waiting for transfers between devices, exchange(): return lax.ppermute(array, ('dp', 'space'), pairs)  5.39 us
    pallas_call x1, Pallas kernels, local(): pl.pallas_call(functools.partial(forward_kernel, peers), out_shape=[jax.S...  2.53 us
    pallas_call x1, Pallas kernels, local(): pl.pallas_call(merge_kernel, out_shape=[jax.ShapeDtypeStruct(shape, BF16)...  1.9 us
    pallas_call x1, Pallas kernels, local(): pl.pallas_call(functools.partial(data_grad_kernel, peers, len(waited)), o...  1.7 us
    ppermute x5, starting transfers between devices, swap(): return lax.ppermute(array, 'space', [(0, 1), (1, 0)])  1.69 us
    ppermute x5, waiting for transfers between devices, swap(): return lax.ppermute(array, 'space', [(0, 1), (1, 0)])  1.21 us
    pallas_call x1, Pallas kernels, local(): pl.pallas_call(own_kernel_grad_kernel, out_shape=[jax.ShapeDtypeStruct(im...  0.95 us
  transfers between devices with their start and end apart: 22, of which 9 were waited for; matrix products, arithmetic and copies ran while one was open for 0% of the time, Pallas kernels for 20%

profile of v15, /device:TPU:0, one launch (start us, length us, event | category | flops | bytes accessed | tf_op | source)
XLA Modules:
  0.0 41.4 jit_solution(3942938740095694834)
XLA Ops:
  0.6 0.5 %collective-permute-start = (bf16[8,96,256]{2,1,0:T(8,128)(2,1)}, bf16[8,96,256]{2,1,0:T(8,128)(2,1)S(1)}, u32[]{:S(2)}, u32[]{:S(2)}) collective-permute-start(bf16[8,96,256]{2,1,0:T(8,128)(2,1)} %bitcast.16), channel_id=1, source_target_pairs={{0,1},{1,0},{2,3},{3,2},{4,5},{5,4},{6,7},{7,6},{8,9},{9,8},{10,11... | collective-permute-start | bytes 1179656 | tf_op jit(solution)/shard_map/ppermute | solution.py:19
  1.1 1.9 %shard_map.84 = (bf16[768,256]{1,0:T(8,128)(2,1)S(1)}, bf16[256,768]{1,0:T(8,128)(2,1)S(1)}, bf16[8,96,768]{2,1,0:T(8,128)(2,1)S(1)}, bf16[768,512]{1,0:T(8,128)(2,1)S(1)}, bf16[9,256,256]{2,1,0:T(8,128)(2,1)S(1)}) custom-call(bf16[8,96,256]{2,1,0:T(8,128)(2,1)} %bitcast.17, bf16[512,256]{1,0:T(8,128)(2,1)} %refs_1_.1, bf16[4,48,256]{2,1,0:T(8,128)(2,1)} %bitcast.18, ...), custom_call_target="tpu_custom_call" | custom-call | flops 805306368 | bytes 4194304 | tf_op jit(solution)/shard_map/pallas_call | solution.py:291
  3.2 1.0 %shard_map.85 = (bf16[18,96,384]{2,1,0:T(8,128)(2,1)S(1)}, f32[256,1152]{1,0:T(8,128)S(1)}) custom-call(bf16[8,96,768]{2,1,0:T(8,128)(2,1)S(1)} %get-tuple-element.30.stack, bf16[256,768]{1,0:T(8,128)(2,1)S(1)} %get-tuple-element.32.merged_t, bf16[8,96,256]{2,1,0:T(8,128)(2,1)S(1)} %collective-permute-done.cot.before.after), custom_call_target="tpu_custom_call" | custom-call | flops 452984832 | bytes 1048576 | tf_op jit(solution)/shard_map/pallas_call | solution.py:318
  4.1 0.7 %collective-permute-done.1.refs_0_.refs_1_ = bf16[8,96,256]{2,1,0:T(8,128)(2,1)S(1)} collective-permute-done((bf16[8,96,256]{2,1,0:T(8,128)(2,1)S(1)}, bf16[8,96,256]{2,1,0:T(8,128)(2,1)S(1)}, u32[]{:S(2)}, u32[]{:S(2)}) %collective-permute-start.1) | collective-permute-done | bytes 393248 | tf_op jit(solution)/shard_map/ppermute | solution.py:19
  4.9 0.8 %shard_map.86 = (f32[576,128]{1,0:T(8,128)S(1)}, bf16[576,128]{1,0:T(8,128)(2,1)S(1)}, bf16[576,128]{1,0:T(8,128)(2,1)S(1)}, bf16[576,128]{1,0:T(8,128)(2,1)S(1)}) custom-call(bf16[18,96,384]{2,1,0:T(8,128)(2,1)S(1)} %get-tuple-element.33.image, f32[256,1152]{1,0:T(8,128)S(1)} %get-tuple-element.34.sums, bf16[768,256]{1,0:T(8,128)(2,1)S(1)} %bitcast.9), custom_call_target="tpu_custom_call" | custom-call | flops 452984832 | bytes 1048576 | tf_op jit(solution)/shard_map/pallas_call | solution.py:327
  5.6 3.6 %collective-permute-start.9 = (bf16[576,128]{1,0:T(8,128)(2,1)S(1)}, bf16[576,128]{1,0:T(8,128)(2,1)S(1)}, u32[]{:S(2)}, u32[]{:S(2)}) collective-permute-start(bf16[576,128]{1,0:T(8,128)(2,1)S(1)} %get-tuple-element.45), channel_id=1, source_target_pairs={{0,6},{1,25},{2,4},{3,27},{4,2},{5,29},{6,0},{7,31},{8,14},{9,17},... | collective-permute-start | bytes 442376 | tf_op jit(solution)/shard_map/ppermute | solution.py:229
  9.3 0.5 %collective-permute-start.10 = (bf16[576,128]{1,0:T(8,128)(2,1)S(1)}, bf16[576,128]{1,0:T(8,128)(2,1)S(1)}, u32[]{:S(2)}, u32[]{:S(2)}) collective-permute-start(bf16[576,128]{1,0:T(8,128)(2,1)S(1)} %get-tuple-element.46), channel_id=1, source_target_pairs={{0,4},{1,17},{2,6},{3,19},{4,0},{5,21},{6,2},{7,23},{8,12},{9,25},... | collective-permute-start | bytes 442376 | tf_op jit(solution)/shard_map/ppermute | solution.py:229
  9.8 0.1 collective-permute-start.11
  9.9 1.7 %shard_map.87 = (bf16[768,256]{1,0:T(8,128)(2,1)S(1)}, bf16[2,96,768]{2,1,0:T(8,128)(2,1)}, f32[512,128]{1,0:T(8,128)S(1)}, bf16[512,128]{1,0:T(8,128)(2,1)S(1)}) custom-call(bf16[8,96,768]{2,1,0:T(8,128)(2,1)S(1)} %get-tuple-element.30.stack, bf16[8,96,256]{2,1,0:T(8,128)(2,1)S(1)} %collective-permute-done.cot.before.after, ...), custom_call_target="tpu_custom_call" | custom-call | flops 1107296256 | bytes 4194304 | tf_op jit(solution)/shard_map/pallas_call | solution.py:335
  11.6 1.0 %collective-permute-start.2 = (bf16[512,128]{1,0:T(8,128)(2,1)S(1)}, bf16[512,128]{1,0:T(8,128)(2,1)S(1)}, u32[]{:S(2)}, u32[]{:S(2)}) collective-permute-start(bf16[512,128]{1,0:T(8,128)(2,1)S(1)} %get-tuple-element.40), channel_id=1, source_target_pairs={{0,1},{1,0},{2,3},{3,2},{4,5},{5,4},{6,7},{7,6},{8,9},{9,8},{10,11... | collective-permute-start | bytes 393224 | tf_op jit(solution)/shard_map/ppermute | solution.py:233
  12.7 1.0 %collective-permute-done.2.got = bf16[512,128]{1,0:T(8,128)(2,1)S(1)} collective-permute-done((bf16[512,128]{1,0:T(8,128)(2,1)S(1)}, bf16[512,128]{1,0:T(8,128)(2,1)S(1)}, u32[]{:S(2)}, u32[]{:S(2)}) %collective-permute-start.2) | collective-permute-done | bytes 131104 | tf_op jit(solution)/shard_map/ppermute | solution.py:233
  13.7 2.5 %collective-permute-start.3 = (bf16[128,128]{1,0:T(8,128)(2,1)S(1)}, bf16[128,128]{1,0:T(8,128)(2,1)S(1)}, u32[]{:S(2)}, u32[]{:S(2)}) collective-permute-start(bf16[128,128]{1,0:T(8,128)(2,1)S(1)} %get-tuple-element.42), channel_id=1, source_target_pairs={{0,6},{1,25},{2,4},{3,27},{4,2},{5,29},{6,0},{7,31},{8,14},{9,17},... | collective-permute-start | bytes 98312 | tf_op jit(solution)/shard_map/ppermute | solution.py:229
  16.2 0.5 %collective-permute-start.4 = (bf16[128,128]{1,0:T(8,128)(2,1)S(1)}, bf16[128,128]{1,0:T(8,128)(2,1)S(1)}, u32[]{:S(2)}, u32[]{:S(2)}) collective-permute-start(bf16[128,128]{1,0:T(8,128)(2,1)S(1)} %get-tuple-element.43), channel_id=1, source_target_pairs={{0,4},{1,17},{2,6},{3,19},{4,0},{5,21},{6,2},{7,23},{8,12},{9,25},... | collective-permute-start | bytes 98312 | tf_op jit(solution)/shard_map/ppermute | solution.py:229
  16.7 0.5 %collective-permute-start.5 = (bf16[128,128]{1,0:T(8,128)(2,1)S(1)}, bf16[128,128]{1,0:T(8,128)(2,1)S(1)}, u32[]{:S(2)}, u32[]{:S(2)}) collective-permute-start(bf16[128,128]{1,0:T(8,128)(2,1)S(1)} %get-tuple-element.44), channel_id=1, source_target_pairs={{0,2},{1,9},{2,0},{3,11},{4,6},{5,13},{6,4},{7,15},{8,10},{9,1},{1... | collective-permute-start | bytes 98312 | tf_op jit(solution)/shard_map/ppermute | solution.py:229
  17.3 3.5 %collective-permute-start.14 = (bf16[576,128]{1,0:T(8,128)(2,1)S(1)}, bf16[576,128]{1,0:T(8,128)(2,1)S(1)}, u32[]{:S(2)}, u32[]{:S(2)}) collective-permute-start(bf16[576,128]{1,0:T(8,128)(2,1)S(1)} %shard_map.91.own), channel_id=1, source_target_pairs={{0,24},{1,7},{2,26},{3,5},{4,28},{5,3},{6,30},{7,1},{8,16},{9,15},... | collective-permute-start | bytes 442376 | tf_op jit(solution)/shard_map/ppermute | solution.py:229
  20.9 0.9 %collective-permute-start.12 = (bf16[576,128]{1,0:T(8,128)(2,1)S(1)}, bf16[576,128]{1,0:T(8,128)(2,1)S(1)}, u32[]{:S(2)}, u32[]{:S(2)}) collective-permute-start(bf16[576,128]{1,0:T(8,128)(2,1)S(1)} %shard_map.91.own), channel_id=1, source_target_pairs={{0,8},{1,3},{2,10},{3,1},{4,12},{5,7},{6,14},{7,5},{8,0},{9,11},{1... | collective-permute-start | bytes 442376 | tf_op jit(solution)/shard_map/ppermute | solution.py:229
  21.8 3.5 %collective-permute-start.8 = (bf16[128,128]{1,0:T(8,128)(2,1)S(1)}, bf16[128,128]{1,0:T(8,128)(2,1)S(1)}, u32[]{:S(2)}, u32[]{:S(2)}) collective-permute-start(bf16[128,128]{1,0:T(8,128)(2,1)S(1)} %shard_map.90.own), channel_id=1, source_target_pairs={{0,24},{1,7},{2,26},{3,5},{4,28},{5,3},{6,30},{7,1},{8,16},{9,15},... | collective-permute-start | bytes 98312 | tf_op jit(solution)/shard_map/ppermute | solution.py:229
  25.3 1.7 %collective-permute-start.6 = (bf16[128,128]{1,0:T(8,128)(2,1)S(1)}, bf16[128,128]{1,0:T(8,128)(2,1)S(1)}, u32[]{:S(2)}, u32[]{:S(2)}) collective-permute-start(bf16[128,128]{1,0:T(8,128)(2,1)S(1)} %shard_map.90.own), channel_id=1, source_target_pairs={{0,8},{1,3},{2,10},{3,1},{4,12},{5,7},{6,14},{7,5},{8,0},{9,11},{1... | collective-permute-start | bytes 98312 | tf_op jit(solution)/shard_map/ppermute | solution.py:229
  27.1 1.0 %collective-permute-done.13.two = bf16[576,128]{1,0:T(8,128)(2,1)S(1)} collective-permute-done((bf16[576,128]{1,0:T(8,128)(2,1)S(1)}, bf16[576,128]{1,0:T(8,128)(2,1)S(1)}, u32[]{:S(2)}, u32[]{:S(2)}) %collective-permute-start.13) | collective-permute-done | bytes 147488 | tf_op jit(solution)/shard_map/ppermute | solution.py:229
  28.2 0.6 %collective-permute-done.8.three = bf16[128,128]{1,0:T(8,128)(2,1)S(1)} collective-permute-done((bf16[128,128]{1,0:T(8,128)(2,1)S(1)}, bf16[128,128]{1,0:T(8,128)(2,1)S(1)}, u32[]{:S(2)}, u32[]{:S(2)}) %collective-permute-start.8) | collective-permute-done | bytes 32800 | tf_op jit(solution)/shard_map/ppermute | solution.py:229
  28.8 1.6 %collective-permute-done.7.two = bf16[128,128]{1,0:T(8,128)(2,1)S(1)} collective-permute-done((bf16[128,128]{1,0:T(8,128)(2,1)S(1)}, bf16[128,128]{1,0:T(8,128)(2,1)S(1)}, u32[]{:S(2)}, u32[]{:S(2)}) %collective-permute-start.7) | collective-permute-done | bytes 32800 | tf_op jit(solution)/shard_map/ppermute | solution.py:229
  30.4 2.5 %collective-permute-start.20 = (bf16[704,128]{1,0:T(8,128)(2,1)S(1)}, bf16[704,128]{1,0:T(8,128)(2,1)S(1)}, u32[]{:S(2)}, u32[]{:S(2)}) collective-permute-start(bf16[704,128]{1,0:T(8,128)(2,1)S(1)} %shard_map.93.array.refs_0_), channel_id=1, source_target_pairs={{0,6},{1,25},{2,4},{3,27},{4,2},{5,29},{6,0},{7,31},{8,14},{9,17},... | collective-permute-start | bytes 540680 | tf_op jit(solution)/shard_map/ppermute | solution.py:229
  33.0 0.5 %collective-permute-start.18 = (bf16[704,128]{1,0:T(8,128)(2,1)S(1)}, bf16[704,128]{1,0:T(8,128)(2,1)S(1)}, u32[]{:S(2)}, u32[]{:S(2)}) collective-permute-start(bf16[704,128]{1,0:T(8,128)(2,1)S(1)} %shard_map.93.array.refs_0_), channel_id=1, source_target_pairs={{0,4},{1,17},{2,6},{3,19},{4,0},{5,21},{6,2},{7,23},{8,12},{9,25},... | collective-permute-start | bytes 540680 | tf_op jit(solution)/shard_map/ppermute | solution.py:229
  33.5 0.5 %collective-permute-start.16 = (bf16[704,128]{1,0:T(8,128)(2,1)S(1)}, bf16[704,128]{1,0:T(8,128)(2,1)S(1)}, u32[]{:S(2)}, u32[]{:S(2)}) collective-permute-start(bf16[704,128]{1,0:T(8,128)(2,1)S(1)} %shard_map.93.array.refs_0_), channel_id=1, source_target_pairs={{0,2},{1,9},{2,0},{3,11},{4,6},{5,13},{6,4},{7,15},{8,10},{9,1},{1... | collective-permute-start | bytes 540680 | tf_op jit(solution)/shard_map/ppermute | solution.py:229
  34.0 2.5 %shard_map.88 = (bf16[8,96,256]{2,1,0:T(8,128)(2,1)}, bf16[4,48,256]{2,1,0:T(8,128)(2,1)}) custom-call(bf16[8,96,256]{2,1,0:T(8,128)(2,1)S(1)} %bitcast.11, bf16[9,256,256]{2,1,0:T(8,128)(2,1)S(1)} %get-tuple-element.29.out_w, bf16[768,256]{1,0:T(8,128)(2,1)S(1)} %get-tuple-element.36.grad, bf16[8,96,256]{2,1,0:T(8,128)(2,1)S(1)} %collective-permute-done.1.refs_0_.refs_1_, ...), custom_call_target="tpu_custom_call" | custom-call | flops 905969664 | bytes 2097152 | tf_op jit(solution)/shard_map/pallas_call | solution.py:356
  36.6 0.3 collective-permute-done.20.refs_3_
  36.9 0.2 collective-permute-start.21
  37.1 1.7 %collective-permute-done.18.refs_2_ = bf16[704,128]{1,0:T(8,128)(2,1)S(1)} collective-permute-done((bf16[704,128]{1,0:T(8,128)(2,1)S(1)}, bf16[704,128]{1,0:T(8,128)(2,1)S(1)}, u32[]{:S(2)}, u32[]{:S(2)}) %collective-permute-start.18) | collective-permute-done | bytes 180256 | tf_op jit(solution)/shard_map/ppermute | solution.py:229
  39.0 0.4 collective-permute-start.17
  39.3 0.9 %shard_map.95 = (bf16[2304,256]{1,0:T(8,128)(2,1)}, bf16[512,256]{1,0:T(8,128)(2,1)}) custom-call(bf16[704,128]{1,0:T(8,128)(2,1)S(1)} %shard_map.93.array.refs_0_, bf16[704,128]{1,0:T(8,128)(2,1)S(1)} %collective-permute-done.16.refs_1_, bf16[704,128]{1,0:T(8,128)(2,1)S(1)} %collective-permute-done.18.refs_2_, ...), custom_call_target="tpu_custom_call" | custom-call | tf_op jit(solution)/shard_map/pallas_call | solution.py:266
  40.3 0.2 collective-permute-done.17.refs_1_
  40.5 0.9 %shard_map.96 = (bf16[2304,256]{1,0:T(8,128)(2,1)}, bf16[512,256]{1,0:T(8,128)(2,1)}) custom-call(bf16[704,128]{1,0:T(8,128)(2,1)S(1)} %collective-permute-done.15.refs_0_, bf16[704,128]{1,0:T(8,128)(2,1)S(1)} %collective-permute-done.17.refs_1_, bf16[704,128]{1,0:T(8,128)(2,1)S(1)} %collective-permute-done.19.refs_2_, ...), custom_call_target="tpu_custom_call", output_to_operand_aliasing={{0}: (4, {}), {1}: (5, {})} | custom-call | tf_op jit(solution)/shard_map/pallas_call | solution.py:268
  (25 shorter events, 0.6 us)
Async XLA Ops:
  0.6 2.6 %collective-permute-start = (bf16[8,96,256]{2,1,0:T(8,128)(2,1)}, bf16[8,96,256]{2,1,0:T(8,128)(2,1)S(1)}, u32[]{:S(2)}, u32[]{:S(2)}) collective-permute-start(bf16[8,96,256]{2,1,0:T(8,128)(2,1)} %bitcast.16), channel_id=1, source_target_pairs={{0,1},{1,0},{2,3},{3,2},{4,5},{5,4},{6,7},{7,6},{8,9},{9,8},{10,11... | collective-permute-start | bytes 1179656 | tf_op jit(solution)/shard_map/ppermute | solution.py:19
  3.1 1.8 %collective-permute-start.1 = (bf16[8,96,256]{2,1,0:T(8,128)(2,1)S(1)}, bf16[8,96,256]{2,1,0:T(8,128)(2,1)S(1)}, u32[]{:S(2)}, u32[]{:S(2)}) collective-permute-start(bf16[8,96,256]{2,1,0:T(8,128)(2,1)S(1)} %bitcast.10), channel_id=1, source_target_pairs={{0,1},{1,0},{2,3},{3,2},{4,5},{5,4},{6,7},{7,6},{8,9},{9,8},{10,11... | collective-permute-start | bytes 1179656 | tf_op jit(solution)/shard_map/ppermute | solution.py:19
  5.6 11.1 %collective-permute-start.9 = (bf16[576,128]{1,0:T(8,128)(2,1)S(1)}, bf16[576,128]{1,0:T(8,128)(2,1)S(1)}, u32[]{:S(2)}, u32[]{:S(2)}) collective-permute-start(bf16[576,128]{1,0:T(8,128)(2,1)S(1)} %get-tuple-element.45), channel_id=1, source_target_pairs={{0,6},{1,25},{2,4},{3,27},{4,2},{5,29},{6,0},{7,31},{8,14},{9,17},... | collective-permute-start | bytes 442376 | tf_op jit(solution)/shard_map/ppermute | solution.py:229
  9.3 8.0 %collective-permute-start.10 = (bf16[576,128]{1,0:T(8,128)(2,1)S(1)}, bf16[576,128]{1,0:T(8,128)(2,1)S(1)}, u32[]{:S(2)}, u32[]{:S(2)}) collective-permute-start(bf16[576,128]{1,0:T(8,128)(2,1)S(1)} %get-tuple-element.46), channel_id=1, source_target_pairs={{0,4},{1,17},{2,6},{3,19},{4,0},{5,21},{6,2},{7,23},{8,12},{9,25},... | collective-permute-start | bytes 442376 | tf_op jit(solution)/shard_map/ppermute | solution.py:229
  9.8 7.5 %collective-permute-start.11 = (bf16[576,128]{1,0:T(8,128)(2,1)S(1)}, bf16[576,128]{1,0:T(8,128)(2,1)S(1)}, u32[]{:S(2)}, u32[]{:S(2)}) collective-permute-start(bf16[576,128]{1,0:T(8,128)(2,1)S(1)} %get-tuple-element.47), channel_id=1, source_target_pairs={{0,2},{1,9},{2,0},{3,11},{4,6},{5,13},{6,4},{7,15},{8,10},{9,1},{1... | collective-permute-start | bytes 442376 | tf_op jit(solution)/shard_map/ppermute | solution.py:229
  11.6 2.0 %collective-permute-start.2 = (bf16[512,128]{1,0:T(8,128)(2,1)S(1)}, bf16[512,128]{1,0:T(8,128)(2,1)S(1)}, u32[]{:S(2)}, u32[]{:S(2)}) collective-permute-start(bf16[512,128]{1,0:T(8,128)(2,1)S(1)} %get-tuple-element.40), channel_id=1, source_target_pairs={{0,1},{1,0},{2,3},{3,2},{4,5},{5,4},{6,7},{7,6},{8,9},{9,8},{10,11... | collective-permute-start | bytes 393224 | tf_op jit(solution)/shard_map/ppermute | solution.py:233
  13.7 7.2 %collective-permute-start.3 = (bf16[128,128]{1,0:T(8,128)(2,1)S(1)}, bf16[128,128]{1,0:T(8,128)(2,1)S(1)}, u32[]{:S(2)}, u32[]{:S(2)}) collective-permute-start(bf16[128,128]{1,0:T(8,128)(2,1)S(1)} %get-tuple-element.42), channel_id=1, source_target_pairs={{0,6},{1,25},{2,4},{3,27},{4,2},{5,29},{6,0},{7,31},{8,14},{9,17},... | collective-permute-start | bytes 98312 | tf_op jit(solution)/shard_map/ppermute | solution.py:229
  16.2 5.6 %collective-permute-start.4 = (bf16[128,128]{1,0:T(8,128)(2,1)S(1)}, bf16[128,128]{1,0:T(8,128)(2,1)S(1)}, u32[]{:S(2)}, u32[]{:S(2)}) collective-permute-start(bf16[128,128]{1,0:T(8,128)(2,1)S(1)} %get-tuple-element.43), channel_id=1, source_target_pairs={{0,4},{1,17},{2,6},{3,19},{4,0},{5,21},{6,2},{7,23},{8,12},{9,25},... | collective-permute-start | bytes 98312 | tf_op jit(solution)/shard_map/ppermute | solution.py:229
  16.7 5.1 %collective-permute-start.5 = (bf16[128,128]{1,0:T(8,128)(2,1)S(1)}, bf16[128,128]{1,0:T(8,128)(2,1)S(1)}, u32[]{:S(2)}, u32[]{:S(2)}) collective-permute-start(bf16[128,128]{1,0:T(8,128)(2,1)S(1)} %get-tuple-element.44), channel_id=1, source_target_pairs={{0,2},{1,9},{2,0},{3,11},{4,6},{5,13},{6,4},{7,15},{8,10},{9,1},{1... | collective-permute-start | bytes 98312 | tf_op jit(solution)/shard_map/ppermute | solution.py:229
  17.3 8.0 %collective-permute-start.14 = (bf16[576,128]{1,0:T(8,128)(2,1)S(1)}, bf16[576,128]{1,0:T(8,128)(2,1)S(1)}, u32[]{:S(2)}, u32[]{:S(2)}) collective-permute-start(bf16[576,128]{1,0:T(8,128)(2,1)S(1)} %shard_map.91.own), channel_id=1, source_target_pairs={{0,24},{1,7},{2,26},{3,5},{4,28},{5,3},{6,30},{7,1},{8,16},{9,15},... | collective-permute-start | bytes 442376 | tf_op jit(solution)/shard_map/ppermute | solution.py:229
  20.8 7.2 %collective-permute-start.13 = (bf16[576,128]{1,0:T(8,128)(2,1)S(1)}, bf16[576,128]{1,0:T(8,128)(2,1)S(1)}, u32[]{:S(2)}, u32[]{:S(2)}) collective-permute-start(bf16[576,128]{1,0:T(8,128)(2,1)S(1)} %shard_map.91.own), channel_id=1, source_target_pairs={{0,16},{1,5},{2,18},{3,7},{4,20},{5,1},{6,22},{7,3},{8,24},{9,13},... | collective-permute-start | bytes 442376 | tf_op jit(solution)/shard_map/ppermute | solution.py:229
  20.9 7.2 %collective-permute-start.12 = (bf16[576,128]{1,0:T(8,128)(2,1)S(1)}, bf16[576,128]{1,0:T(8,128)(2,1)S(1)}, u32[]{:S(2)}, u32[]{:S(2)}) collective-permute-start(bf16[576,128]{1,0:T(8,128)(2,1)S(1)} %shard_map.91.own), channel_id=1, source_target_pairs={{0,8},{1,3},{2,10},{3,1},{4,12},{5,7},{6,14},{7,5},{8,0},{9,11},{1... | collective-permute-start | bytes 442376 | tf_op jit(solution)/shard_map/ppermute | solution.py:229
  21.8 7.0 %collective-permute-start.8 = (bf16[128,128]{1,0:T(8,128)(2,1)S(1)}, bf16[128,128]{1,0:T(8,128)(2,1)S(1)}, u32[]{:S(2)}, u32[]{:S(2)}) collective-permute-start(bf16[128,128]{1,0:T(8,128)(2,1)S(1)} %shard_map.90.own), channel_id=1, source_target_pairs={{0,24},{1,7},{2,26},{3,5},{4,28},{5,3},{6,30},{7,1},{8,16},{9,15},... | collective-permute-start | bytes 98312 | tf_op jit(solution)/shard_map/ppermute | solution.py:229
  25.3 5.1 %collective-permute-start.7 = (bf16[128,128]{1,0:T(8,128)(2,1)S(1)}, bf16[128,128]{1,0:T(8,128)(2,1)S(1)}, u32[]{:S(2)}, u32[]{:S(2)}) collective-permute-start(bf16[128,128]{1,0:T(8,128)(2,1)S(1)} %shard_map.90.own), channel_id=1, source_target_pairs={{0,16},{1,5},{2,18},{3,7},{4,20},{5,1},{6,22},{7,3},{8,24},{9,13},... | collective-permute-start | bytes 98312 | tf_op jit(solution)/shard_map/ppermute | solution.py:229
  25.3 5.1 %collective-permute-start.6 = (bf16[128,128]{1,0:T(8,128)(2,1)S(1)}, bf16[128,128]{1,0:T(8,128)(2,1)S(1)}, u32[]{:S(2)}, u32[]{:S(2)}) collective-permute-start(bf16[128,128]{1,0:T(8,128)(2,1)S(1)} %shard_map.90.own), channel_id=1, source_target_pairs={{0,8},{1,3},{2,10},{3,1},{4,12},{5,7},{6,14},{7,5},{8,0},{9,11},{1... | collective-permute-start | bytes 98312 | tf_op jit(solution)/shard_map/ppermute | solution.py:229
  30.4 6.5 %collective-permute-start.20 = (bf16[704,128]{1,0:T(8,128)(2,1)S(1)}, bf16[704,128]{1,0:T(8,128)(2,1)S(1)}, u32[]{:S(2)}, u32[]{:S(2)}) collective-permute-start(bf16[704,128]{1,0:T(8,128)(2,1)S(1)} %shard_map.93.array.refs_0_), channel_id=1, source_target_pairs={{0,6},{1,25},{2,4},{3,27},{4,2},{5,29},{6,0},{7,31},{8,14},{9,17},... | collective-permute-start | bytes 540680 | tf_op jit(solution)/shard_map/ppermute | solution.py:229
  33.0 5.9 %collective-permute-start.18 = (bf16[704,128]{1,0:T(8,128)(2,1)S(1)}, bf16[704,128]{1,0:T(8,128)(2,1)S(1)}, u32[]{:S(2)}, u32[]{:S(2)}) collective-permute-start(bf16[704,128]{1,0:T(8,128)(2,1)S(1)} %shard_map.93.array.refs_0_), channel_id=1, source_target_pairs={{0,4},{1,17},{2,6},{3,19},{4,0},{5,21},{6,2},{7,23},{8,12},{9,25},... | collective-permute-start | bytes 540680 | tf_op jit(solution)/shard_map/ppermute | solution.py:229
  33.5 5.5 %collective-permute-start.16 = (bf16[704,128]{1,0:T(8,128)(2,1)S(1)}, bf16[704,128]{1,0:T(8,128)(2,1)S(1)}, u32[]{:S(2)}, u32[]{:S(2)}) collective-permute-start(bf16[704,128]{1,0:T(8,128)(2,1)S(1)} %shard_map.93.array.refs_0_), channel_id=1, source_target_pairs={{0,2},{1,9},{2,0},{3,11},{4,6},{5,13},{6,4},{7,15},{8,10},{9,1},{1... | collective-permute-start | bytes 540680 | tf_op jit(solution)/shard_map/ppermute | solution.py:229
  36.6 3.7 %collective-permute-start.15 = (bf16[704,128]{1,0:T(8,128)(2,1)S(1)}, bf16[704,128]{1,0:T(8,128)(2,1)S(1)}, u32[]{:S(2)}, u32[]{:S(2)}) collective-permute-start(bf16[704,128]{1,0:T(8,128)(2,1)S(1)} %shard_map.94), channel_id=1, source_target_pairs={{0,1},{1,0},{2,3},{3,2},{4,5},{5,4},{6,7},{7,6},{8,9},{9,8},{10,11... | collective-permute-start | bytes 540680 | tf_op jit(solution)/shard_map/ppermute | solution.py:233
  36.9 3.3 %collective-permute-start.21 = (bf16[704,128]{1,0:T(8,128)(2,1)S(1)}, bf16[704,128]{1,0:T(8,128)(2,1)S(1)}, u32[]{:S(2)}, u32[]{:S(2)}) collective-permute-start(bf16[704,128]{1,0:T(8,128)(2,1)S(1)} %collective-permute-done.20.refs_3_), channel_id=1, source_target_pairs={{0,1},{1,0},{2,3},{3,2},{4,5},{5,4},{6,7},{7,6},{8,9},{9,8},{10,11... | collective-permute-start | bytes 540680 | tf_op jit(solution)/shard_map/ppermute | solution.py:233
  38.8 1.5 %collective-permute-start.19 = (bf16[704,128]{1,0:T(8,128)(2,1)S(1)}, bf16[704,128]{1,0:T(8,128)(2,1)S(1)}, u32[]{:S(2)}, u32[]{:S(2)}) collective-permute-start(bf16[704,128]{1,0:T(8,128)(2,1)S(1)} %collective-permute-done.18.refs_2_), channel_id=1, source_target_pairs={{0,1},{1,0},{2,3},{3,2},{4,5},{5,4},{6,7},{7,6},{8,9},{9,8},{10,11... | collective-permute-start | bytes 540680 | tf_op jit(solution)/shard_map/ppermute | solution.py:233
  39.0 1.5 %collective-permute-start.17 = (bf16[704,128]{1,0:T(8,128)(2,1)S(1)}, bf16[704,128]{1,0:T(8,128)(2,1)S(1)}, u32[]{:S(2)}, u32[]{:S(2)}) collective-permute-start(bf16[704,128]{1,0:T(8,128)(2,1)S(1)} %collective-permute-done.16.refs_1_), channel_id=1, source_target_pairs={{0,1},{1,0},{2,3},{3,2},{4,5},{5,4},{6,7},{7,6},{8,9},{9,8},{10,11... | collective-permute-start | bytes 540680 | tf_op jit(solution)/shard_map/ppermute | solution.py:233

commit v16 on v12

--- a/solution.py
+++ b/solution.py
@@ -51,11 +51,10 @@
     cot, lat_w, top = near[:3]
     rows, cols, channels = cot.shape
     half = cols // 2
-    copies[0].wait()
+    for copy in copies[:4]:
+        copy.wait()
     for r in range(rows):
         put_shifted(stack, r, cot[r], 1)
-    for copy in copies[1:4]:
-        copy.wait()
     upper = lax.broadcasted_iota(jnp.int32, (cols, half), 0)
     spread = jnp.where(upper // 2 == lax.broadcasted_iota(jnp.int32, (cols, half), 1), 1.0, 0.0).astype(BF16)
     lateral = jnp.dot(feat[...], lat_w[...], preferred_element_type=F32)
@@ -183,13 +182,13 @@
     out[...] = ((near + far) * scale).astype(BF16)
 
 
-def place_kernel(pair, *refs):
+def place_kernel(plan, *refs):
     results, sems = refs[-3:-1], refs[-1]
-    side = lax.axis_index("space")
-    columns, place = (1 - side, places()[1]) if pair else (side, places()[0])
-    lanes = pl.ds(pl.multiple_of(columns * 128, 128), 128)
+    side, (own, other) = lax.axis_index("space"), places()
     copies = []
-    for k, quarter in zip((0, 3, 2, 1), refs):
+    for quarter, (pair, k) in zip(refs, plan):
+        columns, place = (1 - side, other) if pair else (side, own)
+        lanes = pl.ds(pl.multiple_of(columns * 128, 128), 128)
         start = 0
         for result in results:
             share = result.shape[0] // 4
@@ -238,10 +237,13 @@
     three, two, one = [exchange(total, 0, k) for k in (3, 2, 1)]
     quarters = [total, three, two, one]
     results = [((length, 2 * width), BF16) for length in lengths]
-    place = dict(out_specs=[far] * 2, scratch_shapes=[pltpu.SemaphoreType.DMA((8,))])
-    half = call(functools.partial(place_kernel, False), *results, **place)(*quarters)
-    place.update(in_specs=[vmem] * 4 + [far] * 2, input_output_aliases={4: 0, 5: 1})
-    return call(functools.partial(place_kernel, True), *results, **place)(*[swap(one) for one in quarters], *half)
+    others = [swap(one) for one in quarters]
+    place = dict(out_specs=[far] * 2, scratch_shapes=[pltpu.SemaphoreType.DMA((10,))])
+    plan = (False, 0), (False, 3), (False, 2), (False, 1), (True, 0)
+    most = call(functools.partial(place_kernel, plan), *results, **place)(*quarters, others[0])
+    plan = (True, 3), (True, 2), (True, 1)
+    place.update(in_specs=[vmem] * 3 + [far] * 2, input_output_aliases={3: 0, 4: 1})
+    return call(functools.partial(place_kernel, plan), *results, **place)(*others[1:], *most)
 
 
 def local(features, top_down, lateral_weight, out_kernel, cotangent):

time: 40.4 us -> 40.4 us (level)
  no operation moved by 1% of the time
where the time goes in v16:
time: 40.4 us; the launch traced here: 40.2 us
  waiting for transfers between devices  15.9 us (39%)
  starting transfers between devices  13.9 us (34%)
  Pallas kernels  9.76 us (24%)
  between operations  0.72 us (2%)
    ppermute x9, waiting for transfers between devices, exchange(): return lax.ppermute(array, ('dp', 'space'), pairs)  15.6 us
    ppermute x9, starting transfers between devices, exchange(): return lax.ppermute(array, ('dp', 'space'), pairs)  12.2 us
    pallas_call x1, Pallas kernels, local(): pl.pallas_call(functools.partial(forward_kernel, peers), out_shape=[jax.S...  2.53 us
    pallas_call x1, Pallas kernels, local(): pl.pallas_call(merge_kernel, out_shape=[jax.ShapeDtypeStruct(shape, BF16)...  1.94 us
    pallas_call x2, Pallas kernels, sum_everywhere(): call(functools.partial(place_kernel, plan), *results, **place)  1.86 us
    pallas_call x1, Pallas kernels, local(): pl.pallas_call(functools.partial(data_grad_kernel, peers), out_shape=[jax...  1.7 us
    pallas_call x1, Pallas kernels, local(): pl.pallas_call(pair_kernel_grad_kernel, out_shape=jax.ShapeDtypeStruct((9...  1.44 us
    ppermute x5, starting transfers between devices, swap(): return lax.ppermute(array, 'space', [(0, 1), (1, 0)])  1.04 us
  transfers between devices with their start and end apart: 16, of which 8 were waited for; matrix products, arithmetic and copies ran while one was open for 0% of the time, Pallas kernels for 21%

profile of v16, /device:TPU:0, one launch (start us, length us, event | category | flops | bytes accessed | tf_op | source)
XLA Modules:
  0.0 40.2 jit_solution(6242056949806578364)
XLA Ops:
  0.6 0.5 %collective-permute-start = (bf16[8,96,256]{2,1,0:T(8,128)(2,1)}, bf16[8,96,256]{2,1,0:T(8,128)(2,1)S(1)}, u32[]{:S(2)}, u32[]{:S(2)}) collective-permute-start(bf16[8,96,256]{2,1,0:T(8,128)(2,1)} %bitcast.16), channel_id=1, source_target_pairs={{0,1},{1,0},{2,3},{3,2},{4,5},{5,4},{6,7},{7,6},{8,9},{9,8},{10,11... | collective-permute-start | bytes 1179656 | tf_op jit(solution)/shard_map/ppermute | solution.py:19
  1.1 1.9 %shard_map.84 = (bf16[768,256]{1,0:T(8,128)(2,1)S(1)}, bf16[256,768]{1,0:T(8,128)(2,1)S(1)}, bf16[8,96,768]{2,1,0:T(8,128)(2,1)S(1)}, bf16[768,512]{1,0:T(8,128)(2,1)S(1)}, bf16[9,256,256]{2,1,0:T(8,128)(2,1)S(1)}) custom-call(bf16[8,96,256]{2,1,0:T(8,128)(2,1)} %bitcast.17, bf16[512,256]{1,0:T(8,128)(2,1)} %refs_1_.1, bf16[4,48,256]{2,1,0:T(8,128)(2,1)} %bitcast.18, ...), custom_call_target="tpu_custom_call" | custom-call | flops 805306368 | bytes 4194304 | tf_op jit(solution)/shard_map/pallas_call | solution.py:269
  3.1 0.1 collective-permute-start.1
  3.2 1.7 %shard_map.85 = (bf16[768,256]{1,0:T(8,128)(2,1)S(1)}, bf16[2,96,768]{2,1,0:T(8,128)(2,1)}, f32[512,128]{1,0:T(8,128)S(1)}, bf16[512,128]{1,0:T(8,128)(2,1)S(1)}) custom-call(bf16[8,96,768]{2,1,0:T(8,128)(2,1)S(1)} %get-tuple-element.24.stack, bf16[8,96,256]{2,1,0:T(8,128)(2,1)S(1)} %collective-permute-done.before.after.cot, ...), custom_call_target="tpu_custom_call" | custom-call | flops 1107296256 | bytes 4194304 | tf_op jit(solution)/shard_map/pallas_call | solution.py:290
  4.9 0.5 %collective-permute-start.2 = (bf16[512,128]{1,0:T(8,128)(2,1)S(1)}, bf16[512,128]{1,0:T(8,128)(2,1)S(1)}, u32[]{:S(2)}, u32[]{:S(2)}) collective-permute-start(bf16[512,128]{1,0:T(8,128)(2,1)S(1)} %get-tuple-element.31), channel_id=1, source_target_pairs={{0,1},{1,0},{2,3},{3,2},{4,5},{5,4},{6,7},{7,6},{8,9},{9,8},{10,11... | collective-permute-start | bytes 393224 | tf_op jit(solution)/shard_map/ppermute | solution.py:214
  5.5 0.0 collective-permute-done.1.refs_0_.refs_1_
  5.5 1.4 %shard_map.87.kernel_sums = f32[2304,128]{1,0:T(8,128)S(1)} custom-call(bf16[8,96,768]{2,1,0:T(8,128)(2,1)S(1)} %get-tuple-element.24.stack, bf16[256,768]{1,0:T(8,128)(2,1)S(1)} %get-tuple-element.29.merged_t, bf16[8,96,256]{2,1,0:T(8,128)(2,1)S(1)} %collective-permute-done.before.after.cot, bf16[768,256]{1,0:T(8,128)(2,1)S(1)} %bitcast.9), custom_call_target="tpu_custom_call" | custom-call | flops 905969664 | bytes 4194304 | tf_op jit(solution)/shard_map/pallas_call | solution.py:307
  6.9 0.0 collective-permute-done.2.got
  6.9 0.1 shard_map.88
  7.0 3.5 %collective-permute-start.3 = (bf16[704,128]{1,0:T(8,128)(2,1)S(1)}, bf16[704,128]{1,0:T(8,128)(2,1)S(1)}, u32[]{:S(2)}, u32[]{:S(2)}) collective-permute-start(bf16[704,128]{1,0:T(8,128)(2,1)S(1)} %get-tuple-element.33), channel_id=1, source_target_pairs={{0,6},{1,25},{2,4},{3,27},{4,2},{5,29},{6,0},{7,31},{8,14},{9,17},... | collective-permute-start | bytes 540680 | tf_op jit(solution)/shard_map/ppermute | solution.py:210
  10.6 0.5 %collective-permute-start.4 = (bf16[704,128]{1,0:T(8,128)(2,1)S(1)}, bf16[704,128]{1,0:T(8,128)(2,1)S(1)}, u32[]{:S(2)}, u32[]{:S(2)}) collective-permute-start(bf16[704,128]{1,0:T(8,128)(2,1)S(1)} %get-tuple-element.34), channel_id=1, source_target_pairs={{0,4},{1,17},{2,6},{3,19},{4,0},{5,21},{6,2},{7,23},{8,12},{9,25},... | collective-permute-start | bytes 540680 | tf_op jit(solution)/shard_map/ppermute | solution.py:210
  11.1 0.1 collective-permute-start.5
  11.2 2.8 %collective-permute-done.3.three = bf16[704,128]{1,0:T(8,128)(2,1)S(1)} collective-permute-done((bf16[704,128]{1,0:T(8,128)(2,1)S(1)}, bf16[704,128]{1,0:T(8,128)(2,1)S(1)}, u32[]{:S(2)}, u32[]{:S(2)}) %collective-permute-start.3) | collective-permute-done | bytes 180256 | tf_op jit(solution)/shard_map/ppermute | solution.py:210
  14.0 2.0 %collective-permute-done.4.two = bf16[704,128]{1,0:T(8,128)(2,1)S(1)} collective-permute-done((bf16[704,128]{1,0:T(8,128)(2,1)S(1)}, bf16[704,128]{1,0:T(8,128)(2,1)S(1)}, u32[]{:S(2)}, u32[]{:S(2)}) %collective-permute-start.4) | collective-permute-done | bytes 180256 | tf_op jit(solution)/shard_map/ppermute | solution.py:210
  16.1 0.5 %collective-permute-done.5.one = bf16[704,128]{1,0:T(8,128)(2,1)S(1)} collective-permute-done((bf16[704,128]{1,0:T(8,128)(2,1)S(1)}, bf16[704,128]{1,0:T(8,128)(2,1)S(1)}, u32[]{:S(2)}, u32[]{:S(2)}) %collective-permute-start.5) | collective-permute-done | bytes 180256 | tf_op jit(solution)/shard_map/ppermute | solution.py:210
  16.6 0.1 shard_map.89.own
  16.6 3.7 %collective-permute-start.6 = (bf16[704,128]{1,0:T(8,128)(2,1)S(1)}, bf16[704,128]{1,0:T(8,128)(2,1)S(1)}, u32[]{:S(2)}, u32[]{:S(2)}) collective-permute-start(bf16[704,128]{1,0:T(8,128)(2,1)S(1)} %shard_map.89.own), channel_id=1, source_target_pairs={{0,24},{1,7},{2,26},{3,5},{4,28},{5,3},{6,30},{7,1},{8,16},{9,15},... | collective-permute-start | bytes 540680 | tf_op jit(solution)/shard_map/ppermute | solution.py:210
  20.3 0.8 %collective-permute-start.8 = (bf16[704,128]{1,0:T(8,128)(2,1)S(1)}, bf16[704,128]{1,0:T(8,128)(2,1)S(1)}, u32[]{:S(2)}, u32[]{:S(2)}) collective-permute-start(bf16[704,128]{1,0:T(8,128)(2,1)S(1)} %shard_map.89.own), channel_id=1, source_target_pairs={{0,8},{1,3},{2,10},{3,1},{4,12},{5,7},{6,14},{7,5},{8,0},{9,11},{1... | collective-permute-start | bytes 540680 | tf_op jit(solution)/shard_map/ppermute | solution.py:210
  21.1 2.5 %shard_map.86 = (bf16[8,96,256]{2,1,0:T(8,128)(2,1)}, bf16[4,48,256]{2,1,0:T(8,128)(2,1)}) custom-call(bf16[8,96,256]{2,1,0:T(8,128)(2,1)S(1)} %bitcast.11, bf16[9,256,256]{2,1,0:T(8,128)(2,1)S(1)} %get-tuple-element.23.out_w, bf16[768,256]{1,0:T(8,128)(2,1)S(1)} %get-tuple-element.26.grad, bf16[8,96,256]{2,1,0:T(8,128)(2,1)S(1)} %collective-permute-done.1.refs_0_.refs_1_, ...), custom_call_target="tpu_custom_call" | custom-call | flops 905969664 | bytes 2097152 | tf_op jit(solution)/shard_map/pallas_call | solution.py:321
  23.6 0.5 %collective-permute-done.6.three = bf16[704,128]{1,0:T(8,128)(2,1)S(1)} collective-permute-done((bf16[704,128]{1,0:T(8,128)(2,1)S(1)}, bf16[704,128]{1,0:T(8,128)(2,1)S(1)}, u32[]{:S(2)}, u32[]{:S(2)}) %collective-permute-start.6) | collective-permute-done | bytes 180256 | tf_op jit(solution)/shard_map/ppermute | solution.py:210
  24.1 4.9 %collective-permute-done.7.two = bf16[704,128]{1,0:T(8,128)(2,1)S(1)} collective-permute-done((bf16[704,128]{1,0:T(8,128)(2,1)S(1)}, bf16[704,128]{1,0:T(8,128)(2,1)S(1)}, u32[]{:S(2)}, u32[]{:S(2)}) %collective-permute-start.7) | collective-permute-done | bytes 180256 | tf_op jit(solution)/shard_map/ppermute | solution.py:210
  29.0 0.1 shard_map.90.refs_0_
  29.1 2.0 %collective-permute-start.9 = (bf16[704,128]{1,0:T(8,128)(2,1)S(1)}, bf16[704,128]{1,0:T(8,128)(2,1)S(1)}, u32[]{:S(2)}, u32[]{:S(2)}) collective-permute-start(bf16[704,128]{1,0:T(8,128)(2,1)S(1)} %shard_map.90.refs_0_), channel_id=1, source_target_pairs={{0,6},{1,25},{2,4},{3,27},{4,2},{5,29},{6,0},{7,31},{8,14},{9,17},... | collective-permute-start | bytes 540680 | tf_op jit(solution)/shard_map/ppermute | solution.py:210
  31.1 1.0 %collective-permute-start.11 = (bf16[704,128]{1,0:T(8,128)(2,1)S(1)}, bf16[704,128]{1,0:T(8,128)(2,1)S(1)}, u32[]{:S(2)}, u32[]{:S(2)}) collective-permute-start(bf16[704,128]{1,0:T(8,128)(2,1)S(1)} %shard_map.90.refs_0_), channel_id=1, source_target_pairs={{0,4},{1,17},{2,6},{3,19},{4,0},{5,21},{6,2},{7,23},{8,12},{9,25},... | collective-permute-start | bytes 540680 | tf_op jit(solution)/shard_map/ppermute | solution.py:210
  32.1 0.6 %collective-permute-start.13 = (bf16[704,128]{1,0:T(8,128)(2,1)S(1)}, bf16[704,128]{1,0:T(8,128)(2,1)S(1)}, u32[]{:S(2)}, u32[]{:S(2)}) collective-permute-start(bf16[704,128]{1,0:T(8,128)(2,1)S(1)} %shard_map.90.refs_0_), channel_id=1, source_target_pairs={{0,2},{1,9},{2,0},{3,11},{4,6},{5,13},{6,4},{7,15},{8,10},{9,1},{1... | collective-permute-start | bytes 540680 | tf_op jit(solution)/shard_map/ppermute | solution.py:210
  32.7 3.0 %collective-permute-done.9.refs_1_ = bf16[704,128]{1,0:T(8,128)(2,1)S(1)} collective-permute-done((bf16[704,128]{1,0:T(8,128)(2,1)S(1)}, bf16[704,128]{1,0:T(8,128)(2,1)S(1)}, u32[]{:S(2)}, u32[]{:S(2)}) %collective-permute-start.9) | collective-permute-done | bytes 180256 | tf_op jit(solution)/shard_map/ppermute | solution.py:210
  35.7 1.8 %collective-permute-done.11.refs_2_ = bf16[704,128]{1,0:T(8,128)(2,1)S(1)} collective-permute-done((bf16[704,128]{1,0:T(8,128)(2,1)S(1)}, bf16[704,128]{1,0:T(8,128)(2,1)S(1)}, u32[]{:S(2)}, u32[]{:S(2)}) %collective-permute-start.11) | collective-permute-done | bytes 180256 | tf_op jit(solution)/shard_map/ppermute | solution.py:210
  37.5 0.4 %collective-permute-start.12 = (bf16[704,128]{1,0:T(8,128)(2,1)S(1)}, bf16[704,128]{1,0:T(8,128)(2,1)S(1)}, u32[]{:S(2)}, u32[]{:S(2)}) collective-permute-start(bf16[704,128]{1,0:T(8,128)(2,1)S(1)} %collective-permute-done.11.refs_2_), channel_id=1, source_target_pairs={{0,1},{1,0},{2,3},{3,2},{4,5},{5,4},{6,7},{7,6},{8,9},{9,8},{10,11... | collective-permute-start | bytes 540680 | tf_op jit(solution)/shard_map/ppermute | solution.py:214
  37.9 0.1 collective-permute-start.14
  38.0 1.0 %shard_map.91 = (bf16[2304,256]{1,0:T(8,128)(2,1)}, bf16[512,256]{1,0:T(8,128)(2,1)}) custom-call(bf16[704,128]{1,0:T(8,128)(2,1)S(1)} %shard_map.90.refs_0_, bf16[704,128]{1,0:T(8,128)(2,1)S(1)} %collective-permute-done.9.refs_1_, bf16[704,128]{1,0:T(8,128)(2,1)S(1)} %collective-permute-done.11.refs_2_, ...), custom_call_target="tpu_custom_call" | custom-call | tf_op jit(solution)/shard_map/pallas_call | solution.py:243
  39.0 0.3 collective-permute-done.14.refs_2_
  39.3 0.9 %shard_map.92 = (bf16[2304,256]{1,0:T(8,128)(2,1)}, bf16[512,256]{1,0:T(8,128)(2,1)}) custom-call(bf16[704,128]{1,0:T(8,128)(2,1)S(1)} %collective-permute-done.10.refs_0_, bf16[704,128]{1,0:T(8,128)(2,1)S(1)} %collective-permute-done.12.refs_1_, bf16[704,128]{1,0:T(8,128)(2,1)S(1)} %collective-permute-done.14.refs_2_, ...), custom_call_target="tpu_custom_call", output_to_operand_aliasing={{0}: (3, {}), {1}: (4, {})} | custom-call | tf_op jit(solution)/shard_map/pallas_call | solution.py:246
  (9 shorter events, 0.0 us)
Async XLA Ops:
  0.6 2.6 %collective-permute-start = (bf16[8,96,256]{2,1,0:T(8,128)(2,1)}, bf16[8,96,256]{2,1,0:T(8,128)(2,1)S(1)}, u32[]{:S(2)}, u32[]{:S(2)}) collective-permute-start(bf16[8,96,256]{2,1,0:T(8,128)(2,1)} %bitcast.16), channel_id=1, source_target_pairs={{0,1},{1,0},{2,3},{3,2},{4,5},{5,4},{6,7},{7,6},{8,9},{9,8},{10,11... | collective-permute-start | bytes 1179656 | tf_op jit(solution)/shard_map/ppermute | solution.py:19
  3.1 2.4 %collective-permute-start.1 = (bf16[8,96,256]{2,1,0:T(8,128)(2,1)S(1)}, bf16[8,96,256]{2,1,0:T(8,128)(2,1)S(1)}, u32[]{:S(2)}, u32[]{:S(2)}) collective-permute-start(bf16[8,96,256]{2,1,0:T(8,128)(2,1)S(1)} %bitcast.10), channel_id=1, source_target_pairs={{0,1},{1,0},{2,3},{3,2},{4,5},{5,4},{6,7},{7,6},{8,9},{9,8},{10,11... | collective-permute-start | bytes 1179656 | tf_op jit(solution)/shard_map/ppermute | solution.py:19
  4.9 2.0 %collective-permute-start.2 = (bf16[512,128]{1,0:T(8,128)(2,1)S(1)}, bf16[512,128]{1,0:T(8,128)(2,1)S(1)}, u32[]{:S(2)}, u32[]{:S(2)}) collective-permute-start(bf16[512,128]{1,0:T(8,128)(2,1)S(1)} %get-tuple-element.31), channel_id=1, source_target_pairs={{0,1},{1,0},{2,3},{3,2},{4,5},{5,4},{6,7},{7,6},{8,9},{9,8},{10,11... | collective-permute-start | bytes 393224 | tf_op jit(solution)/shard_map/ppermute | solution.py:214
  7.0 7.0 %collective-permute-start.3 = (bf16[704,128]{1,0:T(8,128)(2,1)S(1)}, bf16[704,128]{1,0:T(8,128)(2,1)S(1)}, u32[]{:S(2)}, u32[]{:S(2)}) collective-permute-start(bf16[704,128]{1,0:T(8,128)(2,1)S(1)} %get-tuple-element.33), channel_id=1, source_target_pairs={{0,6},{1,25},{2,4},{3,27},{4,2},{5,29},{6,0},{7,31},{8,14},{9,17},... | collective-permute-start | bytes 540680 | tf_op jit(solution)/shard_map/ppermute | solution.py:210
  10.6 5.5 %collective-permute-start.4 = (bf16[704,128]{1,0:T(8,128)(2,1)S(1)}, bf16[704,128]{1,0:T(8,128)(2,1)S(1)}, u32[]{:S(2)}, u32[]{:S(2)}) collective-permute-start(bf16[704,128]{1,0:T(8,128)(2,1)S(1)} %get-tuple-element.34), channel_id=1, source_target_pairs={{0,4},{1,17},{2,6},{3,19},{4,0},{5,21},{6,2},{7,23},{8,12},{9,25},... | collective-permute-start | bytes 540680 | tf_op jit(solution)/shard_map/ppermute | solution.py:210
  11.1 5.5 %collective-permute-start.5 = (bf16[704,128]{1,0:T(8,128)(2,1)S(1)}, bf16[704,128]{1,0:T(8,128)(2,1)S(1)}, u32[]{:S(2)}, u32[]{:S(2)}) collective-permute-start(bf16[704,128]{1,0:T(8,128)(2,1)S(1)} %get-tuple-element.35), channel_id=1, source_target_pairs={{0,2},{1,9},{2,0},{3,11},{4,6},{5,13},{6,4},{7,15},{8,10},{9,1},{1... | collective-permute-start | bytes 540680 | tf_op jit(solution)/shard_map/ppermute | solution.py:210
  16.6 7.5 %collective-permute-start.6 = (bf16[704,128]{1,0:T(8,128)(2,1)S(1)}, bf16[704,128]{1,0:T(8,128)(2,1)S(1)}, u32[]{:S(2)}, u32[]{:S(2)}) collective-permute-start(bf16[704,128]{1,0:T(8,128)(2,1)S(1)} %shard_map.89.own), channel_id=1, source_target_pairs={{0,24},{1,7},{2,26},{3,5},{4,28},{5,3},{6,30},{7,1},{8,16},{9,15},... | collective-permute-start | bytes 540680 | tf_op jit(solution)/shard_map/ppermute | solution.py:210
  20.3 8.7 %collective-permute-start.7 = (bf16[704,128]{1,0:T(8,128)(2,1)S(1)}, bf16[704,128]{1,0:T(8,128)(2,1)S(1)}, u32[]{:S(2)}, u32[]{:S(2)}) collective-permute-start(bf16[704,128]{1,0:T(8,128)(2,1)S(1)} %shard_map.89.own), channel_id=1, source_target_pairs={{0,16},{1,5},{2,18},{3,7},{4,20},{5,1},{6,22},{7,3},{8,24},{9,13},... | collective-permute-start | bytes 540680 | tf_op jit(solution)/shard_map/ppermute | solution.py:210
  20.3 8.7 %collective-permute-start.8 = (bf16[704,128]{1,0:T(8,128)(2,1)S(1)}, bf16[704,128]{1,0:T(8,128)(2,1)S(1)}, u32[]{:S(2)}, u32[]{:S(2)}) collective-permute-start(bf16[704,128]{1,0:T(8,128)(2,1)S(1)} %shard_map.89.own), channel_id=1, source_target_pairs={{0,8},{1,3},{2,10},{3,1},{4,12},{5,7},{6,14},{7,5},{8,0},{9,11},{1... | collective-permute-start | bytes 540680 | tf_op jit(solution)/shard_map/ppermute | solution.py:210
  29.1 6.6 %collective-permute-start.9 = (bf16[704,128]{1,0:T(8,128)(2,1)S(1)}, bf16[704,128]{1,0:T(8,128)(2,1)S(1)}, u32[]{:S(2)}, u32[]{:S(2)}) collective-permute-start(bf16[704,128]{1,0:T(8,128)(2,1)S(1)} %shard_map.90.refs_0_), channel_id=1, source_target_pairs={{0,6},{1,25},{2,4},{3,27},{4,2},{5,29},{6,0},{7,31},{8,14},{9,17},... | collective-permute-start | bytes 540680 | tf_op jit(solution)/shard_map/ppermute | solution.py:210
  31.1 6.4 %collective-permute-start.11 = (bf16[704,128]{1,0:T(8,128)(2,1)S(1)}, bf16[704,128]{1,0:T(8,128)(2,1)S(1)}, u32[]{:S(2)}, u32[]{:S(2)}) collective-permute-start(bf16[704,128]{1,0:T(8,128)(2,1)S(1)} %shard_map.90.refs_0_), channel_id=1, source_target_pairs={{0,4},{1,17},{2,6},{3,19},{4,0},{5,21},{6,2},{7,23},{8,12},{9,25},... | collective-permute-start | bytes 540680 | tf_op jit(solution)/shard_map/ppermute | solution.py:210
  32.1 5.8 %collective-permute-start.13 = (bf16[704,128]{1,0:T(8,128)(2,1)S(1)}, bf16[704,128]{1,0:T(8,128)(2,1)S(1)}, u32[]{:S(2)}, u32[]{:S(2)}) collective-permute-start(bf16[704,128]{1,0:T(8,128)(2,1)S(1)} %shard_map.90.refs_0_), channel_id=1, source_target_pairs={{0,2},{1,9},{2,0},{3,11},{4,6},{5,13},{6,4},{7,15},{8,10},{9,1},{1... | collective-permute-start | bytes 540680 | tf_op jit(solution)/shard_map/ppermute | solution.py:210
  32.7 5.4 %collective-permute-start.15 = (bf16[704,128]{1,0:T(8,128)(2,1)S(1)}, bf16[704,128]{1,0:T(8,128)(2,1)S(1)}, u32[]{:S(2)}, u32[]{:S(2)}) collective-permute-start(bf16[704,128]{1,0:T(8,128)(2,1)S(1)} %shard_map.90.refs_0_), channel_id=1, source_target_pairs={{0,1},{1,0},{2,3},{3,2},{4,5},{5,4},{6,7},{7,6},{8,9},{9,8},{10,11... | collective-permute-start | bytes 540680 | tf_op jit(solution)/shard_map/ppermute | solution.py:214
  35.7 3.3 %collective-permute-start.10 = (bf16[704,128]{1,0:T(8,128)(2,1)S(1)}, bf16[704,128]{1,0:T(8,128)(2,1)S(1)}, u32[]{:S(2)}, u32[]{:S(2)}) collective-permute-start(bf16[704,128]{1,0:T(8,128)(2,1)S(1)} %collective-permute-done.9.refs_1_), channel_id=1, source_target_pairs={{0,1},{1,0},{2,3},{3,2},{4,5},{5,4},{6,7},{7,6},{8,9},{9,8},{10,11... | collective-permute-start | bytes 540680 | tf_op jit(solution)/shard_map/ppermute | solution.py:214
  37.5 1.5 %collective-permute-start.12 = (bf16[704,128]{1,0:T(8,128)(2,1)S(1)}, bf16[704,128]{1,0:T(8,128)(2,1)S(1)}, u32[]{:S(2)}, u32[]{:S(2)}) collective-permute-start(bf16[704,128]{1,0:T(8,128)(2,1)S(1)} %collective-permute-done.11.refs_2_), channel_id=1, source_target_pairs={{0,1},{1,0},{2,3},{3,2},{4,5},{5,4},{6,7},{7,6},{8,9},{9,8},{10,11... | collective-permute-start | bytes 540680 | tf_op jit(solution)/shard_map/ppermute | solution.py:214
  37.9 1.4 %collective-permute-start.14 = (bf16[704,128]{1,0:T(8,128)(2,1)S(1)}, bf16[704,128]{1,0:T(8,128)(2,1)S(1)}, u32[]{:S(2)}, u32[]{:S(2)}) collective-permute-start(bf16[704,128]{1,0:T(8,128)(2,1)S(1)} %collective-permute-done.13.refs_3_), channel_id=1, source_target_pairs={{0,1},{1,0},{2,3},{3,2},{4,5},{5,4},{6,7},{7,6},{8,9},{9,8},{10,11... | collective-permute-start | bytes 540680 | tf_op jit(solution)/shard_map/ppermute | solution.py:214

commit v17 on v16

--- a/solution.py
+++ b/solution.py
@@ -51,12 +51,13 @@
     cot, lat_w, top = near[:3]
     rows, cols, channels = cot.shape
     half = cols // 2
-    for copy in copies[:4]:
-        copy.wait()
+    upper = lax.broadcasted_iota(jnp.int32, (cols, half), 0)
+    spread = jnp.where(upper // 2 == lax.broadcasted_iota(jnp.int32, (cols, half), 1), 1.0, 0.0).astype(BF16)
+    copies[0].wait()
     for r in range(rows):
         put_shifted(stack, r, cot[r], 1)
-    upper = lax.broadcasted_iota(jnp.int32, (cols, half), 0)
-    spread = jnp.where(upper // 2 == lax.broadcasted_iota(jnp.int32, (cols, half), 1), 1.0, 0.0).astype(BF16)
+    for copy in copies[1:4]:
+        copy.wait()
     lateral = jnp.dot(feat[...], lat_w[...], preferred_element_type=F32)
     for q in range(rows // 2):
         lifted = jnp.dot(spread, top[q], preferred_element_type=F32)

time: 40.4 us -> 40.3 us (level)
  no operation moved by 1% of the time
where the time goes in v17:
time: 40.3 us; the launch traced here: 40.2 us
  waiting for transfers between devices  15.9 us (39%)
  starting transfers between devices  13.9 us (34%)
  Pallas kernels  9.72 us (24%)
  between operations  0.72 us (2%)
    ppermute x9, waiting for transfers between devices, exchange(): return lax.ppermute(array, ('dp', 'space'), pairs)  15.6 us
    ppermute x9, starting transfers between devices, exchange(): return lax.ppermute(array, ('dp', 'space'), pairs)  12.2 us
    pallas_call x1, Pallas kernels, local(): pl.pallas_call(functools.partial(forward_kernel, peers), out_shape=[jax.S...  2.53 us
    pallas_call x1, Pallas kernels, local(): pl.pallas_call(merge_kernel, out_shape=[jax.ShapeDtypeStruct(shape, BF16)...  1.91 us
    pallas_call x2, Pallas kernels, sum_everywhere(): call(functools.partial(place_kernel, plan), *results, **place)  1.86 us
    pallas_call x1, Pallas kernels, local(): pl.pallas_call(functools.partial(data_grad_kernel, peers), out_shape=[jax...  1.7 us
    pallas_call x1, Pallas kernels, local(): pl.pallas_call(pair_kernel_grad_kernel, out_shape=jax.ShapeDtypeStruct((9...  1.43 us
    ppermute x5, starting transfers between devices, swap(): return lax.ppermute(array, 'space', [(0, 1), (1, 0)])  1.03 us
  transfers between devices with their start and end apart: 16, of which 8 were waited for; matrix products, arithmetic and copies ran while one was open for 0% of the time, Pallas kernels for 21%

profile of v17, /device:TPU:0, one launch (start us, length us, event | category | flops | bytes accessed | tf_op | source)
XLA Modules:
  0.0 40.2 jit_solution(762070565895656248)
XLA Ops:
  0.6 0.5 %collective-permute-start = (bf16[8,96,256]{2,1,0:T(8,128)(2,1)}, bf16[8,96,256]{2,1,0:T(8,128)(2,1)S(1)}, u32[]{:S(2)}, u32[]{:S(2)}) collective-permute-start(bf16[8,96,256]{2,1,0:T(8,128)(2,1)} %bitcast.16), channel_id=1, source_target_pairs={{0,1},{1,0},{2,3},{3,2},{4,5},{5,4},{6,7},{7,6},{8,9},{9,8},{10,11... | collective-permute-start | bytes 1179656 | tf_op jit(solution)/shard_map/ppermute | solution.py:19
  1.1 1.9 %shard_map.84 = (bf16[768,256]{1,0:T(8,128)(2,1)S(1)}, bf16[256,768]{1,0:T(8,128)(2,1)S(1)}, bf16[8,96,768]{2,1,0:T(8,128)(2,1)S(1)}, bf16[768,512]{1,0:T(8,128)(2,1)S(1)}, bf16[9,256,256]{2,1,0:T(8,128)(2,1)S(1)}) custom-call(bf16[8,96,256]{2,1,0:T(8,128)(2,1)} %bitcast.17, bf16[512,256]{1,0:T(8,128)(2,1)} %refs_1_.1, bf16[4,48,256]{2,1,0:T(8,128)(2,1)} %bitcast.18, ...), custom_call_target="tpu_custom_call" | custom-call | flops 805306368 | bytes 4194304 | tf_op jit(solution)/shard_map/pallas_call | solution.py:270
  3.1 0.1 collective-permute-start.1
  3.2 0.0 collective-permute-done.before.after.cot
  3.2 1.7 %shard_map.85 = (bf16[768,256]{1,0:T(8,128)(2,1)S(1)}, bf16[2,96,768]{2,1,0:T(8,128)(2,1)}, f32[512,128]{1,0:T(8,128)S(1)}, bf16[512,128]{1,0:T(8,128)(2,1)S(1)}) custom-call(bf16[8,96,768]{2,1,0:T(8,128)(2,1)S(1)} %get-tuple-element.24.stack, bf16[8,96,256]{2,1,0:T(8,128)(2,1)S(1)} %collective-permute-done.before.after.cot, ...), custom_call_target="tpu_custom_call" | custom-call | flops 1107296256 | bytes 4194304 | tf_op jit(solution)/shard_map/pallas_call | solution.py:291
  4.9 0.5 %collective-permute-start.2 = (bf16[512,128]{1,0:T(8,128)(2,1)S(1)}, bf16[512,128]{1,0:T(8,128)(2,1)S(1)}, u32[]{:S(2)}, u32[]{:S(2)}) collective-permute-start(bf16[512,128]{1,0:T(8,128)(2,1)S(1)} %get-tuple-element.31), channel_id=1, source_target_pairs={{0,1},{1,0},{2,3},{3,2},{4,5},{5,4},{6,7},{7,6},{8,9},{9,8},{10,11... | collective-permute-start | bytes 393224 | tf_op jit(solution)/shard_map/ppermute | solution.py:215
  5.4 1.4 %shard_map.87.kernel_sums = f32[2304,128]{1,0:T(8,128)S(1)} custom-call(bf16[8,96,768]{2,1,0:T(8,128)(2,1)S(1)} %get-tuple-element.24.stack, bf16[256,768]{1,0:T(8,128)(2,1)S(1)} %get-tuple-element.29.merged_t, bf16[8,96,256]{2,1,0:T(8,128)(2,1)S(1)} %collective-permute-done.before.after.cot, bf16[768,256]{1,0:T(8,128)(2,1)S(1)} %bitcast.9), custom_call_target="tpu_custom_call" | custom-call | flops 905969664 | bytes 4194304 | tf_op jit(solution)/shard_map/pallas_call | solution.py:308
  6.9 0.0 collective-permute-done.2.got
  6.9 0.1 shard_map.88
  7.0 3.5 %collective-permute-start.3 = (bf16[704,128]{1,0:T(8,128)(2,1)S(1)}, bf16[704,128]{1,0:T(8,128)(2,1)S(1)}, u32[]{:S(2)}, u32[]{:S(2)}) collective-permute-start(bf16[704,128]{1,0:T(8,128)(2,1)S(1)} %get-tuple-element.33), channel_id=1, source_target_pairs={{0,6},{1,25},{2,4},{3,27},{4,2},{5,29},{6,0},{7,31},{8,14},{9,17},... | collective-permute-start | bytes 540680 | tf_op jit(solution)/shard_map/ppermute | solution.py:211
  10.5 0.5 %collective-permute-start.4 = (bf16[704,128]{1,0:T(8,128)(2,1)S(1)}, bf16[704,128]{1,0:T(8,128)(2,1)S(1)}, u32[]{:S(2)}, u32[]{:S(2)}) collective-permute-start(bf16[704,128]{1,0:T(8,128)(2,1)S(1)} %get-tuple-element.34), channel_id=1, source_target_pairs={{0,4},{1,17},{2,6},{3,19},{4,0},{5,21},{6,2},{7,23},{8,12},{9,25},... | collective-permute-start | bytes 540680 | tf_op jit(solution)/shard_map/ppermute | solution.py:211
  11.0 0.1 collective-permute-start.5
  11.2 2.8 %collective-permute-done.3.three = bf16[704,128]{1,0:T(8,128)(2,1)S(1)} collective-permute-done((bf16[704,128]{1,0:T(8,128)(2,1)S(1)}, bf16[704,128]{1,0:T(8,128)(2,1)S(1)}, u32[]{:S(2)}, u32[]{:S(2)}) %collective-permute-start.3) | collective-permute-done | bytes 180256 | tf_op jit(solution)/shard_map/ppermute | solution.py:211
  14.0 2.0 %collective-permute-done.4.two = bf16[704,128]{1,0:T(8,128)(2,1)S(1)} collective-permute-done((bf16[704,128]{1,0:T(8,128)(2,1)S(1)}, bf16[704,128]{1,0:T(8,128)(2,1)S(1)}, u32[]{:S(2)}, u32[]{:S(2)}) %collective-permute-start.4) | collective-permute-done | bytes 180256 | tf_op jit(solution)/shard_map/ppermute | solution.py:211
  16.0 0.5 %collective-permute-done.5.one = bf16[704,128]{1,0:T(8,128)(2,1)S(1)} collective-permute-done((bf16[704,128]{1,0:T(8,128)(2,1)S(1)}, bf16[704,128]{1,0:T(8,128)(2,1)S(1)}, u32[]{:S(2)}, u32[]{:S(2)}) %collective-permute-start.5) | collective-permute-done | bytes 180256 | tf_op jit(solution)/shard_map/ppermute | solution.py:211
  16.5 0.1 shard_map.89.own
  16.6 3.7 %collective-permute-start.6 = (bf16[704,128]{1,0:T(8,128)(2,1)S(1)}, bf16[704,128]{1,0:T(8,128)(2,1)S(1)}, u32[]{:S(2)}, u32[]{:S(2)}) collective-permute-start(bf16[704,128]{1,0:T(8,128)(2,1)S(1)} %shard_map.89.own), channel_id=1, source_target_pairs={{0,24},{1,7},{2,26},{3,5},{4,28},{5,3},{6,30},{7,1},{8,16},{9,15},... | collective-permute-start | bytes 540680 | tf_op jit(solution)/shard_map/ppermute | solution.py:211
  20.3 0.8 %collective-permute-start.8 = (bf16[704,128]{1,0:T(8,128)(2,1)S(1)}, bf16[704,128]{1,0:T(8,128)(2,1)S(1)}, u32[]{:S(2)}, u32[]{:S(2)}) collective-permute-start(bf16[704,128]{1,0:T(8,128)(2,1)S(1)} %shard_map.89.own), channel_id=1, source_target_pairs={{0,8},{1,3},{2,10},{3,1},{4,12},{5,7},{6,14},{7,5},{8,0},{9,11},{1... | collective-permute-start | bytes 540680 | tf_op jit(solution)/shard_map/ppermute | solution.py:211
  21.1 2.5 %shard_map.86 = (bf16[8,96,256]{2,1,0:T(8,128)(2,1)}, bf16[4,48,256]{2,1,0:T(8,128)(2,1)}) custom-call(bf16[8,96,256]{2,1,0:T(8,128)(2,1)S(1)} %bitcast.11, bf16[9,256,256]{2,1,0:T(8,128)(2,1)S(1)} %get-tuple-element.23.out_w, bf16[768,256]{1,0:T(8,128)(2,1)S(1)} %get-tuple-element.26.grad, bf16[8,96,256]{2,1,0:T(8,128)(2,1)S(1)} %collective-permute-done.1.refs_0_.refs_1_, ...), custom_call_target="tpu_custom_call" | custom-call | flops 905969664 | bytes 2097152 | tf_op jit(solution)/shard_map/pallas_call | solution.py:322
  23.6 0.5 %collective-permute-done.6.three = bf16[704,128]{1,0:T(8,128)(2,1)S(1)} collective-permute-done((bf16[704,128]{1,0:T(8,128)(2,1)S(1)}, bf16[704,128]{1,0:T(8,128)(2,1)S(1)}, u32[]{:S(2)}, u32[]{:S(2)}) %collective-permute-start.6) | collective-permute-done | bytes 180256 | tf_op jit(solution)/shard_map/ppermute | solution.py:211
  24.1 4.9 %collective-permute-done.7.two = bf16[704,128]{1,0:T(8,128)(2,1)S(1)} collective-permute-done((bf16[704,128]{1,0:T(8,128)(2,1)S(1)}, bf16[704,128]{1,0:T(8,128)(2,1)S(1)}, u32[]{:S(2)}, u32[]{:S(2)}) %collective-permute-start.7) | collective-permute-done | bytes 180256 | tf_op jit(solution)/shard_map/ppermute | solution.py:211
  29.0 0.1 shard_map.90.refs_0_
  29.1 2.0 %collective-permute-start.9 = (bf16[704,128]{1,0:T(8,128)(2,1)S(1)}, bf16[704,128]{1,0:T(8,128)(2,1)S(1)}, u32[]{:S(2)}, u32[]{:S(2)}) collective-permute-start(bf16[704,128]{1,0:T(8,128)(2,1)S(1)} %shard_map.90.refs_0_), channel_id=1, source_target_pairs={{0,6},{1,25},{2,4},{3,27},{4,2},{5,29},{6,0},{7,31},{8,14},{9,17},... | collective-permute-start | bytes 540680 | tf_op jit(solution)/shard_map/ppermute | solution.py:211
  31.1 1.0 %collective-permute-start.11 = (bf16[704,128]{1,0:T(8,128)(2,1)S(1)}, bf16[704,128]{1,0:T(8,128)(2,1)S(1)}, u32[]{:S(2)}, u32[]{:S(2)}) collective-permute-start(bf16[704,128]{1,0:T(8,128)(2,1)S(1)} %shard_map.90.refs_0_), channel_id=1, source_target_pairs={{0,4},{1,17},{2,6},{3,19},{4,0},{5,21},{6,2},{7,23},{8,12},{9,25},... | collective-permute-start | bytes 540680 | tf_op jit(solution)/shard_map/ppermute | solution.py:211
  32.1 0.6 %collective-permute-start.13 = (bf16[704,128]{1,0:T(8,128)(2,1)S(1)}, bf16[704,128]{1,0:T(8,128)(2,1)S(1)}, u32[]{:S(2)}, u32[]{:S(2)}) collective-permute-start(bf16[704,128]{1,0:T(8,128)(2,1)S(1)} %shard_map.90.refs_0_), channel_id=1, source_target_pairs={{0,2},{1,9},{2,0},{3,11},{4,6},{5,13},{6,4},{7,15},{8,10},{9,1},{1... | collective-permute-start | bytes 540680 | tf_op jit(solution)/shard_map/ppermute | solution.py:211
  32.6 3.0 %collective-permute-done.9.refs_1_ = bf16[704,128]{1,0:T(8,128)(2,1)S(1)} collective-permute-done((bf16[704,128]{1,0:T(8,128)(2,1)S(1)}, bf16[704,128]{1,0:T(8,128)(2,1)S(1)}, u32[]{:S(2)}, u32[]{:S(2)}) %collective-permute-start.9) | collective-permute-done | bytes 180256 | tf_op jit(solution)/shard_map/ppermute | solution.py:211
  35.6 1.8 %collective-permute-done.11.refs_2_ = bf16[704,128]{1,0:T(8,128)(2,1)S(1)} collective-permute-done((bf16[704,128]{1,0:T(8,128)(2,1)S(1)}, bf16[704,128]{1,0:T(8,128)(2,1)S(1)}, u32[]{:S(2)}, u32[]{:S(2)}) %collective-permute-start.11) | collective-permute-done | bytes 180256 | tf_op jit(solution)/shard_map/ppermute | solution.py:211
  37.5 0.4 %collective-permute-start.12 = (bf16[704,128]{1,0:T(8,128)(2,1)S(1)}, bf16[704,128]{1,0:T(8,128)(2,1)S(1)}, u32[]{:S(2)}, u32[]{:S(2)}) collective-permute-start(bf16[704,128]{1,0:T(8,128)(2,1)S(1)} %collective-permute-done.11.refs_2_), channel_id=1, source_target_pairs={{0,1},{1,0},{2,3},{3,2},{4,5},{5,4},{6,7},{7,6},{8,9},{9,8},{10,11... | collective-permute-start | bytes 540680 | tf_op jit(solution)/shard_map/ppermute | solution.py:215
  37.9 0.1 collective-permute-start.14
  38.0 1.0 %shard_map.91 = (bf16[2304,256]{1,0:T(8,128)(2,1)}, bf16[512,256]{1,0:T(8,128)(2,1)}) custom-call(bf16[704,128]{1,0:T(8,128)(2,1)S(1)} %shard_map.90.refs_0_, bf16[704,128]{1,0:T(8,128)(2,1)S(1)} %collective-permute-done.9.refs_1_, bf16[704,128]{1,0:T(8,128)(2,1)S(1)} %collective-permute-done.11.refs_2_, ...), custom_call_target="tpu_custom_call" | custom-call | tf_op jit(solution)/shard_map/pallas_call | solution.py:244
  39.0 0.3 collective-permute-done.14.refs_2_
  39.3 0.9 %shard_map.92 = (bf16[2304,256]{1,0:T(8,128)(2,1)}, bf16[512,256]{1,0:T(8,128)(2,1)}) custom-call(bf16[704,128]{1,0:T(8,128)(2,1)S(1)} %collective-permute-done.10.refs_0_, bf16[704,128]{1,0:T(8,128)(2,1)S(1)} %collective-permute-done.12.refs_1_, bf16[704,128]{1,0:T(8,128)(2,1)S(1)} %collective-permute-done.14.refs_2_, ...), custom_call_target="tpu_custom_call", output_to_operand_aliasing={{0}: (3, {}), {1}: (4, {})} | custom-call | tf_op jit(solution)/shard_map/pallas_call | solution.py:247
  (9 shorter events, 0.0 us)
Async XLA Ops:
  0.6 2.6 %collective-permute-start = (bf16[8,96,256]{2,1,0:T(8,128)(2,1)}, bf16[8,96,256]{2,1,0:T(8,128)(2,1)S(1)}, u32[]{:S(2)}, u32[]{:S(2)}) collective-permute-start(bf16[8,96,256]{2,1,0:T(8,128)(2,1)} %bitcast.16), channel_id=1, source_target_pairs={{0,1},{1,0},{2,3},{3,2},{4,5},{5,4},{6,7},{7,6},{8,9},{9,8},{10,11... | collective-permute-start | bytes 1179656 | tf_op jit(solution)/shard_map/ppermute | solution.py:19
  3.1 2.4 %collective-permute-start.1 = (bf16[8,96,256]{2,1,0:T(8,128)(2,1)S(1)}, bf16[8,96,256]{2,1,0:T(8,128)(2,1)S(1)}, u32[]{:S(2)}, u32[]{:S(2)}) collective-permute-start(bf16[8,96,256]{2,1,0:T(8,128)(2,1)S(1)} %bitcast.10), channel_id=1, source_target_pairs={{0,1},{1,0},{2,3},{3,2},{4,5},{5,4},{6,7},{7,6},{8,9},{9,8},{10,11... | collective-permute-start | bytes 1179656 | tf_op jit(solution)/shard_map/ppermute | solution.py:19
  4.9 2.0 %collective-permute-start.2 = (bf16[512,128]{1,0:T(8,128)(2,1)S(1)}, bf16[512,128]{1,0:T(8,128)(2,1)S(1)}, u32[]{:S(2)}, u32[]{:S(2)}) collective-permute-start(bf16[512,128]{1,0:T(8,128)(2,1)S(1)} %get-tuple-element.31), channel_id=1, source_target_pairs={{0,1},{1,0},{2,3},{3,2},{4,5},{5,4},{6,7},{7,6},{8,9},{9,8},{10,11... | collective-permute-start | bytes 393224 | tf_op jit(solution)/shard_map/ppermute | solution.py:215
  7.0 7.0 %collective-permute-start.3 = (bf16[704,128]{1,0:T(8,128)(2,1)S(1)}, bf16[704,128]{1,0:T(8,128)(2,1)S(1)}, u32[]{:S(2)}, u32[]{:S(2)}) collective-permute-start(bf16[704,128]{1,0:T(8,128)(2,1)S(1)} %get-tuple-element.33), channel_id=1, source_target_pairs={{0,6},{1,25},{2,4},{3,27},{4,2},{5,29},{6,0},{7,31},{8,14},{9,17},... | collective-permute-start | bytes 540680 | tf_op jit(solution)/shard_map/ppermute | solution.py:211
  10.5 5.5 %collective-permute-start.4 = (bf16[704,128]{1,0:T(8,128)(2,1)S(1)}, bf16[704,128]{1,0:T(8,128)(2,1)S(1)}, u32[]{:S(2)}, u32[]{:S(2)}) collective-permute-start(bf16[704,128]{1,0:T(8,128)(2,1)S(1)} %get-tuple-element.34), channel_id=1, source_target_pairs={{0,4},{1,17},{2,6},{3,19},{4,0},{5,21},{6,2},{7,23},{8,12},{9,25},... | collective-permute-start | bytes 540680 | tf_op jit(solution)/shard_map/ppermute | solution.py:211
  11.0 5.5 %collective-permute-start.5 = (bf16[704,128]{1,0:T(8,128)(2,1)S(1)}, bf16[704,128]{1,0:T(8,128)(2,1)S(1)}, u32[]{:S(2)}, u32[]{:S(2)}) collective-permute-start(bf16[704,128]{1,0:T(8,128)(2,1)S(1)} %get-tuple-element.35), channel_id=1, source_target_pairs={{0,2},{1,9},{2,0},{3,11},{4,6},{5,13},{6,4},{7,15},{8,10},{9,1},{1... | collective-permute-start | bytes 540680 | tf_op jit(solution)/shard_map/ppermute | solution.py:211
  16.6 7.5 %collective-permute-start.6 = (bf16[704,128]{1,0:T(8,128)(2,1)S(1)}, bf16[704,128]{1,0:T(8,128)(2,1)S(1)}, u32[]{:S(2)}, u32[]{:S(2)}) collective-permute-start(bf16[704,128]{1,0:T(8,128)(2,1)S(1)} %shard_map.89.own), channel_id=1, source_target_pairs={{0,24},{1,7},{2,26},{3,5},{4,28},{5,3},{6,30},{7,1},{8,16},{9,15},... | collective-permute-start | bytes 540680 | tf_op jit(solution)/shard_map/ppermute | solution.py:211
  20.3 8.7 %collective-permute-start.7 = (bf16[704,128]{1,0:T(8,128)(2,1)S(1)}, bf16[704,128]{1,0:T(8,128)(2,1)S(1)}, u32[]{:S(2)}, u32[]{:S(2)}) collective-permute-start(bf16[704,128]{1,0:T(8,128)(2,1)S(1)} %shard_map.89.own), channel_id=1, source_target_pairs={{0,16},{1,5},{2,18},{3,7},{4,20},{5,1},{6,22},{7,3},{8,24},{9,13},... | collective-permute-start | bytes 540680 | tf_op jit(solution)/shard_map/ppermute | solution.py:211
  20.3 8.7 %collective-permute-start.8 = (bf16[704,128]{1,0:T(8,128)(2,1)S(1)}, bf16[704,128]{1,0:T(8,128)(2,1)S(1)}, u32[]{:S(2)}, u32[]{:S(2)}) collective-permute-start(bf16[704,128]{1,0:T(8,128)(2,1)S(1)} %shard_map.89.own), channel_id=1, source_target_pairs={{0,8},{1,3},{2,10},{3,1},{4,12},{5,7},{6,14},{7,5},{8,0},{9,11},{1... | collective-permute-start | bytes 540680 | tf_op jit(solution)/shard_map/ppermute | solution.py:211
  29.1 6.6 %collective-permute-start.9 = (bf16[704,128]{1,0:T(8,128)(2,1)S(1)}, bf16[704,128]{1,0:T(8,128)(2,1)S(1)}, u32[]{:S(2)}, u32[]{:S(2)}) collective-permute-start(bf16[704,128]{1,0:T(8,128)(2,1)S(1)} %shard_map.90.refs_0_), channel_id=1, source_target_pairs={{0,6},{1,25},{2,4},{3,27},{4,2},{5,29},{6,0},{7,31},{8,14},{9,17},... | collective-permute-start | bytes 540680 | tf_op jit(solution)/shard_map/ppermute | solution.py:211
  31.1 6.4 %collective-permute-start.11 = (bf16[704,128]{1,0:T(8,128)(2,1)S(1)}, bf16[704,128]{1,0:T(8,128)(2,1)S(1)}, u32[]{:S(2)}, u32[]{:S(2)}) collective-permute-start(bf16[704,128]{1,0:T(8,128)(2,1)S(1)} %shard_map.90.refs_0_), channel_id=1, source_target_pairs={{0,4},{1,17},{2,6},{3,19},{4,0},{5,21},{6,2},{7,23},{8,12},{9,25},... | collective-permute-start | bytes 540680 | tf_op jit(solution)/shard_map/ppermute | solution.py:211
  32.1 5.8 %collective-permute-start.13 = (bf16[704,128]{1,0:T(8,128)(2,1)S(1)}, bf16[704,128]{1,0:T(8,128)(2,1)S(1)}, u32[]{:S(2)}, u32[]{:S(2)}) collective-permute-start(bf16[704,128]{1,0:T(8,128)(2,1)S(1)} %shard_map.90.refs_0_), channel_id=1, source_target_pairs={{0,2},{1,9},{2,0},{3,11},{4,6},{5,13},{6,4},{7,15},{8,10},{9,1},{1... | collective-permute-start | bytes 540680 | tf_op jit(solution)/shard_map/ppermute | solution.py:211
  32.6 5.4 %collective-permute-start.15 = (bf16[704,128]{1,0:T(8,128)(2,1)S(1)}, bf16[704,128]{1,0:T(8,128)(2,1)S(1)}, u32[]{:S(2)}, u32[]{:S(2)}) collective-permute-start(bf16[704,128]{1,0:T(8,128)(2,1)S(1)} %shard_map.90.refs_0_), channel_id=1, source_target_pairs={{0,1},{1,0},{2,3},{3,2},{4,5},{5,4},{6,7},{7,6},{8,9},{9,8},{10,11... | collective-permute-start | bytes 540680 | tf_op jit(solution)/shard_map/ppermute | solution.py:215
  35.6 3.3 %collective-permute-start.10 = (bf16[704,128]{1,0:T(8,128)(2,1)S(1)}, bf16[704,128]{1,0:T(8,128)(2,1)S(1)}, u32[]{:S(2)}, u32[]{:S(2)}) collective-permute-start(bf16[704,128]{1,0:T(8,128)(2,1)S(1)} %collective-permute-done.9.refs_1_), channel_id=1, source_target_pairs={{0,1},{1,0},{2,3},{3,2},{4,5},{5,4},{6,7},{7,6},{8,9},{9,8},{10,11... | collective-permute-start | bytes 540680 | tf_op jit(solution)/shard_map/ppermute | solution.py:215
  37.5 1.5 %collective-permute-start.12 = (bf16[704,128]{1,0:T(8,128)(2,1)S(1)}, bf16[704,128]{1,0:T(8,128)(2,1)S(1)}, u32[]{:S(2)}, u32[]{:S(2)}) collective-permute-start(bf16[704,128]{1,0:T(8,128)(2,1)S(1)} %collective-permute-done.11.refs_2_), channel_id=1, source_target_pairs={{0,1},{1,0},{2,3},{3,2},{4,5},{5,4},{6,7},{7,6},{8,9},{9,8},{10,11... | collective-permute-start | bytes 540680 | tf_op jit(solution)/shard_map/ppermute | solution.py:215
  37.9 1.4 %collective-permute-start.14 = (bf16[704,128]{1,0:T(8,128)(2,1)S(1)}, bf16[704,128]{1,0:T(8,128)(2,1)S(1)}, u32[]{:S(2)}, u32[]{:S(2)}) collective-permute-start(bf16[704,128]{1,0:T(8,128)(2,1)S(1)} %collective-permute-done.13.refs_3_), channel_id=1, source_target_pairs={{0,1},{1,0},{2,3},{3,2},{4,5},{5,4},{6,7},{7,6},{8,9},{9,8},{10,11... | collective-permute-start | bytes 540680 | tf_op jit(solution)/shard_map/ppermute | solution.py:215

commit v18 on v17

--- a/solution.py
+++ b/solution.py
@@ -206,7 +206,7 @@
     pairs = []
     for chip in range(16):
         for core in range(2):
-            flip = k if core == step else 4 * k
+            flip = (k if step == 0 else 4 - k) if core == step else 4 * k
             pairs.append((2 * chip + core, 2 * (chip ^ flip) + core))
     return lax.ppermute(array, ("dp", "space"), pairs)
 

time: 40.3 us -> 40.5 us (level)
  no operation moved by 1% of the time
where the time goes in v18:
time: 40.5 us; the launch traced here: 40.3 us
  waiting for transfers between devices  16 us (40%)
  starting transfers between devices  13.9 us (34%)
  Pallas kernels  9.74 us (24%)
  between operations  0.72 us (2%)
    ppermute x9, waiting for transfers between devices, exchange(): return lax.ppermute(array, ('dp', 'space'), pairs)  15.6 us
    ppermute x9, starting transfers between devices, exchange(): return lax.ppermute(array, ('dp', 'space'), pairs)  12.2 us
    pallas_call x1, Pallas kernels, local(): pl.pallas_call(functools.partial(forward_kernel, peers), out_shape=[jax.S...  2.53 us
    pallas_call x1, Pallas kernels, local(): pl.pallas_call(merge_kernel, out_shape=[jax.ShapeDtypeStruct(shape, BF16)...  1.91 us
    pallas_call x2, Pallas kernels, sum_everywhere(): call(functools.partial(place_kernel, plan), *results, **place)  1.88 us
    pallas_call x1, Pallas kernels, local(): pl.pallas_call(functools.partial(data_grad_kernel, peers), out_shape=[jax...  1.7 us
    pallas_call x1, Pallas kernels, local(): pl.pallas_call(pair_kernel_grad_kernel, out_shape=jax.ShapeDtypeStruct((9...  1.43 us
    ppermute x5, starting transfers between devices, swap(): return lax.ppermute(array, 'space', [(0, 1), (1, 0)])  1.1 us
  transfers between devices with their start and end apart: 16, of which 8 were waited for; matrix products, arithmetic and copies ran while one was open for 0% of the time, Pallas kernels for 21%

profile of v18, /device:TPU:0, one launch (start us, length us, event | category | flops | bytes accessed | tf_op | source)
XLA Modules:
  0.0 40.3 jit_solution(11219636973578689896)
XLA Ops:
  0.6 0.5 %collective-permute-start = (bf16[8,96,256]{2,1,0:T(8,128)(2,1)}, bf16[8,96,256]{2,1,0:T(8,128)(2,1)S(1)}, u32[]{:S(2)}, u32[]{:S(2)}) collective-permute-start(bf16[8,96,256]{2,1,0:T(8,128)(2,1)} %bitcast.16), channel_id=1, source_target_pairs={{0,1},{1,0},{2,3},{3,2},{4,5},{5,4},{6,7},{7,6},{8,9},{9,8},{10,11... | collective-permute-start | bytes 1179656 | tf_op jit(solution)/shard_map/ppermute | solution.py:19
  1.1 1.9 %shard_map.84 = (bf16[768,256]{1,0:T(8,128)(2,1)S(1)}, bf16[256,768]{1,0:T(8,128)(2,1)S(1)}, bf16[8,96,768]{2,1,0:T(8,128)(2,1)S(1)}, bf16[768,512]{1,0:T(8,128)(2,1)S(1)}, bf16[9,256,256]{2,1,0:T(8,128)(2,1)S(1)}) custom-call(bf16[8,96,256]{2,1,0:T(8,128)(2,1)} %bitcast.17, bf16[512,256]{1,0:T(8,128)(2,1)} %refs_1_.1, bf16[4,48,256]{2,1,0:T(8,128)(2,1)} %bitcast.18, ...), custom_call_target="tpu_custom_call" | custom-call | flops 805306368 | bytes 4194304 | tf_op jit(solution)/shard_map/pallas_call | solution.py:270
  3.1 0.1 collective-permute-start.1
  3.2 0.0 collective-permute-done.before.after.cot
  3.2 1.7 %shard_map.85 = (bf16[768,256]{1,0:T(8,128)(2,1)S(1)}, bf16[2,96,768]{2,1,0:T(8,128)(2,1)}, f32[512,128]{1,0:T(8,128)S(1)}, bf16[512,128]{1,0:T(8,128)(2,1)S(1)}) custom-call(bf16[8,96,768]{2,1,0:T(8,128)(2,1)S(1)} %get-tuple-element.24.stack, bf16[8,96,256]{2,1,0:T(8,128)(2,1)S(1)} %collective-permute-done.before.after.cot, ...), custom_call_target="tpu_custom_call" | custom-call | flops 1107296256 | bytes 4194304 | tf_op jit(solution)/shard_map/pallas_call | solution.py:291
  4.9 0.5 %collective-permute-start.2 = (bf16[512,128]{1,0:T(8,128)(2,1)S(1)}, bf16[512,128]{1,0:T(8,128)(2,1)S(1)}, u32[]{:S(2)}, u32[]{:S(2)}) collective-permute-start(bf16[512,128]{1,0:T(8,128)(2,1)S(1)} %get-tuple-element.31), channel_id=1, source_target_pairs={{0,1},{1,0},{2,3},{3,2},{4,5},{5,4},{6,7},{7,6},{8,9},{9,8},{10,11... | collective-permute-start | bytes 393224 | tf_op jit(solution)/shard_map/ppermute | solution.py:215
  5.4 1.4 %shard_map.87.kernel_sums = f32[2304,128]{1,0:T(8,128)S(1)} custom-call(bf16[8,96,768]{2,1,0:T(8,128)(2,1)S(1)} %get-tuple-element.24.stack, bf16[256,768]{1,0:T(8,128)(2,1)S(1)} %get-tuple-element.29.merged_t, bf16[8,96,256]{2,1,0:T(8,128)(2,1)S(1)} %collective-permute-done.before.after.cot, bf16[768,256]{1,0:T(8,128)(2,1)S(1)} %bitcast.9), custom_call_target="tpu_custom_call" | custom-call | flops 905969664 | bytes 4194304 | tf_op jit(solution)/shard_map/pallas_call | solution.py:308
  6.9 0.1 shard_map.88
  7.0 3.5 %collective-permute-start.3 = (bf16[704,128]{1,0:T(8,128)(2,1)S(1)}, bf16[704,128]{1,0:T(8,128)(2,1)S(1)}, u32[]{:S(2)}, u32[]{:S(2)}) collective-permute-start(bf16[704,128]{1,0:T(8,128)(2,1)S(1)} %get-tuple-element.33), channel_id=1, source_target_pairs={{0,6},{1,25},{2,4},{3,27},{4,2},{5,29},{6,0},{7,31},{8,14},{9,17},... | collective-permute-start | bytes 540680 | tf_op jit(solution)/shard_map/ppermute | solution.py:211
  10.5 0.5 %collective-permute-start.4 = (bf16[704,128]{1,0:T(8,128)(2,1)S(1)}, bf16[704,128]{1,0:T(8,128)(2,1)S(1)}, u32[]{:S(2)}, u32[]{:S(2)}) collective-permute-start(bf16[704,128]{1,0:T(8,128)(2,1)S(1)} %get-tuple-element.34), channel_id=1, source_target_pairs={{0,4},{1,17},{2,6},{3,19},{4,0},{5,21},{6,2},{7,23},{8,12},{9,25},... | collective-permute-start | bytes 540680 | tf_op jit(solution)/shard_map/ppermute | solution.py:211
  11.0 0.1 collective-permute-start.5
  11.2 2.8 %collective-permute-done.3.three = bf16[704,128]{1,0:T(8,128)(2,1)S(1)} collective-permute-done((bf16[704,128]{1,0:T(8,128)(2,1)S(1)}, bf16[704,128]{1,0:T(8,128)(2,1)S(1)}, u32[]{:S(2)}, u32[]{:S(2)}) %collective-permute-start.3) | collective-permute-done | bytes 180256 | tf_op jit(solution)/shard_map/ppermute | solution.py:211
  14.0 2.0 %collective-permute-done.4.two = bf16[704,128]{1,0:T(8,128)(2,1)S(1)} collective-permute-done((bf16[704,128]{1,0:T(8,128)(2,1)S(1)}, bf16[704,128]{1,0:T(8,128)(2,1)S(1)}, u32[]{:S(2)}, u32[]{:S(2)}) %collective-permute-start.4) | collective-permute-done | bytes 180256 | tf_op jit(solution)/shard_map/ppermute | solution.py:211
  16.0 0.5 %collective-permute-done.5.one = bf16[704,128]{1,0:T(8,128)(2,1)S(1)} collective-permute-done((bf16[704,128]{1,0:T(8,128)(2,1)S(1)}, bf16[704,128]{1,0:T(8,128)(2,1)S(1)}, u32[]{:S(2)}, u32[]{:S(2)}) %collective-permute-start.5) | collective-permute-done | bytes 180256 | tf_op jit(solution)/shard_map/ppermute | solution.py:211
  16.5 0.1 shard_map.89.own
  16.6 3.7 %collective-permute-start.6 = (bf16[704,128]{1,0:T(8,128)(2,1)S(1)}, bf16[704,128]{1,0:T(8,128)(2,1)S(1)}, u32[]{:S(2)}, u32[]{:S(2)}) collective-permute-start(bf16[704,128]{1,0:T(8,128)(2,1)S(1)} %shard_map.89.own), channel_id=1, source_target_pairs={{0,24},{1,3},{2,26},{3,1},{4,28},{5,7},{6,30},{7,5},{8,16},{9,11},... | collective-permute-start | bytes 540680 | tf_op jit(solution)/shard_map/ppermute | solution.py:211
  20.3 0.8 %collective-permute-start.8 = (bf16[704,128]{1,0:T(8,128)(2,1)S(1)}, bf16[704,128]{1,0:T(8,128)(2,1)S(1)}, u32[]{:S(2)}, u32[]{:S(2)}) collective-permute-start(bf16[704,128]{1,0:T(8,128)(2,1)S(1)} %shard_map.89.own), channel_id=1, source_target_pairs={{0,8},{1,7},{2,10},{3,5},{4,12},{5,3},{6,14},{7,1},{8,0},{9,15},{1... | collective-permute-start | bytes 540680 | tf_op jit(solution)/shard_map/ppermute | solution.py:211
  21.1 2.5 %shard_map.86 = (bf16[8,96,256]{2,1,0:T(8,128)(2,1)}, bf16[4,48,256]{2,1,0:T(8,128)(2,1)}) custom-call(bf16[8,96,256]{2,1,0:T(8,128)(2,1)S(1)} %bitcast.11, bf16[9,256,256]{2,1,0:T(8,128)(2,1)S(1)} %get-tuple-element.23.out_w, bf16[768,256]{1,0:T(8,128)(2,1)S(1)} %get-tuple-element.26.grad, bf16[8,96,256]{2,1,0:T(8,128)(2,1)S(1)} %collective-permute-done.1.refs_0_.refs_1_, ...), custom_call_target="tpu_custom_call" | custom-call | flops 905969664 | bytes 2097152 | tf_op jit(solution)/shard_map/pallas_call | solution.py:322
  23.6 0.5 %collective-permute-done.6.three = bf16[704,128]{1,0:T(8,128)(2,1)S(1)} collective-permute-done((bf16[704,128]{1,0:T(8,128)(2,1)S(1)}, bf16[704,128]{1,0:T(8,128)(2,1)S(1)}, u32[]{:S(2)}, u32[]{:S(2)}) %collective-permute-start.6) | collective-permute-done | bytes 180256 | tf_op jit(solution)/shard_map/ppermute | solution.py:211
  24.1 4.9 %collective-permute-done.7.two = bf16[704,128]{1,0:T(8,128)(2,1)S(1)} collective-permute-done((bf16[704,128]{1,0:T(8,128)(2,1)S(1)}, bf16[704,128]{1,0:T(8,128)(2,1)S(1)}, u32[]{:S(2)}, u32[]{:S(2)}) %collective-permute-start.7) | collective-permute-done | bytes 180256 | tf_op jit(solution)/shard_map/ppermute | solution.py:211
  29.0 0.1 shard_map.90.refs_0_
  29.1 2.0 %collective-permute-start.9 = (bf16[704,128]{1,0:T(8,128)(2,1)S(1)}, bf16[704,128]{1,0:T(8,128)(2,1)S(1)}, u32[]{:S(2)}, u32[]{:S(2)}) collective-permute-start(bf16[704,128]{1,0:T(8,128)(2,1)S(1)} %shard_map.90.refs_0_), channel_id=1, source_target_pairs={{0,6},{1,25},{2,4},{3,27},{4,2},{5,29},{6,0},{7,31},{8,14},{9,17},... | collective-permute-start | bytes 540680 | tf_op jit(solution)/shard_map/ppermute | solution.py:211
  31.1 1.0 %collective-permute-start.11 = (bf16[704,128]{1,0:T(8,128)(2,1)S(1)}, bf16[704,128]{1,0:T(8,128)(2,1)S(1)}, u32[]{:S(2)}, u32[]{:S(2)}) collective-permute-start(bf16[704,128]{1,0:T(8,128)(2,1)S(1)} %shard_map.90.refs_0_), channel_id=1, source_target_pairs={{0,4},{1,17},{2,6},{3,19},{4,0},{5,21},{6,2},{7,23},{8,12},{9,25},... | collective-permute-start | bytes 540680 | tf_op jit(solution)/shard_map/ppermute | solution.py:211
  32.1 0.6 %collective-permute-start.13 = (bf16[704,128]{1,0:T(8,128)(2,1)S(1)}, bf16[704,128]{1,0:T(8,128)(2,1)S(1)}, u32[]{:S(2)}, u32[]{:S(2)}) collective-permute-start(bf16[704,128]{1,0:T(8,128)(2,1)S(1)} %shard_map.90.refs_0_), channel_id=1, source_target_pairs={{0,2},{1,9},{2,0},{3,11},{4,6},{5,13},{6,4},{7,15},{8,10},{9,1},{1... | collective-permute-start | bytes 540680 | tf_op jit(solution)/shard_map/ppermute | solution.py:211
  32.6 3.0 %collective-permute-done.9.refs_1_ = bf16[704,128]{1,0:T(8,128)(2,1)S(1)} collective-permute-done((bf16[704,128]{1,0:T(8,128)(2,1)S(1)}, bf16[704,128]{1,0:T(8,128)(2,1)S(1)}, u32[]{:S(2)}, u32[]{:S(2)}) %collective-permute-start.9) | collective-permute-done | bytes 180256 | tf_op jit(solution)/shard_map/ppermute | solution.py:211
  35.6 1.8 %collective-permute-done.11.refs_2_ = bf16[704,128]{1,0:T(8,128)(2,1)S(1)} collective-permute-done((bf16[704,128]{1,0:T(8,128)(2,1)S(1)}, bf16[704,128]{1,0:T(8,128)(2,1)S(1)}, u32[]{:S(2)}, u32[]{:S(2)}) %collective-permute-start.11) | collective-permute-done | bytes 180256 | tf_op jit(solution)/shard_map/ppermute | solution.py:211
  37.5 0.6 %collective-permute-start.12 = (bf16[704,128]{1,0:T(8,128)(2,1)S(1)}, bf16[704,128]{1,0:T(8,128)(2,1)S(1)}, u32[]{:S(2)}, u32[]{:S(2)}) collective-permute-start(bf16[704,128]{1,0:T(8,128)(2,1)S(1)} %collective-permute-done.11.refs_2_), channel_id=1, source_target_pairs={{0,1},{1,0},{2,3},{3,2},{4,5},{5,4},{6,7},{7,6},{8,9},{9,8},{10,11... | collective-permute-start | bytes 540680 | tf_op jit(solution)/shard_map/ppermute | solution.py:215
  38.0 0.0 collective-permute-start.14
  38.1 1.0 %shard_map.91 = (bf16[2304,256]{1,0:T(8,128)(2,1)}, bf16[512,256]{1,0:T(8,128)(2,1)}) custom-call(bf16[704,128]{1,0:T(8,128)(2,1)S(1)} %shard_map.90.refs_0_, bf16[704,128]{1,0:T(8,128)(2,1)S(1)} %collective-permute-done.9.refs_1_, bf16[704,128]{1,0:T(8,128)(2,1)S(1)} %collective-permute-done.11.refs_2_, ...), custom_call_target="tpu_custom_call" | custom-call | tf_op jit(solution)/shard_map/pallas_call | solution.py:244
  39.1 0.0 collective-permute-done.12.refs_1_
  39.1 0.4 collective-permute-done.14.refs_2_
  39.5 0.9 %shard_map.92 = (bf16[2304,256]{1,0:T(8,128)(2,1)}, bf16[512,256]{1,0:T(8,128)(2,1)}) custom-call(bf16[704,128]{1,0:T(8,128)(2,1)S(1)} %collective-permute-done.10.refs_0_, bf16[704,128]{1,0:T(8,128)(2,1)S(1)} %collective-permute-done.12.refs_1_, bf16[704,128]{1,0:T(8,128)(2,1)S(1)} %collective-permute-done.14.refs_2_, ...), custom_call_target="tpu_custom_call", output_to_operand_aliasing={{0}: (3, {}), {1}: (4, {})} | custom-call | tf_op jit(solution)/shard_map/pallas_call | solution.py:247
  (9 shorter events, 0.0 us)
Async XLA Ops:
  0.6 2.6 %collective-permute-start = (bf16[8,96,256]{2,1,0:T(8,128)(2,1)}, bf16[8,96,256]{2,1,0:T(8,128)(2,1)S(1)}, u32[]{:S(2)}, u32[]{:S(2)}) collective-permute-start(bf16[8,96,256]{2,1,0:T(8,128)(2,1)} %bitcast.16), channel_id=1, source_target_pairs={{0,1},{1,0},{2,3},{3,2},{4,5},{5,4},{6,7},{7,6},{8,9},{9,8},{10,11... | collective-permute-start | bytes 1179656 | tf_op jit(solution)/shard_map/ppermute | solution.py:19
  3.1 2.4 %collective-permute-start.1 = (bf16[8,96,256]{2,1,0:T(8,128)(2,1)S(1)}, bf16[8,96,256]{2,1,0:T(8,128)(2,1)S(1)}, u32[]{:S(2)}, u32[]{:S(2)}) collective-permute-start(bf16[8,96,256]{2,1,0:T(8,128)(2,1)S(1)} %bitcast.10), channel_id=1, source_target_pairs={{0,1},{1,0},{2,3},{3,2},{4,5},{5,4},{6,7},{7,6},{8,9},{9,8},{10,11... | collective-permute-start | bytes 1179656 | tf_op jit(solution)/shard_map/ppermute | solution.py:19
  4.9 2.0 %collective-permute-start.2 = (bf16[512,128]{1,0:T(8,128)(2,1)S(1)}, bf16[512,128]{1,0:T(8,128)(2,1)S(1)}, u32[]{:S(2)}, u32[]{:S(2)}) collective-permute-start(bf16[512,128]{1,0:T(8,128)(2,1)S(1)} %get-tuple-element.31), channel_id=1, source_target_pairs={{0,1},{1,0},{2,3},{3,2},{4,5},{5,4},{6,7},{7,6},{8,9},{9,8},{10,11... | collective-permute-start | bytes 393224 | tf_op jit(solution)/shard_map/ppermute | solution.py:215
  7.0 7.0 %collective-permute-start.3 = (bf16[704,128]{1,0:T(8,128)(2,1)S(1)}, bf16[704,128]{1,0:T(8,128)(2,1)S(1)}, u32[]{:S(2)}, u32[]{:S(2)}) collective-permute-start(bf16[704,128]{1,0:T(8,128)(2,1)S(1)} %get-tuple-element.33), channel_id=1, source_target_pairs={{0,6},{1,25},{2,4},{3,27},{4,2},{5,29},{6,0},{7,31},{8,14},{9,17},... | collective-permute-start | bytes 540680 | tf_op jit(solution)/shard_map/ppermute | solution.py:211
  10.5 5.5 %collective-permute-start.4 = (bf16[704,128]{1,0:T(8,128)(2,1)S(1)}, bf16[704,128]{1,0:T(8,128)(2,1)S(1)}, u32[]{:S(2)}, u32[]{:S(2)}) collective-permute-start(bf16[704,128]{1,0:T(8,128)(2,1)S(1)} %get-tuple-element.34), channel_id=1, source_target_pairs={{0,4},{1,17},{2,6},{3,19},{4,0},{5,21},{6,2},{7,23},{8,12},{9,25},... | collective-permute-start | bytes 540680 | tf_op jit(solution)/shard_map/ppermute | solution.py:211
  11.0 5.5 %collective-permute-start.5 = (bf16[704,128]{1,0:T(8,128)(2,1)S(1)}, bf16[704,128]{1,0:T(8,128)(2,1)S(1)}, u32[]{:S(2)}, u32[]{:S(2)}) collective-permute-start(bf16[704,128]{1,0:T(8,128)(2,1)S(1)} %get-tuple-element.35), channel_id=1, source_target_pairs={{0,2},{1,9},{2,0},{3,11},{4,6},{5,13},{6,4},{7,15},{8,10},{9,1},{1... | collective-permute-start | bytes 540680 | tf_op jit(solution)/shard_map/ppermute | solution.py:211
  16.6 7.5 %collective-permute-start.6 = (bf16[704,128]{1,0:T(8,128)(2,1)S(1)}, bf16[704,128]{1,0:T(8,128)(2,1)S(1)}, u32[]{:S(2)}, u32[]{:S(2)}) collective-permute-start(bf16[704,128]{1,0:T(8,128)(2,1)S(1)} %shard_map.89.own), channel_id=1, source_target_pairs={{0,24},{1,3},{2,26},{3,1},{4,28},{5,7},{6,30},{7,5},{8,16},{9,11},... | collective-permute-start | bytes 540680 | tf_op jit(solution)/shard_map/ppermute | solution.py:211
  20.3 8.7 %collective-permute-start.7 = (bf16[704,128]{1,0:T(8,128)(2,1)S(1)}, bf16[704,128]{1,0:T(8,128)(2,1)S(1)}, u32[]{:S(2)}, u32[]{:S(2)}) collective-permute-start(bf16[704,128]{1,0:T(8,128)(2,1)S(1)} %shard_map.89.own), channel_id=1, source_target_pairs={{0,16},{1,5},{2,18},{3,7},{4,20},{5,1},{6,22},{7,3},{8,24},{9,13},... | collective-permute-start | bytes 540680 | tf_op jit(solution)/shard_map/ppermute | solution.py:211
  20.3 8.7 %collective-permute-start.8 = (bf16[704,128]{1,0:T(8,128)(2,1)S(1)}, bf16[704,128]{1,0:T(8,128)(2,1)S(1)}, u32[]{:S(2)}, u32[]{:S(2)}) collective-permute-start(bf16[704,128]{1,0:T(8,128)(2,1)S(1)} %shard_map.89.own), channel_id=1, source_target_pairs={{0,8},{1,7},{2,10},{3,5},{4,12},{5,3},{6,14},{7,1},{8,0},{9,15},{1... | collective-permute-start | bytes 540680 | tf_op jit(solution)/shard_map/ppermute | solution.py:211
  29.1 6.6 %collective-permute-start.9 = (bf16[704,128]{1,0:T(8,128)(2,1)S(1)}, bf16[704,128]{1,0:T(8,128)(2,1)S(1)}, u32[]{:S(2)}, u32[]{:S(2)}) collective-permute-start(bf16[704,128]{1,0:T(8,128)(2,1)S(1)} %shard_map.90.refs_0_), channel_id=1, source_target_pairs={{0,6},{1,25},{2,4},{3,27},{4,2},{5,29},{6,0},{7,31},{8,14},{9,17},... | collective-permute-start | bytes 540680 | tf_op jit(solution)/shard_map/ppermute | solution.py:211
  31.1 6.4 %collective-permute-start.11 = (bf16[704,128]{1,0:T(8,128)(2,1)S(1)}, bf16[704,128]{1,0:T(8,128)(2,1)S(1)}, u32[]{:S(2)}, u32[]{:S(2)}) collective-permute-start(bf16[704,128]{1,0:T(8,128)(2,1)S(1)} %shard_map.90.refs_0_), channel_id=1, source_target_pairs={{0,4},{1,17},{2,6},{3,19},{4,0},{5,21},{6,2},{7,23},{8,12},{9,25},... | collective-permute-start | bytes 540680 | tf_op jit(solution)/shard_map/ppermute | solution.py:211
  32.1 6.0 %collective-permute-start.13 = (bf16[704,128]{1,0:T(8,128)(2,1)S(1)}, bf16[704,128]{1,0:T(8,128)(2,1)S(1)}, u32[]{:S(2)}, u32[]{:S(2)}) collective-permute-start(bf16[704,128]{1,0:T(8,128)(2,1)S(1)} %shard_map.90.refs_0_), channel_id=1, source_target_pairs={{0,2},{1,9},{2,0},{3,11},{4,6},{5,13},{6,4},{7,15},{8,10},{9,1},{1... | collective-permute-start | bytes 540680 | tf_op jit(solution)/shard_map/ppermute | solution.py:211
  32.6 5.4 %collective-permute-start.15 = (bf16[704,128]{1,0:T(8,128)(2,1)S(1)}, bf16[704,128]{1,0:T(8,128)(2,1)S(1)}, u32[]{:S(2)}, u32[]{:S(2)}) collective-permute-start(bf16[704,128]{1,0:T(8,128)(2,1)S(1)} %shard_map.90.refs_0_), channel_id=1, source_target_pairs={{0,1},{1,0},{2,3},{3,2},{4,5},{5,4},{6,7},{7,6},{8,9},{9,8},{10,11... | collective-permute-start | bytes 540680 | tf_op jit(solution)/shard_map/ppermute | solution.py:215
  35.6 3.4 %collective-permute-start.10 = (bf16[704,128]{1,0:T(8,128)(2,1)S(1)}, bf16[704,128]{1,0:T(8,128)(2,1)S(1)}, u32[]{:S(2)}, u32[]{:S(2)}) collective-permute-start(bf16[704,128]{1,0:T(8,128)(2,1)S(1)} %collective-permute-done.9.refs_1_), channel_id=1, source_target_pairs={{0,1},{1,0},{2,3},{3,2},{4,5},{5,4},{6,7},{7,6},{8,9},{9,8},{10,11... | collective-permute-start | bytes 540680 | tf_op jit(solution)/shard_map/ppermute | solution.py:215
  37.5 1.6 %collective-permute-start.12 = (bf16[704,128]{1,0:T(8,128)(2,1)S(1)}, bf16[704,128]{1,0:T(8,128)(2,1)S(1)}, u32[]{:S(2)}, u32[]{:S(2)}) collective-permute-start(bf16[704,128]{1,0:T(8,128)(2,1)S(1)} %collective-permute-done.11.refs_2_), channel_id=1, source_target_pairs={{0,1},{1,0},{2,3},{3,2},{4,5},{5,4},{6,7},{7,6},{8,9},{9,8},{10,11... | collective-permute-start | bytes 540680 | tf_op jit(solution)/shard_map/ppermute | solution.py:215
  38.0 1.4 %collective-permute-start.14 = (bf16[704,128]{1,0:T(8,128)(2,1)S(1)}, bf16[704,128]{1,0:T(8,128)(2,1)S(1)}, u32[]{:S(2)}, u32[]{:S(2)}) collective-permute-start(bf16[704,128]{1,0:T(8,128)(2,1)S(1)} %collective-permute-done.13.refs_3_), channel_id=1, source_target_pairs={{0,1},{1,0},{2,3},{3,2},{4,5},{5,4},{6,7},{7,6},{8,9},{9,8},{10,11... | collective-permute-start | bytes 540680 | tf_op jit(solution)/shard_map/ppermute | solution.py:215

commit v19 on v17

--- a/solution.py
+++ b/solution.py
@@ -43,7 +43,7 @@
 
 
 def merge_kernel(*refs):
-    far, (merged, merged_t, stack, feat, out_w), near, sems = refs[:5], refs[5:10], refs[10:13], refs[13]
+    far, (merged, stack, feat, out_w), near, sems = refs[:5], refs[5:9], refs[9:12], refs[12]
     near = (*near, feat, out_w)
     copies = [pltpu.make_async_copy(a, b, sems.at[i]) for i, (a, b) in enumerate(zip(far, near))]
     for copy in copies:
@@ -63,8 +63,11 @@
         lifted = jnp.dot(spread, top[q], preferred_element_type=F32)
         for r in (2 * q, 2 * q + 1):
             merged[r * cols : (r + 1) * cols, :] = (lateral[r * cols : (r + 1) * cols] + lifted).astype(BF16)
-    merged_t[...] = jnp.transpose(merged[...])
     copies[4].wait()
+
+
+def over_cells(left, right):
+    return lax.dot_general(left, right, (((0,), (0,)), ((), ())), preferred_element_type=F32)
 
 
 def strips_of(stack, halo):
@@ -89,16 +92,16 @@
     theirs[rows, :] = jnp.where(here == 0, values[:, half:], values[:, :half]).astype(BF16)
 
 
-def kernel_grad_kernel(stack, halo, merged_t, out):
-    channels = merged_t.shape[0]
+def kernel_grad_kernel(stack, halo, merged, out):
+    channels = merged.shape[1]
     for i, strip in enumerate(strips_of(stack, halo)):
-        part = jnp.dot(merged_t[...], strip, preferred_element_type=F32)
+        part = over_cells(merged[...], strip)
         for j in range(3):
             start = (3 * i + j) * channels
             out[start : start + channels, :] = part[:, j * channels : (j + 1) * channels]
 
 
-def pair_kernel_grad_kernel(stack, merged_t, cot, merged, out, image):
+def pair_kernel_grad_kernel(stack, merged, cot, other_merged, out, image):
     here = lax.axis_index("space")
     rows, cols, channels = cot.shape
     half = channels // 2
@@ -117,8 +120,8 @@
     for first in (own, other):
         strips = [image[pl.ds(first + 1 - i, rows)].reshape(rows * cols, 3 * half) for i in range(3)]
         cells.append(jnp.concatenate(strips, axis=1))
-    left = jnp.concatenate([merged_t[...], jnp.transpose(merged[...])], axis=1)
-    part = jnp.dot(left, jnp.concatenate(cells, axis=0), preferred_element_type=F32)
+    left = jnp.concatenate([merged[...], other_merged[...]], axis=0)
+    part = over_cells(left, jnp.concatenate(cells, axis=0))
     for tap in range(9):
         out[tap * channels : (tap + 1) * channels, :] = part[:, tap * half : (tap + 1) * half]
 
@@ -129,7 +132,7 @@
     taps = jnp.concatenate([out_w[tap] for tap in range(9)], axis=1)
     total = lax.dot_general(cells, taps, (((1,), (1,)), ((), ())), preferred_element_type=F32)
     grad[...] = total.astype(BF16)
-    put_sums(outs, 0, jnp.dot(jnp.transpose(feat[...]), grad[...], preferred_element_type=F32))
+    put_sums(outs, 0, over_cells(feat[...], grad[...]))
 
 
 def forward_kernel(peers, merged, out_w, grad, *refs):
@@ -267,13 +270,12 @@
         cot_before, cot_after = neighbour_rows(cot)
         arrays = (cot, lateral_weight, top_down[image], features[image].reshape(cells, in_channels), taps)
         arrays = [pltpu.with_memory_space_constraint(array, pltpu.HBM) for array in arrays]
-        merged, merged_t, stack, near_feat, near_taps = pl.pallas_call(
+        merged, stack, near_feat, near_taps = pl.pallas_call(
             merge_kernel,
             out_shape=[
                 jax.ShapeDtypeStruct(shape, BF16)
                 for shape in (
                     (cells, channels),
-                    (channels, cells),
                     (rows, cols, 3 * channels),
                     (cells, in_channels),
                     taps.shape,
@@ -311,14 +313,14 @@
                 scratch_shapes=[pltpu.VMEM((2 * rows + 2, cols, 3 * channels // 2), BF16)],
                 compiler_params=params,
                 cost_estimate=kernel_cost,
-            )(stack, merged_t, cot_after, edges[0].reshape(cells, channels))
+            )(stack, merged.reshape(cells, channels), cot_after, edges[0].reshape(cells, channels))
         else:
             kernel_sums = pl.pallas_call(
                 kernel_grad_kernel,
                 out_shape=jax.ShapeDtypeStruct((9 * channels, channels), F32),
                 compiler_params=params,
                 cost_estimate=kernel_cost,
-            )(stack, halo, merged_t)
+            )(stack, halo, merged.reshape(cells, channels))
         out, grad_top = pl.pallas_call(
             functools.partial(forward_kernel, peers),
             out_shape=[

time: 40.3 us -> 40 us (level)
  waiting for transfers between devices: 15.9 us -> 13.9 us
  starting transfers between devices: 13.9 us -> 15.6 us
    ppermute x9, waiting for transfers between devices: 15.6 us -> 13.5 us  [exchange(): return lax.ppermute(array, ('dp', 'space'), pairs)]
    ppermute x5, starting transfers between devices: 1.03 us -> 2.75 us  [swap(): return lax.ppermute(array, 'space', [(0, 1), (1, 0)])]
  transfers between devices with their start and end apart: 16 -> 16, of which waited for: 8 -> 7; matrix products, arithmetic and copies ran while one was open for 0% -> 0% of each run, Pallas kernels for 21% -> 21%
where the time goes in v19:
time: 40 us; the launch traced here: 39.9 us
  starting transfers between devices  15.6 us (39%)
  waiting for transfers between devices  13.9 us (35%)
  Pallas kernels  9.69 us (24%)
  between operations  0.73 us (2%)
    ppermute x9, waiting for transfers between devices, exchange(): return lax.ppermute(array, ('dp', 'space'), pairs)  13.5 us
    ppermute x9, starting transfers between devices, exchange(): return lax.ppermute(array, ('dp', 'space'), pairs)  12.2 us
    ppermute x5, starting transfers between devices, swap(): return lax.ppermute(array, 'space', [(0, 1), (1, 0)])  2.75 us
    pallas_call x1, Pallas kernels, local(): pl.pallas_call(functools.partial(forward_kernel, peers), out_shape=[jax.S...  2.53 us
    pallas_call x2, Pallas kernels, sum_everywhere(): call(functools.partial(place_kernel, plan), *results, **place)  1.88 us
    pallas_call x1, Pallas kernels, local(): pl.pallas_call(merge_kernel, out_shape=[jax.ShapeDtypeStruct(shape, BF16)...  1.83 us
    pallas_call x1, Pallas kernels, local(): pl.pallas_call(functools.partial(data_grad_kernel, peers), out_shape=[jax...  1.7 us
    pallas_call x1, Pallas kernels, local(): pl.pallas_call(pair_kernel_grad_kernel, out_shape=jax.ShapeDtypeStruct((9...  1.45 us
  transfers between devices with their start and end apart: 16, of which 7 were waited for; matrix products, arithmetic and copies ran while one was open for 0% of the time, Pallas kernels for 21%

profile of v19, /device:TPU:0, one launch (start us, length us, event | category | flops | bytes accessed | tf_op | source)
XLA Modules:
  0.0 39.9 jit_solution(10403179789069625533)
XLA Ops:
  0.6 0.5 %collective-permute-start = (bf16[8,96,256]{2,1,0:T(8,128)(2,1)}, bf16[8,96,256]{2,1,0:T(8,128)(2,1)S(1)}, u32[]{:S(2)}, u32[]{:S(2)}) collective-permute-start(bf16[8,96,256]{2,1,0:T(8,128)(2,1)} %bitcast.16), channel_id=1, source_target_pairs={{0,1},{1,0},{2,3},{3,2},{4,5},{5,4},{6,7},{7,6},{8,9},{9,8},{10,11... | collective-permute-start | bytes 1179656 | tf_op jit(solution)/shard_map/ppermute | solution.py:19
  1.1 1.8 %shard_map.84 = (bf16[768,256]{1,0:T(8,128)(2,1)S(1)}, bf16[8,96,768]{2,1,0:T(8,128)(2,1)S(1)}, bf16[768,512]{1,0:T(8,128)(2,1)S(1)}, bf16[9,256,256]{2,1,0:T(8,128)(2,1)S(1)}) custom-call(bf16[8,96,256]{2,1,0:T(8,128)(2,1)} %bitcast.17, bf16[512,256]{1,0:T(8,128)(2,1)} %refs_1_.1, bf16[4,48,256]{2,1,0:T(8,128)(2,1)} %bitcast.18, bf16[768,512]{1,0:T(8,128)(2,1)} %bitcast.15, ...), custom_call_target="tpu_custom_call" | custom-call | flops 805306368 | bytes 4194304 | tf_op jit(solution)/shard_map/pallas_call | solution.py:273
  3.0 0.1 collective-permute-start.1
  3.1 1.7 %shard_map.85 = (bf16[768,256]{1,0:T(8,128)(2,1)S(1)}, bf16[2,96,768]{2,1,0:T(8,128)(2,1)}, f32[512,128]{1,0:T(8,128)S(1)}, bf16[512,128]{1,0:T(8,128)(2,1)S(1)}) custom-call(bf16[8,96,768]{2,1,0:T(8,128)(2,1)S(1)} %get-tuple-element.23.stack, bf16[8,96,256]{2,1,0:T(8,128)(2,1)S(1)} %collective-permute-done.before.after.cot, ...), custom_call_target="tpu_custom_call" | custom-call | flops 1107296256 | bytes 4194304 | tf_op jit(solution)/shard_map/pallas_call | solution.py:293
  4.8 0.5 %collective-permute-start.2 = (bf16[512,128]{1,0:T(8,128)(2,1)S(1)}, bf16[512,128]{1,0:T(8,128)(2,1)S(1)}, u32[]{:S(2)}, u32[]{:S(2)}) collective-permute-start(bf16[512,128]{1,0:T(8,128)(2,1)S(1)} %get-tuple-element.29), channel_id=1, source_target_pairs={{0,1},{1,0},{2,3},{3,2},{4,5},{5,4},{6,7},{7,6},{8,9},{9,8},{10,11... | collective-permute-start | bytes 393224 | tf_op jit(solution)/shard_map/ppermute | solution.py:218
  5.4 1.5 %shard_map.87.kernel_sums = f32[2304,128]{1,0:T(8,128)S(1)} custom-call(bf16[8,96,768]{2,1,0:T(8,128)(2,1)S(1)} %get-tuple-element.23.stack, bf16[768,256]{1,0:T(8,128)(2,1)S(1)} %get-tuple-element.21.merged, bf16[8,96,256]{2,1,0:T(8,128)(2,1)S(1)} %collective-permute-done.before.after.cot, bf16[768,256]{1,0:T(8,128)(2,1)S(1)} %bitcast.11), custom_call_target="tpu_custom_call" | custom-call | flops 905969664 | bytes 4194304 | tf_op jit(solution)/shard_map/pallas_call | solution.py:310
  6.8 0.1 shard_map.88
  6.9 3.5 %collective-permute-start.3 = (bf16[704,128]{1,0:T(8,128)(2,1)S(1)}, bf16[704,128]{1,0:T(8,128)(2,1)S(1)}, u32[]{:S(2)}, u32[]{:S(2)}) collective-permute-start(bf16[704,128]{1,0:T(8,128)(2,1)S(1)} %get-tuple-element.31), channel_id=1, source_target_pairs={{0,6},{1,25},{2,4},{3,27},{4,2},{5,29},{6,0},{7,31},{8,14},{9,17},... | collective-permute-start | bytes 540680 | tf_op jit(solution)/shard_map/ppermute | solution.py:214
  10.5 0.5 %collective-permute-start.4 = (bf16[704,128]{1,0:T(8,128)(2,1)S(1)}, bf16[704,128]{1,0:T(8,128)(2,1)S(1)}, u32[]{:S(2)}, u32[]{:S(2)}) collective-permute-start(bf16[704,128]{1,0:T(8,128)(2,1)S(1)} %get-tuple-element.32), channel_id=1, source_target_pairs={{0,4},{1,17},{2,6},{3,19},{4,0},{5,21},{6,2},{7,23},{8,12},{9,25},... | collective-permute-start | bytes 540680 | tf_op jit(solution)/shard_map/ppermute | solution.py:214
  11.0 0.1 collective-permute-start.5
  11.1 2.8 %collective-permute-done.3.three = bf16[704,128]{1,0:T(8,128)(2,1)S(1)} collective-permute-done((bf16[704,128]{1,0:T(8,128)(2,1)S(1)}, bf16[704,128]{1,0:T(8,128)(2,1)S(1)}, u32[]{:S(2)}, u32[]{:S(2)}) %collective-permute-start.3) | collective-permute-done | bytes 180256 | tf_op jit(solution)/shard_map/ppermute | solution.py:214
  13.9 2.0 %collective-permute-done.4.two = bf16[704,128]{1,0:T(8,128)(2,1)S(1)} collective-permute-done((bf16[704,128]{1,0:T(8,128)(2,1)S(1)}, bf16[704,128]{1,0:T(8,128)(2,1)S(1)}, u32[]{:S(2)}, u32[]{:S(2)}) %collective-permute-start.4) | collective-permute-done | bytes 180256 | tf_op jit(solution)/shard_map/ppermute | solution.py:214
  16.0 0.5 %collective-permute-done.5.one = bf16[704,128]{1,0:T(8,128)(2,1)S(1)} collective-permute-done((bf16[704,128]{1,0:T(8,128)(2,1)S(1)}, bf16[704,128]{1,0:T(8,128)(2,1)S(1)}, u32[]{:S(2)}, u32[]{:S(2)}) %collective-permute-start.5) | collective-permute-done | bytes 180256 | tf_op jit(solution)/shard_map/ppermute | solution.py:214
  16.5 0.1 shard_map.89.own
  16.6 1.6 %collective-permute-start.8 = (bf16[704,128]{1,0:T(8,128)(2,1)S(1)}, bf16[704,128]{1,0:T(8,128)(2,1)S(1)}, u32[]{:S(2)}, u32[]{:S(2)}) collective-permute-start(bf16[704,128]{1,0:T(8,128)(2,1)S(1)} %shard_map.89.own), channel_id=1, source_target_pairs={{0,8},{1,3},{2,10},{3,1},{4,12},{5,7},{6,14},{7,5},{8,0},{9,11},{1... | collective-permute-start | bytes 540680 | tf_op jit(solution)/shard_map/ppermute | solution.py:214
  18.2 2.6 %collective-permute-start.7 = (bf16[704,128]{1,0:T(8,128)(2,1)S(1)}, bf16[704,128]{1,0:T(8,128)(2,1)S(1)}, u32[]{:S(2)}, u32[]{:S(2)}) collective-permute-start(bf16[704,128]{1,0:T(8,128)(2,1)S(1)} %shard_map.89.own), channel_id=1, source_target_pairs={{0,16},{1,5},{2,18},{3,7},{4,20},{5,1},{6,22},{7,3},{8,24},{9,13},... | collective-permute-start | bytes 540680 | tf_op jit(solution)/shard_map/ppermute | solution.py:214
  20.8 0.2 collective-permute-start.6
  21.0 2.5 %shard_map.86 = (bf16[8,96,256]{2,1,0:T(8,128)(2,1)}, bf16[4,48,256]{2,1,0:T(8,128)(2,1)}) custom-call(bf16[8,96,256]{2,1,0:T(8,128)(2,1)S(1)} %bitcast.10, bf16[9,256,256]{2,1,0:T(8,128)(2,1)S(1)} %get-tuple-element.22.out_w, bf16[768,256]{1,0:T(8,128)(2,1)S(1)} %get-tuple-element.25.grad, bf16[8,96,256]{2,1,0:T(8,128)(2,1)S(1)} %collective-permute-done.1.refs_0_.refs_1_, ...), custom_call_target="tpu_custom_call" | custom-call | flops 905969664 | bytes 2097152 | tf_op jit(solution)/shard_map/pallas_call | solution.py:324
  23.6 4.9 %collective-permute-done.7.two = bf16[704,128]{1,0:T(8,128)(2,1)S(1)} collective-permute-done((bf16[704,128]{1,0:T(8,128)(2,1)S(1)}, bf16[704,128]{1,0:T(8,128)(2,1)S(1)}, u32[]{:S(2)}, u32[]{:S(2)}) %collective-permute-start.7) | collective-permute-done | bytes 180256 | tf_op jit(solution)/shard_map/ppermute | solution.py:214
  28.4 0.1 shard_map.90.refs_0_
  28.6 1.5 %collective-permute-start.13 = (bf16[704,128]{1,0:T(8,128)(2,1)S(1)}, bf16[704,128]{1,0:T(8,128)(2,1)S(1)}, u32[]{:S(2)}, u32[]{:S(2)}) collective-permute-start(bf16[704,128]{1,0:T(8,128)(2,1)S(1)} %shard_map.90.refs_0_), channel_id=1, source_target_pairs={{0,2},{1,9},{2,0},{3,11},{4,6},{5,13},{6,4},{7,15},{8,10},{9,1},{1... | collective-permute-start | bytes 540680 | tf_op jit(solution)/shard_map/ppermute | solution.py:214
  30.1 1.0 %collective-permute-start.11 = (bf16[704,128]{1,0:T(8,128)(2,1)S(1)}, bf16[704,128]{1,0:T(8,128)(2,1)S(1)}, u32[]{:S(2)}, u32[]{:S(2)}) collective-permute-start(bf16[704,128]{1,0:T(8,128)(2,1)S(1)} %shard_map.90.refs_0_), channel_id=1, source_target_pairs={{0,4},{1,17},{2,6},{3,19},{4,0},{5,21},{6,2},{7,23},{8,12},{9,25},... | collective-permute-start | bytes 540680 | tf_op jit(solution)/shard_map/ppermute | solution.py:214
  31.1 1.0 %collective-permute-start.9 = (bf16[704,128]{1,0:T(8,128)(2,1)S(1)}, bf16[704,128]{1,0:T(8,128)(2,1)S(1)}, u32[]{:S(2)}, u32[]{:S(2)}) collective-permute-start(bf16[704,128]{1,0:T(8,128)(2,1)S(1)} %shard_map.90.refs_0_), channel_id=1, source_target_pairs={{0,6},{1,25},{2,4},{3,27},{4,2},{5,29},{6,0},{7,31},{8,14},{9,17},... | collective-permute-start | bytes 540680 | tf_op jit(solution)/shard_map/ppermute | solution.py:214
  32.1 2.0 %collective-permute-done.13.refs_3_ = bf16[704,128]{1,0:T(8,128)(2,1)S(1)} collective-permute-done((bf16[704,128]{1,0:T(8,128)(2,1)S(1)}, bf16[704,128]{1,0:T(8,128)(2,1)S(1)}, u32[]{:S(2)}, u32[]{:S(2)}) %collective-permute-start.13) | collective-permute-done | bytes 180256 | tf_op jit(solution)/shard_map/ppermute | solution.py:214
  34.1 0.3 collective-permute-start.14
  34.4 1.2 %collective-permute-done.11.refs_2_ = bf16[704,128]{1,0:T(8,128)(2,1)S(1)} collective-permute-done((bf16[704,128]{1,0:T(8,128)(2,1)S(1)}, bf16[704,128]{1,0:T(8,128)(2,1)S(1)}, u32[]{:S(2)}, u32[]{:S(2)}) %collective-permute-start.11) | collective-permute-done | bytes 180256 | tf_op jit(solution)/shard_map/ppermute | solution.py:214
  35.6 2.0 %collective-permute-start.12 = (bf16[704,128]{1,0:T(8,128)(2,1)S(1)}, bf16[704,128]{1,0:T(8,128)(2,1)S(1)}, u32[]{:S(2)}, u32[]{:S(2)}) collective-permute-start(bf16[704,128]{1,0:T(8,128)(2,1)S(1)} %collective-permute-done.11.refs_2_), channel_id=1, source_target_pairs={{0,1},{1,0},{2,3},{3,2},{4,5},{5,4},{6,7},{7,6},{8,9},{9,8},{10,11... | collective-permute-start | bytes 540680 | tf_op jit(solution)/shard_map/ppermute | solution.py:218
  37.6 0.0 collective-permute-start.10
  37.6 1.0 %shard_map.91 = (bf16[2304,256]{1,0:T(8,128)(2,1)}, bf16[512,256]{1,0:T(8,128)(2,1)}) custom-call(bf16[704,128]{1,0:T(8,128)(2,1)S(1)} %shard_map.90.refs_0_, bf16[704,128]{1,0:T(8,128)(2,1)S(1)} %collective-permute-done.9.refs_1_, bf16[704,128]{1,0:T(8,128)(2,1)S(1)} %collective-permute-done.11.refs_2_, ...), custom_call_target="tpu_custom_call" | custom-call | tf_op jit(solution)/shard_map/pallas_call | solution.py:247
  38.6 0.0 collective-permute-done.12.refs_1_
  38.6 0.4 collective-permute-done.10.refs_0_
  39.0 0.9 %shard_map.92 = (bf16[2304,256]{1,0:T(8,128)(2,1)}, bf16[512,256]{1,0:T(8,128)(2,1)}) custom-call(bf16[704,128]{1,0:T(8,128)(2,1)S(1)} %collective-permute-done.10.refs_0_, bf16[704,128]{1,0:T(8,128)(2,1)S(1)} %collective-permute-done.12.refs_1_, bf16[704,128]{1,0:T(8,128)(2,1)S(1)} %collective-permute-done.14.refs_2_, ...), custom_call_target="tpu_custom_call", output_to_operand_aliasing={{0}: (3, {}), {1}: (4, {})} | custom-call | tf_op jit(solution)/shard_map/pallas_call | solution.py:250
  (9 shorter events, 0.0 us)
Async XLA Ops:
  0.6 2.5 %collective-permute-start = (bf16[8,96,256]{2,1,0:T(8,128)(2,1)}, bf16[8,96,256]{2,1,0:T(8,128)(2,1)S(1)}, u32[]{:S(2)}, u32[]{:S(2)}) collective-permute-start(bf16[8,96,256]{2,1,0:T(8,128)(2,1)} %bitcast.16), channel_id=1, source_target_pairs={{0,1},{1,0},{2,3},{3,2},{4,5},{5,4},{6,7},{7,6},{8,9},{9,8},{10,11... | collective-permute-start | bytes 1179656 | tf_op jit(solution)/shard_map/ppermute | solution.py:19
  3.0 2.4 %collective-permute-start.1 = (bf16[8,96,256]{2,1,0:T(8,128)(2,1)S(1)}, bf16[8,96,256]{2,1,0:T(8,128)(2,1)S(1)}, u32[]{:S(2)}, u32[]{:S(2)}) collective-permute-start(bf16[8,96,256]{2,1,0:T(8,128)(2,1)S(1)} %bitcast.9), channel_id=1, source_target_pairs={{0,1},{1,0},{2,3},{3,2},{4,5},{5,4},{6,7},{7,6},{8,9},{9,8},{10,11... | collective-permute-start | bytes 1179656 | tf_op jit(solution)/shard_map/ppermute | solution.py:19
  4.8 2.0 %collective-permute-start.2 = (bf16[512,128]{1,0:T(8,128)(2,1)S(1)}, bf16[512,128]{1,0:T(8,128)(2,1)S(1)}, u32[]{:S(2)}, u32[]{:S(2)}) collective-permute-start(bf16[512,128]{1,0:T(8,128)(2,1)S(1)} %get-tuple-element.29), channel_id=1, source_target_pairs={{0,1},{1,0},{2,3},{3,2},{4,5},{5,4},{6,7},{7,6},{8,9},{9,8},{10,11... | collective-permute-start | bytes 393224 | tf_op jit(solution)/shard_map/ppermute | solution.py:218
  6.9 7.0 %collective-permute-start.3 = (bf16[704,128]{1,0:T(8,128)(2,1)S(1)}, bf16[704,128]{1,0:T(8,128)(2,1)S(1)}, u32[]{:S(2)}, u32[]{:S(2)}) collective-permute-start(bf16[704,128]{1,0:T(8,128)(2,1)S(1)} %get-tuple-element.31), channel_id=1, source_target_pairs={{0,6},{1,25},{2,4},{3,27},{4,2},{5,29},{6,0},{7,31},{8,14},{9,17},... | collective-permute-start | bytes 540680 | tf_op jit(solution)/shard_map/ppermute | solution.py:214
  10.5 5.5 %collective-permute-start.4 = (bf16[704,128]{1,0:T(8,128)(2,1)S(1)}, bf16[704,128]{1,0:T(8,128)(2,1)S(1)}, u32[]{:S(2)}, u32[]{:S(2)}) collective-permute-start(bf16[704,128]{1,0:T(8,128)(2,1)S(1)} %get-tuple-element.32), channel_id=1, source_target_pairs={{0,4},{1,17},{2,6},{3,19},{4,0},{5,21},{6,2},{7,23},{8,12},{9,25},... | collective-permute-start | bytes 540680 | tf_op jit(solution)/shard_map/ppermute | solution.py:214
  11.0 5.5 %collective-permute-start.5 = (bf16[704,128]{1,0:T(8,128)(2,1)S(1)}, bf16[704,128]{1,0:T(8,128)(2,1)S(1)}, u32[]{:S(2)}, u32[]{:S(2)}) collective-permute-start(bf16[704,128]{1,0:T(8,128)(2,1)S(1)} %get-tuple-element.33), channel_id=1, source_target_pairs={{0,2},{1,9},{2,0},{3,11},{4,6},{5,13},{6,4},{7,15},{8,10},{9,1},{1... | collective-permute-start | bytes 540680 | tf_op jit(solution)/shard_map/ppermute | solution.py:214
  16.6 7.0 %collective-permute-start.8 = (bf16[704,128]{1,0:T(8,128)(2,1)S(1)}, bf16[704,128]{1,0:T(8,128)(2,1)S(1)}, u32[]{:S(2)}, u32[]{:S(2)}) collective-permute-start(bf16[704,128]{1,0:T(8,128)(2,1)S(1)} %shard_map.89.own), channel_id=1, source_target_pairs={{0,8},{1,3},{2,10},{3,1},{4,12},{5,7},{6,14},{7,5},{8,0},{9,11},{1... | collective-permute-start | bytes 540680 | tf_op jit(solution)/shard_map/ppermute | solution.py:214
  18.2 10.3 %collective-permute-start.7 = (bf16[704,128]{1,0:T(8,128)(2,1)S(1)}, bf16[704,128]{1,0:T(8,128)(2,1)S(1)}, u32[]{:S(2)}, u32[]{:S(2)}) collective-permute-start(bf16[704,128]{1,0:T(8,128)(2,1)S(1)} %shard_map.89.own), channel_id=1, source_target_pairs={{0,16},{1,5},{2,18},{3,7},{4,20},{5,1},{6,22},{7,3},{8,24},{9,13},... | collective-permute-start | bytes 540680 | tf_op jit(solution)/shard_map/ppermute | solution.py:214
  20.8 7.7 %collective-permute-start.6 = (bf16[704,128]{1,0:T(8,128)(2,1)S(1)}, bf16[704,128]{1,0:T(8,128)(2,1)S(1)}, u32[]{:S(2)}, u32[]{:S(2)}) collective-permute-start(bf16[704,128]{1,0:T(8,128)(2,1)S(1)} %shard_map.89.own), channel_id=1, source_target_pairs={{0,24},{1,7},{2,26},{3,5},{4,28},{5,3},{6,30},{7,1},{8,16},{9,15},... | collective-permute-start | bytes 540680 | tf_op jit(solution)/shard_map/ppermute | solution.py:214
  28.6 5.6 %collective-permute-start.13 = (bf16[704,128]{1,0:T(8,128)(2,1)S(1)}, bf16[704,128]{1,0:T(8,128)(2,1)S(1)}, u32[]{:S(2)}, u32[]{:S(2)}) collective-permute-start(bf16[704,128]{1,0:T(8,128)(2,1)S(1)} %shard_map.90.refs_0_), channel_id=1, source_target_pairs={{0,2},{1,9},{2,0},{3,11},{4,6},{5,13},{6,4},{7,15},{8,10},{9,1},{1... | collective-permute-start | bytes 540680 | tf_op jit(solution)/shard_map/ppermute | solution.py:214
  30.1 5.5 %collective-permute-start.11 = (bf16[704,128]{1,0:T(8,128)(2,1)S(1)}, bf16[704,128]{1,0:T(8,128)(2,1)S(1)}, u32[]{:S(2)}, u32[]{:S(2)}) collective-permute-start(bf16[704,128]{1,0:T(8,128)(2,1)S(1)} %shard_map.90.refs_0_), channel_id=1, source_target_pairs={{0,4},{1,17},{2,6},{3,19},{4,0},{5,21},{6,2},{7,23},{8,12},{9,25},... | collective-permute-start | bytes 540680 | tf_op jit(solution)/shard_map/ppermute | solution.py:214
  31.1 6.5 %collective-permute-start.9 = (bf16[704,128]{1,0:T(8,128)(2,1)S(1)}, bf16[704,128]{1,0:T(8,128)(2,1)S(1)}, u32[]{:S(2)}, u32[]{:S(2)}) collective-permute-start(bf16[704,128]{1,0:T(8,128)(2,1)S(1)} %shard_map.90.refs_0_), channel_id=1, source_target_pairs={{0,6},{1,25},{2,4},{3,27},{4,2},{5,29},{6,0},{7,31},{8,14},{9,17},... | collective-permute-start | bytes 540680 | tf_op jit(solution)/shard_map/ppermute | solution.py:214
  32.1 5.5 %collective-permute-start.15 = (bf16[704,128]{1,0:T(8,128)(2,1)S(1)}, bf16[704,128]{1,0:T(8,128)(2,1)S(1)}, u32[]{:S(2)}, u32[]{:S(2)}) collective-permute-start(bf16[704,128]{1,0:T(8,128)(2,1)S(1)} %shard_map.90.refs_0_), channel_id=1, source_target_pairs={{0,1},{1,0},{2,3},{3,2},{4,5},{5,4},{6,7},{7,6},{8,9},{9,8},{10,11... | collective-permute-start | bytes 540680 | tf_op jit(solution)/shard_map/ppermute | solution.py:218
  34.1 4.5 %collective-permute-start.14 = (bf16[704,128]{1,0:T(8,128)(2,1)S(1)}, bf16[704,128]{1,0:T(8,128)(2,1)S(1)}, u32[]{:S(2)}, u32[]{:S(2)}) collective-permute-start(bf16[704,128]{1,0:T(8,128)(2,1)S(1)} %collective-permute-done.13.refs_3_), channel_id=1, source_target_pairs={{0,1},{1,0},{2,3},{3,2},{4,5},{5,4},{6,7},{7,6},{8,9},{9,8},{10,11... | collective-permute-start | bytes 540680 | tf_op jit(solution)/shard_map/ppermute | solution.py:218
  35.6 3.0 %collective-permute-start.12 = (bf16[704,128]{1,0:T(8,128)(2,1)S(1)}, bf16[704,128]{1,0:T(8,128)(2,1)S(1)}, u32[]{:S(2)}, u32[]{:S(2)}) collective-permute-start(bf16[704,128]{1,0:T(8,128)(2,1)S(1)} %collective-permute-done.11.refs_2_), channel_id=1, source_target_pairs={{0,1},{1,0},{2,3},{3,2},{4,5},{5,4},{6,7},{7,6},{8,9},{9,8},{10,11... | collective-permute-start | bytes 540680 | tf_op jit(solution)/shard_map/ppermute | solution.py:218
  37.6 1.4 %collective-permute-start.10 = (bf16[704,128]{1,0:T(8,128)(2,1)S(1)}, bf16[704,128]{1,0:T(8,128)(2,1)S(1)}, u32[]{:S(2)}, u32[]{:S(2)}) collective-permute-start(bf16[704,128]{1,0:T(8,128)(2,1)S(1)} %collective-permute-done.9.refs_1_), channel_id=1, source_target_pairs={{0,1},{1,0},{2,3},{3,2},{4,5},{5,4},{6,7},{7,6},{8,9},{9,8},{10,11... | collective-permute-start | bytes 540680 | tf_op jit(solution)/shard_map/ppermute | solution.py:218

commit v20 on v19

--- a/solution.py
+++ b/solution.py
@@ -180,7 +180,7 @@
     out[...] = total.astype(BF16)
 
 
-def finish_kernel(scale, own, three, two, one, _, out):
+def finish_kernel(scale, own, one, two, three, _, out):
     near = own[...].astype(F32) + one[...].astype(F32)
     far = two[...].astype(F32) + three[...].astype(F32)
     out[...] = ((near + far) * scale).astype(BF16)
@@ -237,15 +237,15 @@
     [total] = call(add_kernel, (quarter, BF16))(own, three, two, one)
     three, two, one = [exchange(total, 1, k) for k in (3, 2, 1)]
     finish = call(functools.partial(finish_kernel, scale), (quarter, BF16), in_specs=[vmem] * 4 + [far])
-    [total] = finish(total, three, two, one, after)
+    [total] = finish(total, one, two, three, after)
     three, two, one = [exchange(total, 0, k) for k in (3, 2, 1)]
-    quarters = [total, three, two, one]
+    quarters = [total, one, two, three]
     results = [((length, 2 * width), BF16) for length in lengths]
     others = [swap(one) for one in quarters]
     place = dict(out_specs=[far] * 2, scratch_shapes=[pltpu.SemaphoreType.DMA((10,))])
-    plan = (False, 0), (False, 3), (False, 2), (False, 1), (True, 0)
+    plan = (False, 0), (False, 1), (False, 2), (False, 3), (True, 0)
     most = call(functools.partial(place_kernel, plan), *results, **place)(*quarters, others[0])
-    plan = (True, 3), (True, 2), (True, 1)
+    plan = (True, 1), (True, 2), (True, 3)
     place.update(in_specs=[vmem] * 3 + [far] * 2, input_output_aliases={3: 0, 4: 1})
     return call(functools.partial(place_kernel, plan), *results, **place)(*others[1:], *most)
 

time: 40 us -> 40.3 us (level)
  waiting for transfers between devices: 13.9 us -> 15.9 us
  starting transfers between devices: 15.6 us -> 13.9 us
    ppermute x9, waiting for transfers between devices: 13.5 us -> 15.6 us  [exchange(): return lax.ppermute(array, ('dp', 'space'), pairs)]
    ppermute x5, starting transfers between devices: 2.75 us -> 1.04 us  [swap(): return lax.ppermute(array, 'space', [(0, 1), (1, 0)])]
  transfers between devices with their start and end apart: 16 -> 16, of which waited for: 7 -> 8; matrix products, arithmetic and copies ran while one was open for 0% -> 0% of each run, Pallas kernels for 21% -> 21%
where the time goes in v20:
time: 40.3 us; the launch traced here: 40.1 us
  waiting for transfers between devices  15.9 us (39%)
  starting transfers between devices  13.9 us (34%)
  Pallas kernels  9.67 us (24%)
  between operations  0.72 us (2%)
    ppermute x9, waiting for transfers between devices, exchange(): return lax.ppermute(array, ('dp', 'space'), pairs)  15.6 us
    ppermute x9, starting transfers between devices, exchange(): return lax.ppermute(array, ('dp', 'space'), pairs)  12.2 us
    pallas_call x1, Pallas kernels, local(): pl.pallas_call(functools.partial(forward_kernel, peers), out_shape=[jax.S...  2.53 us
    pallas_call x2, Pallas kernels, sum_everywhere(): call(functools.partial(place_kernel, plan), *results, **place)  1.86 us
    pallas_call x1, Pallas kernels, local(): pl.pallas_call(merge_kernel, out_shape=[jax.ShapeDtypeStruct(shape, BF16)...  1.83 us
    pallas_call x1, Pallas kernels, local(): pl.pallas_call(functools.partial(data_grad_kernel, peers), out_shape=[jax...  1.7 us
    pallas_call x1, Pallas kernels, local(): pl.pallas_call(pair_kernel_grad_kernel, out_shape=jax.ShapeDtypeStruct((9...  1.45 us
    ppermute x5, starting transfers between devices, swap(): return lax.ppermute(array, 'space', [(0, 1), (1, 0)])  1.04 us
  transfers between devices with their start and end apart: 16, of which 8 were waited for; matrix products, arithmetic and copies ran while one was open for 0% of the time, Pallas kernels for 21%

profile of v20, /device:TPU:0, one launch (start us, length us, event | category | flops | bytes accessed | tf_op | source)
XLA Modules:
  0.0 40.1 jit_solution(2535877749408358906)
XLA Ops:
  0.6 0.5 %collective-permute-start = (bf16[8,96,256]{2,1,0:T(8,128)(2,1)}, bf16[8,96,256]{2,1,0:T(8,128)(2,1)S(1)}, u32[]{:S(2)}, u32[]{:S(2)}) collective-permute-start(bf16[8,96,256]{2,1,0:T(8,128)(2,1)} %bitcast.16), channel_id=1, source_target_pairs={{0,1},{1,0},{2,3},{3,2},{4,5},{5,4},{6,7},{7,6},{8,9},{9,8},{10,11... | collective-permute-start | bytes 1179656 | tf_op jit(solution)/shard_map/ppermute | solution.py:19
  1.1 1.8 %shard_map.84 = (bf16[768,256]{1,0:T(8,128)(2,1)S(1)}, bf16[8,96,768]{2,1,0:T(8,128)(2,1)S(1)}, bf16[768,512]{1,0:T(8,128)(2,1)S(1)}, bf16[9,256,256]{2,1,0:T(8,128)(2,1)S(1)}) custom-call(bf16[8,96,256]{2,1,0:T(8,128)(2,1)} %bitcast.17, bf16[512,256]{1,0:T(8,128)(2,1)} %refs_1_.1, bf16[4,48,256]{2,1,0:T(8,128)(2,1)} %bitcast.18, bf16[768,512]{1,0:T(8,128)(2,1)} %bitcast.15, ...), custom_call_target="tpu_custom_call" | custom-call | flops 805306368 | bytes 4194304 | tf_op jit(solution)/shard_map/pallas_call | solution.py:273
  3.0 0.1 collective-permute-start.1
  3.1 1.7 %shard_map.85 = (bf16[768,256]{1,0:T(8,128)(2,1)S(1)}, bf16[2,96,768]{2,1,0:T(8,128)(2,1)}, f32[512,128]{1,0:T(8,128)S(1)}, bf16[512,128]{1,0:T(8,128)(2,1)S(1)}) custom-call(bf16[8,96,768]{2,1,0:T(8,128)(2,1)S(1)} %get-tuple-element.23.stack, bf16[8,96,256]{2,1,0:T(8,128)(2,1)S(1)} %collective-permute-done.before.after.cot, ...), custom_call_target="tpu_custom_call" | custom-call | flops 1107296256 | bytes 4194304 | tf_op jit(solution)/shard_map/pallas_call | solution.py:293
  4.8 0.5 %collective-permute-start.2 = (bf16[512,128]{1,0:T(8,128)(2,1)S(1)}, bf16[512,128]{1,0:T(8,128)(2,1)S(1)}, u32[]{:S(2)}, u32[]{:S(2)}) collective-permute-start(bf16[512,128]{1,0:T(8,128)(2,1)S(1)} %get-tuple-element.29), channel_id=1, source_target_pairs={{0,1},{1,0},{2,3},{3,2},{4,5},{5,4},{6,7},{7,6},{8,9},{9,8},{10,11... | collective-permute-start | bytes 393224 | tf_op jit(solution)/shard_map/ppermute | solution.py:218
  5.4 1.5 %shard_map.87.kernel_sums = f32[2304,128]{1,0:T(8,128)S(1)} custom-call(bf16[8,96,768]{2,1,0:T(8,128)(2,1)S(1)} %get-tuple-element.23.stack, bf16[768,256]{1,0:T(8,128)(2,1)S(1)} %get-tuple-element.21.merged, bf16[8,96,256]{2,1,0:T(8,128)(2,1)S(1)} %collective-permute-done.before.after.cot, bf16[768,256]{1,0:T(8,128)(2,1)S(1)} %bitcast.11), custom_call_target="tpu_custom_call" | custom-call | flops 905969664 | bytes 4194304 | tf_op jit(solution)/shard_map/pallas_call | solution.py:310
  6.8 0.0 collective-permute-done.2.got
  6.8 0.1 shard_map.88
  6.9 3.5 %collective-permute-start.3 = (bf16[704,128]{1,0:T(8,128)(2,1)S(1)}, bf16[704,128]{1,0:T(8,128)(2,1)S(1)}, u32[]{:S(2)}, u32[]{:S(2)}) collective-permute-start(bf16[704,128]{1,0:T(8,128)(2,1)S(1)} %get-tuple-element.31), channel_id=1, source_target_pairs={{0,6},{1,25},{2,4},{3,27},{4,2},{5,29},{6,0},{7,31},{8,14},{9,17},... | collective-permute-start | bytes 540680 | tf_op jit(solution)/shard_map/ppermute | solution.py:214
  10.5 0.5 %collective-permute-start.4 = (bf16[704,128]{1,0:T(8,128)(2,1)S(1)}, bf16[704,128]{1,0:T(8,128)(2,1)S(1)}, u32[]{:S(2)}, u32[]{:S(2)}) collective-permute-start(bf16[704,128]{1,0:T(8,128)(2,1)S(1)} %get-tuple-element.32), channel_id=1, source_target_pairs={{0,4},{1,17},{2,6},{3,19},{4,0},{5,21},{6,2},{7,23},{8,12},{9,25},... | collective-permute-start | bytes 540680 | tf_op jit(solution)/shard_map/ppermute | solution.py:214
  11.0 0.1 collective-permute-start.5
  11.1 2.8 %collective-permute-done.3.three = bf16[704,128]{1,0:T(8,128)(2,1)S(1)} collective-permute-done((bf16[704,128]{1,0:T(8,128)(2,1)S(1)}, bf16[704,128]{1,0:T(8,128)(2,1)S(1)}, u32[]{:S(2)}, u32[]{:S(2)}) %collective-permute-start.3) | collective-permute-done | bytes 180256 | tf_op jit(solution)/shard_map/ppermute | solution.py:214
  13.9 2.0 %collective-permute-done.4.two = bf16[704,128]{1,0:T(8,128)(2,1)S(1)} collective-permute-done((bf16[704,128]{1,0:T(8,128)(2,1)S(1)}, bf16[704,128]{1,0:T(8,128)(2,1)S(1)}, u32[]{:S(2)}, u32[]{:S(2)}) %collective-permute-start.4) | collective-permute-done | bytes 180256 | tf_op jit(solution)/shard_map/ppermute | solution.py:214
  16.0 0.5 %collective-permute-done.5.one = bf16[704,128]{1,0:T(8,128)(2,1)S(1)} collective-permute-done((bf16[704,128]{1,0:T(8,128)(2,1)S(1)}, bf16[704,128]{1,0:T(8,128)(2,1)S(1)}, u32[]{:S(2)}, u32[]{:S(2)}) %collective-permute-start.5) | collective-permute-done | bytes 180256 | tf_op jit(solution)/shard_map/ppermute | solution.py:214
  16.5 0.1 shard_map.89.own
  16.6 3.7 %collective-permute-start.8 = (bf16[704,128]{1,0:T(8,128)(2,1)S(1)}, bf16[704,128]{1,0:T(8,128)(2,1)S(1)}, u32[]{:S(2)}, u32[]{:S(2)}) collective-permute-start(bf16[704,128]{1,0:T(8,128)(2,1)S(1)} %shard_map.89.own), channel_id=1, source_target_pairs={{0,24},{1,7},{2,26},{3,5},{4,28},{5,3},{6,30},{7,1},{8,16},{9,15},... | collective-permute-start | bytes 540680 | tf_op jit(solution)/shard_map/ppermute | solution.py:214
  20.2 0.8 %collective-permute-start.6 = (bf16[704,128]{1,0:T(8,128)(2,1)S(1)}, bf16[704,128]{1,0:T(8,128)(2,1)S(1)}, u32[]{:S(2)}, u32[]{:S(2)}) collective-permute-start(bf16[704,128]{1,0:T(8,128)(2,1)S(1)} %shard_map.89.own), channel_id=1, source_target_pairs={{0,8},{1,3},{2,10},{3,1},{4,12},{5,7},{6,14},{7,5},{8,0},{9,11},{1... | collective-permute-start | bytes 540680 | tf_op jit(solution)/shard_map/ppermute | solution.py:214
  21.0 2.5 %shard_map.86 = (bf16[8,96,256]{2,1,0:T(8,128)(2,1)}, bf16[4,48,256]{2,1,0:T(8,128)(2,1)}) custom-call(bf16[8,96,256]{2,1,0:T(8,128)(2,1)S(1)} %bitcast.10, bf16[9,256,256]{2,1,0:T(8,128)(2,1)S(1)} %get-tuple-element.22.out_w, bf16[768,256]{1,0:T(8,128)(2,1)S(1)} %get-tuple-element.25.grad, bf16[8,96,256]{2,1,0:T(8,128)(2,1)S(1)} %collective-permute-done.1.refs_0_.refs_1_, ...), custom_call_target="tpu_custom_call" | custom-call | flops 905969664 | bytes 2097152 | tf_op jit(solution)/shard_map/pallas_call | solution.py:324
  23.5 0.5 %collective-permute-done.8.three = bf16[704,128]{1,0:T(8,128)(2,1)S(1)} collective-permute-done((bf16[704,128]{1,0:T(8,128)(2,1)S(1)}, bf16[704,128]{1,0:T(8,128)(2,1)S(1)}, u32[]{:S(2)}, u32[]{:S(2)}) %collective-permute-start.8) | collective-permute-done | bytes 180256 | tf_op jit(solution)/shard_map/ppermute | solution.py:214
  24.0 4.9 %collective-permute-done.7.two = bf16[704,128]{1,0:T(8,128)(2,1)S(1)} collective-permute-done((bf16[704,128]{1,0:T(8,128)(2,1)S(1)}, bf16[704,128]{1,0:T(8,128)(2,1)S(1)}, u32[]{:S(2)}, u32[]{:S(2)}) %collective-permute-start.7) | collective-permute-done | bytes 180256 | tf_op jit(solution)/shard_map/ppermute | solution.py:214
  28.9 0.1 shard_map.90.refs_0_
  29.0 2.0 %collective-permute-start.13 = (bf16[704,128]{1,0:T(8,128)(2,1)S(1)}, bf16[704,128]{1,0:T(8,128)(2,1)S(1)}, u32[]{:S(2)}, u32[]{:S(2)}) collective-permute-start(bf16[704,128]{1,0:T(8,128)(2,1)S(1)} %shard_map.90.refs_0_), channel_id=1, source_target_pairs={{0,6},{1,25},{2,4},{3,27},{4,2},{5,29},{6,0},{7,31},{8,14},{9,17},... | collective-permute-start | bytes 540680 | tf_op jit(solution)/shard_map/ppermute | solution.py:214
  31.0 1.0 %collective-permute-start.11 = (bf16[704,128]{1,0:T(8,128)(2,1)S(1)}, bf16[704,128]{1,0:T(8,128)(2,1)S(1)}, u32[]{:S(2)}, u32[]{:S(2)}) collective-permute-start(bf16[704,128]{1,0:T(8,128)(2,1)S(1)} %shard_map.90.refs_0_), channel_id=1, source_target_pairs={{0,4},{1,17},{2,6},{3,19},{4,0},{5,21},{6,2},{7,23},{8,12},{9,25},... | collective-permute-start | bytes 540680 | tf_op jit(solution)/shard_map/ppermute | solution.py:214
  32.0 0.6 %collective-permute-start.9 = (bf16[704,128]{1,0:T(8,128)(2,1)S(1)}, bf16[704,128]{1,0:T(8,128)(2,1)S(1)}, u32[]{:S(2)}, u32[]{:S(2)}) collective-permute-start(bf16[704,128]{1,0:T(8,128)(2,1)S(1)} %shard_map.90.refs_0_), channel_id=1, source_target_pairs={{0,2},{1,9},{2,0},{3,11},{4,6},{5,13},{6,4},{7,15},{8,10},{9,1},{1... | collective-permute-start | bytes 540680 | tf_op jit(solution)/shard_map/ppermute | solution.py:214
  32.6 0.0 collective-permute-start.15
  32.6 3.0 %collective-permute-done.13.refs_3_ = bf16[704,128]{1,0:T(8,128)(2,1)S(1)} collective-permute-done((bf16[704,128]{1,0:T(8,128)(2,1)S(1)}, bf16[704,128]{1,0:T(8,128)(2,1)S(1)}, u32[]{:S(2)}, u32[]{:S(2)}) %collective-permute-start.13) | collective-permute-done | bytes 180256 | tf_op jit(solution)/shard_map/ppermute | solution.py:214
  35.6 1.8 %collective-permute-done.11.refs_2_ = bf16[704,128]{1,0:T(8,128)(2,1)S(1)} collective-permute-done((bf16[704,128]{1,0:T(8,128)(2,1)S(1)}, bf16[704,128]{1,0:T(8,128)(2,1)S(1)}, u32[]{:S(2)}, u32[]{:S(2)}) %collective-permute-start.11) | collective-permute-done | bytes 180256 | tf_op jit(solution)/shard_map/ppermute | solution.py:214
  37.4 0.4 %collective-permute-start.12 = (bf16[704,128]{1,0:T(8,128)(2,1)S(1)}, bf16[704,128]{1,0:T(8,128)(2,1)S(1)}, u32[]{:S(2)}, u32[]{:S(2)}) collective-permute-start(bf16[704,128]{1,0:T(8,128)(2,1)S(1)} %collective-permute-done.11.refs_2_), channel_id=1, source_target_pairs={{0,1},{1,0},{2,3},{3,2},{4,5},{5,4},{6,7},{7,6},{8,9},{9,8},{10,11... | collective-permute-start | bytes 540680 | tf_op jit(solution)/shard_map/ppermute | solution.py:218
  37.8 0.1 collective-permute-start.10
  37.9 1.0 %shard_map.91 = (bf16[2304,256]{1,0:T(8,128)(2,1)}, bf16[512,256]{1,0:T(8,128)(2,1)}) custom-call(bf16[704,128]{1,0:T(8,128)(2,1)S(1)} %shard_map.90.refs_0_, bf16[704,128]{1,0:T(8,128)(2,1)S(1)} %collective-permute-done.9.refs_1_, bf16[704,128]{1,0:T(8,128)(2,1)S(1)} %collective-permute-done.11.refs_2_, ...), custom_call_target="tpu_custom_call" | custom-call | tf_op jit(solution)/shard_map/pallas_call | solution.py:247
  38.9 0.3 collective-permute-done.10.refs_0_
  39.3 0.9 %shard_map.92 = (bf16[2304,256]{1,0:T(8,128)(2,1)}, bf16[512,256]{1,0:T(8,128)(2,1)}) custom-call(bf16[704,128]{1,0:T(8,128)(2,1)S(1)} %collective-permute-done.10.refs_0_, bf16[704,128]{1,0:T(8,128)(2,1)S(1)} %collective-permute-done.12.refs_1_, bf16[704,128]{1,0:T(8,128)(2,1)S(1)} %collective-permute-done.14.refs_2_, ...), custom_call_target="tpu_custom_call", output_to_operand_aliasing={{0}: (3, {}), {1}: (4, {})} | custom-call | tf_op jit(solution)/shard_map/pallas_call | solution.py:250
  (9 shorter events, 0.0 us)
Async XLA Ops:
  0.6 2.5 %collective-permute-start = (bf16[8,96,256]{2,1,0:T(8,128)(2,1)}, bf16[8,96,256]{2,1,0:T(8,128)(2,1)S(1)}, u32[]{:S(2)}, u32[]{:S(2)}) collective-permute-start(bf16[8,96,256]{2,1,0:T(8,128)(2,1)} %bitcast.16), channel_id=1, source_target_pairs={{0,1},{1,0},{2,3},{3,2},{4,5},{5,4},{6,7},{7,6},{8,9},{9,8},{10,11... | collective-permute-start | bytes 1179656 | tf_op jit(solution)/shard_map/ppermute | solution.py:19
  3.0 2.4 %collective-permute-start.1 = (bf16[8,96,256]{2,1,0:T(8,128)(2,1)S(1)}, bf16[8,96,256]{2,1,0:T(8,128)(2,1)S(1)}, u32[]{:S(2)}, u32[]{:S(2)}) collective-permute-start(bf16[8,96,256]{2,1,0:T(8,128)(2,1)S(1)} %bitcast.9), channel_id=1, source_target_pairs={{0,1},{1,0},{2,3},{3,2},{4,5},{5,4},{6,7},{7,6},{8,9},{9,8},{10,11... | collective-permute-start | bytes 1179656 | tf_op jit(solution)/shard_map/ppermute | solution.py:19
  4.8 2.0 %collective-permute-start.2 = (bf16[512,128]{1,0:T(8,128)(2,1)S(1)}, bf16[512,128]{1,0:T(8,128)(2,1)S(1)}, u32[]{:S(2)}, u32[]{:S(2)}) collective-permute-start(bf16[512,128]{1,0:T(8,128)(2,1)S(1)} %get-tuple-element.29), channel_id=1, source_target_pairs={{0,1},{1,0},{2,3},{3,2},{4,5},{5,4},{6,7},{7,6},{8,9},{9,8},{10,11... | collective-permute-start | bytes 393224 | tf_op jit(solution)/shard_map/ppermute | solution.py:218
  6.9 7.0 %collective-permute-start.3 = (bf16[704,128]{1,0:T(8,128)(2,1)S(1)}, bf16[704,128]{1,0:T(8,128)(2,1)S(1)}, u32[]{:S(2)}, u32[]{:S(2)}) collective-permute-start(bf16[704,128]{1,0:T(8,128)(2,1)S(1)} %get-tuple-element.31), channel_id=1, source_target_pairs={{0,6},{1,25},{2,4},{3,27},{4,2},{5,29},{6,0},{7,31},{8,14},{9,17},... | collective-permute-start | bytes 540680 | tf_op jit(solution)/shard_map/ppermute | solution.py:214
  10.5 5.5 %collective-permute-start.4 = (bf16[704,128]{1,0:T(8,128)(2,1)S(1)}, bf16[704,128]{1,0:T(8,128)(2,1)S(1)}, u32[]{:S(2)}, u32[]{:S(2)}) collective-permute-start(bf16[704,128]{1,0:T(8,128)(2,1)S(1)} %get-tuple-element.32), channel_id=1, source_target_pairs={{0,4},{1,17},{2,6},{3,19},{4,0},{5,21},{6,2},{7,23},{8,12},{9,25},... | collective-permute-start | bytes 540680 | tf_op jit(solution)/shard_map/ppermute | solution.py:214
  11.0 5.5 %collective-permute-start.5 = (bf16[704,128]{1,0:T(8,128)(2,1)S(1)}, bf16[704,128]{1,0:T(8,128)(2,1)S(1)}, u32[]{:S(2)}, u32[]{:S(2)}) collective-permute-start(bf16[704,128]{1,0:T(8,128)(2,1)S(1)} %get-tuple-element.33), channel_id=1, source_target_pairs={{0,2},{1,9},{2,0},{3,11},{4,6},{5,13},{6,4},{7,15},{8,10},{9,1},{1... | collective-permute-start | bytes 540680 | tf_op jit(solution)/shard_map/ppermute | solution.py:214
  16.6 7.5 %collective-permute-start.8 = (bf16[704,128]{1,0:T(8,128)(2,1)S(1)}, bf16[704,128]{1,0:T(8,128)(2,1)S(1)}, u32[]{:S(2)}, u32[]{:S(2)}) collective-permute-start(bf16[704,128]{1,0:T(8,128)(2,1)S(1)} %shard_map.89.own), channel_id=1, source_target_pairs={{0,24},{1,7},{2,26},{3,5},{4,28},{5,3},{6,30},{7,1},{8,16},{9,15},... | collective-permute-start | bytes 540680 | tf_op jit(solution)/shard_map/ppermute | solution.py:214
  20.2 8.7 %collective-permute-start.7 = (bf16[704,128]{1,0:T(8,128)(2,1)S(1)}, bf16[704,128]{1,0:T(8,128)(2,1)S(1)}, u32[]{:S(2)}, u32[]{:S(2)}) collective-permute-start(bf16[704,128]{1,0:T(8,128)(2,1)S(1)} %shard_map.89.own), channel_id=1, source_target_pairs={{0,16},{1,5},{2,18},{3,7},{4,20},{5,1},{6,22},{7,3},{8,24},{9,13},... | collective-permute-start | bytes 540680 | tf_op jit(solution)/shard_map/ppermute | solution.py:214
  20.2 8.7 %collective-permute-start.6 = (bf16[704,128]{1,0:T(8,128)(2,1)S(1)}, bf16[704,128]{1,0:T(8,128)(2,1)S(1)}, u32[]{:S(2)}, u32[]{:S(2)}) collective-permute-start(bf16[704,128]{1,0:T(8,128)(2,1)S(1)} %shard_map.89.own), channel_id=1, source_target_pairs={{0,8},{1,3},{2,10},{3,1},{4,12},{5,7},{6,14},{7,5},{8,0},{9,11},{1... | collective-permute-start | bytes 540680 | tf_op jit(solution)/shard_map/ppermute | solution.py:214
  29.0 6.6 %collective-permute-start.13 = (bf16[704,128]{1,0:T(8,128)(2,1)S(1)}, bf16[704,128]{1,0:T(8,128)(2,1)S(1)}, u32[]{:S(2)}, u32[]{:S(2)}) collective-permute-start(bf16[704,128]{1,0:T(8,128)(2,1)S(1)} %shard_map.90.refs_0_), channel_id=1, source_target_pairs={{0,6},{1,25},{2,4},{3,27},{4,2},{5,29},{6,0},{7,31},{8,14},{9,17},... | collective-permute-start | bytes 540680 | tf_op jit(solution)/shard_map/ppermute | solution.py:214
  31.0 6.4 %collective-permute-start.11 = (bf16[704,128]{1,0:T(8,128)(2,1)S(1)}, bf16[704,128]{1,0:T(8,128)(2,1)S(1)}, u32[]{:S(2)}, u32[]{:S(2)}) collective-permute-start(bf16[704,128]{1,0:T(8,128)(2,1)S(1)} %shard_map.90.refs_0_), channel_id=1, source_target_pairs={{0,4},{1,17},{2,6},{3,19},{4,0},{5,21},{6,2},{7,23},{8,12},{9,25},... | collective-permute-start | bytes 540680 | tf_op jit(solution)/shard_map/ppermute | solution.py:214
  32.0 5.8 %collective-permute-start.9 = (bf16[704,128]{1,0:T(8,128)(2,1)S(1)}, bf16[704,128]{1,0:T(8,128)(2,1)S(1)}, u32[]{:S(2)}, u32[]{:S(2)}) collective-permute-start(bf16[704,128]{1,0:T(8,128)(2,1)S(1)} %shard_map.90.refs_0_), channel_id=1, source_target_pairs={{0,2},{1,9},{2,0},{3,11},{4,6},{5,13},{6,4},{7,15},{8,10},{9,1},{1... | collective-permute-start | bytes 540680 | tf_op jit(solution)/shard_map/ppermute | solution.py:214
  32.6 5.4 %collective-permute-start.15 = (bf16[704,128]{1,0:T(8,128)(2,1)S(1)}, bf16[704,128]{1,0:T(8,128)(2,1)S(1)}, u32[]{:S(2)}, u32[]{:S(2)}) collective-permute-start(bf16[704,128]{1,0:T(8,128)(2,1)S(1)} %shard_map.90.refs_0_), channel_id=1, source_target_pairs={{0,1},{1,0},{2,3},{3,2},{4,5},{5,4},{6,7},{7,6},{8,9},{9,8},{10,11... | collective-permute-start | bytes 540680 | tf_op jit(solution)/shard_map/ppermute | solution.py:218
  35.6 3.3 %collective-permute-start.14 = (bf16[704,128]{1,0:T(8,128)(2,1)S(1)}, bf16[704,128]{1,0:T(8,128)(2,1)S(1)}, u32[]{:S(2)}, u32[]{:S(2)}) collective-permute-start(bf16[704,128]{1,0:T(8,128)(2,1)S(1)} %collective-permute-done.13.refs_3_), channel_id=1, source_target_pairs={{0,1},{1,0},{2,3},{3,2},{4,5},{5,4},{6,7},{7,6},{8,9},{9,8},{10,11... | collective-permute-start | bytes 540680 | tf_op jit(solution)/shard_map/ppermute | solution.py:218
  37.4 1.5 %collective-permute-start.12 = (bf16[704,128]{1,0:T(8,128)(2,1)S(1)}, bf16[704,128]{1,0:T(8,128)(2,1)S(1)}, u32[]{:S(2)}, u32[]{:S(2)}) collective-permute-start(bf16[704,128]{1,0:T(8,128)(2,1)S(1)} %collective-permute-done.11.refs_2_), channel_id=1, source_target_pairs={{0,1},{1,0},{2,3},{3,2},{4,5},{5,4},{6,7},{7,6},{8,9},{9,8},{10,11... | collective-permute-start | bytes 540680 | tf_op jit(solution)/shard_map/ppermute | solution.py:218
  37.8 1.4 %collective-permute-start.10 = (bf16[704,128]{1,0:T(8,128)(2,1)S(1)}, bf16[704,128]{1,0:T(8,128)(2,1)S(1)}, u32[]{:S(2)}, u32[]{:S(2)}) collective-permute-start(bf16[704,128]{1,0:T(8,128)(2,1)S(1)} %collective-permute-done.9.refs_1_), channel_id=1, source_target_pairs={{0,1},{1,0},{2,3},{3,2},{4,5},{5,4},{6,7},{7,6},{8,9},{9,8},{10,11... | collective-permute-start | bytes 540680 | tf_op jit(solution)/shard_map/ppermute | solution.py:218

commit v21 on v19

--- a/solution.py
+++ b/solution.py
@@ -180,7 +180,7 @@
     out[...] = total.astype(BF16)
 
 
-def finish_kernel(scale, own, three, two, one, _, out):
+def finish_kernel(scale, own, one, two, three, _, out):
     near = own[...].astype(F32) + one[...].astype(F32)
     far = two[...].astype(F32) + three[...].astype(F32)
     out[...] = ((near + far) * scale).astype(BF16)
@@ -237,7 +237,7 @@
     [total] = call(add_kernel, (quarter, BF16))(own, three, two, one)
     three, two, one = [exchange(total, 1, k) for k in (3, 2, 1)]
     finish = call(functools.partial(finish_kernel, scale), (quarter, BF16), in_specs=[vmem] * 4 + [far])
-    [total] = finish(total, three, two, one, after)
+    [total] = finish(total, one, two, three, after)
     three, two, one = [exchange(total, 0, k) for k in (3, 2, 1)]
     quarters = [total, three, two, one]
     results = [((length, 2 * width), BF16) for length in lengths]

time: 40 us -> 40.4 us (1.010)
  waiting for transfers between devices: 13.9 us -> 15.2 us
  starting transfers between devices: 15.6 us -> 14.7 us
    ppermute x9, waiting for transfers between devices: 13.5 us -> 14.8 us  [exchange(): return lax.ppermute(array, ('dp', 'space'), pairs)]
    ppermute x5, starting transfers between devices: 2.75 us -> 1.89 us  [swap(): return lax.ppermute(array, 'space', [(0, 1), (1, 0)])]
  transfers between devices with their start and end apart: 16 -> 16, of which waited for: 7 -> 9; matrix products, arithmetic and copies ran while one was open for 0% -> 0% of each run, Pallas kernels for 21% -> 21%
where the time goes in v21:
time: 40.4 us; the launch traced here: 40.3 us
  waiting for transfers between devices  15.2 us (38%)
  starting transfers between devices  14.7 us (36%)
  Pallas kernels  9.67 us (24%)
  between operations  0.72 us (2%)
    ppermute x9, waiting for transfers between devices, exchange(): return lax.ppermute(array, ('dp', 'space'), pairs)  14.8 us
    ppermute x9, starting transfers between devices, exchange(): return lax.ppermute(array, ('dp', 'space'), pairs)  12.2 us
    pallas_call x1, Pallas kernels, local(): pl.pallas_call(functools.partial(forward_kernel, peers), out_shape=[jax.S...  2.53 us
    ppermute x5, starting transfers between devices, swap(): return lax.ppermute(array, 'space', [(0, 1), (1, 0)])  1.89 us
    pallas_call x2, Pallas kernels, sum_everywhere(): call(functools.partial(place_kernel, plan), *results, **place)  1.86 us
    pallas_call x1, Pallas kernels, local(): pl.pallas_call(merge_kernel, out_shape=[jax.ShapeDtypeStruct(shape, BF16)...  1.83 us
    pallas_call x1, Pallas kernels, local(): pl.pallas_call(functools.partial(data_grad_kernel, peers), out_shape=[jax...  1.7 us
    pallas_call x1, Pallas kernels, local(): pl.pallas_call(pair_kernel_grad_kernel, out_shape=jax.ShapeDtypeStruct((9...  1.45 us
  transfers between devices with their start and end apart: 16, of which 9 were waited for; matrix products, arithmetic and copies ran while one was open for 0% of the time, Pallas kernels for 21%

profile of v21, /device:TPU:0, one launch (start us, length us, event | category | flops | bytes accessed | tf_op | source)
XLA Modules:
  0.0 40.3 jit_solution(8843799129280530463)
XLA Ops:
  0.6 0.5 %collective-permute-start = (bf16[8,96,256]{2,1,0:T(8,128)(2,1)}, bf16[8,96,256]{2,1,0:T(8,128)(2,1)S(1)}, u32[]{:S(2)}, u32[]{:S(2)}) collective-permute-start(bf16[8,96,256]{2,1,0:T(8,128)(2,1)} %bitcast.16), channel_id=1, source_target_pairs={{0,1},{1,0},{2,3},{3,2},{4,5},{5,4},{6,7},{7,6},{8,9},{9,8},{10,11... | collective-permute-start | bytes 1179656 | tf_op jit(solution)/shard_map/ppermute | solution.py:19
  1.1 1.8 %shard_map.84 = (bf16[768,256]{1,0:T(8,128)(2,1)S(1)}, bf16[8,96,768]{2,1,0:T(8,128)(2,1)S(1)}, bf16[768,512]{1,0:T(8,128)(2,1)S(1)}, bf16[9,256,256]{2,1,0:T(8,128)(2,1)S(1)}) custom-call(bf16[8,96,256]{2,1,0:T(8,128)(2,1)} %bitcast.17, bf16[512,256]{1,0:T(8,128)(2,1)} %refs_1_.1, bf16[4,48,256]{2,1,0:T(8,128)(2,1)} %bitcast.18, bf16[768,512]{1,0:T(8,128)(2,1)} %bitcast.15, ...), custom_call_target="tpu_custom_call" | custom-call | flops 805306368 | bytes 4194304 | tf_op jit(solution)/shard_map/pallas_call | solution.py:273
  3.0 0.1 collective-permute-start.1
  3.1 1.7 %shard_map.85 = (bf16[768,256]{1,0:T(8,128)(2,1)S(1)}, bf16[2,96,768]{2,1,0:T(8,128)(2,1)}, f32[512,128]{1,0:T(8,128)S(1)}, bf16[512,128]{1,0:T(8,128)(2,1)S(1)}) custom-call(bf16[8,96,768]{2,1,0:T(8,128)(2,1)S(1)} %get-tuple-element.23.stack, bf16[8,96,256]{2,1,0:T(8,128)(2,1)S(1)} %collective-permute-done.before.after.cot, ...), custom_call_target="tpu_custom_call" | custom-call | flops 1107296256 | bytes 4194304 | tf_op jit(solution)/shard_map/pallas_call | solution.py:293
  4.8 0.5 %collective-permute-start.2 = (bf16[512,128]{1,0:T(8,128)(2,1)S(1)}, bf16[512,128]{1,0:T(8,128)(2,1)S(1)}, u32[]{:S(2)}, u32[]{:S(2)}) collective-permute-start(bf16[512,128]{1,0:T(8,128)(2,1)S(1)} %get-tuple-element.29), channel_id=1, source_target_pairs={{0,1},{1,0},{2,3},{3,2},{4,5},{5,4},{6,7},{7,6},{8,9},{9,8},{10,11... | collective-permute-start | bytes 393224 | tf_op jit(solution)/shard_map/ppermute | solution.py:218
  5.3 0.0 collective-permute-done.1.refs_0_.refs_1_
  5.4 1.5 %shard_map.87.kernel_sums = f32[2304,128]{1,0:T(8,128)S(1)} custom-call(bf16[8,96,768]{2,1,0:T(8,128)(2,1)S(1)} %get-tuple-element.23.stack, bf16[768,256]{1,0:T(8,128)(2,1)S(1)} %get-tuple-element.21.merged, bf16[8,96,256]{2,1,0:T(8,128)(2,1)S(1)} %collective-permute-done.before.after.cot, bf16[768,256]{1,0:T(8,128)(2,1)S(1)} %bitcast.11), custom_call_target="tpu_custom_call" | custom-call | flops 905969664 | bytes 4194304 | tf_op jit(solution)/shard_map/pallas_call | solution.py:310
  6.8 0.0 collective-permute-done.2.got
  6.8 0.1 shard_map.88
  6.9 3.5 %collective-permute-start.3 = (bf16[704,128]{1,0:T(8,128)(2,1)S(1)}, bf16[704,128]{1,0:T(8,128)(2,1)S(1)}, u32[]{:S(2)}, u32[]{:S(2)}) collective-permute-start(bf16[704,128]{1,0:T(8,128)(2,1)S(1)} %get-tuple-element.31), channel_id=1, source_target_pairs={{0,6},{1,25},{2,4},{3,27},{4,2},{5,29},{6,0},{7,31},{8,14},{9,17},... | collective-permute-start | bytes 540680 | tf_op jit(solution)/shard_map/ppermute | solution.py:214
  10.5 0.5 %collective-permute-start.4 = (bf16[704,128]{1,0:T(8,128)(2,1)S(1)}, bf16[704,128]{1,0:T(8,128)(2,1)S(1)}, u32[]{:S(2)}, u32[]{:S(2)}) collective-permute-start(bf16[704,128]{1,0:T(8,128)(2,1)S(1)} %get-tuple-element.32), channel_id=1, source_target_pairs={{0,4},{1,17},{2,6},{3,19},{4,0},{5,21},{6,2},{7,23},{8,12},{9,25},... | collective-permute-start | bytes 540680 | tf_op jit(solution)/shard_map/ppermute | solution.py:214
  11.0 0.1 collective-permute-start.5
  11.1 2.8 %collective-permute-done.3.three = bf16[704,128]{1,0:T(8,128)(2,1)S(1)} collective-permute-done((bf16[704,128]{1,0:T(8,128)(2,1)S(1)}, bf16[704,128]{1,0:T(8,128)(2,1)S(1)}, u32[]{:S(2)}, u32[]{:S(2)}) %collective-permute-start.3) | collective-permute-done | bytes 180256 | tf_op jit(solution)/shard_map/ppermute | solution.py:214
  13.9 2.0 %collective-permute-done.4.two = bf16[704,128]{1,0:T(8,128)(2,1)S(1)} collective-permute-done((bf16[704,128]{1,0:T(8,128)(2,1)S(1)}, bf16[704,128]{1,0:T(8,128)(2,1)S(1)}, u32[]{:S(2)}, u32[]{:S(2)}) %collective-permute-start.4) | collective-permute-done | bytes 180256 | tf_op jit(solution)/shard_map/ppermute | solution.py:214
  16.0 0.5 %collective-permute-done.5.one = bf16[704,128]{1,0:T(8,128)(2,1)S(1)} collective-permute-done((bf16[704,128]{1,0:T(8,128)(2,1)S(1)}, bf16[704,128]{1,0:T(8,128)(2,1)S(1)}, u32[]{:S(2)}, u32[]{:S(2)}) %collective-permute-start.5) | collective-permute-done | bytes 180256 | tf_op jit(solution)/shard_map/ppermute | solution.py:214
  16.5 0.1 shard_map.89.own
  16.6 3.7 %collective-permute-start.8 = (bf16[704,128]{1,0:T(8,128)(2,1)S(1)}, bf16[704,128]{1,0:T(8,128)(2,1)S(1)}, u32[]{:S(2)}, u32[]{:S(2)}) collective-permute-start(bf16[704,128]{1,0:T(8,128)(2,1)S(1)} %shard_map.89.own), channel_id=1, source_target_pairs={{0,24},{1,7},{2,26},{3,5},{4,28},{5,3},{6,30},{7,1},{8,16},{9,15},... | collective-permute-start | bytes 540680 | tf_op jit(solution)/shard_map/ppermute | solution.py:214
  20.2 0.8 %collective-permute-start.6 = (bf16[704,128]{1,0:T(8,128)(2,1)S(1)}, bf16[704,128]{1,0:T(8,128)(2,1)S(1)}, u32[]{:S(2)}, u32[]{:S(2)}) collective-permute-start(bf16[704,128]{1,0:T(8,128)(2,1)S(1)} %shard_map.89.own), channel_id=1, source_target_pairs={{0,8},{1,3},{2,10},{3,1},{4,12},{5,7},{6,14},{7,5},{8,0},{9,11},{1... | collective-permute-start | bytes 540680 | tf_op jit(solution)/shard_map/ppermute | solution.py:214
  21.0 2.5 %shard_map.86 = (bf16[8,96,256]{2,1,0:T(8,128)(2,1)}, bf16[4,48,256]{2,1,0:T(8,128)(2,1)}) custom-call(bf16[8,96,256]{2,1,0:T(8,128)(2,1)S(1)} %bitcast.10, bf16[9,256,256]{2,1,0:T(8,128)(2,1)S(1)} %get-tuple-element.22.out_w, bf16[768,256]{1,0:T(8,128)(2,1)S(1)} %get-tuple-element.25.grad, bf16[8,96,256]{2,1,0:T(8,128)(2,1)S(1)} %collective-permute-done.1.refs_0_.refs_1_, ...), custom_call_target="tpu_custom_call" | custom-call | flops 905969664 | bytes 2097152 | tf_op jit(solution)/shard_map/pallas_call | solution.py:324
  23.5 0.5 %collective-permute-done.8.three = bf16[704,128]{1,0:T(8,128)(2,1)S(1)} collective-permute-done((bf16[704,128]{1,0:T(8,128)(2,1)S(1)}, bf16[704,128]{1,0:T(8,128)(2,1)S(1)}, u32[]{:S(2)}, u32[]{:S(2)}) %collective-permute-start.8) | collective-permute-done | bytes 180256 | tf_op jit(solution)/shard_map/ppermute | solution.py:214
  24.0 4.9 %collective-permute-done.7.two = bf16[704,128]{1,0:T(8,128)(2,1)S(1)} collective-permute-done((bf16[704,128]{1,0:T(8,128)(2,1)S(1)}, bf16[704,128]{1,0:T(8,128)(2,1)S(1)}, u32[]{:S(2)}, u32[]{:S(2)}) %collective-permute-start.7) | collective-permute-done | bytes 180256 | tf_op jit(solution)/shard_map/ppermute | solution.py:214
  28.9 0.1 shard_map.90.refs_0_
  29.0 1.5 %collective-permute-start.13 = (bf16[704,128]{1,0:T(8,128)(2,1)S(1)}, bf16[704,128]{1,0:T(8,128)(2,1)S(1)}, u32[]{:S(2)}, u32[]{:S(2)}) collective-permute-start(bf16[704,128]{1,0:T(8,128)(2,1)S(1)} %shard_map.90.refs_0_), channel_id=1, source_target_pairs={{0,2},{1,9},{2,0},{3,11},{4,6},{5,13},{6,4},{7,15},{8,10},{9,1},{1... | collective-permute-start | bytes 540680 | tf_op jit(solution)/shard_map/ppermute | solution.py:214
  30.6 1.0 %collective-permute-start.11 = (bf16[704,128]{1,0:T(8,128)(2,1)S(1)}, bf16[704,128]{1,0:T(8,128)(2,1)S(1)}, u32[]{:S(2)}, u32[]{:S(2)}) collective-permute-start(bf16[704,128]{1,0:T(8,128)(2,1)S(1)} %shard_map.90.refs_0_), channel_id=1, source_target_pairs={{0,4},{1,17},{2,6},{3,19},{4,0},{5,21},{6,2},{7,23},{8,12},{9,25},... | collective-permute-start | bytes 540680 | tf_op jit(solution)/shard_map/ppermute | solution.py:214
  31.6 1.0 %collective-permute-start.9 = (bf16[704,128]{1,0:T(8,128)(2,1)S(1)}, bf16[704,128]{1,0:T(8,128)(2,1)S(1)}, u32[]{:S(2)}, u32[]{:S(2)}) collective-permute-start(bf16[704,128]{1,0:T(8,128)(2,1)S(1)} %shard_map.90.refs_0_), channel_id=1, source_target_pairs={{0,6},{1,25},{2,4},{3,27},{4,2},{5,29},{6,0},{7,31},{8,14},{9,17},... | collective-permute-start | bytes 540680 | tf_op jit(solution)/shard_map/ppermute | solution.py:214
  32.6 2.0 %collective-permute-done.13.refs_3_ = bf16[704,128]{1,0:T(8,128)(2,1)S(1)} collective-permute-done((bf16[704,128]{1,0:T(8,128)(2,1)S(1)}, bf16[704,128]{1,0:T(8,128)(2,1)S(1)}, u32[]{:S(2)}, u32[]{:S(2)}) %collective-permute-start.13) | collective-permute-done | bytes 180256 | tf_op jit(solution)/shard_map/ppermute | solution.py:214
  34.6 1.5 %collective-permute-done.11.refs_2_ = bf16[704,128]{1,0:T(8,128)(2,1)S(1)} collective-permute-done((bf16[704,128]{1,0:T(8,128)(2,1)S(1)}, bf16[704,128]{1,0:T(8,128)(2,1)S(1)}, u32[]{:S(2)}, u32[]{:S(2)}) %collective-permute-start.11) | collective-permute-done | bytes 180256 | tf_op jit(solution)/shard_map/ppermute | solution.py:214
  36.1 1.4 %collective-permute-start.12 = (bf16[704,128]{1,0:T(8,128)(2,1)S(1)}, bf16[704,128]{1,0:T(8,128)(2,1)S(1)}, u32[]{:S(2)}, u32[]{:S(2)}) collective-permute-start(bf16[704,128]{1,0:T(8,128)(2,1)S(1)} %collective-permute-done.11.refs_2_), channel_id=1, source_target_pairs={{0,1},{1,0},{2,3},{3,2},{4,5},{5,4},{6,7},{7,6},{8,9},{9,8},{10,11... | collective-permute-start | bytes 540680 | tf_op jit(solution)/shard_map/ppermute | solution.py:218
  37.4 0.6 %collective-permute-done.9.refs_1_ = bf16[704,128]{1,0:T(8,128)(2,1)S(1)} collective-permute-done((bf16[704,128]{1,0:T(8,128)(2,1)S(1)}, bf16[704,128]{1,0:T(8,128)(2,1)S(1)}, u32[]{:S(2)}, u32[]{:S(2)}) %collective-permute-start.9) | collective-permute-done | bytes 180256 | tf_op jit(solution)/shard_map/ppermute | solution.py:214
  38.0 1.0 %shard_map.91 = (bf16[2304,256]{1,0:T(8,128)(2,1)}, bf16[512,256]{1,0:T(8,128)(2,1)}) custom-call(bf16[704,128]{1,0:T(8,128)(2,1)S(1)} %shard_map.90.refs_0_, bf16[704,128]{1,0:T(8,128)(2,1)S(1)} %collective-permute-done.9.refs_1_, bf16[704,128]{1,0:T(8,128)(2,1)S(1)} %collective-permute-done.11.refs_2_, ...), custom_call_target="tpu_custom_call" | custom-call | tf_op jit(solution)/shard_map/pallas_call | solution.py:247
  39.0 0.4 collective-permute-done.10.refs_0_
  39.4 0.9 %shard_map.92 = (bf16[2304,256]{1,0:T(8,128)(2,1)}, bf16[512,256]{1,0:T(8,128)(2,1)}) custom-call(bf16[704,128]{1,0:T(8,128)(2,1)S(1)} %collective-permute-done.10.refs_0_, bf16[704,128]{1,0:T(8,128)(2,1)S(1)} %collective-permute-done.12.refs_1_, bf16[704,128]{1,0:T(8,128)(2,1)S(1)} %collective-permute-done.14.refs_2_, ...), custom_call_target="tpu_custom_call", output_to_operand_aliasing={{0}: (3, {}), {1}: (4, {})} | custom-call | tf_op jit(solution)/shard_map/pallas_call | solution.py:250
  (9 shorter events, 0.0 us)
Async XLA Ops:
  0.6 2.5 %collective-permute-start = (bf16[8,96,256]{2,1,0:T(8,128)(2,1)}, bf16[8,96,256]{2,1,0:T(8,128)(2,1)S(1)}, u32[]{:S(2)}, u32[]{:S(2)}) collective-permute-start(bf16[8,96,256]{2,1,0:T(8,128)(2,1)} %bitcast.16), channel_id=1, source_target_pairs={{0,1},{1,0},{2,3},{3,2},{4,5},{5,4},{6,7},{7,6},{8,9},{9,8},{10,11... | collective-permute-start | bytes 1179656 | tf_op jit(solution)/shard_map/ppermute | solution.py:19
  3.0 2.4 %collective-permute-start.1 = (bf16[8,96,256]{2,1,0:T(8,128)(2,1)S(1)}, bf16[8,96,256]{2,1,0:T(8,128)(2,1)S(1)}, u32[]{:S(2)}, u32[]{:S(2)}) collective-permute-start(bf16[8,96,256]{2,1,0:T(8,128)(2,1)S(1)} %bitcast.9), channel_id=1, source_target_pairs={{0,1},{1,0},{2,3},{3,2},{4,5},{5,4},{6,7},{7,6},{8,9},{9,8},{10,11... | collective-permute-start | bytes 1179656 | tf_op jit(solution)/shard_map/ppermute | solution.py:19
  4.8 2.0 %collective-permute-start.2 = (bf16[512,128]{1,0:T(8,128)(2,1)S(1)}, bf16[512,128]{1,0:T(8,128)(2,1)S(1)}, u32[]{:S(2)}, u32[]{:S(2)}) collective-permute-start(bf16[512,128]{1,0:T(8,128)(2,1)S(1)} %get-tuple-element.29), channel_id=1, source_target_pairs={{0,1},{1,0},{2,3},{3,2},{4,5},{5,4},{6,7},{7,6},{8,9},{9,8},{10,11... | collective-permute-start | bytes 393224 | tf_op jit(solution)/shard_map/ppermute | solution.py:218
  6.9 7.0 %collective-permute-start.3 = (bf16[704,128]{1,0:T(8,128)(2,1)S(1)}, bf16[704,128]{1,0:T(8,128)(2,1)S(1)}, u32[]{:S(2)}, u32[]{:S(2)}) collective-permute-start(bf16[704,128]{1,0:T(8,128)(2,1)S(1)} %get-tuple-element.31), channel_id=1, source_target_pairs={{0,6},{1,25},{2,4},{3,27},{4,2},{5,29},{6,0},{7,31},{8,14},{9,17},... | collective-permute-start | bytes 540680 | tf_op jit(solution)/shard_map/ppermute | solution.py:214
  10.5 5.5 %collective-permute-start.4 = (bf16[704,128]{1,0:T(8,128)(2,1)S(1)}, bf16[704,128]{1,0:T(8,128)(2,1)S(1)}, u32[]{:S(2)}, u32[]{:S(2)}) collective-permute-start(bf16[704,128]{1,0:T(8,128)(2,1)S(1)} %get-tuple-element.32), channel_id=1, source_target_pairs={{0,4},{1,17},{2,6},{3,19},{4,0},{5,21},{6,2},{7,23},{8,12},{9,25},... | collective-permute-start | bytes 540680 | tf_op jit(solution)/shard_map/ppermute | solution.py:214
  11.0 5.5 %collective-permute-start.5 = (bf16[704,128]{1,0:T(8,128)(2,1)S(1)}, bf16[704,128]{1,0:T(8,128)(2,1)S(1)}, u32[]{:S(2)}, u32[]{:S(2)}) collective-permute-start(bf16[704,128]{1,0:T(8,128)(2,1)S(1)} %get-tuple-element.33), channel_id=1, source_target_pairs={{0,2},{1,9},{2,0},{3,11},{4,6},{5,13},{6,4},{7,15},{8,10},{9,1},{1... | collective-permute-start | bytes 540680 | tf_op jit(solution)/shard_map/ppermute | solution.py:214
  16.6 7.5 %collective-permute-start.8 = (bf16[704,128]{1,0:T(8,128)(2,1)S(1)}, bf16[704,128]{1,0:T(8,128)(2,1)S(1)}, u32[]{:S(2)}, u32[]{:S(2)}) collective-permute-start(bf16[704,128]{1,0:T(8,128)(2,1)S(1)} %shard_map.89.own), channel_id=1, source_target_pairs={{0,24},{1,7},{2,26},{3,5},{4,28},{5,3},{6,30},{7,1},{8,16},{9,15},... | collective-permute-start | bytes 540680 | tf_op jit(solution)/shard_map/ppermute | solution.py:214
  20.2 8.7 %collective-permute-start.7 = (bf16[704,128]{1,0:T(8,128)(2,1)S(1)}, bf16[704,128]{1,0:T(8,128)(2,1)S(1)}, u32[]{:S(2)}, u32[]{:S(2)}) collective-permute-start(bf16[704,128]{1,0:T(8,128)(2,1)S(1)} %shard_map.89.own), channel_id=1, source_target_pairs={{0,16},{1,5},{2,18},{3,7},{4,20},{5,1},{6,22},{7,3},{8,24},{9,13},... | collective-permute-start | bytes 540680 | tf_op jit(solution)/shard_map/ppermute | solution.py:214
  20.2 8.7 %collective-permute-start.6 = (bf16[704,128]{1,0:T(8,128)(2,1)S(1)}, bf16[704,128]{1,0:T(8,128)(2,1)S(1)}, u32[]{:S(2)}, u32[]{:S(2)}) collective-permute-start(bf16[704,128]{1,0:T(8,128)(2,1)S(1)} %shard_map.89.own), channel_id=1, source_target_pairs={{0,8},{1,3},{2,10},{3,1},{4,12},{5,7},{6,14},{7,5},{8,0},{9,11},{1... | collective-permute-start | bytes 540680 | tf_op jit(solution)/shard_map/ppermute | solution.py:214
  29.0 5.6 %collective-permute-start.13 = (bf16[704,128]{1,0:T(8,128)(2,1)S(1)}, bf16[704,128]{1,0:T(8,128)(2,1)S(1)}, u32[]{:S(2)}, u32[]{:S(2)}) collective-permute-start(bf16[704,128]{1,0:T(8,128)(2,1)S(1)} %shard_map.90.refs_0_), channel_id=1, source_target_pairs={{0,2},{1,9},{2,0},{3,11},{4,6},{5,13},{6,4},{7,15},{8,10},{9,1},{1... | collective-permute-start | bytes 540680 | tf_op jit(solution)/shard_map/ppermute | solution.py:214
  30.6 5.5 %collective-permute-start.11 = (bf16[704,128]{1,0:T(8,128)(2,1)S(1)}, bf16[704,128]{1,0:T(8,128)(2,1)S(1)}, u32[]{:S(2)}, u32[]{:S(2)}) collective-permute-start(bf16[704,128]{1,0:T(8,128)(2,1)S(1)} %shard_map.90.refs_0_), channel_id=1, source_target_pairs={{0,4},{1,17},{2,6},{3,19},{4,0},{5,21},{6,2},{7,23},{8,12},{9,25},... | collective-permute-start | bytes 540680 | tf_op jit(solution)/shard_map/ppermute | solution.py:214
  31.6 6.4 %collective-permute-start.9 = (bf16[704,128]{1,0:T(8,128)(2,1)S(1)}, bf16[704,128]{1,0:T(8,128)(2,1)S(1)}, u32[]{:S(2)}, u32[]{:S(2)}) collective-permute-start(bf16[704,128]{1,0:T(8,128)(2,1)S(1)} %shard_map.90.refs_0_), channel_id=1, source_target_pairs={{0,6},{1,25},{2,4},{3,27},{4,2},{5,29},{6,0},{7,31},{8,14},{9,17},... | collective-permute-start | bytes 540680 | tf_op jit(solution)/shard_map/ppermute | solution.py:214
  32.6 5.4 %collective-permute-start.15 = (bf16[704,128]{1,0:T(8,128)(2,1)S(1)}, bf16[704,128]{1,0:T(8,128)(2,1)S(1)}, u32[]{:S(2)}, u32[]{:S(2)}) collective-permute-start(bf16[704,128]{1,0:T(8,128)(2,1)S(1)} %shard_map.90.refs_0_), channel_id=1, source_target_pairs={{0,1},{1,0},{2,3},{3,2},{4,5},{5,4},{6,7},{7,6},{8,9},{9,8},{10,11... | collective-permute-start | bytes 540680 | tf_op jit(solution)/shard_map/ppermute | solution.py:218
  34.6 4.4 %collective-permute-start.14 = (bf16[704,128]{1,0:T(8,128)(2,1)S(1)}, bf16[704,128]{1,0:T(8,128)(2,1)S(1)}, u32[]{:S(2)}, u32[]{:S(2)}) collective-permute-start(bf16[704,128]{1,0:T(8,128)(2,1)S(1)} %collective-permute-done.13.refs_3_), channel_id=1, source_target_pairs={{0,1},{1,0},{2,3},{3,2},{4,5},{5,4},{6,7},{7,6},{8,9},{9,8},{10,11... | collective-permute-start | bytes 540680 | tf_op jit(solution)/shard_map/ppermute | solution.py:218
  36.1 2.9 %collective-permute-start.12 = (bf16[704,128]{1,0:T(8,128)(2,1)S(1)}, bf16[704,128]{1,0:T(8,128)(2,1)S(1)}, u32[]{:S(2)}, u32[]{:S(2)}) collective-permute-start(bf16[704,128]{1,0:T(8,128)(2,1)S(1)} %collective-permute-done.11.refs_2_), channel_id=1, source_target_pairs={{0,1},{1,0},{2,3},{3,2},{4,5},{5,4},{6,7},{7,6},{8,9},{9,8},{10,11... | collective-permute-start | bytes 540680 | tf_op jit(solution)/shard_map/ppermute | solution.py:218
  38.0 1.4 %collective-permute-start.10 = (bf16[704,128]{1,0:T(8,128)(2,1)S(1)}, bf16[704,128]{1,0:T(8,128)(2,1)S(1)}, u32[]{:S(2)}, u32[]{:S(2)}) collective-permute-start(bf16[704,128]{1,0:T(8,128)(2,1)S(1)} %collective-permute-done.9.refs_1_), channel_id=1, source_target_pairs={{0,1},{1,0},{2,3},{3,2},{4,5},{5,4},{6,7},{7,6},{8,9},{9,8},{10,11... | collective-permute-start | bytes 540680 | tf_op jit(solution)/shard_map/ppermute | solution.py:218

commit v22 on v20

--- a/solution.py
+++ b/solution.py
@@ -180,7 +180,7 @@
     out[...] = total.astype(BF16)
 
 
-def finish_kernel(scale, own, one, two, three, _, out):
+def finish_kernel(scale, own, three, two, one, _, out):
     near = own[...].astype(F32) + one[...].astype(F32)
     far = two[...].astype(F32) + three[...].astype(F32)
     out[...] = ((near + far) * scale).astype(BF16)
@@ -237,7 +237,7 @@
     [total] = call(add_kernel, (quarter, BF16))(own, three, two, one)
     three, two, one = [exchange(total, 1, k) for k in (3, 2, 1)]
     finish = call(functools.partial(finish_kernel, scale), (quarter, BF16), in_specs=[vmem] * 4 + [far])
-    [total] = finish(total, one, two, three, after)
+    [total] = finish(total, three, two, one, after)
     three, two, one = [exchange(total, 0, k) for k in (3, 2, 1)]
     quarters = [total, one, two, three]
     results = [((length, 2 * width), BF16) for length in lengths]

time: 40.3 us -> 44.8 us (1.11)
  the two profiles are of different devices: /device:TPU:0 before, /device:TPU:17 now
where the time goes in v22:
time: 44.8 us; the launch traced here: 44.7 us
  starting transfers between devices  26.7 us (60%)
  Pallas kernels  9.67 us (22%)
  waiting for transfers between devices  7.57 us (17%)
  between operations  0.73 us (2%)
    ppermute x5, starting transfers between devices, swap(): return lax.ppermute(array, 'space', [(0, 1), (1, 0)])  14.3 us
    ppermute x9, starting transfers between devices, exchange(): return lax.ppermute(array, ('dp', 'space'), pairs)  11.5 us
    ppermute x9, waiting for transfers between devices, exchange(): return lax.ppermute(array, ('dp', 'space'), pairs)  7.53 us
    pallas_call x1, Pallas kernels, local(): pl.pallas_call(functools.partial(forward_kernel, peers), out_shape=[jax.S...  2.53 us
    pallas_call x2, Pallas kernels, sum_everywhere(): call(functools.partial(place_kernel, plan), *results, **place)  1.86 us
    pallas_call x1, Pallas kernels, local(): pl.pallas_call(merge_kernel, out_shape=[jax.ShapeDtypeStruct(shape, BF16)...  1.83 us
    pallas_call x1, Pallas kernels, local(): pl.pallas_call(functools.partial(data_grad_kernel, peers), out_shape=[jax...  1.7 us
    pallas_call x1, Pallas kernels, local(): pl.pallas_call(pair_kernel_grad_kernel, out_shape=jax.ShapeDtypeStruct((9...  1.45 us
  transfers between devices with their start and end apart: 16, of which 4 were waited for; matrix products, arithmetic and copies ran while one was open for 0% of the time, Pallas kernels for 19%

profile of v22, /device:TPU:17, one launch (start us, length us, event | category | flops | bytes accessed | tf_op | source)
XLA Modules:
  0.0 44.7 jit_solution(7374374889283722747)
XLA Ops:
  0.6 0.7 %collective-permute-start = (bf16[8,96,256]{2,1,0:T(8,128)(2,1)}, bf16[8,96,256]{2,1,0:T(8,128)(2,1)S(1)}, u32[]{:S(2)}, u32[]{:S(2)}) collective-permute-start(bf16[8,96,256]{2,1,0:T(8,128)(2,1)} %bitcast.16), channel_id=1, source_target_pairs={{0,1},{1,0},{2,3},{3,2},{4,5},{5,4},{6,7},{7,6},{8,9},{9,8},{10,11... | collective-permute-start | bytes 1179656 | tf_op jit(solution)/shard_map/ppermute | solution.py:19
  1.4 1.8 %shard_map.84 = (bf16[768,256]{1,0:T(8,128)(2,1)S(1)}, bf16[8,96,768]{2,1,0:T(8,128)(2,1)S(1)}, bf16[768,512]{1,0:T(8,128)(2,1)S(1)}, bf16[9,256,256]{2,1,0:T(8,128)(2,1)S(1)}) custom-call(bf16[8,96,256]{2,1,0:T(8,128)(2,1)} %bitcast.17, bf16[512,256]{1,0:T(8,128)(2,1)} %refs_1_.1, bf16[4,48,256]{2,1,0:T(8,128)(2,1)} %bitcast.18, bf16[768,512]{1,0:T(8,128)(2,1)} %bitcast.15, ...), custom_call_target="tpu_custom_call" | custom-call | flops 805306368 | bytes 4194304 | tf_op jit(solution)/shard_map/pallas_call | solution.py:273
  3.2 0.1 collective-permute-start.1
  3.3 1.7 %shard_map.85 = (bf16[768,256]{1,0:T(8,128)(2,1)S(1)}, bf16[2,96,768]{2,1,0:T(8,128)(2,1)}, f32[512,128]{1,0:T(8,128)S(1)}, bf16[512,128]{1,0:T(8,128)(2,1)S(1)}) custom-call(bf16[8,96,768]{2,1,0:T(8,128)(2,1)S(1)} %get-tuple-element.23.stack, bf16[8,96,256]{2,1,0:T(8,128)(2,1)S(1)} %collective-permute-done.before.after.cot, ...), custom_call_target="tpu_custom_call" | custom-call | flops 1107296256 | bytes 4194304 | tf_op jit(solution)/shard_map/pallas_call | solution.py:293
  5.0 0.6 %collective-permute-start.2 = (bf16[512,128]{1,0:T(8,128)(2,1)S(1)}, bf16[512,128]{1,0:T(8,128)(2,1)S(1)}, u32[]{:S(2)}, u32[]{:S(2)}) collective-permute-start(bf16[512,128]{1,0:T(8,128)(2,1)S(1)} %get-tuple-element.29), channel_id=1, source_target_pairs={{0,1},{1,0},{2,3},{3,2},{4,5},{5,4},{6,7},{7,6},{8,9},{9,8},{10,11... | collective-permute-start | bytes 393224 | tf_op jit(solution)/shard_map/ppermute | solution.py:218
  5.6 0.0 collective-permute-done.1.refs_0_.refs_1_
  5.6 1.5 %shard_map.87.kernel_sums = f32[2304,128]{1,0:T(8,128)S(1)} custom-call(bf16[8,96,768]{2,1,0:T(8,128)(2,1)S(1)} %get-tuple-element.23.stack, bf16[768,256]{1,0:T(8,128)(2,1)S(1)} %get-tuple-element.21.merged, bf16[8,96,256]{2,1,0:T(8,128)(2,1)S(1)} %collective-permute-done.before.after.cot, bf16[768,256]{1,0:T(8,128)(2,1)S(1)} %bitcast.11), custom_call_target="tpu_custom_call" | custom-call | flops 905969664 | bytes 4194304 | tf_op jit(solution)/shard_map/pallas_call | solution.py:310
  7.0 0.1 shard_map.88
  7.2 0.2 collective-permute-start.3
  7.4 3.2 %collective-permute-start.4 = (bf16[704,128]{1,0:T(8,128)(2,1)S(1)}, bf16[704,128]{1,0:T(8,128)(2,1)S(1)}, u32[]{:S(2)}, u32[]{:S(2)}) collective-permute-start(bf16[704,128]{1,0:T(8,128)(2,1)S(1)} %get-tuple-element.32), channel_id=1, source_target_pairs={{0,4},{1,17},{2,6},{3,19},{4,0},{5,21},{6,2},{7,23},{8,12},{9,25},... | collective-permute-start | bytes 540680 | tf_op jit(solution)/shard_map/ppermute | solution.py:214
  10.6 0.0 collective-permute-start.5
  10.6 3.1 %collective-permute-done.3.three = bf16[704,128]{1,0:T(8,128)(2,1)S(1)} collective-permute-done((bf16[704,128]{1,0:T(8,128)(2,1)S(1)}, bf16[704,128]{1,0:T(8,128)(2,1)S(1)}, u32[]{:S(2)}, u32[]{:S(2)}) %collective-permute-start.3) | collective-permute-done | bytes 180256 | tf_op jit(solution)/shard_map/ppermute | solution.py:214
  13.7 1.9 %collective-permute-done.4.two = bf16[704,128]{1,0:T(8,128)(2,1)S(1)} collective-permute-done((bf16[704,128]{1,0:T(8,128)(2,1)S(1)}, bf16[704,128]{1,0:T(8,128)(2,1)S(1)}, u32[]{:S(2)}, u32[]{:S(2)}) %collective-permute-start.4) | collective-permute-done | bytes 180256 | tf_op jit(solution)/shard_map/ppermute | solution.py:214
  15.6 0.1 shard_map.89.own
  15.7 1.3 %collective-permute-start.8 = (bf16[704,128]{1,0:T(8,128)(2,1)S(1)}, bf16[704,128]{1,0:T(8,128)(2,1)S(1)}, u32[]{:S(2)}, u32[]{:S(2)}) collective-permute-start(bf16[704,128]{1,0:T(8,128)(2,1)S(1)} %shard_map.89.own), channel_id=1, source_target_pairs={{0,8},{1,3},{2,10},{3,1},{4,12},{5,7},{6,14},{7,5},{8,0},{9,11},{1... | collective-permute-start | bytes 540680 | tf_op jit(solution)/shard_map/ppermute | solution.py:214
  17.0 1.2 %collective-permute-start.7 = (bf16[704,128]{1,0:T(8,128)(2,1)S(1)}, bf16[704,128]{1,0:T(8,128)(2,1)S(1)}, u32[]{:S(2)}, u32[]{:S(2)}) collective-permute-start(bf16[704,128]{1,0:T(8,128)(2,1)S(1)} %shard_map.89.own), channel_id=1, source_target_pairs={{0,16},{1,5},{2,18},{3,7},{4,20},{5,1},{6,22},{7,3},{8,24},{9,13},... | collective-permute-start | bytes 540680 | tf_op jit(solution)/shard_map/ppermute | solution.py:214
  18.2 0.2 collective-permute-start.6
  18.4 2.5 %shard_map.86 = (bf16[8,96,256]{2,1,0:T(8,128)(2,1)}, bf16[4,48,256]{2,1,0:T(8,128)(2,1)}) custom-call(bf16[8,96,256]{2,1,0:T(8,128)(2,1)S(1)} %bitcast.10, bf16[9,256,256]{2,1,0:T(8,128)(2,1)S(1)} %get-tuple-element.22.out_w, bf16[768,256]{1,0:T(8,128)(2,1)S(1)} %get-tuple-element.25.grad, bf16[8,96,256]{2,1,0:T(8,128)(2,1)S(1)} %collective-permute-done.1.refs_0_.refs_1_, ...), custom_call_target="tpu_custom_call" | custom-call | flops 905969664 | bytes 2097152 | tf_op jit(solution)/shard_map/pallas_call | solution.py:324
  21.0 0.0 collective-permute-done.8.one
  21.0 1.6 %collective-permute-done.7.two = bf16[704,128]{1,0:T(8,128)(2,1)S(1)} collective-permute-done((bf16[704,128]{1,0:T(8,128)(2,1)S(1)}, bf16[704,128]{1,0:T(8,128)(2,1)S(1)}, u32[]{:S(2)}, u32[]{:S(2)}) %collective-permute-start.7) | collective-permute-done | bytes 180256 | tf_op jit(solution)/shard_map/ppermute | solution.py:214
  22.6 0.9 %collective-permute-done.6.three = bf16[704,128]{1,0:T(8,128)(2,1)S(1)} collective-permute-done((bf16[704,128]{1,0:T(8,128)(2,1)S(1)}, bf16[704,128]{1,0:T(8,128)(2,1)S(1)}, u32[]{:S(2)}, u32[]{:S(2)}) %collective-permute-start.6) | collective-permute-done | bytes 180256 | tf_op jit(solution)/shard_map/ppermute | solution.py:214
  23.5 0.1 shard_map.90.refs_0_
  23.6 2.1 %collective-permute-start.13 = (bf16[704,128]{1,0:T(8,128)(2,1)S(1)}, bf16[704,128]{1,0:T(8,128)(2,1)S(1)}, u32[]{:S(2)}, u32[]{:S(2)}) collective-permute-start(bf16[704,128]{1,0:T(8,128)(2,1)S(1)} %shard_map.90.refs_0_), channel_id=1, source_target_pairs={{0,6},{1,25},{2,4},{3,27},{4,2},{5,29},{6,0},{7,31},{8,14},{9,17},... | collective-permute-start | bytes 540680 | tf_op jit(solution)/shard_map/ppermute | solution.py:214
  25.7 3.3 %collective-permute-start.11 = (bf16[704,128]{1,0:T(8,128)(2,1)S(1)}, bf16[704,128]{1,0:T(8,128)(2,1)S(1)}, u32[]{:S(2)}, u32[]{:S(2)}) collective-permute-start(bf16[704,128]{1,0:T(8,128)(2,1)S(1)} %shard_map.90.refs_0_), channel_id=1, source_target_pairs={{0,4},{1,17},{2,6},{3,19},{4,0},{5,21},{6,2},{7,23},{8,12},{9,25},... | collective-permute-start | bytes 540680 | tf_op jit(solution)/shard_map/ppermute | solution.py:214
  29.0 0.0 collective-permute-start.9
  29.0 8.3 %collective-permute-start.15 = (bf16[704,128]{1,0:T(8,128)(2,1)S(1)}, bf16[704,128]{1,0:T(8,128)(2,1)S(1)}, u32[]{:S(2)}, u32[]{:S(2)}) collective-permute-start(bf16[704,128]{1,0:T(8,128)(2,1)S(1)} %shard_map.90.refs_0_), channel_id=1, source_target_pairs={{0,1},{1,0},{2,3},{3,2},{4,5},{5,4},{6,7},{7,6},{8,9},{9,8},{10,11... | collective-permute-start | bytes 540680 | tf_op jit(solution)/shard_map/ppermute | solution.py:218
  37.3 2.6 %collective-permute-start.14 = (bf16[704,128]{1,0:T(8,128)(2,1)S(1)}, bf16[704,128]{1,0:T(8,128)(2,1)S(1)}, u32[]{:S(2)}, u32[]{:S(2)}) collective-permute-start(bf16[704,128]{1,0:T(8,128)(2,1)S(1)} %collective-permute-done.13.refs_3_), channel_id=1, source_target_pairs={{0,1},{1,0},{2,3},{3,2},{4,5},{5,4},{6,7},{7,6},{8,9},{9,8},{10,11... | collective-permute-start | bytes 540680 | tf_op jit(solution)/shard_map/ppermute | solution.py:218
  39.9 2.0 %collective-permute-start.12 = (bf16[704,128]{1,0:T(8,128)(2,1)S(1)}, bf16[704,128]{1,0:T(8,128)(2,1)S(1)}, u32[]{:S(2)}, u32[]{:S(2)}) collective-permute-start(bf16[704,128]{1,0:T(8,128)(2,1)S(1)} %collective-permute-done.11.refs_2_), channel_id=1, source_target_pairs={{0,1},{1,0},{2,3},{3,2},{4,5},{5,4},{6,7},{7,6},{8,9},{9,8},{10,11... | collective-permute-start | bytes 540680 | tf_op jit(solution)/shard_map/ppermute | solution.py:218
  41.9 0.8 %collective-permute-start.10 = (bf16[704,128]{1,0:T(8,128)(2,1)S(1)}, bf16[704,128]{1,0:T(8,128)(2,1)S(1)}, u32[]{:S(2)}, u32[]{:S(2)}) collective-permute-start(bf16[704,128]{1,0:T(8,128)(2,1)S(1)} %collective-permute-done.9.refs_1_), channel_id=1, source_target_pairs={{0,1},{1,0},{2,3},{3,2},{4,5},{5,4},{6,7},{7,6},{8,9},{9,8},{10,11... | collective-permute-start | bytes 540680 | tf_op jit(solution)/shard_map/ppermute | solution.py:218
  42.8 1.0 %shard_map.91 = (bf16[2304,256]{1,0:T(8,128)(2,1)}, bf16[512,256]{1,0:T(8,128)(2,1)}) custom-call(bf16[704,128]{1,0:T(8,128)(2,1)S(1)} %shard_map.90.refs_0_, bf16[704,128]{1,0:T(8,128)(2,1)S(1)} %collective-permute-done.9.refs_1_, bf16[704,128]{1,0:T(8,128)(2,1)S(1)} %collective-permute-done.11.refs_2_, ...), custom_call_target="tpu_custom_call" | custom-call | tf_op jit(solution)/shard_map/pallas_call | solution.py:247
  43.8 0.0 collective-permute-done.10.refs_0_
  43.8 0.9 %shard_map.92 = (bf16[2304,256]{1,0:T(8,128)(2,1)}, bf16[512,256]{1,0:T(8,128)(2,1)}) custom-call(bf16[704,128]{1,0:T(8,128)(2,1)S(1)} %collective-permute-done.10.refs_0_, bf16[704,128]{1,0:T(8,128)(2,1)S(1)} %collective-permute-done.12.refs_1_, bf16[704,128]{1,0:T(8,128)(2,1)S(1)} %collective-permute-done.14.refs_2_, ...), custom_call_target="tpu_custom_call", output_to_operand_aliasing={{0}: (3, {}), {1}: (4, {})} | custom-call | tf_op jit(solution)/shard_map/pallas_call | solution.py:250
  (9 shorter events, 0.0 us)
Async XLA Ops:
  0.6 2.7 %collective-permute-start = (bf16[8,96,256]{2,1,0:T(8,128)(2,1)}, bf16[8,96,256]{2,1,0:T(8,128)(2,1)S(1)}, u32[]{:S(2)}, u32[]{:S(2)}) collective-permute-start(bf16[8,96,256]{2,1,0:T(8,128)(2,1)} %bitcast.16), channel_id=1, source_target_pairs={{0,1},{1,0},{2,3},{3,2},{4,5},{5,4},{6,7},{7,6},{8,9},{9,8},{10,11... | collective-permute-start | bytes 1179656 | tf_op jit(solution)/shard_map/ppermute | solution.py:19
  3.2 2.4 %collective-permute-start.1 = (bf16[8,96,256]{2,1,0:T(8,128)(2,1)S(1)}, bf16[8,96,256]{2,1,0:T(8,128)(2,1)S(1)}, u32[]{:S(2)}, u32[]{:S(2)}) collective-permute-start(bf16[8,96,256]{2,1,0:T(8,128)(2,1)S(1)} %bitcast.9), channel_id=1, source_target_pairs={{0,1},{1,0},{2,3},{3,2},{4,5},{5,4},{6,7},{7,6},{8,9},{9,8},{10,11... | collective-permute-start | bytes 1179656 | tf_op jit(solution)/shard_map/ppermute | solution.py:19
  5.0 2.0 %collective-permute-start.2 = (bf16[512,128]{1,0:T(8,128)(2,1)S(1)}, bf16[512,128]{1,0:T(8,128)(2,1)S(1)}, u32[]{:S(2)}, u32[]{:S(2)}) collective-permute-start(bf16[512,128]{1,0:T(8,128)(2,1)S(1)} %get-tuple-element.29), channel_id=1, source_target_pairs={{0,1},{1,0},{2,3},{3,2},{4,5},{5,4},{6,7},{7,6},{8,9},{9,8},{10,11... | collective-permute-start | bytes 393224 | tf_op jit(solution)/shard_map/ppermute | solution.py:218
  7.2 6.5 %collective-permute-start.3 = (bf16[704,128]{1,0:T(8,128)(2,1)S(1)}, bf16[704,128]{1,0:T(8,128)(2,1)S(1)}, u32[]{:S(2)}, u32[]{:S(2)}) collective-permute-start(bf16[704,128]{1,0:T(8,128)(2,1)S(1)} %get-tuple-element.31), channel_id=1, source_target_pairs={{0,6},{1,25},{2,4},{3,27},{4,2},{5,29},{6,0},{7,31},{8,14},{9,17},... | collective-permute-start | bytes 540680 | tf_op jit(solution)/shard_map/ppermute | solution.py:214
  7.4 8.2 %collective-permute-start.4 = (bf16[704,128]{1,0:T(8,128)(2,1)S(1)}, bf16[704,128]{1,0:T(8,128)(2,1)S(1)}, u32[]{:S(2)}, u32[]{:S(2)}) collective-permute-start(bf16[704,128]{1,0:T(8,128)(2,1)S(1)} %get-tuple-element.32), channel_id=1, source_target_pairs={{0,4},{1,17},{2,6},{3,19},{4,0},{5,21},{6,2},{7,23},{8,12},{9,25},... | collective-permute-start | bytes 540680 | tf_op jit(solution)/shard_map/ppermute | solution.py:214
  10.6 5.0 %collective-permute-start.5 = (bf16[704,128]{1,0:T(8,128)(2,1)S(1)}, bf16[704,128]{1,0:T(8,128)(2,1)S(1)}, u32[]{:S(2)}, u32[]{:S(2)}) collective-permute-start(bf16[704,128]{1,0:T(8,128)(2,1)S(1)} %get-tuple-element.33), channel_id=1, source_target_pairs={{0,2},{1,9},{2,0},{3,11},{4,6},{5,13},{6,4},{7,15},{8,10},{9,1},{1... | collective-permute-start | bytes 540680 | tf_op jit(solution)/shard_map/ppermute | solution.py:214
  15.7 5.3 %collective-permute-start.8 = (bf16[704,128]{1,0:T(8,128)(2,1)S(1)}, bf16[704,128]{1,0:T(8,128)(2,1)S(1)}, u32[]{:S(2)}, u32[]{:S(2)}) collective-permute-start(bf16[704,128]{1,0:T(8,128)(2,1)S(1)} %shard_map.89.own), channel_id=1, source_target_pairs={{0,8},{1,3},{2,10},{3,1},{4,12},{5,7},{6,14},{7,5},{8,0},{9,11},{1... | collective-permute-start | bytes 540680 | tf_op jit(solution)/shard_map/ppermute | solution.py:214
  17.0 5.6 %collective-permute-start.7 = (bf16[704,128]{1,0:T(8,128)(2,1)S(1)}, bf16[704,128]{1,0:T(8,128)(2,1)S(1)}, u32[]{:S(2)}, u32[]{:S(2)}) collective-permute-start(bf16[704,128]{1,0:T(8,128)(2,1)S(1)} %shard_map.89.own), channel_id=1, source_target_pairs={{0,16},{1,5},{2,18},{3,7},{4,20},{5,1},{6,22},{7,3},{8,24},{9,13},... | collective-permute-start | bytes 540680 | tf_op jit(solution)/shard_map/ppermute | solution.py:214
  18.2 5.2 %collective-permute-start.6 = (bf16[704,128]{1,0:T(8,128)(2,1)S(1)}, bf16[704,128]{1,0:T(8,128)(2,1)S(1)}, u32[]{:S(2)}, u32[]{:S(2)}) collective-permute-start(bf16[704,128]{1,0:T(8,128)(2,1)S(1)} %shard_map.89.own), channel_id=1, source_target_pairs={{0,24},{1,7},{2,26},{3,5},{4,28},{5,3},{6,30},{7,1},{8,16},{9,15},... | collective-permute-start | bytes 540680 | tf_op jit(solution)/shard_map/ppermute | solution.py:214
  23.6 13.7 %collective-permute-start.13 = (bf16[704,128]{1,0:T(8,128)(2,1)S(1)}, bf16[704,128]{1,0:T(8,128)(2,1)S(1)}, u32[]{:S(2)}, u32[]{:S(2)}) collective-permute-start(bf16[704,128]{1,0:T(8,128)(2,1)S(1)} %shard_map.90.refs_0_), channel_id=1, source_target_pairs={{0,6},{1,25},{2,4},{3,27},{4,2},{5,29},{6,0},{7,31},{8,14},{9,17},... | collective-permute-start | bytes 540680 | tf_op jit(solution)/shard_map/ppermute | solution.py:214
  25.7 14.2 %collective-permute-start.11 = (bf16[704,128]{1,0:T(8,128)(2,1)S(1)}, bf16[704,128]{1,0:T(8,128)(2,1)S(1)}, u32[]{:S(2)}, u32[]{:S(2)}) collective-permute-start(bf16[704,128]{1,0:T(8,128)(2,1)S(1)} %shard_map.90.refs_0_), channel_id=1, source_target_pairs={{0,4},{1,17},{2,6},{3,19},{4,0},{5,21},{6,2},{7,23},{8,12},{9,25},... | collective-permute-start | bytes 540680 | tf_op jit(solution)/shard_map/ppermute | solution.py:214
  29.0 12.9 %collective-permute-start.9 = (bf16[704,128]{1,0:T(8,128)(2,1)S(1)}, bf16[704,128]{1,0:T(8,128)(2,1)S(1)}, u32[]{:S(2)}, u32[]{:S(2)}) collective-permute-start(bf16[704,128]{1,0:T(8,128)(2,1)S(1)} %shard_map.90.refs_0_), channel_id=1, source_target_pairs={{0,2},{1,9},{2,0},{3,11},{4,6},{5,13},{6,4},{7,15},{8,10},{9,1},{1... | collective-permute-start | bytes 540680 | tf_op jit(solution)/shard_map/ppermute | solution.py:214
  29.0 13.8 %collective-permute-start.15 = (bf16[704,128]{1,0:T(8,128)(2,1)S(1)}, bf16[704,128]{1,0:T(8,128)(2,1)S(1)}, u32[]{:S(2)}, u32[]{:S(2)}) collective-permute-start(bf16[704,128]{1,0:T(8,128)(2,1)S(1)} %shard_map.90.refs_0_), channel_id=1, source_target_pairs={{0,1},{1,0},{2,3},{3,2},{4,5},{5,4},{6,7},{7,6},{8,9},{9,8},{10,11... | collective-permute-start | bytes 540680 | tf_op jit(solution)/shard_map/ppermute | solution.py:218
  37.3 6.5 %collective-permute-start.14 = (bf16[704,128]{1,0:T(8,128)(2,1)S(1)}, bf16[704,128]{1,0:T(8,128)(2,1)S(1)}, u32[]{:S(2)}, u32[]{:S(2)}) collective-permute-start(bf16[704,128]{1,0:T(8,128)(2,1)S(1)} %collective-permute-done.13.refs_3_), channel_id=1, source_target_pairs={{0,1},{1,0},{2,3},{3,2},{4,5},{5,4},{6,7},{7,6},{8,9},{9,8},{10,11... | collective-permute-start | bytes 540680 | tf_op jit(solution)/shard_map/ppermute | solution.py:218
  39.9 3.9 %collective-permute-start.12 = (bf16[704,128]{1,0:T(8,128)(2,1)S(1)}, bf16[704,128]{1,0:T(8,128)(2,1)S(1)}, u32[]{:S(2)}, u32[]{:S(2)}) collective-permute-start(bf16[704,128]{1,0:T(8,128)(2,1)S(1)} %collective-permute-done.11.refs_2_), channel_id=1, source_target_pairs={{0,1},{1,0},{2,3},{3,2},{4,5},{5,4},{6,7},{7,6},{8,9},{9,8},{10,11... | collective-permute-start | bytes 540680 | tf_op jit(solution)/shard_map/ppermute | solution.py:218
  41.9 1.9 %collective-permute-start.10 = (bf16[704,128]{1,0:T(8,128)(2,1)S(1)}, bf16[704,128]{1,0:T(8,128)(2,1)S(1)}, u32[]{:S(2)}, u32[]{:S(2)}) collective-permute-start(bf16[704,128]{1,0:T(8,128)(2,1)S(1)} %collective-permute-done.9.refs_1_), channel_id=1, source_target_pairs={{0,1},{1,0},{2,3},{3,2},{4,5},{5,4},{6,7},{7,6},{8,9},{9,8},{10,11... | collective-permute-start | bytes 540680 | tf_op jit(solution)/shard_map/ppermute | solution.py:218
